TPU v7x, 128 devices: a whole 4x4x4 slice. The times are simulated.
128 devices in a mesh: tower: 4 (over x_lo, core), dp: 32 (over z, x_hi, y).
Axes of the slice: x: 4 (x_hi: 2, x_lo: 2; x = x_hi * 2 + x_lo), y: 4, z: 4, core: 2. Of those that a mesh axis runs over, the one named last changes fastest.
Arguments:
- image_feats: bfloat16 [12288, 1664], P('dp'), may hold values from -80 to 80
- text_feats: bfloat16 [12288, 1024], P('dp'), may hold values from -80 to 80
- image_weight: bfloat16 [1664, 1024], replicated, may hold values from -0.15625 to 0.15625
- text_weight: bfloat16 [1024, 1024], replicated, may hold values from -0.1875 to 0.1875
- partner: int32 [12288], P('dp'), may hold values from 0 to 12287, each once
- log_scale: float32 [1], replicated, may hold values from 2.1 to 2.5
- logit_bias: float32 [1], replicated, may hold values from -10 to -8
Outputs:
- proj_grads: float32 [2688, 1024], P(('tower', 'dp'))
All inputs are finite; a program needn't handle non-finite values.
Results may differ from a plain program's by a relative error of at most 0.00055.
The roundings to bfloat16 on the way count: a program that leaves them out, or rounds other values in their place, can miss the bound.
Values may be sent and summed in bfloat16 or wider, within the bound.
No kernel may reach another device: no remote copies, remote signals or barrier semaphores. Data moves between devices by JAX's collectives and lax.ppermute only.
A program may use at most 128 MiB of HBM per device.

v0:
```python
import jax
import jax.numpy as jnp
from jax import lax
from jax.sharding import Mesh, PartitionSpec as P

AXES = ("xl", "core", "z", "xh", "y")
SIZES = {"xl": 2, "core": 2, "z": 4, "xh": 2, "y": 4}
DP = ("z", "xh", "y")
TOWER = ("xl", "core")
GROUP = 24
SWAP = [(0, 1), (1, 0)]
FLIP = [(0, 3), (1, 2), (2, 1), (3, 0)]


def embed_rows(features, weight):
    projected = jnp.dot(features, weight, preferred_element_type=jnp.float32)
    inverse = lax.rsqrt(jnp.sum(projected * projected, axis=1) + 1e-06).astype(jnp.bfloat16)
    inverse = lax.optimization_barrier(inverse)
    embedded = (projected * inverse.astype(jnp.float32)[:, None]).astype(jnp.bfloat16)
    return (lax.optimization_barrier(embedded), inverse)


def back_rows(embedded, inverse, gradients):
    widened = embedded.astype(jnp.float32)
    inner_sum = jnp.sum(widened * gradients, axis=1, keepdims=True)
    return (inverse.astype(jnp.float32)[:, None] * (gradients - widened * inner_sum)).astype(
        jnp.bfloat16
    )


def body(image_feats, text_feats, image_weight, text_weight, partner, log_scale, logit_bias):
    rows, width = text_feats.shape[0], image_weight.shape[1]
    half, quarter = rows // 2, rows // 4
    out_rows = (image_feats.shape[1] + text_feats.shape[1]) // 4
    own_rows = out_rows // 32
    xl, core = lax.axis_index("xl"), lax.axis_index("core")
    z, xh, y = lax.axis_index("z"), lax.axis_index("xh"), lax.axis_index("y")
    text_half = jnp.where(xl == xh, 0, 1)
    text_quarter = text_half * 2 + core
    logit_scale = jnp.exp(log_scale[0])
    logit_shift = logit_bias[0]

    def rows_at(array, start, count):
        return lax.dynamic_slice_in_dim(array, start, count, 0)

    half_images, image_inverse = embed_rows(rows_at(image_feats, core * half, half), image_weight)
    own_texts, text_inverse = embed_rows(
        rows_at(text_feats, text_quarter * quarter, quarter), text_weight
    )
    other_texts = lax.ppermute(own_texts, ("xl", "xh"), FLIP)
    pair_texts = jnp.concatenate([own_texts, other_texts], 0)
    sent = jnp.broadcast_to(pair_texts[None], (4, half, width))
    texts = lax.all_to_all(sent, "y", split_axis=0, concat_axis=0, tiled=True)
    texts = texts.reshape(4 * half, width)
    mine = lax.all_gather(half_images, "z", axis=0, tiled=True)
    theirs = lax.ppermute(mine, "core", SWAP)
    images = jnp.concatenate([mine, theirs], 0)

    sent = jnp.broadcast_to(partner[None], (4, rows))
    partners = lax.all_to_all(sent, "z", split_axis=0, concat_axis=0, tiled=True)
    partners = partners.reshape(4, 2, half)
    partners = jnp.concatenate(
        [
            lax.dynamic_index_in_dim(partners, core, 1, keepdims=False).reshape(-1),
            lax.dynamic_index_in_dim(partners, 1 - core, 1, keepdims=False).reshape(-1),
        ]
    )

    logits = (
        logit_scale
        * lax.dot_general(
            images, texts, (((1,), (1,)), ((), ())), preferred_element_type=jnp.float32
        )
        + logit_shift
    )
    place = lax.iota(jnp.int32, 4 * half)
    text_xh = jnp.where(place % half < quarter, xh, 1 - xh)
    columns = ((z * 2 + text_xh) * 4 + place // half) * rows
    columns = columns + text_quarter * quarter + place % quarter
    labels = jnp.where(partners[:, None] == columns[None, :], 1.0, -1.0).astype(jnp.float32)
    slopes = -labels * jax.nn.sigmoid(-labels * logits)
    coefficient = (logit_scale * slopes).astype(jnp.bfloat16)
    given = jnp.dot(coefficient[4 * half :], texts, preferred_element_type=jnp.float32)
    taken = lax.ppermute(given, "core", SWAP)
    text_part = lax.dot_general(
        coefficient, images, (((0,), (0,)), ((), ())), preferred_element_type=jnp.float32
    )
    kept = jnp.dot(coefficient[: 4 * half], texts, preferred_element_type=jnp.float32)

    image_sum = lax.psum_scatter(kept + taken, "z", scatter_dimension=0, tiled=True)
    image_got = lax.ppermute(rows_at(image_sum, (1 - xl) * quarter, quarter), "xl", SWAP)
    image_grad = rows_at(image_sum, xl * quarter, quarter) + image_got

    text_terms = lax.all_to_all(
        text_part.reshape(4, half, width), "y", split_axis=0, concat_axis=0, tiled=True
    )
    text_sum = jnp.sum(text_terms, axis=0)
    text_grad = text_sum[:quarter] + lax.ppermute(text_sum[quarter:], ("xl", "xh"), FLIP)

    image_back = back_rows(
        rows_at(half_images, xl * quarter, quarter),
        rows_at(image_inverse, xl * quarter, quarter),
        image_grad,
    )
    text_back = back_rows(own_texts, text_inverse, text_grad)
    image_backs = lax.all_gather(image_back, TOWER, axis=0, tiled=True)
    text_backs = lax.all_gather(text_back, TOWER, axis=0, tiled=True)

    image_order = jnp.concatenate(
        [image_feats[i * quarter : (i + 1) * quarter] for i in (0, 2, 1, 3)], 0
    )
    text_order = jnp.concatenate(
        [rows_at(text_feats, xh * half, half), rows_at(text_feats, (1 - xh) * half, half)], 0
    )
    tower = xl * 2 + core
    place = lax.iota(jnp.int32, 32 * GROUP)
    wanted = tower * out_rows + (place // GROUP) * own_rows + place % GROUP
    wanted = jnp.where(place % GROUP < own_rows, wanted, -1)

    def chosen(feats, first):
        index = first + lax.iota(jnp.int32, feats.shape[1])
        select = (wanted[:, None] == index[None, :]).astype(jnp.bfloat16)
        return lax.dot_general(
            select, feats, (((1,), (1,)), ((), ())), preferred_element_type=jnp.float32
        ).astype(jnp.bfloat16)

    image_columns = chosen(image_order, 0)
    text_columns = chosen(text_order, image_feats.shape[1])
    terms = jnp.dot(image_columns, image_backs, preferred_element_type=jnp.float32) + jnp.dot(
        text_columns, text_backs, preferred_element_type=jnp.float32
    )
    spread = lax.all_to_all(
        terms.reshape(32, GROUP, width), DP, split_axis=0, concat_axis=0, tiled=True
    )
    return jnp.sum(spread, axis=0)[:own_rows]


def solution(mesh):
    fine = Mesh(mesh.devices.reshape([SIZES[a] for a in AXES]), AXES)
    placed = (P(DP, None), P(DP, None), P(), P(), P(DP), P(), P())
    return jax.shard_map(
        body, mesh=fine, in_specs=placed, out_specs=P(TOWER + DP, None), check_vma=False
    )
```

profile of v0, /device:TPU:1, one launch (start us, length us, event | category | flops | bytes accessed | tf_op | source)
XLA Modules:
  0.0 262.5 jit_solution(4278210465322844681)
XLA Ops:
  6.5 2.0 copy-done
  8.5 2.1 multiply_reduce_fusion
  11.5 3.0 %multiply_reduce_fusion.1 = (f32[96]{0:T(128)S(1)}, f32[96,1024]{1,0:T(8,128)}) fusion(bf16[1024,1024]{1,0:T(8,128)(2,1)} %param.10, bf16[384,1024]{1,0:T(8,128)(2,1)} %param.8, s32[]{:T(128)S(6)} %select_n.111), kind=kOutput, calls=%fused_computation.46 | convolution fusion | flops 201523104 | bytes 2687364 | tf_op jit(solution)/shard_map/dot_general | solution.py:16
  14.6 27.0 %all-gather.2.cloned.1.call-done = bf16[768,1024]{1,0:T(8,128)(2,1)} async-done(((bf16[192,1024]{1,0:T(8,128)(2,1)}), bf16[768,1024]{1,0:T(8,128)(2,1)}) %all-gather.2.cloned.1.call-update) | async-done | bytes 1572880 | tf_op jit(solution)/shard_map/all_gather | solution.py:55
  44.1 2.4 collective-permute-start.1
  47.1 3.2 %all-to-all-start = ((s32[4,1,384]{2,1,0:T(1,128)}), s32[4,1,384]{2,1,0:T(1,128)S(1)}, u32[]{:S(2)}, u32[]{:S(2)}) async-start(s32[4,1,384]{2,1,0:T(1,128)} %broadcast_in_dim.21), calls=%async_computation | async-start | bytes 12288 | tf_op jit(solution)/shard_map/all_to_all | solution.py:60
  50.3 1.8 collective-permute-done.1
  52.1 1.8 pad_maximum_fusion
  54.5 2.4 broadcast_in_dim.27
  56.8 4.3 %all-to-all-start.1 = ((bf16[4,192,1024]{2,1,0:T(8,128)(2,1)}), bf16[4,192,1024]{2,1,0:T(8,128)(2,1)}, u32[]{:S(2)}, u32[]{:S(2)}) async-start(bf16[4,192,1024]{2,1,0:T(8,128)(2,1)} %broadcast_in_dim.27), calls=%async_computation.1 | async-start | bytes 3145728 | tf_op jit(solution)/shard_map/all_to_all | solution.py:53
  62.9 2.7 %constant_dynamic-update-slice_fusion.1 = bf16[1536,1024]{1,0:T(8,128)(2,1)} fusion(bf16[768,1024]{1,0:T(8,128)(2,1)} %all-gather.2.cloned.1.call-done), kind=kLoop, calls=%fused_computation.51 | loop fusion | bytes 3145728
  65.6 2.8 %constant_dynamic-update-slice_fusion = bf16[1536,1024]{1,0:T(8,128)(2,1)} fusion(bf16[1536,1024]{1,0:T(8,128)(2,1)} %constant_dynamic-update-slice_fusion.1, bf16[768,1024]{1,0:T(8,128)(2,1)} %collective-permute-done), kind=kLoop, calls=%fused_computation.50 | loop fusion | bytes 3145728 | tf_op jit(solution)/shard_map/concatenate | solution.py:57
  68.3 12.2 %all-to-all-done.1 = bf16[4,192,1024]{2,1,0:T(8,128)(2,1)} async-done(((bf16[4,192,1024]{2,1,0:T(8,128)(2,1)}), bf16[4,192,1024]{2,1,0:T(8,128)(2,1)}, u32[]{:S(2)}, u32[]{:S(2)}) %all-to-all-start.1) | async-done | bytes 1572896 | tf_op jit(solution)/shard_map/all_to_all | solution.py:53
  80.5 6.4 %multiply_convert_fusion = bf16[1536,768]{1,0:T(8,128)(2,1)S(1)} fusion(bf16[1536,1024]{1,0:T(8,128)(2,1)} %constant_dynamic-update-slice_fusion, bf16[768,1024]{1,0:T(8,128)(2,1)} %bitcast.1, f32[]{:T(128)} %bitcast.16, s32[768]{0:T(1024)S(1)} %fusion.58, f32[]{:T(128)} %bitcast, s32[1536]{0:T(1024)S(1)} %pad_add_fusion), kind=kOutput, calls=%fused_computation.2 | convolution fusion | flops 2430074880 | bytes 7087112 | tf_op jit(solution)/shard_map/dot_general | solution.py:71
  87.0 3.6 %fusion.24 = f32[768,1024]{1,0:T(8,128)S(1)} fusion(bf16[768,1024]{1,0:T(8,128)(2,1)} %bitcast.1, bf16[1536,768]{1,0:T(8,128)(2,1)S(1)} %multiply_convert_fusion), kind=kOutput, calls=%fused_computation.20 | convolution fusion | flops 1207959552 | bytes 5898240 | tf_op jit(solution)/shard_map/dot_general | solution.py:83
  90.6 2.4 collective-permute-start.2
  93.1 5.3 %collective-permute-done.2 = f32[768,1024]{1,0:T(8,128)S(1)} collective-permute-done((f32[768,1024]{1,0:T(8,128)S(1)}, f32[768,1024]{1,0:T(8,128)S(1)}, u32[]{:S(2)}, u32[]{:S(2)}) %collective-permute-start.2) | collective-permute-done | bytes 3145760 | tf_op jit(solution)/shard_map/ppermute | solution.py:84
  98.4 4.5 %convolution_add_fusion.1 = f32[768,1024]{1,0:T(8,128)} fusion(f32[768,1024]{1,0:T(8,128)S(1)} %collective-permute-done.2, bf16[768,1024]{1,0:T(8,128)(2,1)} %bitcast.1, bf16[1536,768]{1,0:T(8,128)(2,1)S(1)} %multiply_convert_fusion), kind=kOutput, calls=%fused_computation.7 | convolution fusion | flops 1208745984 | bytes 9043968 | tf_op jit(solution)/shard_map/dot_general | solution.py:88
  102.9 7.0 %fusion.76 = f32[768,1024]{1,0:T(8,128)} fusion(bf16[1536,768]{1,0:T(8,128)(2,1)} %copy-done.6, bf16[1536,1024]{1,0:T(8,128)(2,1)} %constant_dynamic-update-slice_fusion), kind=kOutput, calls=%fused_computation.98 | convolution fusion | flops 2415919104 | bytes 8650752 | tf_op jit(solution)/shard_map/dot_general | solution.py:85
  109.8 4.6 %all-to-all-start.2 = ((f32[4,192,1024]{2,1,0:T(8,128)}), f32[4,192,1024]{2,1,0:T(8,128)}, u32[]{:S(2)}, u32[]{:S(2)}) async-start(f32[4,192,1024]{2,1,0:T(8,128)} %bitcast.17), calls=%async_computation.3 | async-start | bytes 6291456 | tf_op jit(solution)/shard_map/all_to_all | solution.py:94
  114.6 2.1 constant_dynamic-slice_fusion.1
  116.7 35.1 %all-to-all-done.2 = f32[4,192,1024]{2,1,0:T(8,128)} async-done(((f32[4,192,1024]{2,1,0:T(8,128)}), f32[4,192,1024]{2,1,0:T(8,128)}, u32[]{:S(2)}, u32[]{:S(2)}) %all-to-all-start.2) | async-done | bytes 3145760 | tf_op jit(solution)/shard_map/all_to_all | solution.py:94
  151.9 3.1 %reduce_sum.57 = f32[192,1024]{1,0:T(8,128)} reduce(f32[4,192,1024]{2,1,0:T(8,128)} %all-to-all-done.2, f32[]{:T(128)} %constant.86.clone.1), dimensions={0}, to_apply=%region_4.5 | reduce | flops 589824 | bytes 3932164 | tf_op jit(solution)/shard_map/reduce_sum | solution.py:97
  156.1 2.1 collective-permute-start.4
  158.2 2.3 fusion.75
  160.6 6.4 %collective-permute-done.4 = f32[96,1024]{1,0:T(8,128)S(1)} collective-permute-done((f32[96,1024]{1,0:T(8,128)S(1)}, f32[96,1024]{1,0:T(8,128)S(1)}, u32[]{:S(2)}, u32[]{:S(2)}) %collective-permute-start.4) | collective-permute-done | bytes 393248 | tf_op jit(solution)/shard_map/ppermute | solution.py:98
  171.4 15.6 %all_gather.11 = bf16[384,1024]{1,0:T(8,128)(2,1)} all-gather(bf16[96,1024]{1,0:T(8,128)(2,1)S(1)} %fusion.44), channel_id=1, replica_groups=mesh['xl'=2,'core'=2,'z'=4,'xh'=2,'y'=4] {'xl','core'}, dimensions={0}, use_global_device_ids=true | all-gather | bytes 983040 | tf_op jit(solution)/shard_map/all_gather | solution.py:107
  187.3 9.2 %all_gather.10 = bf16[384,1024]{1,0:T(8,128)(2,1)} all-gather(bf16[96,1024]{1,0:T(8,128)(2,1)S(1)} %fusion.40), channel_id=1, replica_groups=mesh['xl'=2,'core'=2,'z'=4,'xh'=2,'y'=4] {'xl','core'}, dimensions={0}, use_global_device_ids=true | all-gather | bytes 983040 | tf_op jit(solution)/shard_map/all_gather | solution.py:106
  196.5 5.6 %fusion.14 = f32[768,1024]{1,0:T(8,128)} fusion(bf16[384,1024]{1,0:T(8,128)(2,1)} %all_gather.10, s32[768]{0:T(1024)S(1)} %fusion.50, bf16[96,1664]{1,0:T(8,128)(2,1)} %get-tuple-element.10, bf16[96,1664]{1,0:T(8,128)(2,1)} %get-tuple-element.8, bf16[96,1664]{1,0:T(8,128)(2,1)} %get-tuple-element.9, bf16[96,1664]{1,0:T(8,128)(2,1)} %get-tuple-element.7), kind=kOutput, calls=%fused_computation.15 | convolution fusion | flops 1592131584 | bytes 5213184 | tf_op jit(solution)/shard_map/dot_general | solution.py:129
  202.1 5.9 %convolution_add_fusion = f32[768,1024]{1,0:T(8,128)} fusion(f32[768,1024]{1,0:T(8,128)} %fusion.14, bf16[384,1024]{1,0:T(8,128)(2,1)} %all_gather.11, s32[1024]{0:T(1024)S(1)} %iota_add_fusion, s32[768]{0:T(1024)S(1)} %fusion.50, bf16[192,1024]{1,0:T(8,128)(2,1)} %get-tuple-element.12, bf16[192,1024]{1,0:T(8,128)(2,1)} %get-tuple-element.11), kind=kOutput, calls=%fused_computation.6 | convolution fusion | flops 1211400192 | bytes 7871488 | tf_op jit(solution)/shard_map/dot_general | solution.py:129
  208.0 45.0 %all_to_all.21 = f32[32,24,1024]{2,1,0:T(8,128)} all-to-all(f32[32,24,1024]{2,1,0:T(8,128)} %bitcast.18), channel_id=1, replica_groups=mesh['xl'=2,'core'=2,'z'=4,'xh'=2,'y'=4] {'z','xh','y'}, dimensions={0} | all-to-all | bytes 6291456 | tf_op jit(solution)/shard_map/all_to_all | solution.py:132
  253.0 2.7 %reduce_sum.59 = f32[24,1024]{1,0:T(8,128)} reduce(f32[32,24,1024]{2,1,0:T(8,128)} %all_to_all.21, f32[]{:T(128)} %constant.86.clone.1), dimensions={0}, to_apply=%region_6.7 | reduce | flops 761856 | bytes 3244036 | tf_op jit(solution)/shard_map/reduce_sum | solution.py:135
  (46 shorter events, 10.8 us)
Async XLA Ops:
  6.5 2.0 copy-start
  6.5 35.1 %all-gather.2.cloned.1.call-start = ((), (), s32[]{:S(2)}) async-start(), calls=%async_computation.5 | async-start | bytes 1966080 | tf_op jit(solution)/shard_map/all_gather | solution.py:55
  10.6 35.9 %copy-start.5 = (s32[384]{0:T(512)S(1)}, s32[384]{0:T(512)}, u32[]{:S(2)}) copy-start(s32[384]{0:T(512)} %param.11) | copy-start | bytes 4612
  41.6 24.0 %collective-permute-start = (bf16[768,1024]{1,0:T(8,128)(2,1)}, bf16[768,1024]{1,0:T(8,128)(2,1)}, u32[]{:S(2)}, u32[]{:S(2)}) collective-permute-start(bf16[768,1024]{1,0:T(8,128)(2,1)} %all-gather.2.cloned.1.call-done), channel_id=1, source_target_pairs={{0,32},{32,0},{1,33},{33,1},{2,34},{34,2},{3,35},{35,3},{4,36},{36... | collective-permute-start | bytes 4718600 | tf_op jit(solution)/shard_map/ppermute | solution.py:56
  44.1 8.1 %collective-permute-start.1 = (bf16[96,1024]{1,0:T(8,128)(2,1)}, bf16[96,1024]{1,0:T(8,128)(2,1)}, u32[]{:S(2)}, u32[]{:S(2)}) collective-permute-start(bf16[96,1024]{1,0:T(8,128)(2,1)} %multiply_convert_fusion.2), channel_id=1, source_target_pairs={{0,68},{4,64},{64,4},{68,0},{1,69},{5,65},{65,5},{69,1},{2,70},{6,... | collective-permute-start | bytes 589832 | tf_op jit(solution)/shard_map/ppermute | solution.py:50
  47.1 7.4 %all-to-all-start = ((s32[4,1,384]{2,1,0:T(1,128)}), s32[4,1,384]{2,1,0:T(1,128)S(1)}, u32[]{:S(2)}, u32[]{:S(2)}) async-start(s32[4,1,384]{2,1,0:T(1,128)} %broadcast_in_dim.21), calls=%async_computation | async-start | bytes 12288 | tf_op jit(solution)/shard_map/all_to_all | solution.py:60
  56.8 23.7 %all-to-all-start.1 = ((bf16[4,192,1024]{2,1,0:T(8,128)(2,1)}), bf16[4,192,1024]{2,1,0:T(8,128)(2,1)}, u32[]{:S(2)}, u32[]{:S(2)}) async-start(bf16[4,192,1024]{2,1,0:T(8,128)(2,1)} %broadcast_in_dim.27), calls=%async_computation.1 | async-start | bytes 3145728 | tf_op jit(solution)/shard_map/all_to_all | solution.py:53
  61.2 107.7 %reduce-scatter.2.cloned.1.call-start = ((), (), s32[]{:S(2)}) async-start(), calls=%async_computation.6 | async-start | bytes 3932160 | tf_op jit(solution)/shard_map/reduce_scatter | solution.py:90
  87.0 11.4 %copy-start.6 = (bf16[1536,768]{1,0:T(8,128)(2,1)}, bf16[1536,768]{1,0:T(8,128)(2,1)S(1)}, u32[]{:S(2)}) copy-start(bf16[1536,768]{1,0:T(8,128)(2,1)S(1)} %multiply_convert_fusion) | copy-start | bytes 7077892
  90.6 7.7 %collective-permute-start.2 = (f32[768,1024]{1,0:T(8,128)S(1)}, f32[768,1024]{1,0:T(8,128)S(1)}, u32[]{:S(2)}, u32[]{:S(2)}) collective-permute-start(f32[768,1024]{1,0:T(8,128)S(1)} %fusion.24), channel_id=1, source_target_pairs={{0,32},{32,0},{1,33},{33,1},{2,34},{34,2},{3,35},{35,3},{4,36},{36... | collective-permute-start | bytes 9437192 | tf_op jit(solution)/shard_map/ppermute | solution.py:84
  109.8 42.0 %all-to-all-start.2 = ((f32[4,192,1024]{2,1,0:T(8,128)}), f32[4,192,1024]{2,1,0:T(8,128)}, u32[]{:S(2)}, u32[]{:S(2)}) async-start(f32[4,192,1024]{2,1,0:T(8,128)} %bitcast.17), calls=%async_computation.3 | async-start | bytes 6291456 | tf_op jit(solution)/shard_map/all_to_all | solution.py:94
  155.0 12.7 %copy-start.1 = (f32[192,1024]{1,0:T(8,128)S(1)}, f32[192,1024]{1,0:T(8,128)}, u32[]{:S(2)}) copy-start(f32[192,1024]{1,0:T(8,128)} %reduce_sum.57) | copy-start | bytes 2359300
  156.1 10.9 %collective-permute-start.4 = (f32[96,1024]{1,0:T(8,128)S(1)}, f32[96,1024]{1,0:T(8,128)S(1)}, u32[]{:S(2)}, u32[]{:S(2)}) collective-permute-start(f32[96,1024]{1,0:T(8,128)S(1)} %slice.39), channel_id=1, source_target_pairs={{0,68},{4,64},{64,4},{68,0},{1,69},{5,65},{65,5},{69,1},{2,70},{6,... | collective-permute-start | bytes 1179656 | tf_op jit(solution)/shard_map/ppermute | solution.py:98
  167.0 0.8 copy-start.4
  168.8 18.1 %copy-start.2 = (bf16[192,1024]{1,0:T(8,128)(2,1)S(1)}, bf16[192,1024]{1,0:T(8,128)(2,1)}, u32[]{:S(2)}) copy-start(bf16[192,1024]{1,0:T(8,128)(2,1)} %multiply_convert_fusion.1) | copy-start | bytes 1179652
  168.9 18.1 %copy-start.3 = (f32[192,1024]{1,0:T(8,128)S(1)}, f32[192,1024]{1,0:T(8,128)}, u32[]{:S(2)}) copy-start(f32[192,1024]{1,0:T(8,128)} %reduce-scatter.2.cloned.1.call-done) | copy-start | bytes 2359300
  170.0 17.0 %collective-permute-start.3 = (f32[96,1024]{1,0:T(8,128)S(1)}, f32[96,1024]{1,0:T(8,128)S(1)}, u32[]{:S(2)}, u32[]{:S(2)}) collective-permute-start(f32[96,1024]{1,0:T(8,128)S(1)} %constant_dynamic-slice_fusion.2), channel_id=1, source_target_pairs={{0,64},{64,0},{1,65},{65,1},{2,66},{66,2},{3,67},{67,3},{4,68},{68... | collective-permute-start | bytes 1179656 | tf_op jit(solution)/shard_map/ppermute | solution.py:91
Sparse Core Ops, SparseCore 0:
  11.6 29.9 all-gather.1
  103.0 35.4 reduce-scatter.1
where the time goes:
time: 264 us; the launch traced here: 263 us
  waiting for transfers between devices  88.4 us (33%)
  blocking collectives  69.8 us (26%)
  matrix products  38.1 us (14%)
  starting transfers between devices  20 us (8%)
  local copies, waits for them, and re-layouts  18.1 us (7%)
  between operations  14.9 us (6%)
  other arithmetic  13.2 us (5%)
    all_to_all x1, blocking collectives, body(): lax.all_to_all(terms.reshape(32, GROUP, width), DP, split_axis=0, concat_...  45 us
    all_to_all x1, waiting for transfers between devices, body(): lax.all_to_all(text_part.reshape(4, half, width), 'y', split_axis=0, conc...  35.1 us
    all_gather x1, waiting for transfers between devices, body(): mine = lax.all_gather(half_images, 'z', axis=0, tiled=True)  27 us
    all_gather x1, blocking collectives, body(): text_backs = lax.all_gather(text_back, TOWER, axis=0, tiled=True)  15.6 us
    all_to_all x1, waiting for transfers between devices, body(): texts = lax.all_to_all(sent, 'y', split_axis=0, concat_axis=0, tiled=True)  12.2 us
    all_gather x1, blocking collectives, body(): image_backs = lax.all_gather(image_back, TOWER, axis=0, tiled=True)  9.17 us
    dot_general x1, matrix products, body(): lax.dot_general(coefficient, images, (((0,), (0,)), ((), ())), preferred_...  6.95 us
    dot_general x1, matrix products, body(): lax.dot_general(images, texts, (((1,), (1,)), ((), ())), preferred_elemen...  6.43 us
  transfers between devices with their start and end apart: 10, of which 7 were waited for; matrix products, arithmetic and copies ran while one was open for 13% of the time, Pallas kernels for 0%

commit v1 on v0

--- a/solution.py
+++ b/solution.py
@@ -28,6 +28,23 @@
     )
 
 
+def to_all(block, axis):
+    sent = jnp.broadcast_to(block[None], (4,) + block.shape)
+    got = lax.all_to_all(sent, axis, split_axis=0, concat_axis=0, tiled=True)
+    return got.reshape((-1,) + block.shape[1:])
+
+
+def reduce_blocks(terms, own_rows):
+    largest = jnp.maximum(jnp.max(jnp.abs(terms), axis=(1, 2), keepdims=True), 1e-30)
+    exponent = jnp.ceil(jnp.log2(largest) * 16.0 + 0.01)
+    coded = jnp.round(terms * (32767.0 * jnp.exp2(exponent * -0.0625)))
+    row = lax.broadcasted_iota(jnp.int32, terms.shape, 1)
+    coded = jnp.where(row == own_rows, exponent, coded).astype(jnp.int16)
+    got = lax.all_to_all(coded, DP, split_axis=0, concat_axis=0, tiled=True)
+    scale = jnp.exp2(got[:, own_rows, :1].astype(jnp.float32) * 0.0625) * (1.0 / 32767.0)
+    return jnp.sum(got[:, :own_rows].astype(jnp.float32) * scale[:, :, None], axis=0)
+
+
 def body(image_feats, text_feats, image_weight, text_weight, partner, log_scale, logit_bias):
     rows, width = text_feats.shape[0], image_weight.shape[1]
     half, quarter = rows // 2, rows // 4
@@ -43,22 +60,17 @@
     def rows_at(array, start, count):
         return lax.dynamic_slice_in_dim(array, start, count, 0)
 
-    half_images, image_inverse = embed_rows(rows_at(image_feats, core * half, half), image_weight)
     own_texts, text_inverse = embed_rows(
         rows_at(text_feats, text_quarter * quarter, quarter), text_weight
     )
     other_texts = lax.ppermute(own_texts, ("xl", "xh"), FLIP)
-    pair_texts = jnp.concatenate([own_texts, other_texts], 0)
-    sent = jnp.broadcast_to(pair_texts[None], (4, half, width))
-    texts = lax.all_to_all(sent, "y", split_axis=0, concat_axis=0, tiled=True)
-    texts = texts.reshape(4 * half, width)
-    mine = lax.all_gather(half_images, "z", axis=0, tiled=True)
+    half_images, image_inverse = embed_rows(rows_at(image_feats, core * half, half), image_weight)
+    mine = to_all(half_images, "z")
+    texts = to_all(jnp.concatenate([own_texts, other_texts], 0), "y")
     theirs = lax.ppermute(mine, "core", SWAP)
     images = jnp.concatenate([mine, theirs], 0)
 
-    sent = jnp.broadcast_to(partner[None], (4, rows))
-    partners = lax.all_to_all(sent, "z", split_axis=0, concat_axis=0, tiled=True)
-    partners = partners.reshape(4, 2, half)
+    partners = to_all(partner, "z").reshape(4, 2, half)
     partners = jnp.concatenate(
         [
             lax.dynamic_index_in_dim(partners, core, 1, keepdims=False).reshape(-1),
@@ -80,22 +92,29 @@
     labels = jnp.where(partners[:, None] == columns[None, :], 1.0, -1.0).astype(jnp.float32)
     slopes = -labels * jax.nn.sigmoid(-labels * logits)
     coefficient = (logit_scale * slopes).astype(jnp.bfloat16)
-    given = jnp.dot(coefficient[4 * half :], texts, preferred_element_type=jnp.float32)
-    taken = lax.ppermute(given, "core", SWAP)
     text_part = lax.dot_general(
         coefficient, images, (((0,), (0,)), ((), ())), preferred_element_type=jnp.float32
     )
+    given = jnp.dot(coefficient[4 * half :], texts, preferred_element_type=jnp.float32)
+    taken = lax.ppermute(given, "core", SWAP)
     kept = jnp.dot(coefficient[: 4 * half], texts, preferred_element_type=jnp.float32)
-
-    image_sum = lax.psum_scatter(kept + taken, "z", scatter_dimension=0, tiled=True)
-    image_got = lax.ppermute(rows_at(image_sum, (1 - xl) * quarter, quarter), "xl", SWAP)
-    image_grad = rows_at(image_sum, xl * quarter, quarter) + image_got
 
     text_terms = lax.all_to_all(
         text_part.reshape(4, half, width), "y", split_axis=0, concat_axis=0, tiled=True
     )
-    text_sum = jnp.sum(text_terms, axis=0)
-    text_grad = text_sum[:quarter] + lax.ppermute(text_sum[quarter:], ("xl", "xh"), FLIP)
+    image_terms = lax.all_to_all(
+        (kept + taken).reshape(4, half, width), "z", split_axis=0, concat_axis=0, tiled=True
+    )
+    text_got = lax.ppermute(jnp.sum(text_terms[:, quarter:], axis=0), ("xl", "xh"), FLIP)
+    text_grad = jnp.sum(text_terms[:, :quarter], axis=0) + text_got
+    image_got = lax.ppermute(
+        jnp.sum(lax.dynamic_slice_in_dim(image_terms, (1 - xl) * quarter, quarter, 1), axis=0),
+        "xl",
+        SWAP,
+    )
+    image_grad = image_got + jnp.sum(
+        lax.dynamic_slice_in_dim(image_terms, xl * quarter, quarter, 1), axis=0
+    )
 
     image_back = back_rows(
         rows_at(half_images, xl * quarter, quarter),
@@ -129,10 +148,7 @@
     terms = jnp.dot(image_columns, image_backs, preferred_element_type=jnp.float32) + jnp.dot(
         text_columns, text_backs, preferred_element_type=jnp.float32
     )
-    spread = lax.all_to_all(
-        terms.reshape(32, GROUP, width), DP, split_axis=0, concat_axis=0, tiled=True
-    )
-    return jnp.sum(spread, axis=0)[:own_rows]
+    return reduce_blocks(terms.reshape(32, GROUP, width), own_rows)
 
 
 def solution(mesh):

time: 264 us -> 253 us (0.958)
  blocking collectives: 69.8 us -> 52.5 us
  between operations: 14.9 us -> 1.57 us
  starting transfers between devices: 20 us -> 32 us
  waiting for transfers between devices: 88.4 us -> 95.9 us
  local copies, waits for them, and re-layouts: 18.1 us -> 11.9 us
  other arithmetic: 13.2 us -> 17.4 us
    all_to_all x2 -> x4, waiting for transfers between devices: 12.7 us -> 54 us  [the longest x3 35 us: to_all(): got = lax.all_to_all(sent, axis, split_axis=0, concat_axis=0, tiled=True)]
    all_gather x1 -> x0, waiting for transfers between devices: 27 us -> none  [body(): mine = lax.all_gather(half_images, 'z', axis=0, tiled=True)]
    all_to_all x1, blocking collectives: 45 us -> 27.5 us  [reduce_blocks(): got = lax.all_to_all(coded, DP, split_axis=0, concat_axis=0, tiled=True)]
    all_to_all x2 -> x4, starting transfers between devices: 7.59 us -> 18.2 us  [the longest x3 13.6 us: to_all(): got = lax.all_to_all(sent, axis, split_axis=0, concat_axis=0, tiled=True)]
    ppermute x1, waiting for transfers between devices: 5.29 us -> 0.01 us  [body(): taken = lax.ppermute(given, 'core', SWAP)]
    all_to_all x1, waiting for transfers between devices: 35.1 us -> 32 us  [body(): lax.all_to_all(text_part.reshape(4, half, width), 'y', split_axis=0, conc...]
    convert_element_type x0 -> x1, other arithmetic: none -> 2.82 us  [reduce_blocks(): coded = jnp.where(row == own_rows, exponent, coded).astype(jnp.int16)]
    concatenate x1 -> x0, local copies, waits for them, and re-layouts: 2.76 us -> none  [body(): images = jnp.concatenate([mine, theirs], 0)]
  transfers between devices with their start and end apart: 10 -> 10, of which waited for: 7 -> 7; matrix products, arithmetic and copies ran while one was open for 13% -> 12% of each run, Pallas kernels for 0% -> 0%
where the time goes in v1:
time: 253 us; the launch traced here: 252 us
  waiting for transfers between devices  95.9 us (38%)
  blocking collectives  52.5 us (21%)
  matrix products  40.3 us (16%)
  starting transfers between devices  32 us (13%)
  other arithmetic  17.4 us (7%)
  local copies, waits for them, and re-layouts  11.9 us (5%)
    all_to_all x3, waiting for transfers between devices, to_all(): got = lax.all_to_all(sent, axis, split_axis=0, concat_axis=0, tiled=True)  35 us
    all_to_all x1, waiting for transfers between devices, body(): lax.all_to_all(text_part.reshape(4, half, width), 'y', split_axis=0, conc...  32 us
    all_to_all x1, blocking collectives, reduce_blocks(): got = lax.all_to_all(coded, DP, split_axis=0, concat_axis=0, tiled=True)  27.5 us
    all_to_all x1, waiting for transfers between devices, body(): lax.all_to_all((kept + taken).reshape(4, half, width), 'z', split_axis=0,...  19 us
    all_gather x1, blocking collectives, body(): text_backs = lax.all_gather(text_back, TOWER, axis=0, tiled=True)  15.8 us
    all_to_all x3, starting transfers between devices, to_all(): got = lax.all_to_all(sent, axis, split_axis=0, concat_axis=0, tiled=True)  13.6 us
    all_gather x1, blocking collectives, body(): image_backs = lax.all_gather(image_back, TOWER, axis=0, tiled=True)  9.17 us
    ppermute x1, waiting for transfers between devices, body(): lax.ppermute(jnp.sum(text_terms[:, quarter:], axis=0), ('xl', 'xh'), FLIP)  8.19 us
  transfers between devices with their start and end apart: 10, of which 7 were waited for; matrix products, arithmetic and copies ran while one was open for 12% of the time, Pallas kernels for 0%

profile of v1, /device:TPU:1, one launch (start us, length us, event | category | flops | bytes accessed | tf_op | source)
XLA Modules:
  0.0 251.7 jit_solution(10773570552659097909)
XLA Ops:
  0.0 2.0 copy-done
  2.0 2.1 multiply_reduce_fusion.1
  6.3 6.0 %all-to-all-start.1 = ((bf16[4,192,1024]{2,1,0:T(8,128)(2,1)}), bf16[4,192,1024]{2,1,0:T(8,128)(2,1)}, u32[]{:S(2)}, u32[]{:S(2)}) async-start(bf16[4,192,1024]{2,1,0:T(8,128)(2,1)} %broadcast_in_dim.34), calls=%async_computation.1 | async-start | bytes 3145728 | tf_op jit(solution)/shard_map/all_to_all | solution.py:33
  12.3 3.0 %multiply_reduce_fusion.2 = (f32[96]{0:T(128)S(1)}, f32[96,1024]{1,0:T(8,128)}) fusion(bf16[1024,1024]{1,0:T(8,128)(2,1)} %param.10, bf16[384,1024]{1,0:T(8,128)(2,1)} %param.8, s32[]{:T(128)S(6)} %select_n.115), kind=kOutput, calls=%fused_computation.53 | convolution fusion | flops 201523104 | bytes 2687364 | tf_op jit(solution)/shard_map/dot_general | solution.py:16
  15.3 16.9 %all-to-all-done.1 = bf16[4,192,1024]{2,1,0:T(8,128)(2,1)} async-done(((bf16[4,192,1024]{2,1,0:T(8,128)(2,1)}), bf16[4,192,1024]{2,1,0:T(8,128)(2,1)}, u32[]{:S(2)}, u32[]{:S(2)}) %all-to-all-start.1) | async-done | bytes 1572896 | tf_op jit(solution)/shard_map/all_to_all | solution.py:33
  32.2 1.9 collective-permute-start
  35.9 2.5 collective-permute-start.1
  39.0 3.2 %all-to-all-start = ((s32[4,1,384]{2,1,0:T(1,128)}), s32[4,1,384]{2,1,0:T(1,128)S(1)}, u32[]{:S(2)}, u32[]{:S(2)}) async-start(s32[4,1,384]{2,1,0:T(1,128)} %broadcast_in_dim.28), calls=%async_computation | async-start | bytes 12288 | tf_op jit(solution)/shard_map/all_to_all | solution.py:33
  46.3 2.4 broadcast_in_dim.35
  48.7 4.3 %all-to-all-start.2 = ((bf16[4,192,1024]{2,1,0:T(8,128)(2,1)}), bf16[4,192,1024]{2,1,0:T(8,128)(2,1)}, u32[]{:S(2)}, u32[]{:S(2)}) async-start(bf16[4,192,1024]{2,1,0:T(8,128)(2,1)} %broadcast_in_dim.35), calls=%async_computation.2 | async-start | bytes 3145728 | tf_op jit(solution)/shard_map/all_to_all | solution.py:33
  54.7 17.5 %all-to-all-done.2 = bf16[4,192,1024]{2,1,0:T(8,128)(2,1)} async-done(((bf16[4,192,1024]{2,1,0:T(8,128)(2,1)}), bf16[4,192,1024]{2,1,0:T(8,128)(2,1)}, u32[]{:S(2)}, u32[]{:S(2)}) %all-to-all-start.2) | async-done | bytes 1572896 | tf_op jit(solution)/shard_map/all_to_all | solution.py:33
  72.3 6.4 %multiply_convert_fusion = bf16[1536,768]{1,0:T(8,128)(2,1)S(1)} fusion(bf16[768,1024]{1,0:T(8,128)(2,1)} %bitcast.2, f32[]{:T(128)} %bitcast.17, s32[768]{0:T(1024)S(1)} %fusion.59, f32[]{:T(128)} %bitcast, s32[1536]{0:T(1024)S(1)} %pad_add_fusion, bf16[768,1024]{1,0:T(8,128)(2,1)} %collective-permute-done, bf16[768,1024]{1,0:T(8,128)(2,1)} %bitcast.1), kind=kOutput, calls=%fused_computation.2 | convolution fusion | flops 2436366336 | bytes 7087112 | tf_op jit(solution)/shard_map/dot_general | solution.py:83
  78.7 5.3 %fusion.25 = f32[768,1024]{1,0:T(8,128)} fusion(bf16[768,1024]{1,0:T(8,128)(2,1)} %bitcast.2, bf16[1536,768]{1,0:T(8,128)(2,1)S(1)} %multiply_convert_fusion), kind=kOutput, calls=%fused_computation.29 | convolution fusion | flops 1207959552 | bytes 5898240 | tf_op jit(solution)/shard_map/dot_general | solution.py:98
  84.0 2.5 %collective-permute-start.2 = (f32[768,1024]{1,0:T(8,128)}, f32[768,1024]{1,0:T(8,128)}, u32[]{:S(2)}, u32[]{:S(2)}) collective-permute-start(f32[768,1024]{1,0:T(8,128)} %fusion.25), channel_id=1, source_target_pairs={{0,32},{32,0},{1,33},{33,1},{2,34},{34,2},{3,35},{35,3},{4,36},{36... | collective-permute-start | bytes 9437192 | tf_op jit(solution)/shard_map/ppermute | solution.py:99
  86.5 6.2 %fusion.4 = f32[768,1024]{1,0:T(8,128)} fusion(bf16[1536,768]{1,0:T(8,128)(2,1)S(1)} %multiply_convert_fusion, bf16[768,1024]{1,0:T(8,128)(2,1)} %collective-permute-done, bf16[768,1024]{1,0:T(8,128)(2,1)} %bitcast.1), kind=kOutput, calls=%fused_computation.10 | convolution fusion | flops 2422210560 | bytes 8650752 | tf_op jit(solution)/shard_map/dot_general | solution.py:95
  92.8 4.6 %all-to-all-start.4 = ((f32[4,192,1024]{2,1,0:T(8,128)}), f32[4,192,1024]{2,1,0:T(8,128)}, u32[]{:S(2)}, u32[]{:S(2)}) async-start(f32[4,192,1024]{2,1,0:T(8,128)} %bitcast.19), calls=%async_computation.4 | async-start | bytes 6291456 | tf_op jit(solution)/shard_map/all_to_all | solution.py:102
  97.4 5.8 %convolution_add_fusion.1 = f32[768,1024]{1,0:T(8,128)} fusion(f32[768,1024]{1,0:T(8,128)} %collective-permute-done.2, bf16[768,1024]{1,0:T(8,128)(2,1)} %bitcast.2, bf16[1536,768]{1,0:T(8,128)(2,1)} %copy-done.7), kind=kOutput, calls=%fused_computation.12 | convolution fusion | flops 1208745984 | bytes 9043968 | tf_op jit(solution)/shard_map/dot_general | solution.py:100
  103.2 32.0 %all-to-all-done.4 = f32[4,192,1024]{2,1,0:T(8,128)} async-done(((f32[4,192,1024]{2,1,0:T(8,128)}), f32[4,192,1024]{2,1,0:T(8,128)}, u32[]{:S(2)}, u32[]{:S(2)}) %all-to-all-start.4) | async-done | bytes 3145760 | tf_op jit(solution)/shard_map/all_to_all | solution.py:102
  135.2 4.6 %all-to-all-start.3 = ((f32[4,192,1024]{2,1,0:T(8,128)}), f32[4,192,1024]{2,1,0:T(8,128)}, u32[]{:S(2)}, u32[]{:S(2)}) async-start(f32[4,192,1024]{2,1,0:T(8,128)} %bitcast.18), calls=%async_computation.3 | async-start | bytes 6291456 | tf_op jit(solution)/shard_map/all_to_all | solution.py:105
  140.0 2.2 constant_dynamic-slice_fusion.1
  142.1 2.3 slice_reduce_fusion
  144.4 2.2 collective-permute-start.4
  147.7 8.2 %collective-permute-done.4 = f32[96,1024]{1,0:T(8,128)S(1)} collective-permute-done((f32[96,1024]{1,0:T(8,128)S(1)}, f32[96,1024]{1,0:T(8,128)S(1)}, u32[]{:S(2)}, u32[]{:S(2)}) %collective-permute-start.4) | collective-permute-done | bytes 393248 | tf_op jit(solution)/shard_map/ppermute | solution.py:108
  157.8 19.0 %all-to-all-done.3 = f32[4,192,1024]{2,1,0:T(8,128)} async-done(((f32[4,192,1024]{2,1,0:T(8,128)}), f32[4,192,1024]{2,1,0:T(8,128)}, u32[]{:S(2)}, u32[]{:S(2)}) %all-to-all-start.3) | async-done | bytes 3145760 | tf_op jit(solution)/shard_map/all_to_all | solution.py:105
  176.8 2.4 dynamic-slice_reduce_fusion
  180.3 15.8 %all_gather.7 = bf16[384,1024]{1,0:T(8,128)(2,1)} all-gather(bf16[96,1024]{1,0:T(8,128)(2,1)S(1)} %fusion.45), channel_id=1, replica_groups=mesh['xl'=2,'core'=2,'z'=4,'xh'=2,'y'=4] {'xl','core'}, dimensions={0}, use_global_device_ids=true | all-gather | bytes 983040 | tf_op jit(solution)/shard_map/all_gather | solution.py:126
  196.4 9.2 %all_gather.6 = bf16[384,1024]{1,0:T(8,128)(2,1)} all-gather(bf16[96,1024]{1,0:T(8,128)(2,1)S(1)} %fusion.41), channel_id=1, replica_groups=mesh['xl'=2,'core'=2,'z'=4,'xh'=2,'y'=4] {'xl','core'}, dimensions={0}, use_global_device_ids=true | all-gather | bytes 983040 | tf_op jit(solution)/shard_map/all_gather | solution.py:125
  205.6 5.6 %fusion.15 = f32[768,1024]{1,0:T(8,128)} fusion(bf16[384,1024]{1,0:T(8,128)(2,1)} %all_gather.6, s32[768]{0:T(1024)S(1)} %fusion.51, bf16[96,1664]{1,0:T(8,128)(2,1)} %get-tuple-element.20, bf16[96,1664]{1,0:T(8,128)(2,1)} %get-tuple-element.18, bf16[96,1664]{1,0:T(8,128)(2,1)} %get-tuple-element.19, bf16[96,1664]{1,0:T(8,128)(2,1)} %get-tuple-element.17), kind=kOutput, calls=%fused_computation.24 | convolution fusion | flops 1592131584 | bytes 5213184 | tf_op jit(solution)/shard_map/dot_general | solution.py:148
  211.2 5.9 %abs_reduce_fusion = (f32[768]{0:T(1024)S(1)}, f32[768,1024]{1,0:T(8,128)}) fusion(f32[768,1024]{1,0:T(8,128)} %fusion.15, bf16[384,1024]{1,0:T(8,128)(2,1)} %all_gather.7, s32[1024]{0:T(1024)S(1)} %iota_add_fusion, s32[768]{0:T(1024)S(1)} %fusion.51, bf16[192,1024]{1,0:T(8,128)(2,1)} %get-tuple-element.22, bf16[192,1024]{1,0:T(8,128)(2,1)} %get-tuple-element.21), kind=kOutput, calls=%fused_computation.6 | convolution fusion | flops 1212972288 | bytes 7874560 | tf_op jit(solution)/shard_map/dot_general | solution.py:148
  217.3 2.8 %select_convert_fusion = s16[32,24,1024]{2,1,0:T(8,128)(2,1)S(1)} fusion(f32[32,24,1024]{2,1,0:T(8,128)} %bitcast.20, f32[32]{0:T(128)S(1)} %get-tuple-element.11, f32[32]{0:T(128)S(1)} %get-tuple-element.12, pred[24]{0:T(512)(128)(4,1)S(1)} %iota_compare_fusion.6), kind=kLoop, calls=%fused_computation.5 | loop fusion | flops 3145728 | bytes 4718872 | tf_op jit(solution)/shard_map/convert_element_type | solution.py:42
  220.1 27.5 %all_to_all.31 = s16[32,24,1024]{2,1,0:T(8,128)(2,1)S(1)} all-to-all(s16[32,24,1024]{2,1,0:T(8,128)(2,1)S(1)} %select_convert_fusion), channel_id=1, replica_groups=mesh['xl'=2,'core'=2,'z'=4,'xh'=2,'y'=4] {'z','xh','y'}, dimensions={0} | all-to-all | bytes 3145728 | tf_op jit(solution)/shard_map/all_to_all | solution.py:43
  248.9 2.7 %multiply_reduce_fusion = f32[21,1024]{1,0:T(8,128)} fusion(s16[32,24,1024]{2,1,0:T(8,128)(2,1)} %copy-done.1, f32[32]{0:T(128)S(1)} %multiply_bitcast_fusion), kind=kLoop, calls=%fused_computation.4 | loop fusion | flops 2042880 | bytes 1462400 | tf_op jit(solution)/shard_map/reduce_sum | solution.py:45
  (52 shorter events, 15.1 us)
Async XLA Ops:
  0.0 2.0 copy-start
  4.2 0.8 copy-start.2
  6.3 32.1 %copy-start.6 = (s32[384]{0:T(512)S(1)}, s32[384]{0:T(512)}, u32[]{:S(2)}) copy-start(s32[384]{0:T(512)} %param.11) | copy-start | bytes 4612
  6.3 25.9 %all-to-all-start.1 = ((bf16[4,192,1024]{2,1,0:T(8,128)(2,1)}), bf16[4,192,1024]{2,1,0:T(8,128)(2,1)}, u32[]{:S(2)}, u32[]{:S(2)}) async-start(bf16[4,192,1024]{2,1,0:T(8,128)(2,1)} %broadcast_in_dim.34), calls=%async_computation.1 | async-start | bytes 3145728 | tf_op jit(solution)/shard_map/all_to_all | solution.py:33
  32.2 40.1 %collective-permute-start = (bf16[768,1024]{1,0:T(8,128)(2,1)}, bf16[768,1024]{1,0:T(8,128)(2,1)}, u32[]{:S(2)}, u32[]{:S(2)}) collective-permute-start(bf16[768,1024]{1,0:T(8,128)(2,1)} %bitcast.1), channel_id=1, source_target_pairs={{0,32},{32,0},{1,33},{33,1},{2,34},{34,2},{3,35},{35,3},{4,36},{36... | collective-permute-start | bytes 4718600 | tf_op jit(solution)/shard_map/ppermute | solution.py:70
  35.9 8.1 %collective-permute-start.1 = (bf16[96,1024]{1,0:T(8,128)(2,1)}, bf16[96,1024]{1,0:T(8,128)(2,1)}, u32[]{:S(2)}, u32[]{:S(2)}) collective-permute-start(bf16[96,1024]{1,0:T(8,128)(2,1)} %multiply_convert_fusion.2), channel_id=1, source_target_pairs={{0,68},{4,64},{64,4},{68,0},{1,69},{5,65},{65,5},{69,1},{2,70},{6,... | collective-permute-start | bytes 589832 | tf_op jit(solution)/shard_map/ppermute | solution.py:66
  39.0 7.4 %all-to-all-start = ((s32[4,1,384]{2,1,0:T(1,128)}), s32[4,1,384]{2,1,0:T(1,128)S(1)}, u32[]{:S(2)}, u32[]{:S(2)}) async-start(s32[4,1,384]{2,1,0:T(1,128)} %broadcast_in_dim.28), calls=%async_computation | async-start | bytes 12288 | tf_op jit(solution)/shard_map/all_to_all | solution.py:33
  48.7 23.6 %all-to-all-start.2 = ((bf16[4,192,1024]{2,1,0:T(8,128)(2,1)}), bf16[4,192,1024]{2,1,0:T(8,128)(2,1)}, u32[]{:S(2)}, u32[]{:S(2)}) async-start(bf16[4,192,1024]{2,1,0:T(8,128)(2,1)} %broadcast_in_dim.35), calls=%async_computation.2 | async-start | bytes 3145728 | tf_op jit(solution)/shard_map/all_to_all | solution.py:33
  78.7 7.8 %copy-start.7 = (bf16[1536,768]{1,0:T(8,128)(2,1)}, bf16[1536,768]{1,0:T(8,128)(2,1)S(1)}, u32[]{:S(2)}) copy-start(bf16[1536,768]{1,0:T(8,128)(2,1)S(1)} %multiply_convert_fusion) | copy-start | bytes 7077892
  84.0 13.4 %collective-permute-start.2 = (f32[768,1024]{1,0:T(8,128)}, f32[768,1024]{1,0:T(8,128)}, u32[]{:S(2)}, u32[]{:S(2)}) collective-permute-start(f32[768,1024]{1,0:T(8,128)} %fusion.25), channel_id=1, source_target_pairs={{0,32},{32,0},{1,33},{33,1},{2,34},{34,2},{3,35},{35,3},{4,36},{36... | collective-permute-start | bytes 9437192 | tf_op jit(solution)/shard_map/ppermute | solution.py:99
  92.8 42.5 %all-to-all-start.4 = ((f32[4,192,1024]{2,1,0:T(8,128)}), f32[4,192,1024]{2,1,0:T(8,128)}, u32[]{:S(2)}, u32[]{:S(2)}) async-start(f32[4,192,1024]{2,1,0:T(8,128)} %bitcast.19), calls=%async_computation.4 | async-start | bytes 6291456 | tf_op jit(solution)/shard_map/all_to_all | solution.py:102
  135.2 41.6 %all-to-all-start.3 = ((f32[4,192,1024]{2,1,0:T(8,128)}), f32[4,192,1024]{2,1,0:T(8,128)}, u32[]{:S(2)}, u32[]{:S(2)}) async-start(f32[4,192,1024]{2,1,0:T(8,128)} %bitcast.18), calls=%async_computation.3 | async-start | bytes 6291456 | tf_op jit(solution)/shard_map/all_to_all | solution.py:105
  140.0 6.6 %copy-start.4 = (bf16[384,1664]{1,0:T(8,128)(2,1)S(1)}, bf16[384,1664]{1,0:T(8,128)(2,1)}, u32[]{:S(2)}) copy-start(bf16[384,1664]{1,0:T(8,128)(2,1)} %param.7) | copy-start | bytes 3833860
  144.4 11.4 %collective-permute-start.4 = (f32[96,1024]{1,0:T(8,128)S(1)}, f32[96,1024]{1,0:T(8,128)S(1)}, u32[]{:S(2)}, u32[]{:S(2)}) collective-permute-start(f32[96,1024]{1,0:T(8,128)S(1)} %get-tuple-element.5), channel_id=1, source_target_pairs={{0,68},{4,64},{64,4},{68,0},{1,69},{5,65},{65,5},{69,1},{2,70},{6,... | collective-permute-start | bytes 1179656 | tf_op jit(solution)/shard_map/ppermute | solution.py:108
  176.8 2.5 copy-start.5
  176.8 19.4 %copy-start.3 = (bf16[192,1024]{1,0:T(8,128)(2,1)S(1)}, bf16[192,1024]{1,0:T(8,128)(2,1)}, u32[]{:S(2)}) copy-start(bf16[192,1024]{1,0:T(8,128)(2,1)} %copy-done.2) | copy-start | bytes 1179652
  179.1 17.0 %collective-permute-start.3 = (f32[96,1024]{1,0:T(8,128)S(1)}, f32[96,1024]{1,0:T(8,128)S(1)}, u32[]{:S(2)}, u32[]{:S(2)}) collective-permute-start(f32[96,1024]{1,0:T(8,128)S(1)} %get-tuple-element.8), channel_id=1, source_target_pairs={{0,64},{64,0},{1,65},{65,1},{2,66},{66,2},{3,67},{67,3},{4,68},{68... | collective-permute-start | bytes 1179656 | tf_op jit(solution)/shard_map/ppermute | solution.py:110
  247.7 1.2 copy-start.1

commit v2 on v0

v2 whole, which is shorter than its diff:
```python
import math

import jax
import jax.numpy as jnp
from jax import lax
from jax.experimental import pallas as pl
from jax.experimental.pallas import tpu as pltpu
from jax.sharding import Mesh, PartitionSpec as P

AXES = ("xl", "core", "z", "xh", "y")
SIZES = {"xl": 2, "core": 2, "z": 4, "xh": 2, "y": 4}
DP = ("z", "xh", "y")
TOWER = ("xl", "core")
SWAP = [(0, 1), (1, 0)]
FLIP = [(0, 3), (1, 2), (2, 1), (3, 0)]
ROWS = 384
HALF, QUARTER = 192, 96
EXTRA = 16
E = 1024
TILE = 4 * HALF
OWN = 21
GROUP = 24
SLICE = E // 4
STEP = 8
NT = (((1,), (1,)), ((), ()))
TN = (((0,), (0,)), ((), ()))
OCTAVE = math.log(2.0) / 16.0
F32, BF16 = jnp.float32, jnp.bfloat16


def shifted(array, axis, by):
    return lax.ppermute(array, axis, [(i, (i + by) % 4) for i in range(4)])


def call(kernel, outs, flops, moved, limit=16, **options):
    return pl.pallas_call(
        kernel,
        out_shape=outs,
        cost_estimate=pl.CostEstimate(flops=flops, bytes_accessed=moved, transcendentals=0),
        compiler_params=pltpu.CompilerParams(vmem_limit_bytes=limit << 20),
        **options,
    )


def shape(*dims, dtype=F32):
    return jax.ShapeDtypeStruct(dims, dtype)


VMEM = pl.BlockSpec(memory_space=pltpu.VMEM)
SMEM = pl.BlockSpec(memory_space=pltpu.SMEM)
ANY = pl.BlockSpec(memory_space=pl.ANY)


def position(where_ref):
    index = where_ref[0]
    xl, core, z, xh, y = index // 64, index // 32 % 2, index // 8 % 4, index // 4 % 2, index % 4
    return xl, core, z, xh, y, (xl + xh) % 2 * 2 + core


def normalised(pre_ref, inverse_ref):
    pre = pre_ref[...]
    total = jnp.sum(pre * pre, axis=1, keepdims=True)
    inverse = lax.rsqrt(total + 1e-06).astype(BF16).astype(F32)
    inverse_ref[...] = jnp.broadcast_to(inverse[:QUARTER], (QUARTER, 128))
    return (pre * inverse).astype(BF16)


def embed_kernel(
    where_ref, partner_ref, text_feats, image_feats, text_weight, image_weight,
    text_ref, text_inverse, load_ref, image_inverse,
    text_rows, image_rows, text_held, image_held, text_pre, image_pre, sems,
):
    count = 0

    def begin(source, target):
        nonlocal count
        copy = pltpu.make_async_copy(source, target, sems.at[count])
        copy.start()
        count += 1
        return copy

    xl, core, _, _, _, text_quarter = position(where_ref)
    places = core * 2 + xl, core * 2 + 1 - xl

    def rows(place):
        return pl.ds(pl.multiple_of(place * QUARTER, QUARTER), QUARTER)

    def begin_weight(weight, held, ends):
        spans = [slice(a, b) for a, b in zip((0,) + ends, ends)]
        return [(span, begin(weight.at[span], held.at[span])) for span in spans]

    def project(rows_ref, held, waits, pre_ref):
        for i, (span, copy) in enumerate(waits):
            copy.wait()
            got = jnp.dot(rows_ref[:, span], held[span, :], preferred_element_type=F32)
            pre_ref[...] = got if i == 0 else pre_ref[...] + got

    text_copy = begin(text_feats.at[rows(text_quarter)], text_rows)
    text_waits = begin_weight(text_weight, text_held, (256, 512, 768, 1024))
    image_copies = [
        begin(image_feats.at[rows(place)], image_rows.at[i * QUARTER : (i + 1) * QUARTER])
        for i, place in enumerate(places)
    ]
    image_waits = begin_weight(image_weight, image_held, (384, 768, 1152, 1664))

    text_copy.wait()
    project(text_rows, text_held, text_waits, text_pre)
    text_ref[...] = normalised(text_pre, text_inverse)
    for copy in image_copies:
        copy.wait()
    project(image_rows, image_held, image_waits, image_pre)
    load_ref[:HALF, :] = normalised(image_pre, image_inverse)

    partner = jnp.concatenate([partner_ref[i : i + 1, :] for i in range(3)], 1).astype(F32)
    partner = jnp.broadcast_to(partner, (EXTRA, ROWS))
    lane = lax.broadcasted_iota(jnp.int32, (EXTRA, ROWS), 1)
    row = lax.broadcasted_iota(jnp.int32, (EXTRA, ROWS), 0)
    chosen = jnp.zeros((EXTRA, ROWS), F32)
    for i, place in enumerate(places):
        moved = pltpu.roll(partner, (i + 4 - place) % 4 * QUARTER, 1)
        chosen = jnp.where(lane // QUARTER == i, moved, chosen)
    high = jnp.floor(chosen * (1.0 / 128.0))
    parts = jnp.where(row == 0, high, jnp.where(row == 1, chosen - 128.0 * high, 0.0))
    load_ref[HALF:, :] = jnp.zeros((EXTRA, E), BF16)
    load_ref[HALF:, :ROWS] = parts.astype(BF16)


def ring_gather(block, axis):
    before, after = shifted(block, axis, 1), shifted(block, axis, -1)
    far_low = shifted(before[:QUARTER], axis, 1)
    far_high = shifted(after[QUARTER:], axis, -1)
    return block, after, before, far_low, far_high


def ring_scatter(far_low, far_high, after, before, mine, axis, crossed):
    far = shifted(far_low + crossed(far_high), axis, 2)
    got_right, got_left = shifted(after, axis, 1), shifted(before, axis, -1)
    high = mine[QUARTER:] + got_right[QUARTER:] + got_left[QUARTER:]
    return mine, got_right, got_left, far, crossed(high)


ORDER = ((2, 0), (2, 1), (1, 0), (1, 1), (3, 0), (3, 1), (0, 0), (0, 1))


def in_order(refs, out_ref):
    me, after, before, far_low, far_high = refs
    for place, (step, half) in enumerate(ORDER):
        ref = (me, after, far_high if half else far_low, before)[step]
        start = 0 if step == 2 else half * QUARTER
        out_ref[place * QUARTER : (place + 1) * QUARTER, :] = ref[start : start + QUARTER, :]


def images_kernel(me, after, before, far_low, far_high, out_ref):
    in_order((me, after, before, far_low, far_high), out_ref)
    lane = lax.broadcasted_iota(jnp.int32, (EXTRA, E), 1)
    carried = [ref[start:, :].astype(F32) for ref, start in (
        (me, HALF), (after, HALF), (far_high, QUARTER), (before, HALF)
    )]
    total = jnp.zeros((EXTRA, E), F32)
    for place, (step, half) in enumerate(ORDER):
        inside = (lane >= half * QUARTER) & (lane < (half + 1) * QUARTER)
        piece = jnp.where(inside, carried[step], 0.0)
        total += pltpu.roll(piece, (place - half) * QUARTER % E, 1)
    out_ref[TILE:, :] = total.astype(BF16)


def coefficients(where_ref, scalar_ref, images_ref, texts_ref, coef_ref):
    _, _, z, xh, y, text_quarter = position(where_ref)
    parts = images_ref[TILE:, :TILE].astype(F32)
    partner = (parts[0:1] * 128.0 + parts[1:2]).astype(jnp.int32)
    scale, shift = scalar_ref[0], scalar_ref[1]
    row = lax.broadcasted_iota(jnp.int32, (HALF, 1), 0)
    for block in range(4):
        rows = slice(block * HALF, (block + 1) * HALF)
        low, high = (
            ((z * 2 + (1 - xh if half else xh)) * 4 + lax.rem(y + step, 4)) * ROWS
            + text_quarter * QUARTER
            for step, half in ORDER[2 * block : 2 * block + 2]
        )
        index = row + jnp.where(row < QUARTER, low, high - QUARTER)
        logits = scale * lax.dot_general(
            texts_ref[rows, :], images_ref[:TILE, :], NT, preferred_element_type=F32
        ) + shift
        own = index == partner
        slopes = jnp.where(own, -scale, scale) / (1.0 + jnp.exp(jnp.where(own, logits, -logits)))
        coef_ref[rows, :] = slopes.astype(BF16)


def image_terms(coef_ref, texts_ref, part):
    return lax.dot_general(
        coef_ref[:, part * ROWS : (part + 1) * ROWS], texts_ref[...], TN,
        preferred_element_type=F32,
    )


def share_out(got, outs):
    start = 0
    for out in outs:
        out[...] = got[start : start + out.shape[0]]
        start += out.shape[0]


def own_kernel(
    where_ref, scalar_ref, me, after, before, far_low, far_high, images_ref, early_a, early_b,
    texts_ref, coef_ref,
):
    in_order((me, after, before, far_low, far_high), texts_ref)
    coefficients(where_ref, scalar_ref, images_ref, texts_ref, coef_ref)


def given_kernel(where_ref, scalar_ref, texts_ref, images_ref, coef_ref, given_ref):
    coefficients(where_ref, scalar_ref, images_ref, texts_ref, coef_ref)
    given_ref[...] = image_terms(coef_ref, texts_ref, 0)


def given_rest_kernel(texts_ref, coef_ref, given_ref):
    given_ref[...] = image_terms(coef_ref, texts_ref, 1)


def text_kernel(part, own_coef, images_ref, others_coef, others_ref, *outs):
    rows = slice(part * ROWS, (part + 1) * ROWS)
    got = jnp.dot(own_coef[rows, :], images_ref[:TILE, :], preferred_element_type=F32)
    got += jnp.dot(others_coef[rows, :], others_ref[:TILE, :], preferred_element_type=F32)
    share_out(got, outs)


def kept_kernel(part, texts_ref, coef_ref, taken_ref, *outs):
    share_out(image_terms(coef_ref, texts_ref, part) + taken_ref[...], outs)


def back_kernel(*refs):
    *inputs, out_ref = refs
    for tower in range(2):
        mine, right, left, far, got, emb, inverse = inputs[tower * 7 : tower * 7 + 7]
        gradients = mine[:QUARTER, :] + right[:QUARTER, :] + left[:QUARTER, :]
        gradients += far[...] + got[...]
        widened = emb[:QUARTER, :].astype(F32)
        inner_sum = jnp.sum(widened * gradients, axis=1, keepdims=True)
        value = (inverse[:, :1] * (gradients - widened * inner_sum)).astype(BF16)
        for i in range(4):
            out_ref[i, tower * QUARTER : (tower + 1) * QUARTER, :] = value[
                :, i * SLICE : (i + 1) * SLICE
            ]


def terms_kernel(images_ref, texts_ref, backs_ref, out_ref, both_ref):
    for i in range(4):
        for part in range(2):
            both_ref[part, i * QUARTER : (i + 1) * QUARTER, :] = backs_ref[
                i, part * QUARTER : (part + 1) * QUARTER, :
            ]
    rows = STEP * GROUP
    steps = 128 // STEP
    last = images_ref.shape[0] // rows - 1
    first = steps - texts_ref.shape[0] // rows
    for step in range(steps):
        terms = jnp.zeros((rows, SLICE), F32)
        if step <= last:
            terms += jnp.dot(
                images_ref[step * rows : (step + 1) * rows, :], both_ref[0],
                preferred_element_type=F32,
            )
        if step >= first:
            terms += jnp.dot(
                texts_ref[(step - first) * rows : (step - first + 1) * rows, :], both_ref[1],
                preferred_element_type=F32,
            )
        terms = terms.reshape(STEP, GROUP, SLICE)
        largest = jnp.max(jnp.max(jnp.abs(terms), axis=1), axis=1, keepdims=True)
        exponent = jnp.ceil(jnp.log(jnp.maximum(largest, 1e-30)) * (1.0 / OCTAVE) + 0.01)
        factor = 32767.0 * jnp.exp(exponent * -OCTAVE)
        row = lax.broadcasted_iota(jnp.int32, terms.shape, 1)
        coded = jnp.where(row == OWN, exponent[:, :, None], jnp.round(terms * factor[:, :, None]))
        out_ref[step * STEP : (step + 1) * STEP] = coded.astype(jnp.int32).astype(jnp.int16)


def total_kernel(coded_ref, out_ref):
    for part in range(4):
        total = jnp.zeros((GROUP, SLICE), F32)
        for i in range(32):
            terms = coded_ref[part * 32 + i].astype(jnp.int32).astype(F32)
            total += terms * (jnp.exp(terms[OWN : OWN + 1, :] * OCTAVE) * (1.0 / 32767.0))
        out_ref[:, part * SLICE : (part + 1) * SLICE] = total[:OWN]


def groups_kernel(where_ref, image_feats, text_feats, early, image_out, text_out, held_ref):
    def fill(feats_ref, out_ref, starts, start, first):
        depth = feats_ref.shape[1]
        for i, at in enumerate(starts):
            held_ref[i * QUARTER : (i + 1) * QUARTER, :depth] = feats_ref[at, :]
        for i in range(out_ref.shape[0] // (STEP * GROUP)):
            begin = (first + i) * STEP * OWN - start
            low = min(max(begin // 128 * 128, 0), depth - ROWS)
            row = lax.broadcasted_iota(jnp.int32, (STEP * GROUP, ROWS), 0)
            lane = lax.broadcasted_iota(jnp.int32, (STEP * GROUP, ROWS), 1)
            inside = lax.rem(row, GROUP)
            wanted = lax.div(row, GROUP) * OWN + inside + (begin - low)
            select = jnp.where((inside < OWN) & (wanted == lane), 1.0, 0.0).astype(BF16)
            out_ref[i * STEP * GROUP : (i + 1) * STEP * GROUP, :] = lax.dot_general(
                select, held_ref[:, low : low + ROWS], NT, preferred_element_type=F32
            ).astype(BF16)

    width = image_feats.shape[1]
    quarters = [pl.ds(i * QUARTER, QUARTER) for i in (0, 2, 1, 3)]
    fill(image_feats, image_out, quarters, 0, 0)
    _, _, _, xh, _, _ = position(where_ref)
    half = [xh, xh, 1 - xh, 1 - xh]
    quarters = [
        pl.ds(pl.multiple_of(half[i] * HALF + i % 2 * QUARTER, QUARTER), QUARTER) for i in range(4)
    ]
    fill(text_feats, text_out, quarters, width, width // OWN // STEP)


def body(image_feats, text_feats, image_weight, text_weight, partner, log_scale, logit_bias):
    where = lax.axis_index(AXES).astype(jnp.int32).reshape(1)
    scalars = jnp.concatenate([jnp.exp(log_scale), logit_bias])

    depth = image_feats.shape[1]
    own_texts, text_inverse, load, image_inverse = call(
        embed_kernel,
        [
            shape(QUARTER, E, dtype=BF16), shape(QUARTER, 128),
            shape(HALF + EXTRA, E, dtype=BF16), shape(QUARTER, 128),
        ],
        2 * (QUARTER * E + HALF * depth) * E, 8 << 20, 60,
        in_specs=[SMEM, VMEM] + [ANY] * 4, out_specs=[VMEM] * 4,
        scratch_shapes=[
            pltpu.VMEM((QUARTER, E), BF16), pltpu.VMEM((HALF, depth), BF16),
            pltpu.VMEM((E, E), BF16), pltpu.VMEM((depth, E), BF16),
            pltpu.VMEM((QUARTER, E), F32), pltpu.VMEM((HALF, E), F32),
            pltpu.SemaphoreType.DMA((11,)),
        ],
    )(where, partner.reshape(3, 128), text_feats, image_feats, text_weight, image_weight)
    other_texts = lax.ppermute(own_texts, ("xl", "xh"), FLIP)
    pair = jnp.concatenate([own_texts, other_texts], 0)
    image_pieces, text_pieces = ring_gather(load, "z"), ring_gather(pair, "y")
    images = call(
        images_kernel, shape(TILE + EXTRA, E, dtype=BF16), 0, 4 << 20,
        in_specs=[VMEM] * 5, out_specs=VMEM,
    )(*image_pieces)
    others = lax.ppermute(images, "core", SWAP)

    last, first = (depth - 1) // OWN // STEP, depth // OWN // STEP
    image_groups, text_groups = call(
        groups_kernel,
        [
            shape((last + 1) * STEP * GROUP, ROWS, dtype=BF16),
            shape((128 // STEP - first) * STEP * GROUP, ROWS, dtype=BF16),
        ],
        2 * 17 * STEP * GROUP * ROWS * ROWS, 5 << 20,
        in_specs=[SMEM, VMEM, VMEM, ANY], out_specs=[VMEM] * 2,
        scratch_shapes=[pltpu.VMEM((ROWS, depth), BF16)],
    )(where, image_feats, text_feats, image_pieces[2])

    flops = 2 * TILE * TILE * E
    coef, texts = shape(TILE, TILE, dtype=BF16), shape(TILE, E, dtype=BF16)
    ways = [shape(QUARTER, E)] * 2 + [shape(HALF, E)]
    rest = [shape(HALF, E)] * 2

    def run(kernel, outs, share, count, *options):
        return call(
            lambda *refs: kernel(*options, *refs), outs, int(share * flops), 6 << 20, 24,
            in_specs=[VMEM] * count, out_specs=[VMEM] * len(outs),
        )

    texts, own_coef = call(
        own_kernel, [texts, coef], 16 * flops, 6 << 20, 24,
        in_specs=[SMEM] * 2 + [VMEM] * 6 + [ANY] * 2, out_specs=[VMEM] * 2,
    )(where, scalars, *text_pieces, images, image_groups, text_groups)
    others_coef, given = call(
        given_kernel, [coef, shape(ROWS, E)], 2 * flops, 8 << 20, 24,
        in_specs=[SMEM] * 2 + [VMEM] * 2, out_specs=[VMEM] * 2,
    )(where, scalars, texts, others)
    taken = lax.ppermute(given, "core", SWAP)
    sides = own_coef, images, others_coef, others
    text_ways = run(text_kernel, ways, 1, 4, 0)(*sides)
    given_rest, = run(given_rest_kernel, [shape(ROWS, E)], 0.5, 2)(texts, others_coef)
    taken_rest = lax.ppermute(given_rest, "core", SWAP)
    image_ways = run(kept_kernel, ways, 0.5, 3, 0)(texts, own_coef, taken)
    text_rest = run(text_kernel, rest, 8, 4, 1)(*sides)
    image_rest = run(kept_kernel, rest, 0.5, 3, 1)(texts, own_coef, taken_rest)
    text_sums = ring_scatter(
        *text_ways, *text_rest, "y", lambda a: lax.ppermute(a, ("xl", "xh"), FLIP)
    )
    image_sums = ring_scatter(
        *image_ways, *image_rest, "z", lambda a: lax.ppermute(a, "xl", SWAP)
    )

    backs = call(
        back_kernel, shape(4, HALF, SLICE, dtype=BF16), 0, 6 << 20,
        in_specs=[VMEM] * 14, out_specs=VMEM,
    )(*image_sums, load, image_inverse, *text_sums, own_texts, text_inverse)
    backs = lax.all_to_all(backs, TOWER, split_axis=0, concat_axis=0, tiled=True)

    coded = call(
        terms_kernel, shape(128, GROUP, SLICE, dtype=jnp.int16),
        4 * 128 * GROUP * ROWS * SLICE, 6 << 20, 24,
        in_specs=[VMEM] * 3, out_specs=VMEM,
        scratch_shapes=[pltpu.VMEM((2, ROWS, SLICE), BF16)],
    )(image_groups, text_groups, backs)
    coded = lax.all_to_all(coded, AXES, split_axis=0, concat_axis=0, tiled=True)
    return call(total_kernel, shape(OWN, E), 0, 2 << 20, in_specs=[VMEM], out_specs=VMEM)(coded)


def solution(mesh):
    fine = Mesh(mesh.devices.reshape([SIZES[a] for a in AXES]), AXES)
    placed = (P(DP, None), P(DP, None), P(), P(), P(DP), P(), P())
    return jax.shard_map(
        body, mesh=fine, in_specs=placed, out_specs=P(TOWER + DP, None), check_vma=False
    )
```

time: 264 us -> 132 us (0.50)
  waiting for transfers between devices: 88.4 us -> 25.1 us
  matrix products: 38.1 us -> 0 us
  Pallas kernels: 0 us -> 22.6 us
  blocking collectives: 69.8 us -> 49.5 us
  local copies, waits for them, and re-layouts: 18.1 us -> 1.04 us
  between operations: 14.9 us -> 1.6 us
  other arithmetic: 13.2 us -> 0.33 us
  starting transfers between devices: 20 us -> 31.6 us
    all_to_all x3 -> x0, waiting for transfers between devices: 47.9 us -> none  [the longest x1 35.1 us: body(): lax.all_to_all(text_part.reshape(4, half, width), 'y', split_axis=0, conc...]
    dot_general x8 -> x0, matrix products: 38.1 us -> none  [the longest x1 6.95 us: body(): lax.dot_general(coefficient, images, (((0,), (0,)), ((), ())), preferred_...]
    all_gather x1 -> x0, waiting for transfers between devices: 27 us -> none  [body(): mine = lax.all_gather(half_images, 'z', axis=0, tiled=True)]
    all_gather x2 -> x0, blocking collectives: 24.7 us -> none  [the longest x1 15.6 us: body(): text_backs = lax.all_gather(text_back, TOWER, axis=0, tiled=True)]
    ppermute x3 -> x20, starting transfers between devices: 2.91 us -> 27.6 us  [the longest x14 23 us: shifted(): return lax.ppermute(array, axis, [(i, (i + by) % 4) for i in range(4)])]
    pallas_call x0 -> x13, Pallas kernels: none -> 22.6 us  [the longest x1 4.89 us: body(): call(embed_kernel, [shape(QUARTER, E, dtype=BF16), shape(QUARTER, 128), s...]
    ppermute x3 -> x20, waiting for transfers between devices: 6.38 us -> 25.1 us  [the longest x14 16.8 us: shifted(): return lax.ppermute(array, axis, [(i, (i + by) % 4) for i in range(4)])]
    all_to_all x3 -> x0, starting transfers between devices: 12.2 us -> none  [the longest x1 4.65 us: body(): lax.all_to_all(text_part.reshape(4, half, width), 'y', split_axis=0, conc...]
  transfers between devices with their start and end apart: 10 -> 22, of which waited for: 7 -> 9; matrix products, arithmetic and copies ran while one was open for 13% -> 1% of each run, Pallas kernels for 0% -> 8%
where the time goes in v2:
time: 132 us
  blocking collectives  49.5 us (38%)
  starting transfers between devices  31.6 us (24%)
  waiting for transfers between devices  25.1 us (19%)
  Pallas kernels  22.6 us (17%)
  between operations  1.6 us (1%)
    all_to_all x1, blocking collectives, body(): coded = lax.all_to_all(coded, AXES, split_axis=0, concat_axis=0, tiled=True)  30.4 us
    ppermute x14, starting transfers between devices, shifted(): return lax.ppermute(array, axis, [(i, (i + by) % 4) for i in range(4)])  23 us
    all_to_all x1, blocking collectives, body(): lax.all_to_all(backs, TOWER, split_axis=0, concat_axis=0, tiled=True)  19.1 us
    ppermute x14, waiting for transfers between devices, shifted(): return lax.ppermute(array, axis, [(i, (i + by) % 4) for i in range(4)])  16.8 us
    ppermute x2, waiting for transfers between devices, body(): lax.ppermute(a, ('xl', 'xh'), FLIP)  6.47 us
    pallas_call x1, Pallas kernels, body(): call(embed_kernel, [shape(QUARTER, E, dtype=BF16), shape(QUARTER, 128), s...  4.89 us
    pallas_call x1, Pallas kernels, body(): call(given_kernel, [coef, shape(ROWS, E)], 2 * flops, 8 << 20, 24, in_spe...  3.92 us
    ppermute x1, starting transfers between devices, body(): other_texts = lax.ppermute(own_texts, ('xl', 'xh'), FLIP)  3.39 us
  transfers between devices with their start and end apart: 22, of which 9 were waited for; matrix products, arithmetic and copies ran while one was open for 1% of the time, Pallas kernels for 8%

profile of v2, /device:TPU:1, one launch (start us, length us, event | category | flops | bytes accessed | tf_op | source)
XLA Modules:
  0.0 131.7 jit_solution(8874345536289926287)
XLA Ops:
  0.0 4.9 %shard_map.73 = (bf16[96,1024]{1,0:T(8,128)(2,1)}, f32[96,128]{1,0:T(8,128)}, bf16[208,1024]{1,0:T(8,128)(2,1)}, f32[96,128]{1,0:T(8,128)}) custom-call(s32[1]{0:T(128)} %bitcast.where_ref, s32[3,128]{1,0:T(4,128)} %bitcast.2, bf16[384,1024]{1,0:T(8,128)(2,1)} %text_feats.3, bf16[384,1664]{1,0:T(8,128)(2,1)} %image_feats.3, bf16[1024,1024]{1,0:T(8,128)(2,1)} %text_weight.1, ...), custom_call_target="tpu_custom_call" | custom-call | flops 855638016 | bytes 8388608 | tf_op jit(solution)/shard_map/pallas_call | solution.py:319
  4.9 3.4 %collective-permute-start.1 = (bf16[96,1024]{1,0:T(8,128)(2,1)}, bf16[96,1024]{1,0:T(8,128)(2,1)S(1)}, u32[]{:S(2)}, u32[]{:S(2)}) collective-permute-start(bf16[96,1024]{1,0:T(8,128)(2,1)} %get-tuple-element.28.refs_12_), channel_id=1, source_target_pairs={{0,68},{4,64},{64,4},{68,0},{1,69},{5,65},{65,5},{69,1},{2,70},{6,... | collective-permute-start | bytes 589832 | tf_op jit(solution)/shard_map/ppermute | solution.py:334
  8.3 1.6 %collective-permute-start = (bf16[208,1024]{1,0:T(8,128)(2,1)}, bf16[208,1024]{1,0:T(8,128)(2,1)S(1)}, u32[]{:S(2)}, u32[]{:S(2)}) collective-permute-start(bf16[208,1024]{1,0:T(8,128)(2,1)} %get-tuple-element.25.me.refs_5_), channel_id=1, source_target_pairs={{0,8},{8,16},{16,24},{24,0},{1,9},{9,17},{17,25},{25,1},{2,10},{10... | collective-permute-start | bytes 1277960 | tf_op jit(solution)/shard_map/ppermute | solution.py:32
  9.9 2.1 %collective-permute-start.6 = (bf16[208,1024]{1,0:T(8,128)(2,1)}, bf16[208,1024]{1,0:T(8,128)(2,1)S(1)}, u32[]{:S(2)}, u32[]{:S(2)}) collective-permute-start(bf16[208,1024]{1,0:T(8,128)(2,1)} %get-tuple-element.25.me.refs_5_), channel_id=1, source_target_pairs={{0,24},{8,0},{16,8},{24,16},{1,25},{9,1},{17,9},{25,17},{2,26},{10... | collective-permute-start | bytes 1277960 | tf_op jit(solution)/shard_map/ppermute | solution.py:32
  13.1 1.4 %collective-permute-start.3 = (bf16[192,1024]{1,0:T(8,128)(2,1)S(1)}, bf16[192,1024]{1,0:T(8,128)(2,1)S(1)}, u32[]{:S(2)}, u32[]{:S(2)}) collective-permute-start(bf16[192,1024]{1,0:T(8,128)(2,1)S(1)} %constant_dynamic-update-slice_fusion.me), channel_id=1, source_target_pairs={{0,1},{1,2},{2,3},{3,0},{4,5},{5,6},{6,7},{7,4},{8,9},{9,10},{10,1... | collective-permute-start | bytes 1179656 | tf_op jit(solution)/shard_map/ppermute | solution.py:32
  14.4 1.5 %collective-permute-start.2 = (bf16[192,1024]{1,0:T(8,128)(2,1)S(1)}, bf16[192,1024]{1,0:T(8,128)(2,1)S(1)}, u32[]{:S(2)}, u32[]{:S(2)}) collective-permute-start(bf16[192,1024]{1,0:T(8,128)(2,1)S(1)} %constant_dynamic-update-slice_fusion.me), channel_id=1, source_target_pairs={{0,3},{1,0},{2,1},{3,2},{4,7},{5,4},{6,5},{7,6},{8,11},{9,8},{10,9... | collective-permute-start | bytes 1179656 | tf_op jit(solution)/shard_map/ppermute | solution.py:32
  15.9 4.7 %collective-permute-done.6.after = bf16[208,1024]{1,0:T(8,128)(2,1)S(1)} collective-permute-done((bf16[208,1024]{1,0:T(8,128)(2,1)}, bf16[208,1024]{1,0:T(8,128)(2,1)S(1)}, u32[]{:S(2)}, u32[]{:S(2)}) %collective-permute-start.6) | collective-permute-done | bytes 426016 | tf_op jit(solution)/shard_map/ppermute | solution.py:32
  20.7 3.3 %collective-permute-start.8 = (bf16[112,1024]{1,0:T(8,128)(2,1)S(1)}, bf16[112,1024]{1,0:T(8,128)(2,1)S(1)}, u32[]{:S(2)}, u32[]{:S(2)}) collective-permute-start(bf16[112,1024]{1,0:T(8,128)(2,1)S(1)} %slice.43), channel_id=1, source_target_pairs={{0,24},{8,0},{16,8},{24,16},{1,25},{9,1},{17,9},{25,17},{2,26},{10... | collective-permute-start | bytes 688136 | tf_op jit(solution)/shard_map/ppermute | solution.py:32
  25.5 1.4 %collective-permute-start.4 = (bf16[96,1024]{1,0:T(8,128)(2,1)S(1)}, bf16[96,1024]{1,0:T(8,128)(2,1)S(1)}, u32[]{:S(2)}, u32[]{:S(2)}) collective-permute-start(bf16[96,1024]{1,0:T(8,128)(2,1)S(1)} %slice.40), channel_id=1, source_target_pairs={{0,1},{1,2},{2,3},{3,0},{4,5},{5,6},{6,7},{7,4},{8,9},{9,10},{10,1... | collective-permute-start | bytes 589832 | tf_op jit(solution)/shard_map/ppermute | solution.py:32
  26.8 1.5 %collective-permute-start.5 = (bf16[96,1024]{1,0:T(8,128)(2,1)S(1)}, bf16[96,1024]{1,0:T(8,128)(2,1)S(1)}, u32[]{:S(2)}, u32[]{:S(2)}) collective-permute-start(bf16[96,1024]{1,0:T(8,128)(2,1)S(1)} %slice.41), channel_id=1, source_target_pairs={{0,3},{1,0},{2,1},{3,2},{4,7},{5,4},{6,5},{7,6},{8,11},{9,8},{10,9... | collective-permute-start | bytes 589832 | tf_op jit(solution)/shard_map/ppermute | solution.py:32
  28.4 2.1 %shard_map.74 = (bf16[1920,384]{1,0:T(8,128)(2,1)S(1)}, bf16[1344,384]{1,0:T(8,128)(2,1)S(1)}) custom-call(s32[1]{0:T(128)} %bitcast.where_ref, bf16[384,1664]{1,0:T(8,128)(2,1)S(1)} %copy-done.1, bf16[384,1024]{1,0:T(8,128)(2,1)S(1)} %copy-done.2, bf16[208,1024]{1,0:T(8,128)(2,1)S(1)} %collective-permute-done.early.before), custom_call_target="tpu_custom_call" | custom-call | flops 962592768 | bytes 5242880 | tf_op jit(solution)/shard_map/pallas_call | solution.py:344
  31.3 3.4 %collective-permute-start.9 = (bf16[784,1024]{1,0:T(8,128)(2,1)S(1)}, bf16[784,1024]{1,0:T(8,128)(2,1)S(1)}, u32[]{:S(2)}, u32[]{:S(2)}) collective-permute-start(bf16[784,1024]{1,0:T(8,128)(2,1)S(1)} %shard_map.75.images_ref.refs_1_), channel_id=1, source_target_pairs={{0,32},{32,0},{1,33},{33,1},{2,34},{34,2},{3,35},{35,3},{4,36},{36... | collective-permute-start | bytes 4816904 | tf_op jit(solution)/shard_map/ppermute | solution.py:341
  34.7 3.3 %shard_map.76 = (bf16[768,1024]{1,0:T(8,128)(2,1)S(1)}, bf16[768,768]{1,0:T(8,128)(2,1)S(1)}) custom-call(s32[1]{0:T(128)} %bitcast.where_ref, f32[2]{0:T(128)S(1)} %pad_maximum_fusion.scalar_ref, bf16[192,1024]{1,0:T(8,128)(2,1)S(1)} %constant_dynamic-update-slice_fusion.me, bf16[192,1024]{1,0:T(8,128)(2,1)S(1)} %collective-permute-done.2.after, ...), custom_call_target="tpu_custom_call" | custom-call | flops 19327352832 | bytes 6291456 | tf_op jit(solution)/shard_map/pallas_call | solution.py:366
  37.9 3.9 %shard_map.77 = (bf16[768,768]{1,0:T(8,128)(2,1)S(1)}, f32[384,1024]{1,0:T(8,128)S(1)}) custom-call(s32[1]{0:T(128)} %bitcast.where_ref, f32[2]{0:T(128)S(1)} %pad_maximum_fusion.scalar_ref, bf16[768,1024]{1,0:T(8,128)(2,1)S(1)} %get-tuple-element.29.texts_ref.refs_0_, bf16[784,1024]{1,0:T(8,128)(2,1)S(1)} %collective-permute-done.9.images_ref.refs_3_), custom_call_target="tpu_custom_call" | custom-call | flops 2415919104 | bytes 8388608 | tf_op jit(solution)/shard_map/pallas_call | solution.py:370
  43.5 1.4 %shard_map.82 = (f32[96,1024]{1,0:T(8,128)S(1)}, f32[96,1024]{1,0:T(8,128)S(1)}, f32[192,1024]{1,0:T(8,128)S(1)}) custom-call(bf16[768,768]{1,0:T(8,128)(2,1)S(1)} %get-tuple-element.30.refs_1_.refs_0_, bf16[784,1024]{1,0:T(8,128)(2,1)S(1)} %shard_map.75.images_ref.refs_1_, bf16[768,768]{1,0:T(8,128)(2,1)S(1)} %get-tuple-element.31.refs_1_.refs_2_, ...), custom_call_target="tpu_custom_call" | custom-call | flops 1207959552 | bytes 6291456 | tf_op jit(solution)/shard_map/pallas_call | solution.py:376
  44.9 1.4 %collective-permute-start.17 = (f32[192,1024]{1,0:T(8,128)S(1)}, f32[192,1024]{1,0:T(8,128)S(1)}, u32[]{:S(2)}, u32[]{:S(2)}) collective-permute-start(f32[192,1024]{1,0:T(8,128)S(1)} %get-tuple-element.40), channel_id=1, source_target_pairs={{0,1},{1,2},{2,3},{3,0},{4,5},{5,6},{6,7},{7,4},{8,9},{9,10},{10,1... | collective-permute-start | bytes 2359304 | tf_op jit(solution)/shard_map/ppermute | solution.py:32
  46.3 1.4 %shard_map.81 = (f32[192,1024]{1,0:T(8,128)S(1)}, f32[192,1024]{1,0:T(8,128)S(1)}) custom-call(bf16[768,768]{1,0:T(8,128)(2,1)S(1)} %get-tuple-element.30.refs_1_.refs_0_, bf16[784,1024]{1,0:T(8,128)(2,1)S(1)} %shard_map.75.images_ref.refs_1_, bf16[768,768]{1,0:T(8,128)(2,1)S(1)} %get-tuple-element.31.refs_1_.refs_2_, ...), custom_call_target="tpu_custom_call" | custom-call | flops 9663676416 | bytes 6291456 | tf_op jit(solution)/shard_map/pallas_call | solution.py:380
  47.7 1.5 %collective-permute-start.18 = (f32[192,1024]{1,0:T(8,128)S(1)}, f32[192,1024]{1,0:T(8,128)S(1)}, u32[]{:S(2)}, u32[]{:S(2)}) collective-permute-start(f32[192,1024]{1,0:T(8,128)S(1)} %get-tuple-element.41), channel_id=1, source_target_pairs={{0,3},{1,0},{2,1},{3,2},{4,7},{5,4},{6,5},{7,6},{8,11},{9,8},{10,9... | collective-permute-start | bytes 2359304 | tf_op jit(solution)/shard_map/ppermute | solution.py:32
  50.5 1.7 %collective-permute-start.12 = (f32[192,1024]{1,0:T(8,128)S(1)}, f32[192,1024]{1,0:T(8,128)S(1)}, u32[]{:S(2)}, u32[]{:S(2)}) collective-permute-start(f32[192,1024]{1,0:T(8,128)S(1)} %get-tuple-element.34), channel_id=1, source_target_pairs={{0,8},{8,16},{16,24},{24,0},{1,9},{9,17},{17,25},{25,1},{2,10},{10... | collective-permute-start | bytes 2359304 | tf_op jit(solution)/shard_map/ppermute | solution.py:32
  53.1 2.2 %collective-permute-start.13 = (f32[192,1024]{1,0:T(8,128)S(1)}, f32[192,1024]{1,0:T(8,128)S(1)}, u32[]{:S(2)}, u32[]{:S(2)}) collective-permute-start(f32[192,1024]{1,0:T(8,128)S(1)} %get-tuple-element.35), channel_id=1, source_target_pairs={{0,24},{8,0},{16,8},{24,16},{1,25},{9,1},{17,9},{25,17},{2,26},{10... | collective-permute-start | bytes 2359304 | tf_op jit(solution)/shard_map/ppermute | solution.py:32
  55.3 4.9 %collective-permute-done.19 = f32[96,1024]{1,0:T(8,128)S(1)} collective-permute-done((f32[96,1024]{1,0:T(8,128)S(1)}, f32[96,1024]{1,0:T(8,128)S(1)}, u32[]{:S(2)}, u32[]{:S(2)}) %collective-permute-start.19) | collective-permute-done | bytes 393248 | tf_op jit(solution)/shard_map/ppermute | solution.py:383
  60.3 4.8 %collective-permute-done.17.refs_8_ = f32[192,1024]{1,0:T(8,128)S(1)} collective-permute-done((f32[192,1024]{1,0:T(8,128)S(1)}, f32[192,1024]{1,0:T(8,128)S(1)}, u32[]{:S(2)}, u32[]{:S(2)}) %collective-permute-start.17) | collective-permute-done | bytes 786464 | tf_op jit(solution)/shard_map/ppermute | solution.py:32
  65.1 1.8 %collective-permute-start.20 = (f32[96,1024]{1,0:T(8,128)S(1)}, f32[96,1024]{1,0:T(8,128)S(1)}, u32[]{:S(2)}, u32[]{:S(2)}) collective-permute-start(f32[96,1024]{1,0:T(8,128)S(1)} %add.37), channel_id=1, source_target_pairs={{0,2},{1,3},{2,0},{3,1},{4,6},{5,7},{6,4},{7,5},{8,10},{9,11},{10,... | collective-permute-start | bytes 1179656 | tf_op jit(solution)/shard_map/ppermute | solution.py:32
  67.3 1.8 %collective-permute-done.14 = f32[96,1024]{1,0:T(8,128)S(1)} collective-permute-done((f32[96,1024]{1,0:T(8,128)S(1)}, f32[96,1024]{1,0:T(8,128)S(1)}, u32[]{:S(2)}, u32[]{:S(2)}) %collective-permute-start.14) | collective-permute-done | bytes 393248 | tf_op jit(solution)/shard_map/ppermute | solution.py:386
  69.1 1.6 %collective-permute-start.15 = (f32[96,1024]{1,0:T(8,128)S(1)}, f32[96,1024]{1,0:T(8,128)S(1)}, u32[]{:S(2)}, u32[]{:S(2)}) collective-permute-start(f32[96,1024]{1,0:T(8,128)S(1)} %add.34), channel_id=1, source_target_pairs={{0,16},{8,24},{16,0},{24,8},{1,17},{9,25},{17,1},{25,9},{2,18},{10... | collective-permute-start | bytes 1179656 | tf_op jit(solution)/shard_map/ppermute | solution.py:32
  71.4 4.8 %collective-permute-done.20.refs_10_ = f32[96,1024]{1,0:T(8,128)S(1)} collective-permute-done((f32[96,1024]{1,0:T(8,128)S(1)}, f32[96,1024]{1,0:T(8,128)S(1)}, u32[]{:S(2)}, u32[]{:S(2)}) %collective-permute-start.20) | collective-permute-done | bytes 393248 | tf_op jit(solution)/shard_map/ppermute | solution.py:32
  76.1 1.5 %collective-permute-done.21.refs_11_ = f32[96,1024]{1,0:T(8,128)S(1)} collective-permute-done((f32[96,1024]{1,0:T(8,128)S(1)}, f32[96,1024]{1,0:T(8,128)S(1)}, u32[]{:S(2)}, u32[]{:S(2)}) %collective-permute-start.21) | collective-permute-done | bytes 393248 | tf_op jit(solution)/shard_map/ppermute | solution.py:383
  77.6 1.4 %collective-permute-done.15.refs_3_ = f32[96,1024]{1,0:T(8,128)S(1)} collective-permute-done((f32[96,1024]{1,0:T(8,128)S(1)}, f32[96,1024]{1,0:T(8,128)S(1)}, u32[]{:S(2)}, u32[]{:S(2)}) %collective-permute-start.15) | collective-permute-done | bytes 393248 | tf_op jit(solution)/shard_map/ppermute | solution.py:32
  79.5 19.1 %all_to_all.10.backs_ref = bf16[4,192,256]{2,1,0:T(8,128)(2,1)S(1)} all-to-all(bf16[4,192,256]{2,1,0:T(8,128)(2,1)S(1)} %shard_map.83), channel_id=1, replica_groups=mesh['xl'=2,'core'=2,'z'=4,'xh'=2,'y'=4] {'xl','core'}, dimensions={0} | all-to-all | bytes 786432 | tf_op jit(solution)/shard_map/all_to_all | solution.py:393
  98.7 1.4 %shard_map.84 = s16[128,24,256]{2,1,0:T(8,128)(2,1)S(1)} custom-call(bf16[1920,384]{1,0:T(8,128)(2,1)S(1)} %get-tuple-element.26.early_a.images_ref, bf16[1344,384]{1,0:T(8,128)(2,1)S(1)} %get-tuple-element.27.early_b.texts_ref, bf16[4,192,256]{2,1,0:T(8,128)(2,1)S(1)} %all_to_all.10.backs_ref), custom_call_target="tpu_custom_call" | custom-call | flops 1207959552 | bytes 6291456 | tf_op jit(solution)/shard_map/pallas_call | solution.py:395
  100.1 30.4 %all_to_all.11.coded_ref = s16[128,24,256]{2,1,0:T(8,128)(2,1)S(1)} all-to-all(s16[128,24,256]{2,1,0:T(8,128)(2,1)S(1)} %shard_map.84), channel_id=1, replica_groups=mesh['xl'=2,'core'=2,'z'=4,'xh'=2,'y'=4] {'xl','core','z','xh','y'}, dimensions={0} | all-to-all | bytes 3145728 | tf_op jit(solution)/shard_map/all_to_all | solution.py:401
  130.5 1.2 shard_map.85
  (50 shorter events, 7.3 us)
Async XLA Ops:
  4.9 23.5 %copy-start.1 = (bf16[384,1664]{1,0:T(8,128)(2,1)S(1)}, bf16[384,1664]{1,0:T(8,128)(2,1)}, u32[]{:S(2)}) copy-start(bf16[384,1664]{1,0:T(8,128)(2,1)} %image_feats.3) | copy-start | bytes 3833860
  4.9 23.5 %copy-start.2 = (bf16[384,1024]{1,0:T(8,128)(2,1)S(1)}, bf16[384,1024]{1,0:T(8,128)(2,1)}, u32[]{:S(2)}) copy-start(bf16[384,1024]{1,0:T(8,128)(2,1)} %text_feats.3) | copy-start | bytes 2359300
  4.9 8.1 %collective-permute-start.1 = (bf16[96,1024]{1,0:T(8,128)(2,1)}, bf16[96,1024]{1,0:T(8,128)(2,1)S(1)}, u32[]{:S(2)}, u32[]{:S(2)}) collective-permute-start(bf16[96,1024]{1,0:T(8,128)(2,1)} %get-tuple-element.28.refs_12_), channel_id=1, source_target_pairs={{0,68},{4,64},{64,4},{68,0},{1,69},{5,65},{65,5},{69,1},{2,70},{6,... | collective-permute-start | bytes 589832 | tf_op jit(solution)/shard_map/ppermute | solution.py:334
  8.3 17.0 %collective-permute-start = (bf16[208,1024]{1,0:T(8,128)(2,1)}, bf16[208,1024]{1,0:T(8,128)(2,1)S(1)}, u32[]{:S(2)}, u32[]{:S(2)}) collective-permute-start(bf16[208,1024]{1,0:T(8,128)(2,1)} %get-tuple-element.25.me.refs_5_), channel_id=1, source_target_pairs={{0,8},{8,16},{16,24},{24,0},{1,9},{9,17},{17,25},{25,1},{2,10},{10... | collective-permute-start | bytes 1277960 | tf_op jit(solution)/shard_map/ppermute | solution.py:32
  9.9 10.7 %collective-permute-start.6 = (bf16[208,1024]{1,0:T(8,128)(2,1)}, bf16[208,1024]{1,0:T(8,128)(2,1)S(1)}, u32[]{:S(2)}, u32[]{:S(2)}) collective-permute-start(bf16[208,1024]{1,0:T(8,128)(2,1)} %get-tuple-element.25.me.refs_5_), channel_id=1, source_target_pairs={{0,24},{8,0},{16,8},{24,16},{1,25},{9,1},{17,9},{25,17},{2,26},{10... | collective-permute-start | bytes 1277960 | tf_op jit(solution)/shard_map/ppermute | solution.py:32
  13.1 12.4 %collective-permute-start.3 = (bf16[192,1024]{1,0:T(8,128)(2,1)S(1)}, bf16[192,1024]{1,0:T(8,128)(2,1)S(1)}, u32[]{:S(2)}, u32[]{:S(2)}) collective-permute-start(bf16[192,1024]{1,0:T(8,128)(2,1)S(1)} %constant_dynamic-update-slice_fusion.me), channel_id=1, source_target_pairs={{0,1},{1,2},{2,3},{3,0},{4,5},{5,6},{6,7},{7,4},{8,9},{9,10},{10,1... | collective-permute-start | bytes 1179656 | tf_op jit(solution)/shard_map/ppermute | solution.py:32
  14.4 12.4 %collective-permute-start.2 = (bf16[192,1024]{1,0:T(8,128)(2,1)S(1)}, bf16[192,1024]{1,0:T(8,128)(2,1)S(1)}, u32[]{:S(2)}, u32[]{:S(2)}) collective-permute-start(bf16[192,1024]{1,0:T(8,128)(2,1)S(1)} %constant_dynamic-update-slice_fusion.me), channel_id=1, source_target_pairs={{0,3},{1,0},{2,1},{3,2},{4,7},{5,4},{6,5},{7,6},{8,11},{9,8},{10,9... | collective-permute-start | bytes 1179656 | tf_op jit(solution)/shard_map/ppermute | solution.py:32
  20.7 10.5 %collective-permute-start.8 = (bf16[112,1024]{1,0:T(8,128)(2,1)S(1)}, bf16[112,1024]{1,0:T(8,128)(2,1)S(1)}, u32[]{:S(2)}, u32[]{:S(2)}) collective-permute-start(bf16[112,1024]{1,0:T(8,128)(2,1)S(1)} %slice.43), channel_id=1, source_target_pairs={{0,24},{8,0},{16,8},{24,16},{1,25},{9,1},{17,9},{25,17},{2,26},{10... | collective-permute-start | bytes 688136 | tf_op jit(solution)/shard_map/ppermute | solution.py:32
  25.3 5.8 %collective-permute-start.7 = (bf16[96,1024]{1,0:T(8,128)(2,1)S(1)}, bf16[96,1024]{1,0:T(8,128)(2,1)S(1)}, u32[]{:S(2)}, u32[]{:S(2)}) collective-permute-start(bf16[96,1024]{1,0:T(8,128)(2,1)S(1)} %slice.42), channel_id=1, source_target_pairs={{0,8},{8,16},{16,24},{24,0},{1,9},{9,17},{17,25},{25,1},{2,10},{10... | collective-permute-start | bytes 589832 | tf_op jit(solution)/shard_map/ppermute | solution.py:32
  25.5 9.2 %collective-permute-start.4 = (bf16[96,1024]{1,0:T(8,128)(2,1)S(1)}, bf16[96,1024]{1,0:T(8,128)(2,1)S(1)}, u32[]{:S(2)}, u32[]{:S(2)}) collective-permute-start(bf16[96,1024]{1,0:T(8,128)(2,1)S(1)} %slice.40), channel_id=1, source_target_pairs={{0,1},{1,2},{2,3},{3,0},{4,5},{5,6},{6,7},{7,4},{8,9},{9,10},{10,1... | collective-permute-start | bytes 589832 | tf_op jit(solution)/shard_map/ppermute | solution.py:32
  26.8 7.8 %collective-permute-start.5 = (bf16[96,1024]{1,0:T(8,128)(2,1)S(1)}, bf16[96,1024]{1,0:T(8,128)(2,1)S(1)}, u32[]{:S(2)}, u32[]{:S(2)}) collective-permute-start(bf16[96,1024]{1,0:T(8,128)(2,1)S(1)} %slice.41), channel_id=1, source_target_pairs={{0,3},{1,0},{2,1},{3,2},{4,7},{5,4},{6,5},{7,6},{8,11},{9,8},{10,9... | collective-permute-start | bytes 589832 | tf_op jit(solution)/shard_map/ppermute | solution.py:32
  28.4 2.7 %copy-start = (bf16[208,1024]{1,0:T(8,128)(2,1)S(1)}, bf16[208,1024]{1,0:T(8,128)(2,1)}, u32[]{:S(2)}) copy-start(bf16[208,1024]{1,0:T(8,128)(2,1)} %get-tuple-element.25.me.refs_5_) | copy-start | bytes 1277956
  31.3 6.6 %collective-permute-start.9 = (bf16[784,1024]{1,0:T(8,128)(2,1)S(1)}, bf16[784,1024]{1,0:T(8,128)(2,1)S(1)}, u32[]{:S(2)}, u32[]{:S(2)}) collective-permute-start(bf16[784,1024]{1,0:T(8,128)(2,1)S(1)} %shard_map.75.images_ref.refs_1_), channel_id=1, source_target_pairs={{0,32},{32,0},{1,33},{33,1},{2,34},{34,2},{3,35},{35,3},{4,36},{36... | collective-permute-start | bytes 4816904 | tf_op jit(solution)/shard_map/ppermute | solution.py:341
  41.9 7.9 %collective-permute-start.11 = (f32[384,1024]{1,0:T(8,128)S(1)}, f32[384,1024]{1,0:T(8,128)S(1)}, u32[]{:S(2)}, u32[]{:S(2)}) collective-permute-start(f32[384,1024]{1,0:T(8,128)S(1)} %get-tuple-element.33), channel_id=1, source_target_pairs={{0,32},{32,0},{1,33},{33,1},{2,34},{34,2},{3,35},{35,3},{4,36},{36... | collective-permute-start | bytes 4718600 | tf_op jit(solution)/shard_map/ppermute | solution.py:374
  43.3 9.0 %collective-permute-start.10 = (f32[384,1024]{1,0:T(8,128)S(1)}, f32[384,1024]{1,0:T(8,128)S(1)}, u32[]{:S(2)}, u32[]{:S(2)}) collective-permute-start(f32[384,1024]{1,0:T(8,128)S(1)} %shard_map.78), channel_id=1, source_target_pairs={{0,32},{32,0},{1,33},{33,1},{2,34},{34,2},{3,35},{35,3},{4,36},{36... | collective-permute-start | bytes 4718600 | tf_op jit(solution)/shard_map/ppermute | solution.py:378
  44.9 20.2 %collective-permute-start.17 = (f32[192,1024]{1,0:T(8,128)S(1)}, f32[192,1024]{1,0:T(8,128)S(1)}, u32[]{:S(2)}, u32[]{:S(2)}) collective-permute-start(f32[192,1024]{1,0:T(8,128)S(1)} %get-tuple-element.40), channel_id=1, source_target_pairs={{0,1},{1,2},{2,3},{3,0},{4,5},{5,6},{6,7},{7,4},{8,9},{9,10},{10,1... | collective-permute-start | bytes 2359304 | tf_op jit(solution)/shard_map/ppermute | solution.py:32
  47.7 19.2 %collective-permute-start.18 = (f32[192,1024]{1,0:T(8,128)S(1)}, f32[192,1024]{1,0:T(8,128)S(1)}, u32[]{:S(2)}, u32[]{:S(2)}) collective-permute-start(f32[192,1024]{1,0:T(8,128)S(1)} %get-tuple-element.41), channel_id=1, source_target_pairs={{0,3},{1,0},{2,1},{3,2},{4,7},{5,4},{6,5},{7,6},{8,11},{9,8},{10,9... | collective-permute-start | bytes 2359304 | tf_op jit(solution)/shard_map/ppermute | solution.py:32
  49.2 11.0 %collective-permute-start.19 = (f32[96,1024]{1,0:T(8,128)S(1)}, f32[96,1024]{1,0:T(8,128)S(1)}, u32[]{:S(2)}, u32[]{:S(2)}) collective-permute-start(f32[96,1024]{1,0:T(8,128)S(1)} %get-tuple-element.43), channel_id=1, source_target_pairs={{0,68},{4,64},{64,4},{68,0},{1,69},{5,65},{65,5},{69,1},{2,70},{6,... | collective-permute-start | bytes 1179656 | tf_op jit(solution)/shard_map/ppermute | solution.py:383
  50.5 20.6 %collective-permute-start.12 = (f32[192,1024]{1,0:T(8,128)S(1)}, f32[192,1024]{1,0:T(8,128)S(1)}, u32[]{:S(2)}, u32[]{:S(2)}) collective-permute-start(f32[192,1024]{1,0:T(8,128)S(1)} %get-tuple-element.34), channel_id=1, source_target_pairs={{0,8},{8,16},{16,24},{24,0},{1,9},{9,17},{17,25},{25,1},{2,10},{10... | collective-permute-start | bytes 2359304 | tf_op jit(solution)/shard_map/ppermute | solution.py:32
  53.1 18.1 %collective-permute-start.13 = (f32[192,1024]{1,0:T(8,128)S(1)}, f32[192,1024]{1,0:T(8,128)S(1)}, u32[]{:S(2)}, u32[]{:S(2)}) collective-permute-start(f32[192,1024]{1,0:T(8,128)S(1)} %get-tuple-element.35), channel_id=1, source_target_pairs={{0,24},{8,0},{16,8},{24,16},{1,25},{9,1},{17,9},{25,17},{2,26},{10... | collective-permute-start | bytes 2359304 | tf_op jit(solution)/shard_map/ppermute | solution.py:32
  60.2 8.9 %collective-permute-start.14 = (f32[96,1024]{1,0:T(8,128)S(1)}, f32[96,1024]{1,0:T(8,128)S(1)}, u32[]{:S(2)}, u32[]{:S(2)}) collective-permute-start(f32[96,1024]{1,0:T(8,128)S(1)} %get-tuple-element.37), channel_id=1, source_target_pairs={{0,64},{64,0},{1,65},{65,1},{2,66},{66,2},{3,67},{67,3},{4,68},{68... | collective-permute-start | bytes 1179656 | tf_op jit(solution)/shard_map/ppermute | solution.py:386
  65.1 11.0 %collective-permute-start.20 = (f32[96,1024]{1,0:T(8,128)S(1)}, f32[96,1024]{1,0:T(8,128)S(1)}, u32[]{:S(2)}, u32[]{:S(2)}) collective-permute-start(f32[96,1024]{1,0:T(8,128)S(1)} %add.37), channel_id=1, source_target_pairs={{0,2},{1,3},{2,0},{3,1},{4,6},{5,7},{6,4},{7,5},{8,10},{9,11},{10,... | collective-permute-start | bytes 1179656 | tf_op jit(solution)/shard_map/ppermute | solution.py:32
  67.0 12.1 %copy-start.3 = (bf16[96,1024]{1,0:T(8,128)(2,1)S(1)}, bf16[96,1024]{1,0:T(8,128)(2,1)}, u32[]{:S(2)}) copy-start(bf16[96,1024]{1,0:T(8,128)(2,1)} %get-tuple-element.28.refs_12_) | copy-start | bytes 589828
  67.0 12.1 %copy-start.4 = (f32[96,128]{1,0:T(8,128)S(1)}, f32[96,128]{1,0:T(8,128)}, u32[]{:S(2)}) copy-start(f32[96,128]{1,0:T(8,128)} %get-tuple-element.44.refs_13_) | copy-start | bytes 147460
  67.0 12.1 %copy-start.5 = (f32[96,128]{1,0:T(8,128)S(1)}, f32[96,128]{1,0:T(8,128)}, u32[]{:S(2)}) copy-start(f32[96,128]{1,0:T(8,128)} %get-tuple-element.38.refs_6_) | copy-start | bytes 147460
  67.0 10.7 %collective-permute-start.21 = (f32[96,1024]{1,0:T(8,128)S(1)}, f32[96,1024]{1,0:T(8,128)S(1)}, u32[]{:S(2)}, u32[]{:S(2)}) collective-permute-start(f32[96,1024]{1,0:T(8,128)S(1)} %slice_add_fusion), channel_id=1, source_target_pairs={{0,68},{4,64},{64,4},{68,0},{1,69},{5,65},{65,5},{69,1},{2,70},{6,... | collective-permute-start | bytes 1179656 | tf_op jit(solution)/shard_map/ppermute | solution.py:383
  69.1 9.9 %collective-permute-start.15 = (f32[96,1024]{1,0:T(8,128)S(1)}, f32[96,1024]{1,0:T(8,128)S(1)}, u32[]{:S(2)}, u32[]{:S(2)}) collective-permute-start(f32[96,1024]{1,0:T(8,128)S(1)} %add.34), channel_id=1, source_target_pairs={{0,16},{8,24},{16,0},{24,8},{1,17},{9,25},{17,1},{25,9},{2,18},{10... | collective-permute-start | bytes 1179656 | tf_op jit(solution)/shard_map/ppermute | solution.py:32
  71.3 7.8 %collective-permute-start.16 = (f32[96,1024]{1,0:T(8,128)S(1)}, f32[96,1024]{1,0:T(8,128)S(1)}, u32[]{:S(2)}, u32[]{:S(2)}) collective-permute-start(f32[96,1024]{1,0:T(8,128)S(1)} %slice_add_fusion.2), channel_id=1, source_target_pairs={{0,64},{64,0},{1,65},{65,1},{2,66},{66,2},{3,67},{67,3},{4,68},{68... | collective-permute-start | bytes 1179656 | tf_op jit(solution)/shard_map/ppermute | solution.py:386

commit v3 on v2

--- a/solution.py
+++ b/solution.py
@@ -132,11 +132,18 @@
     return block, after, before, far_low, far_high
 
 
+def far_kernel(low_ref, high_ref, early_ref, out_ref):
+    out_ref[...] = low_ref[...] + high_ref[...]
+
+
 def ring_scatter(far_low, far_high, after, before, mine, axis, crossed):
-    far = shifted(far_low + crossed(far_high), axis, 2)
+    far = crossed(far_high)
     got_right, got_left = shifted(after, axis, 1), shifted(before, axis, -1)
+    far = call(
+        far_kernel, shape(QUARTER, E), 0, 1 << 20, in_specs=[VMEM, VMEM, ANY], out_specs=VMEM
+    )(far_low, far, got_left)
     high = mine[QUARTER:] + got_right[QUARTER:] + got_left[QUARTER:]
-    return mine, got_right, got_left, far, crossed(high)
+    return mine, got_right, got_left, shifted(far, axis, 2), crossed(high)
 
 
 ORDER = ((2, 0), (2, 1), (1, 0), (1, 1), (3, 0), (3, 1), (0, 0), (0, 1))
@@ -164,26 +171,23 @@
     out_ref[TILE:, :] = total.astype(BF16)
 
 
-def coefficients(where_ref, scalar_ref, images_ref, texts_ref, coef_ref):
+def coefficients(where_ref, scale_ref, shift_ref, images_ref, texts_ref, coef_ref):
     _, _, z, xh, y, text_quarter = position(where_ref)
     parts = images_ref[TILE:, :TILE].astype(F32)
     partner = (parts[0:1] * 128.0 + parts[1:2]).astype(jnp.int32)
-    scale, shift = scalar_ref[0], scalar_ref[1]
-    row = lax.broadcasted_iota(jnp.int32, (HALF, 1), 0)
-    for block in range(4):
-        rows = slice(block * HALF, (block + 1) * HALF)
-        low, high = (
-            ((z * 2 + (1 - xh if half else xh)) * 4 + lax.rem(y + step, 4)) * ROWS
-            + text_quarter * QUARTER
-            for step, half in ORDER[2 * block : 2 * block + 2]
-        )
-        index = row + jnp.where(row < QUARTER, low, high - QUARTER)
-        logits = scale * lax.dot_general(
-            texts_ref[rows, :], images_ref[:TILE, :], NT, preferred_element_type=F32
-        ) + shift
-        own = index == partner
-        slopes = jnp.where(own, -scale, scale) / (1.0 + jnp.exp(jnp.where(own, logits, -logits)))
-        coef_ref[rows, :] = slopes.astype(BF16)
+    scale, shift = jnp.exp(jnp.full((1, 1), scale_ref[0], F32)), shift_ref[0]
+    row = lax.broadcasted_iota(jnp.int32, (TILE, 1), 0)
+    index = row
+    for place, (step, half) in enumerate(ORDER):
+        block = (z * 2 + (1 - xh if half else xh)) * 4 + lax.rem(y + step, 4)
+        start = block * ROWS + text_quarter * QUARTER
+        index = jnp.where(row // QUARTER == place, row + (start - place * QUARTER), index)
+    logits = scale * lax.dot_general(
+        texts_ref[...], images_ref[:TILE, :], NT, preferred_element_type=F32
+    ) + shift
+    own = index == partner
+    slopes = jnp.where(own, -scale, scale) / (1.0 + jnp.exp(jnp.where(own, logits, -logits)))
+    coef_ref[...] = slopes.astype(BF16)
 
 
 def image_terms(coef_ref, texts_ref, part):
@@ -201,15 +205,15 @@
 
 
 def own_kernel(
-    where_ref, scalar_ref, me, after, before, far_low, far_high, images_ref, early_a, early_b,
+    where_ref, scale_ref, shift_ref, me, after, before, far_low, far_high, images_ref, early_a, early_b,
     texts_ref, coef_ref,
 ):
     in_order((me, after, before, far_low, far_high), texts_ref)
-    coefficients(where_ref, scalar_ref, images_ref, texts_ref, coef_ref)
-
-
-def given_kernel(where_ref, scalar_ref, texts_ref, images_ref, coef_ref, given_ref):
-    coefficients(where_ref, scalar_ref, images_ref, texts_ref, coef_ref)
+    coefficients(where_ref, scale_ref, shift_ref, images_ref, texts_ref, coef_ref)
+
+
+def given_kernel(where_ref, scale_ref, shift_ref, texts_ref, images_ref, coef_ref, given_ref):
+    coefficients(where_ref, scale_ref, shift_ref, images_ref, texts_ref, coef_ref)
     given_ref[...] = image_terms(coef_ref, texts_ref, 0)
 
 
@@ -313,8 +317,6 @@
 
 def body(image_feats, text_feats, image_weight, text_weight, partner, log_scale, logit_bias):
     where = lax.axis_index(AXES).astype(jnp.int32).reshape(1)
-    scalars = jnp.concatenate([jnp.exp(log_scale), logit_bias])
-
     depth = image_feats.shape[1]
     own_texts, text_inverse, load, image_inverse = call(
         embed_kernel,
@@ -365,12 +367,12 @@
 
     texts, own_coef = call(
         own_kernel, [texts, coef], 16 * flops, 6 << 20, 24,
-        in_specs=[SMEM] * 2 + [VMEM] * 6 + [ANY] * 2, out_specs=[VMEM] * 2,
-    )(where, scalars, *text_pieces, images, image_groups, text_groups)
+        in_specs=[SMEM] * 3 + [VMEM] * 6 + [ANY] * 2, out_specs=[VMEM] * 2,
+    )(where, log_scale, logit_bias, *text_pieces, images, image_groups, text_groups)
     others_coef, given = call(
         given_kernel, [coef, shape(ROWS, E)], 2 * flops, 8 << 20, 24,
-        in_specs=[SMEM] * 2 + [VMEM] * 2, out_specs=[VMEM] * 2,
-    )(where, scalars, texts, others)
+        in_specs=[SMEM] * 3 + [VMEM] * 2, out_specs=[VMEM] * 2,
+    )(where, log_scale, logit_bias, texts, others)
     taken = lax.ppermute(given, "core", SWAP)
     sides = own_coef, images, others_coef, others
     text_ways = run(text_kernel, ways, 1, 4, 0)(*sides)

time: 132 us -> 129 us (0.977)
  blocking collectives: 49.5 us -> 45.1 us
  starting transfers between devices: 31.6 us -> 35.6 us
  Pallas kernels: 22.6 us -> 20.2 us
    ppermute x2, waiting for transfers between devices: 1.8 us -> 8.46 us  [body(): lax.ppermute(a, 'xl', SWAP)]
    ppermute x2, waiting for transfers between devices: 6.47 us -> 0.01 us  [body(): lax.ppermute(a, ('xl', 'xh'), FLIP)]
    all_to_all x1, blocking collectives: 19.1 us -> 13.3 us  [body(): lax.all_to_all(backs, TOWER, split_axis=0, concat_axis=0, tiled=True)]
    ppermute x2, starting transfers between devices: 0.81 us -> 3.94 us  [body(): lax.ppermute(a, ('xl', 'xh'), FLIP)]
    ppermute x14, starting transfers between devices: 23 us -> 24.6 us  [shifted(): return lax.ppermute(array, axis, [(i, (i + by) % 4) for i in range(4)])]
    all_to_all x1, blocking collectives: 30.4 us -> 31.8 us  [body(): coded = lax.all_to_all(coded, AXES, split_axis=0, concat_axis=0, tiled=True)]
  transfers between devices with their start and end apart: 22 -> 22, of which waited for: 9 -> 9; matrix products, arithmetic and copies ran while one was open for 1% -> 1% of each run, Pallas kernels for 8% -> 7%
where the time goes in v3:
time: 129 us
  blocking collectives  45.1 us (35%)
  starting transfers between devices  35.6 us (28%)
  waiting for transfers between devices  25.2 us (20%)
  Pallas kernels  20.2 us (16%)
  between operations  1.56 us (1%)
    all_to_all x1, blocking collectives, body(): coded = lax.all_to_all(coded, AXES, split_axis=0, concat_axis=0, tiled=True)  31.8 us
    ppermute x14, starting transfers between devices, shifted(): return lax.ppermute(array, axis, [(i, (i + by) % 4) for i in range(4)])  24.6 us
    ppermute x14, waiting for transfers between devices, shifted(): return lax.ppermute(array, axis, [(i, (i + by) % 4) for i in range(4)])  15.6 us
    all_to_all x1, blocking collectives, body(): lax.all_to_all(backs, TOWER, split_axis=0, concat_axis=0, tiled=True)  13.3 us
    ppermute x2, waiting for transfers between devices, body(): lax.ppermute(a, 'xl', SWAP)  8.46 us
    pallas_call x1, Pallas kernels, body(): call(embed_kernel, [shape(QUARTER, E, dtype=BF16), shape(QUARTER, 128), s...  4.89 us
    ppermute x2, starting transfers between devices, body(): lax.ppermute(a, ('xl', 'xh'), FLIP)  3.94 us
    ppermute x1, starting transfers between devices, body(): other_texts = lax.ppermute(own_texts, ('xl', 'xh'), FLIP)  3.39 us
  transfers between devices with their start and end apart: 22, of which 9 were waited for; matrix products, arithmetic and copies ran while one was open for 1% of the time, Pallas kernels for 7%

profile of v3, /device:TPU:1, one launch (start us, length us, event | category | flops | bytes accessed | tf_op | source)
XLA Modules:
  0.0 128.9 jit_solution(2676544134738838259)
XLA Ops:
  0.0 4.9 %shard_map.73 = (bf16[96,1024]{1,0:T(8,128)(2,1)}, f32[96,128]{1,0:T(8,128)}, bf16[208,1024]{1,0:T(8,128)(2,1)}, f32[96,128]{1,0:T(8,128)}) custom-call(s32[1]{0:T(128)} %bitcast.where_ref, s32[3,128]{1,0:T(4,128)} %bitcast.2, bf16[384,1024]{1,0:T(8,128)(2,1)} %text_feats.3, bf16[384,1664]{1,0:T(8,128)(2,1)} %image_feats.3, bf16[1024,1024]{1,0:T(8,128)(2,1)} %text_weight.1, ...), custom_call_target="tpu_custom_call" | custom-call | flops 855638016 | bytes 8388608 | tf_op jit(solution)/shard_map/pallas_call | solution.py:321
  4.9 3.4 %collective-permute-start.1 = (bf16[96,1024]{1,0:T(8,128)(2,1)}, bf16[96,1024]{1,0:T(8,128)(2,1)S(1)}, u32[]{:S(2)}, u32[]{:S(2)}) collective-permute-start(bf16[96,1024]{1,0:T(8,128)(2,1)} %get-tuple-element.28.refs_12_), channel_id=1, source_target_pairs={{0,68},{4,64},{64,4},{68,0},{1,69},{5,65},{65,5},{69,1},{2,70},{6,... | collective-permute-start | bytes 589832 | tf_op jit(solution)/shard_map/ppermute | solution.py:336
  8.3 1.6 %collective-permute-start = (bf16[208,1024]{1,0:T(8,128)(2,1)}, bf16[208,1024]{1,0:T(8,128)(2,1)S(1)}, u32[]{:S(2)}, u32[]{:S(2)}) collective-permute-start(bf16[208,1024]{1,0:T(8,128)(2,1)} %get-tuple-element.25.me.refs_5_), channel_id=1, source_target_pairs={{0,8},{8,16},{16,24},{24,0},{1,9},{9,17},{17,25},{25,1},{2,10},{10... | collective-permute-start | bytes 1277960 | tf_op jit(solution)/shard_map/ppermute | solution.py:32
  9.9 2.1 %collective-permute-start.6 = (bf16[208,1024]{1,0:T(8,128)(2,1)}, bf16[208,1024]{1,0:T(8,128)(2,1)S(1)}, u32[]{:S(2)}, u32[]{:S(2)}) collective-permute-start(bf16[208,1024]{1,0:T(8,128)(2,1)} %get-tuple-element.25.me.refs_5_), channel_id=1, source_target_pairs={{0,24},{8,0},{16,8},{24,16},{1,25},{9,1},{17,9},{25,17},{2,26},{10... | collective-permute-start | bytes 1277960 | tf_op jit(solution)/shard_map/ppermute | solution.py:32
  13.1 1.4 %collective-permute-start.3 = (bf16[192,1024]{1,0:T(8,128)(2,1)S(1)}, bf16[192,1024]{1,0:T(8,128)(2,1)S(1)}, u32[]{:S(2)}, u32[]{:S(2)}) collective-permute-start(bf16[192,1024]{1,0:T(8,128)(2,1)S(1)} %constant_dynamic-update-slice_fusion.me), channel_id=1, source_target_pairs={{0,1},{1,2},{2,3},{3,0},{4,5},{5,6},{6,7},{7,4},{8,9},{9,10},{10,1... | collective-permute-start | bytes 1179656 | tf_op jit(solution)/shard_map/ppermute | solution.py:32
  14.4 1.5 %collective-permute-start.2 = (bf16[192,1024]{1,0:T(8,128)(2,1)S(1)}, bf16[192,1024]{1,0:T(8,128)(2,1)S(1)}, u32[]{:S(2)}, u32[]{:S(2)}) collective-permute-start(bf16[192,1024]{1,0:T(8,128)(2,1)S(1)} %constant_dynamic-update-slice_fusion.me), channel_id=1, source_target_pairs={{0,3},{1,0},{2,1},{3,2},{4,7},{5,4},{6,5},{7,6},{8,11},{9,8},{10,9... | collective-permute-start | bytes 1179656 | tf_op jit(solution)/shard_map/ppermute | solution.py:32
  15.9 4.7 %collective-permute-done.6.after = bf16[208,1024]{1,0:T(8,128)(2,1)S(1)} collective-permute-done((bf16[208,1024]{1,0:T(8,128)(2,1)}, bf16[208,1024]{1,0:T(8,128)(2,1)S(1)}, u32[]{:S(2)}, u32[]{:S(2)}) %collective-permute-start.6) | collective-permute-done | bytes 426016 | tf_op jit(solution)/shard_map/ppermute | solution.py:32
  20.7 3.3 %collective-permute-start.8 = (bf16[112,1024]{1,0:T(8,128)(2,1)S(1)}, bf16[112,1024]{1,0:T(8,128)(2,1)S(1)}, u32[]{:S(2)}, u32[]{:S(2)}) collective-permute-start(bf16[112,1024]{1,0:T(8,128)(2,1)S(1)} %slice.43), channel_id=1, source_target_pairs={{0,24},{8,0},{16,8},{24,16},{1,25},{9,1},{17,9},{25,17},{2,26},{10... | collective-permute-start | bytes 688136 | tf_op jit(solution)/shard_map/ppermute | solution.py:32
  24.1 1.4 %collective-permute-start.4 = (bf16[96,1024]{1,0:T(8,128)(2,1)S(1)}, bf16[96,1024]{1,0:T(8,128)(2,1)S(1)}, u32[]{:S(2)}, u32[]{:S(2)}) collective-permute-start(bf16[96,1024]{1,0:T(8,128)(2,1)S(1)} %slice.40), channel_id=1, source_target_pairs={{0,1},{1,2},{2,3},{3,0},{4,5},{5,6},{6,7},{7,4},{8,9},{9,10},{10,1... | collective-permute-start | bytes 589832 | tf_op jit(solution)/shard_map/ppermute | solution.py:32
  25.5 1.5 %collective-permute-start.5 = (bf16[96,1024]{1,0:T(8,128)(2,1)S(1)}, bf16[96,1024]{1,0:T(8,128)(2,1)S(1)}, u32[]{:S(2)}, u32[]{:S(2)}) collective-permute-start(bf16[96,1024]{1,0:T(8,128)(2,1)S(1)} %slice.41), channel_id=1, source_target_pairs={{0,3},{1,0},{2,1},{3,2},{4,7},{5,4},{6,5},{7,6},{8,11},{9,8},{10,9... | collective-permute-start | bytes 589832 | tf_op jit(solution)/shard_map/ppermute | solution.py:32
  28.3 2.1 %shard_map.74 = (bf16[1920,384]{1,0:T(8,128)(2,1)S(1)}, bf16[1344,384]{1,0:T(8,128)(2,1)S(1)}) custom-call(s32[1]{0:T(128)} %bitcast.where_ref, bf16[384,1664]{1,0:T(8,128)(2,1)S(1)} %copy-done.1, bf16[384,1024]{1,0:T(8,128)(2,1)S(1)} %copy-done.2, bf16[208,1024]{1,0:T(8,128)(2,1)S(1)} %collective-permute-done.early.before), custom_call_target="tpu_custom_call" | custom-call | flops 962592768 | bytes 5242880 | tf_op jit(solution)/shard_map/pallas_call | solution.py:346
  30.6 2.7 %collective-permute-start.9 = (bf16[784,1024]{1,0:T(8,128)(2,1)S(1)}, bf16[784,1024]{1,0:T(8,128)(2,1)S(1)}, u32[]{:S(2)}, u32[]{:S(2)}) collective-permute-start(bf16[784,1024]{1,0:T(8,128)(2,1)S(1)} %shard_map.75.images_ref.refs_1_), channel_id=1, source_target_pairs={{0,32},{32,0},{1,33},{33,1},{2,34},{34,2},{3,35},{35,3},{4,36},{36... | collective-permute-start | bytes 4816904 | tf_op jit(solution)/shard_map/ppermute | solution.py:343
  33.4 2.0 %shard_map.76 = (bf16[768,1024]{1,0:T(8,128)(2,1)S(1)}, bf16[768,768]{1,0:T(8,128)(2,1)S(1)}) custom-call(s32[1]{0:T(128)} %bitcast.where_ref, f32[1]{0:T(128)S(6)} %copy.9.scale_ref, f32[1]{0:T(128)S(6)} %copy.10.shift_ref, bf16[192,1024]{1,0:T(8,128)(2,1)S(1)} %constant_dynamic-update-slice_fusion.me, bf16[192,1024]{1,0:T(8,128)(2,1)S(1)} %collective-permute-done.2.after, ...), custom_call_target="tpu_custom_call" | custom-call | flops 19327352832 | bytes 6291456 | tf_op jit(solution)/shard_map/pallas_call | solution.py:368
  36.4 2.8 %shard_map.77 = (bf16[768,768]{1,0:T(8,128)(2,1)S(1)}, f32[384,1024]{1,0:T(8,128)S(1)}) custom-call(s32[1]{0:T(128)} %bitcast.where_ref, f32[1]{0:T(128)S(6)} %copy.9.scale_ref, f32[1]{0:T(128)S(6)} %copy.10.shift_ref, bf16[768,1024]{1,0:T(8,128)(2,1)S(1)} %get-tuple-element.29.texts_ref.refs_0_, bf16[784,1024]{1,0:T(8,128)(2,1)S(1)} %collective-permute-done.9.images_ref.refs_3_), custom_call_target="tpu_custom_call" | custom-call | flops 2415919104 | bytes 8388608 | tf_op jit(solution)/shard_map/pallas_call | solution.py:372
  40.9 1.4 %shard_map.83 = (f32[96,1024]{1,0:T(8,128)S(1)}, f32[96,1024]{1,0:T(8,128)S(1)}, f32[192,1024]{1,0:T(8,128)S(1)}) custom-call(bf16[768,768]{1,0:T(8,128)(2,1)S(1)} %get-tuple-element.30.refs_1_.refs_0_, bf16[784,1024]{1,0:T(8,128)(2,1)S(1)} %shard_map.75.images_ref.refs_1_, bf16[768,768]{1,0:T(8,128)(2,1)S(1)} %get-tuple-element.31.refs_1_.refs_2_, ...), custom_call_target="tpu_custom_call" | custom-call | flops 1207959552 | bytes 6291456 | tf_op jit(solution)/shard_map/pallas_call | solution.py:378
  42.3 1.3 %collective-permute-start.17 = (f32[192,1024]{1,0:T(8,128)S(1)}, f32[192,1024]{1,0:T(8,128)S(1)}, u32[]{:S(2)}, u32[]{:S(2)}) collective-permute-start(f32[192,1024]{1,0:T(8,128)S(1)} %get-tuple-element.40), channel_id=1, source_target_pairs={{0,1},{1,2},{2,3},{3,0},{4,5},{5,6},{6,7},{7,4},{8,9},{9,10},{10,1... | collective-permute-start | bytes 2359304 | tf_op jit(solution)/shard_map/ppermute | solution.py:32
  43.6 1.4 %shard_map.82 = (f32[192,1024]{1,0:T(8,128)S(1)}, f32[192,1024]{1,0:T(8,128)S(1)}) custom-call(bf16[768,768]{1,0:T(8,128)(2,1)S(1)} %get-tuple-element.30.refs_1_.refs_0_, bf16[784,1024]{1,0:T(8,128)(2,1)S(1)} %shard_map.75.images_ref.refs_1_, bf16[768,768]{1,0:T(8,128)(2,1)S(1)} %get-tuple-element.31.refs_1_.refs_2_, ...), custom_call_target="tpu_custom_call" | custom-call | flops 9663676416 | bytes 6291456 | tf_op jit(solution)/shard_map/pallas_call | solution.py:382
  45.0 1.5 %collective-permute-start.18 = (f32[192,1024]{1,0:T(8,128)S(1)}, f32[192,1024]{1,0:T(8,128)S(1)}, u32[]{:S(2)}, u32[]{:S(2)}) collective-permute-start(f32[192,1024]{1,0:T(8,128)S(1)} %get-tuple-element.41), channel_id=1, source_target_pairs={{0,3},{1,0},{2,1},{3,2},{4,7},{5,4},{6,5},{7,6},{8,11},{9,8},{10,9... | collective-permute-start | bytes 2359304 | tf_op jit(solution)/shard_map/ppermute | solution.py:32
  47.3 1.4 %collective-permute-start.12 = (f32[192,1024]{1,0:T(8,128)S(1)}, f32[192,1024]{1,0:T(8,128)S(1)}, u32[]{:S(2)}, u32[]{:S(2)}) collective-permute-start(f32[192,1024]{1,0:T(8,128)S(1)} %get-tuple-element.34), channel_id=1, source_target_pairs={{0,8},{8,16},{16,24},{24,0},{1,9},{9,17},{17,25},{25,1},{2,10},{10... | collective-permute-start | bytes 2359304 | tf_op jit(solution)/shard_map/ppermute | solution.py:32
  49.5 2.2 %collective-permute-start.13 = (f32[192,1024]{1,0:T(8,128)S(1)}, f32[192,1024]{1,0:T(8,128)S(1)}, u32[]{:S(2)}, u32[]{:S(2)}) collective-permute-start(f32[192,1024]{1,0:T(8,128)S(1)} %get-tuple-element.35), channel_id=1, source_target_pairs={{0,24},{8,0},{16,8},{24,16},{1,25},{9,1},{17,9},{25,17},{2,26},{10... | collective-permute-start | bytes 2359304 | tf_op jit(solution)/shard_map/ppermute | solution.py:32
  51.7 2.5 %collective-permute-start.19 = (f32[96,1024]{1,0:T(8,128)S(1)}, f32[96,1024]{1,0:T(8,128)S(1)}, u32[]{:S(2)}, u32[]{:S(2)}) collective-permute-start(f32[96,1024]{1,0:T(8,128)S(1)} %get-tuple-element.43), channel_id=1, source_target_pairs={{0,68},{4,64},{64,4},{68,0},{1,69},{5,65},{65,5},{69,1},{2,70},{6,... | collective-permute-start | bytes 1179656 | tf_op jit(solution)/shard_map/ppermute | solution.py:385
  54.2 8.1 %collective-permute-done.17.refs_8_ = f32[192,1024]{1,0:T(8,128)S(1)} collective-permute-done((f32[192,1024]{1,0:T(8,128)S(1)}, f32[192,1024]{1,0:T(8,128)S(1)}, u32[]{:S(2)}, u32[]{:S(2)}) %collective-permute-start.17) | collective-permute-done | bytes 786464 | tf_op jit(solution)/shard_map/ppermute | solution.py:32
  62.3 1.2 collective-permute-done.18.early_ref.refs_9_
  63.6 1.5 %collective-permute-start.21 = (f32[96,1024]{1,0:T(8,128)S(1)}, f32[96,1024]{1,0:T(8,128)S(1)}, u32[]{:S(2)}, u32[]{:S(2)}) collective-permute-start(f32[96,1024]{1,0:T(8,128)S(1)} %slice_add_fusion), channel_id=1, source_target_pairs={{0,68},{4,64},{64,4},{68,0},{1,69},{5,65},{65,5},{69,1},{2,70},{6,... | collective-permute-start | bytes 1179656 | tf_op jit(solution)/shard_map/ppermute | solution.py:385
  65.1 2.0 %collective-permute-start.20 = (f32[96,1024]{1,0:T(8,128)S(1)}, f32[96,1024]{1,0:T(8,128)S(1)}, u32[]{:S(2)}, u32[]{:S(2)}) collective-permute-start(f32[96,1024]{1,0:T(8,128)S(1)} %shard_map.84), channel_id=1, source_target_pairs={{0,2},{1,3},{2,0},{3,1},{4,6},{5,7},{6,4},{7,5},{8,10},{9,11},{10,... | collective-permute-start | bytes 1179656 | tf_op jit(solution)/shard_map/ppermute | solution.py:32
  68.0 3.8 %collective-permute-done.14.high_ref = f32[96,1024]{1,0:T(8,128)S(1)} collective-permute-done((f32[96,1024]{1,0:T(8,128)S(1)}, f32[96,1024]{1,0:T(8,128)S(1)}, u32[]{:S(2)}, u32[]{:S(2)}) %collective-permute-start.14) | collective-permute-done | bytes 393248 | tf_op jit(solution)/shard_map/ppermute | solution.py:388
  71.8 3.3 %collective-permute-start.15 = (f32[96,1024]{1,0:T(8,128)S(1)}, f32[96,1024]{1,0:T(8,128)S(1)}, u32[]{:S(2)}, u32[]{:S(2)}) collective-permute-start(f32[96,1024]{1,0:T(8,128)S(1)} %shard_map.81), channel_id=1, source_target_pairs={{0,16},{8,24},{16,0},{24,8},{1,17},{9,25},{17,1},{25,9},{2,18},{10... | collective-permute-start | bytes 1179656 | tf_op jit(solution)/shard_map/ppermute | solution.py:32
  75.5 4.7 %collective-permute-done.16.refs_4_ = f32[96,1024]{1,0:T(8,128)S(1)} collective-permute-done((f32[96,1024]{1,0:T(8,128)S(1)}, f32[96,1024]{1,0:T(8,128)S(1)}, u32[]{:S(2)}, u32[]{:S(2)}) %collective-permute-start.16) | collective-permute-done | bytes 393248 | tf_op jit(solution)/shard_map/ppermute | solution.py:388
  81.1 13.3 %all_to_all.10.backs_ref = bf16[4,192,256]{2,1,0:T(8,128)(2,1)S(1)} all-to-all(bf16[4,192,256]{2,1,0:T(8,128)(2,1)S(1)} %shard_map.85), channel_id=1, replica_groups=mesh['xl'=2,'core'=2,'z'=4,'xh'=2,'y'=4] {'xl','core'}, dimensions={0} | all-to-all | bytes 786432 | tf_op jit(solution)/shard_map/all_to_all | solution.py:395
  94.4 1.4 %shard_map.86 = s16[128,24,256]{2,1,0:T(8,128)(2,1)S(1)} custom-call(bf16[1920,384]{1,0:T(8,128)(2,1)S(1)} %get-tuple-element.26.early_a.images_ref, bf16[1344,384]{1,0:T(8,128)(2,1)S(1)} %get-tuple-element.27.early_b.texts_ref, bf16[4,192,256]{2,1,0:T(8,128)(2,1)S(1)} %all_to_all.10.backs_ref), custom_call_target="tpu_custom_call" | custom-call | flops 1207959552 | bytes 6291456 | tf_op jit(solution)/shard_map/pallas_call | solution.py:397
  95.8 31.8 %all_to_all.11.coded_ref = s16[128,24,256]{2,1,0:T(8,128)(2,1)S(1)} all-to-all(s16[128,24,256]{2,1,0:T(8,128)(2,1)S(1)} %shard_map.86), channel_id=1, replica_groups=mesh['xl'=2,'core'=2,'z'=4,'xh'=2,'y'=4] {'xl','core','z','xh','y'}, dimensions={0} | all-to-all | bytes 3145728 | tf_op jit(solution)/shard_map/all_to_all | solution.py:403
  127.6 1.2 shard_map.87
  (49 shorter events, 7.9 us)
Async XLA Ops:
  4.9 23.4 %copy-start.1 = (bf16[384,1664]{1,0:T(8,128)(2,1)S(1)}, bf16[384,1664]{1,0:T(8,128)(2,1)}, u32[]{:S(2)}) copy-start(bf16[384,1664]{1,0:T(8,128)(2,1)} %image_feats.3) | copy-start | bytes 3833860
  4.9 23.4 %copy-start.2 = (bf16[384,1024]{1,0:T(8,128)(2,1)S(1)}, bf16[384,1024]{1,0:T(8,128)(2,1)}, u32[]{:S(2)}) copy-start(bf16[384,1024]{1,0:T(8,128)(2,1)} %text_feats.3) | copy-start | bytes 2359300
  4.9 8.1 %collective-permute-start.1 = (bf16[96,1024]{1,0:T(8,128)(2,1)}, bf16[96,1024]{1,0:T(8,128)(2,1)S(1)}, u32[]{:S(2)}, u32[]{:S(2)}) collective-permute-start(bf16[96,1024]{1,0:T(8,128)(2,1)} %get-tuple-element.28.refs_12_), channel_id=1, source_target_pairs={{0,68},{4,64},{64,4},{68,0},{1,69},{5,65},{65,5},{69,1},{2,70},{6,... | collective-permute-start | bytes 589832 | tf_op jit(solution)/shard_map/ppermute | solution.py:336
  8.3 15.7 %collective-permute-start = (bf16[208,1024]{1,0:T(8,128)(2,1)}, bf16[208,1024]{1,0:T(8,128)(2,1)S(1)}, u32[]{:S(2)}, u32[]{:S(2)}) collective-permute-start(bf16[208,1024]{1,0:T(8,128)(2,1)} %get-tuple-element.25.me.refs_5_), channel_id=1, source_target_pairs={{0,8},{8,16},{16,24},{24,0},{1,9},{9,17},{17,25},{25,1},{2,10},{10... | collective-permute-start | bytes 1277960 | tf_op jit(solution)/shard_map/ppermute | solution.py:32
  9.9 10.7 %collective-permute-start.6 = (bf16[208,1024]{1,0:T(8,128)(2,1)}, bf16[208,1024]{1,0:T(8,128)(2,1)S(1)}, u32[]{:S(2)}, u32[]{:S(2)}) collective-permute-start(bf16[208,1024]{1,0:T(8,128)(2,1)} %get-tuple-element.25.me.refs_5_), channel_id=1, source_target_pairs={{0,24},{8,0},{16,8},{24,16},{1,25},{9,1},{17,9},{25,17},{2,26},{10... | collective-permute-start | bytes 1277960 | tf_op jit(solution)/shard_map/ppermute | solution.py:32
  13.1 11.0 %collective-permute-start.3 = (bf16[192,1024]{1,0:T(8,128)(2,1)S(1)}, bf16[192,1024]{1,0:T(8,128)(2,1)S(1)}, u32[]{:S(2)}, u32[]{:S(2)}) collective-permute-start(bf16[192,1024]{1,0:T(8,128)(2,1)S(1)} %constant_dynamic-update-slice_fusion.me), channel_id=1, source_target_pairs={{0,1},{1,2},{2,3},{3,0},{4,5},{5,6},{6,7},{7,4},{8,9},{9,10},{10,1... | collective-permute-start | bytes 1179656 | tf_op jit(solution)/shard_map/ppermute | solution.py:32
  14.4 11.0 %collective-permute-start.2 = (bf16[192,1024]{1,0:T(8,128)(2,1)S(1)}, bf16[192,1024]{1,0:T(8,128)(2,1)S(1)}, u32[]{:S(2)}, u32[]{:S(2)}) collective-permute-start(bf16[192,1024]{1,0:T(8,128)(2,1)S(1)} %constant_dynamic-update-slice_fusion.me), channel_id=1, source_target_pairs={{0,3},{1,0},{2,1},{3,2},{4,7},{5,4},{6,5},{7,6},{8,11},{9,8},{10,9... | collective-permute-start | bytes 1179656 | tf_op jit(solution)/shard_map/ppermute | solution.py:32
  20.7 9.8 %collective-permute-start.8 = (bf16[112,1024]{1,0:T(8,128)(2,1)S(1)}, bf16[112,1024]{1,0:T(8,128)(2,1)S(1)}, u32[]{:S(2)}, u32[]{:S(2)}) collective-permute-start(bf16[112,1024]{1,0:T(8,128)(2,1)S(1)} %slice.43), channel_id=1, source_target_pairs={{0,24},{8,0},{16,8},{24,16},{1,25},{9,1},{17,9},{25,17},{2,26},{10... | collective-permute-start | bytes 688136 | tf_op jit(solution)/shard_map/ppermute | solution.py:32
  24.0 6.5 %collective-permute-start.7 = (bf16[96,1024]{1,0:T(8,128)(2,1)S(1)}, bf16[96,1024]{1,0:T(8,128)(2,1)S(1)}, u32[]{:S(2)}, u32[]{:S(2)}) collective-permute-start(bf16[96,1024]{1,0:T(8,128)(2,1)S(1)} %slice.42), channel_id=1, source_target_pairs={{0,8},{8,16},{16,24},{24,0},{1,9},{9,17},{17,25},{25,1},{2,10},{10... | collective-permute-start | bytes 589832 | tf_op jit(solution)/shard_map/ppermute | solution.py:32
  24.1 9.2 %collective-permute-start.4 = (bf16[96,1024]{1,0:T(8,128)(2,1)S(1)}, bf16[96,1024]{1,0:T(8,128)(2,1)S(1)}, u32[]{:S(2)}, u32[]{:S(2)}) collective-permute-start(bf16[96,1024]{1,0:T(8,128)(2,1)S(1)} %slice.40), channel_id=1, source_target_pairs={{0,1},{1,2},{2,3},{3,0},{4,5},{5,6},{6,7},{7,4},{8,9},{9,10},{10,1... | collective-permute-start | bytes 589832 | tf_op jit(solution)/shard_map/ppermute | solution.py:32
  25.5 7.9 %collective-permute-start.5 = (bf16[96,1024]{1,0:T(8,128)(2,1)S(1)}, bf16[96,1024]{1,0:T(8,128)(2,1)S(1)}, u32[]{:S(2)}, u32[]{:S(2)}) collective-permute-start(bf16[96,1024]{1,0:T(8,128)(2,1)S(1)} %slice.41), channel_id=1, source_target_pairs={{0,3},{1,0},{2,1},{3,2},{4,7},{5,4},{6,5},{7,6},{8,11},{9,8},{10,9... | collective-permute-start | bytes 589832 | tf_op jit(solution)/shard_map/ppermute | solution.py:32
  28.3 2.2 %copy-start = (bf16[208,1024]{1,0:T(8,128)(2,1)S(1)}, bf16[208,1024]{1,0:T(8,128)(2,1)}, u32[]{:S(2)}) copy-start(bf16[208,1024]{1,0:T(8,128)(2,1)} %get-tuple-element.25.me.refs_5_) | copy-start | bytes 1277956
  30.6 5.8 %collective-permute-start.9 = (bf16[784,1024]{1,0:T(8,128)(2,1)S(1)}, bf16[784,1024]{1,0:T(8,128)(2,1)S(1)}, u32[]{:S(2)}, u32[]{:S(2)}) collective-permute-start(bf16[784,1024]{1,0:T(8,128)(2,1)S(1)} %shard_map.75.images_ref.refs_1_), channel_id=1, source_target_pairs={{0,32},{32,0},{1,33},{33,1},{2,34},{34,2},{3,35},{35,3},{4,36},{36... | collective-permute-start | bytes 4816904 | tf_op jit(solution)/shard_map/ppermute | solution.py:343
  39.2 7.3 %collective-permute-start.11 = (f32[384,1024]{1,0:T(8,128)S(1)}, f32[384,1024]{1,0:T(8,128)S(1)}, u32[]{:S(2)}, u32[]{:S(2)}) collective-permute-start(f32[384,1024]{1,0:T(8,128)S(1)} %get-tuple-element.33), channel_id=1, source_target_pairs={{0,32},{32,0},{1,33},{33,1},{2,34},{34,2},{3,35},{35,3},{4,36},{36... | collective-permute-start | bytes 4718600 | tf_op jit(solution)/shard_map/ppermute | solution.py:376
  40.7 8.0 %collective-permute-start.10 = (f32[384,1024]{1,0:T(8,128)S(1)}, f32[384,1024]{1,0:T(8,128)S(1)}, u32[]{:S(2)}, u32[]{:S(2)}) collective-permute-start(f32[384,1024]{1,0:T(8,128)S(1)} %shard_map.78), channel_id=1, source_target_pairs={{0,32},{32,0},{1,33},{33,1},{2,34},{34,2},{3,35},{35,3},{4,36},{36... | collective-permute-start | bytes 4718600 | tf_op jit(solution)/shard_map/ppermute | solution.py:380
  42.3 20.0 %collective-permute-start.17 = (f32[192,1024]{1,0:T(8,128)S(1)}, f32[192,1024]{1,0:T(8,128)S(1)}, u32[]{:S(2)}, u32[]{:S(2)}) collective-permute-start(f32[192,1024]{1,0:T(8,128)S(1)} %get-tuple-element.40), channel_id=1, source_target_pairs={{0,1},{1,2},{2,3},{3,0},{4,5},{5,6},{6,7},{7,4},{8,9},{9,10},{10,1... | collective-permute-start | bytes 2359304 | tf_op jit(solution)/shard_map/ppermute | solution.py:32
  45.0 18.5 %collective-permute-start.18 = (f32[192,1024]{1,0:T(8,128)S(1)}, f32[192,1024]{1,0:T(8,128)S(1)}, u32[]{:S(2)}, u32[]{:S(2)}) collective-permute-start(f32[192,1024]{1,0:T(8,128)S(1)} %get-tuple-element.41), channel_id=1, source_target_pairs={{0,3},{1,0},{2,1},{3,2},{4,7},{5,4},{6,5},{7,6},{8,11},{9,8},{10,9... | collective-permute-start | bytes 2359304 | tf_op jit(solution)/shard_map/ppermute | solution.py:32
  47.3 20.5 %collective-permute-start.12 = (f32[192,1024]{1,0:T(8,128)S(1)}, f32[192,1024]{1,0:T(8,128)S(1)}, u32[]{:S(2)}, u32[]{:S(2)}) collective-permute-start(f32[192,1024]{1,0:T(8,128)S(1)} %get-tuple-element.34), channel_id=1, source_target_pairs={{0,8},{8,16},{16,24},{24,0},{1,9},{9,17},{17,25},{25,1},{2,10},{10... | collective-permute-start | bytes 2359304 | tf_op jit(solution)/shard_map/ppermute | solution.py:32
  49.5 18.3 %collective-permute-start.13 = (f32[192,1024]{1,0:T(8,128)S(1)}, f32[192,1024]{1,0:T(8,128)S(1)}, u32[]{:S(2)}, u32[]{:S(2)}) collective-permute-start(f32[192,1024]{1,0:T(8,128)S(1)} %get-tuple-element.35), channel_id=1, source_target_pairs={{0,24},{8,0},{16,8},{24,16},{1,25},{9,1},{17,9},{25,17},{2,26},{10... | collective-permute-start | bytes 2359304 | tf_op jit(solution)/shard_map/ppermute | solution.py:32
  51.7 13.3 %collective-permute-start.19 = (f32[96,1024]{1,0:T(8,128)S(1)}, f32[96,1024]{1,0:T(8,128)S(1)}, u32[]{:S(2)}, u32[]{:S(2)}) collective-permute-start(f32[96,1024]{1,0:T(8,128)S(1)} %get-tuple-element.43), channel_id=1, source_target_pairs={{0,68},{4,64},{64,4},{68,0},{1,69},{5,65},{65,5},{69,1},{2,70},{6,... | collective-permute-start | bytes 1179656 | tf_op jit(solution)/shard_map/ppermute | solution.py:385
  62.3 9.4 %collective-permute-start.14 = (f32[96,1024]{1,0:T(8,128)S(1)}, f32[96,1024]{1,0:T(8,128)S(1)}, u32[]{:S(2)}, u32[]{:S(2)}) collective-permute-start(f32[96,1024]{1,0:T(8,128)S(1)} %get-tuple-element.37), channel_id=1, source_target_pairs={{0,64},{64,0},{1,65},{65,1},{2,66},{66,2},{3,67},{67,3},{4,68},{68... | collective-permute-start | bytes 1179656 | tf_op jit(solution)/shard_map/ppermute | solution.py:388
  63.6 11.5 %collective-permute-start.21 = (f32[96,1024]{1,0:T(8,128)S(1)}, f32[96,1024]{1,0:T(8,128)S(1)}, u32[]{:S(2)}, u32[]{:S(2)}) collective-permute-start(f32[96,1024]{1,0:T(8,128)S(1)} %slice_add_fusion), channel_id=1, source_target_pairs={{0,68},{4,64},{64,4},{68,0},{1,69},{5,65},{65,5},{69,1},{2,70},{6,... | collective-permute-start | bytes 1179656 | tf_op jit(solution)/shard_map/ppermute | solution.py:385
  65.1 10.4 %collective-permute-start.20 = (f32[96,1024]{1,0:T(8,128)S(1)}, f32[96,1024]{1,0:T(8,128)S(1)}, u32[]{:S(2)}, u32[]{:S(2)}) collective-permute-start(f32[96,1024]{1,0:T(8,128)S(1)} %shard_map.84), channel_id=1, source_target_pairs={{0,2},{1,3},{2,0},{3,1},{4,6},{5,7},{6,4},{7,5},{8,10},{9,11},{10,... | collective-permute-start | bytes 1179656 | tf_op jit(solution)/shard_map/ppermute | solution.py:32
  67.8 12.9 %copy-start.3 = (bf16[96,1024]{1,0:T(8,128)(2,1)S(1)}, bf16[96,1024]{1,0:T(8,128)(2,1)}, u32[]{:S(2)}) copy-start(bf16[96,1024]{1,0:T(8,128)(2,1)} %get-tuple-element.28.refs_12_) | copy-start | bytes 589828
  67.8 12.9 %copy-start.4 = (f32[96,128]{1,0:T(8,128)S(1)}, f32[96,128]{1,0:T(8,128)}, u32[]{:S(2)}) copy-start(f32[96,128]{1,0:T(8,128)} %get-tuple-element.44.refs_13_) | copy-start | bytes 147460
  67.8 12.9 %copy-start.5 = (f32[96,128]{1,0:T(8,128)S(1)}, f32[96,128]{1,0:T(8,128)}, u32[]{:S(2)}) copy-start(f32[96,128]{1,0:T(8,128)} %get-tuple-element.38.refs_6_) | copy-start | bytes 147460
  67.9 12.3 %collective-permute-start.16 = (f32[96,1024]{1,0:T(8,128)S(1)}, f32[96,1024]{1,0:T(8,128)S(1)}, u32[]{:S(2)}, u32[]{:S(2)}) collective-permute-start(f32[96,1024]{1,0:T(8,128)S(1)} %slice_add_fusion.2), channel_id=1, source_target_pairs={{0,64},{64,0},{1,65},{65,1},{2,66},{66,2},{3,67},{67,3},{4,68},{68... | collective-permute-start | bytes 1179656 | tf_op jit(solution)/shard_map/ppermute | solution.py:388
  71.8 8.9 %collective-permute-start.15 = (f32[96,1024]{1,0:T(8,128)S(1)}, f32[96,1024]{1,0:T(8,128)S(1)}, u32[]{:S(2)}, u32[]{:S(2)}) collective-permute-start(f32[96,1024]{1,0:T(8,128)S(1)} %shard_map.81), channel_id=1, source_target_pairs={{0,16},{8,24},{16,0},{24,8},{1,17},{9,25},{17,1},{25,9},{2,18},{10... | collective-permute-start | bytes 1179656 | tf_op jit(solution)/shard_map/ppermute | solution.py:32

commit v4 on v3

--- a/solution.py
+++ b/solution.py
@@ -136,12 +136,28 @@
     out_ref[...] = low_ref[...] + high_ref[...]
 
 
+def add_kernel(low_ref, high_ref, out_ref):
+    out_ref[...] = low_ref[...] + high_ref[...]
+
+
+def behind_kernel(far_ref, early_ref, out_ref):
+    out_ref[...] = far_ref[...]
+
+
 def ring_scatter(far_low, far_high, after, before, mine, axis, crossed):
     far = crossed(far_high)
     got_right, got_left = shifted(after, axis, 1), shifted(before, axis, -1)
-    far = call(
-        far_kernel, shape(QUARTER, E), 0, 1 << 20, in_specs=[VMEM, VMEM, ANY], out_specs=VMEM
-    )(far_low, far, got_left)
+    if axis == "z":
+        far = call(
+            far_kernel, shape(QUARTER, E), 0, 1 << 20, in_specs=[VMEM, VMEM, ANY], out_specs=VMEM
+        )(far_low, far, got_left)
+    else:
+        far = call(
+            add_kernel, shape(QUARTER, E), 4 << 30, 1 << 20, in_specs=[VMEM] * 2, out_specs=VMEM
+        )(far_low, far)
+        far = call(
+            behind_kernel, shape(QUARTER, E), 0, 1 << 20, in_specs=[VMEM, ANY], out_specs=VMEM
+        )(far, got_left)
     high = mine[QUARTER:] + got_right[QUARTER:] + got_left[QUARTER:]
     return mine, got_right, got_left, shifted(far, axis, 2), crossed(high)
 

time: 129 us -> 128 us (level)
    ppermute x2, waiting for transfers between devices: 8.46 us -> 2.36 us  [body(): lax.ppermute(a, 'xl', SWAP)]
    ppermute x14, waiting for transfers between devices: 15.6 us -> 18.6 us  [shifted(): return lax.ppermute(array, axis, [(i, (i + by) % 4) for i in range(4)])]
    ppermute x2, waiting for transfers between devices: 0.01 us -> 2.13 us  [body(): lax.ppermute(a, ('xl', 'xh'), FLIP)]
    ppermute x14, starting transfers between devices: 24.6 us -> 26.5 us  [shifted(): return lax.ppermute(array, axis, [(i, (i + by) % 4) for i in range(4)])]
    ppermute x2, starting transfers between devices: 3.94 us -> 2.37 us  [body(): lax.ppermute(a, ('xl', 'xh'), FLIP)]
  transfers between devices with their start and end apart: 22 -> 22, of which waited for: 9 -> 10; matrix products, arithmetic and copies ran while one was open for 1% -> 1% of each run, Pallas kernels for 7% -> 7%
where the time goes in v4:
time: 128 us; the launch traced here: 127 us
  blocking collectives  44.1 us (34%)
  starting transfers between devices  36 us (28%)
  waiting for transfers between devices  24.2 us (19%)
  Pallas kernels  20.3 us (16%)
  between operations  1.58 us (1%)
    all_to_all x1, blocking collectives, body(): coded = lax.all_to_all(coded, AXES, split_axis=0, concat_axis=0, tiled=True)  31.8 us
    ppermute x14, starting transfers between devices, shifted(): return lax.ppermute(array, axis, [(i, (i + by) % 4) for i in range(4)])  26.5 us
    ppermute x14, waiting for transfers between devices, shifted(): return lax.ppermute(array, axis, [(i, (i + by) % 4) for i in range(4)])  18.6 us
    all_to_all x1, blocking collectives, body(): lax.all_to_all(backs, TOWER, split_axis=0, concat_axis=0, tiled=True)  12.4 us
    pallas_call x1, Pallas kernels, body(): call(embed_kernel, [shape(QUARTER, E, dtype=BF16), shape(QUARTER, 128), s...  4.89 us
    ppermute x1, starting transfers between devices, body(): other_texts = lax.ppermute(own_texts, ('xl', 'xh'), FLIP)  3.39 us
    pallas_call x1, Pallas kernels, body(): call(given_kernel, [coef, shape(ROWS, E)], 2 * flops, 8 << 20, 24, in_spe...  2.8 us
    ppermute x1, starting transfers between devices, body(): others = lax.ppermute(images, 'core', SWAP)  2.72 us
  transfers between devices with their start and end apart: 22, of which 10 were waited for; matrix products, arithmetic and copies ran while one was open for 1% of the time, Pallas kernels for 7%

profile of v4, /device:TPU:1, one launch (start us, length us, event | category | flops | bytes accessed | tf_op | source)
XLA Modules:
  0.0 127.4 jit_solution(14985947092855689686)
XLA Ops:
  0.0 4.9 %shard_map.73 = (bf16[96,1024]{1,0:T(8,128)(2,1)}, f32[96,128]{1,0:T(8,128)}, bf16[208,1024]{1,0:T(8,128)(2,1)}, f32[96,128]{1,0:T(8,128)}) custom-call(s32[1]{0:T(128)} %bitcast.where_ref, s32[3,128]{1,0:T(4,128)} %bitcast.2, bf16[384,1024]{1,0:T(8,128)(2,1)} %text_feats.3, bf16[384,1664]{1,0:T(8,128)(2,1)} %image_feats.3, bf16[1024,1024]{1,0:T(8,128)(2,1)} %text_weight.1, ...), custom_call_target="tpu_custom_call" | custom-call | flops 855638016 | bytes 8388608 | tf_op jit(solution)/shard_map/pallas_call | solution.py:337
  4.9 3.4 %collective-permute-start.1 = (bf16[96,1024]{1,0:T(8,128)(2,1)}, bf16[96,1024]{1,0:T(8,128)(2,1)S(1)}, u32[]{:S(2)}, u32[]{:S(2)}) collective-permute-start(bf16[96,1024]{1,0:T(8,128)(2,1)} %get-tuple-element.28.refs_12_), channel_id=1, source_target_pairs={{0,68},{4,64},{64,4},{68,0},{1,69},{5,65},{65,5},{69,1},{2,70},{6,... | collective-permute-start | bytes 589832 | tf_op jit(solution)/shard_map/ppermute | solution.py:352
  8.3 1.6 %collective-permute-start = (bf16[208,1024]{1,0:T(8,128)(2,1)}, bf16[208,1024]{1,0:T(8,128)(2,1)S(1)}, u32[]{:S(2)}, u32[]{:S(2)}) collective-permute-start(bf16[208,1024]{1,0:T(8,128)(2,1)} %get-tuple-element.25.me.refs_5_), channel_id=1, source_target_pairs={{0,8},{8,16},{16,24},{24,0},{1,9},{9,17},{17,25},{25,1},{2,10},{10... | collective-permute-start | bytes 1277960 | tf_op jit(solution)/shard_map/ppermute | solution.py:32
  9.9 2.1 %collective-permute-start.6 = (bf16[208,1024]{1,0:T(8,128)(2,1)}, bf16[208,1024]{1,0:T(8,128)(2,1)S(1)}, u32[]{:S(2)}, u32[]{:S(2)}) collective-permute-start(bf16[208,1024]{1,0:T(8,128)(2,1)} %get-tuple-element.25.me.refs_5_), channel_id=1, source_target_pairs={{0,24},{8,0},{16,8},{24,16},{1,25},{9,1},{17,9},{25,17},{2,26},{10... | collective-permute-start | bytes 1277960 | tf_op jit(solution)/shard_map/ppermute | solution.py:32
  13.1 1.4 %collective-permute-start.3 = (bf16[192,1024]{1,0:T(8,128)(2,1)S(1)}, bf16[192,1024]{1,0:T(8,128)(2,1)S(1)}, u32[]{:S(2)}, u32[]{:S(2)}) collective-permute-start(bf16[192,1024]{1,0:T(8,128)(2,1)S(1)} %constant_dynamic-update-slice_fusion.me), channel_id=1, source_target_pairs={{0,1},{1,2},{2,3},{3,0},{4,5},{5,6},{6,7},{7,4},{8,9},{9,10},{10,1... | collective-permute-start | bytes 1179656 | tf_op jit(solution)/shard_map/ppermute | solution.py:32
  14.4 1.5 %collective-permute-start.2 = (bf16[192,1024]{1,0:T(8,128)(2,1)S(1)}, bf16[192,1024]{1,0:T(8,128)(2,1)S(1)}, u32[]{:S(2)}, u32[]{:S(2)}) collective-permute-start(bf16[192,1024]{1,0:T(8,128)(2,1)S(1)} %constant_dynamic-update-slice_fusion.me), channel_id=1, source_target_pairs={{0,3},{1,0},{2,1},{3,2},{4,7},{5,4},{6,5},{7,6},{8,11},{9,8},{10,9... | collective-permute-start | bytes 1179656 | tf_op jit(solution)/shard_map/ppermute | solution.py:32
  15.9 4.7 %collective-permute-done.6.after = bf16[208,1024]{1,0:T(8,128)(2,1)S(1)} collective-permute-done((bf16[208,1024]{1,0:T(8,128)(2,1)}, bf16[208,1024]{1,0:T(8,128)(2,1)S(1)}, u32[]{:S(2)}, u32[]{:S(2)}) %collective-permute-start.6) | collective-permute-done | bytes 426016 | tf_op jit(solution)/shard_map/ppermute | solution.py:32
  20.7 3.3 %collective-permute-start.8 = (bf16[112,1024]{1,0:T(8,128)(2,1)S(1)}, bf16[112,1024]{1,0:T(8,128)(2,1)S(1)}, u32[]{:S(2)}, u32[]{:S(2)}) collective-permute-start(bf16[112,1024]{1,0:T(8,128)(2,1)S(1)} %slice.43), channel_id=1, source_target_pairs={{0,24},{8,0},{16,8},{24,16},{1,25},{9,1},{17,9},{25,17},{2,26},{10... | collective-permute-start | bytes 688136 | tf_op jit(solution)/shard_map/ppermute | solution.py:32
  24.1 1.4 %collective-permute-start.4 = (bf16[96,1024]{1,0:T(8,128)(2,1)S(1)}, bf16[96,1024]{1,0:T(8,128)(2,1)S(1)}, u32[]{:S(2)}, u32[]{:S(2)}) collective-permute-start(bf16[96,1024]{1,0:T(8,128)(2,1)S(1)} %slice.40), channel_id=1, source_target_pairs={{0,1},{1,2},{2,3},{3,0},{4,5},{5,6},{6,7},{7,4},{8,9},{9,10},{10,1... | collective-permute-start | bytes 589832 | tf_op jit(solution)/shard_map/ppermute | solution.py:32
  25.5 1.5 %collective-permute-start.5 = (bf16[96,1024]{1,0:T(8,128)(2,1)S(1)}, bf16[96,1024]{1,0:T(8,128)(2,1)S(1)}, u32[]{:S(2)}, u32[]{:S(2)}) collective-permute-start(bf16[96,1024]{1,0:T(8,128)(2,1)S(1)} %slice.41), channel_id=1, source_target_pairs={{0,3},{1,0},{2,1},{3,2},{4,7},{5,4},{6,5},{7,6},{8,11},{9,8},{10,9... | collective-permute-start | bytes 589832 | tf_op jit(solution)/shard_map/ppermute | solution.py:32
  28.3 2.1 %shard_map.74 = (bf16[1920,384]{1,0:T(8,128)(2,1)S(1)}, bf16[1344,384]{1,0:T(8,128)(2,1)S(1)}) custom-call(s32[1]{0:T(128)} %bitcast.where_ref, bf16[384,1664]{1,0:T(8,128)(2,1)S(1)} %copy-done.1, bf16[384,1024]{1,0:T(8,128)(2,1)S(1)} %copy-done.2, bf16[208,1024]{1,0:T(8,128)(2,1)S(1)} %collective-permute-done.early.before), custom_call_target="tpu_custom_call" | custom-call | flops 962592768 | bytes 5242880 | tf_op jit(solution)/shard_map/pallas_call | solution.py:362
  30.6 2.7 %collective-permute-start.9 = (bf16[784,1024]{1,0:T(8,128)(2,1)S(1)}, bf16[784,1024]{1,0:T(8,128)(2,1)S(1)}, u32[]{:S(2)}, u32[]{:S(2)}) collective-permute-start(bf16[784,1024]{1,0:T(8,128)(2,1)S(1)} %shard_map.75.images_ref.refs_1_), channel_id=1, source_target_pairs={{0,32},{32,0},{1,33},{33,1},{2,34},{34,2},{3,35},{35,3},{4,36},{36... | collective-permute-start | bytes 4816904 | tf_op jit(solution)/shard_map/ppermute | solution.py:359
  33.4 2.0 %shard_map.76 = (bf16[768,1024]{1,0:T(8,128)(2,1)S(1)}, bf16[768,768]{1,0:T(8,128)(2,1)S(1)}) custom-call(s32[1]{0:T(128)} %bitcast.where_ref, f32[1]{0:T(128)S(6)} %copy.9.scale_ref, f32[1]{0:T(128)S(6)} %copy.10.shift_ref, bf16[192,1024]{1,0:T(8,128)(2,1)S(1)} %constant_dynamic-update-slice_fusion.me, bf16[192,1024]{1,0:T(8,128)(2,1)S(1)} %collective-permute-done.2.after, ...), custom_call_target="tpu_custom_call" | custom-call | flops 19327352832 | bytes 6291456 | tf_op jit(solution)/shard_map/pallas_call | solution.py:384
  36.4 2.8 %shard_map.77 = (bf16[768,768]{1,0:T(8,128)(2,1)S(1)}, f32[384,1024]{1,0:T(8,128)S(1)}) custom-call(s32[1]{0:T(128)} %bitcast.where_ref, f32[1]{0:T(128)S(6)} %copy.9.scale_ref, f32[1]{0:T(128)S(6)} %copy.10.shift_ref, bf16[768,1024]{1,0:T(8,128)(2,1)S(1)} %get-tuple-element.29.texts_ref.refs_0_, bf16[784,1024]{1,0:T(8,128)(2,1)S(1)} %collective-permute-done.9.images_ref.refs_3_), custom_call_target="tpu_custom_call" | custom-call | flops 2415919104 | bytes 8388608 | tf_op jit(solution)/shard_map/pallas_call | solution.py:388
  40.9 1.4 %shard_map.83 = (f32[96,1024]{1,0:T(8,128)S(1)}, f32[96,1024]{1,0:T(8,128)S(1)}, f32[192,1024]{1,0:T(8,128)S(1)}) custom-call(bf16[768,768]{1,0:T(8,128)(2,1)S(1)} %get-tuple-element.30.refs_1_.refs_0_, bf16[784,1024]{1,0:T(8,128)(2,1)S(1)} %shard_map.75.images_ref.refs_1_, bf16[768,768]{1,0:T(8,128)(2,1)S(1)} %get-tuple-element.31.refs_1_.refs_2_, ...), custom_call_target="tpu_custom_call" | custom-call | flops 1207959552 | bytes 6291456 | tf_op jit(solution)/shard_map/pallas_call | solution.py:394
  42.3 1.3 %collective-permute-start.17 = (f32[192,1024]{1,0:T(8,128)S(1)}, f32[192,1024]{1,0:T(8,128)S(1)}, u32[]{:S(2)}, u32[]{:S(2)}) collective-permute-start(f32[192,1024]{1,0:T(8,128)S(1)} %get-tuple-element.40), channel_id=1, source_target_pairs={{0,1},{1,2},{2,3},{3,0},{4,5},{5,6},{6,7},{7,4},{8,9},{9,10},{10,1... | collective-permute-start | bytes 2359304 | tf_op jit(solution)/shard_map/ppermute | solution.py:32
  44.6 1.4 %shard_map.82 = (f32[192,1024]{1,0:T(8,128)S(1)}, f32[192,1024]{1,0:T(8,128)S(1)}) custom-call(bf16[768,768]{1,0:T(8,128)(2,1)S(1)} %get-tuple-element.30.refs_1_.refs_0_, bf16[784,1024]{1,0:T(8,128)(2,1)S(1)} %shard_map.75.images_ref.refs_1_, bf16[768,768]{1,0:T(8,128)(2,1)S(1)} %get-tuple-element.31.refs_1_.refs_2_, ...), custom_call_target="tpu_custom_call" | custom-call | flops 9663676416 | bytes 6291456 | tf_op jit(solution)/shard_map/pallas_call | solution.py:398
  46.0 2.7 %collective-permute-start.18 = (f32[192,1024]{1,0:T(8,128)S(1)}, f32[192,1024]{1,0:T(8,128)S(1)}, u32[]{:S(2)}, u32[]{:S(2)}) collective-permute-start(f32[192,1024]{1,0:T(8,128)S(1)} %get-tuple-element.41), channel_id=1, source_target_pairs={{0,3},{1,0},{2,1},{3,2},{4,7},{5,4},{6,5},{7,6},{8,11},{9,8},{10,9... | collective-permute-start | bytes 2359304 | tf_op jit(solution)/shard_map/ppermute | solution.py:32
  49.5 1.7 %collective-permute-start.12 = (f32[192,1024]{1,0:T(8,128)S(1)}, f32[192,1024]{1,0:T(8,128)S(1)}, u32[]{:S(2)}, u32[]{:S(2)}) collective-permute-start(f32[192,1024]{1,0:T(8,128)S(1)} %get-tuple-element.34), channel_id=1, source_target_pairs={{0,8},{8,16},{16,24},{24,0},{1,9},{9,17},{17,25},{25,1},{2,10},{10... | collective-permute-start | bytes 2359304 | tf_op jit(solution)/shard_map/ppermute | solution.py:32
  52.0 2.2 %collective-permute-start.13 = (f32[192,1024]{1,0:T(8,128)S(1)}, f32[192,1024]{1,0:T(8,128)S(1)}, u32[]{:S(2)}, u32[]{:S(2)}) collective-permute-start(f32[192,1024]{1,0:T(8,128)S(1)} %get-tuple-element.35), channel_id=1, source_target_pairs={{0,24},{8,0},{16,8},{24,16},{1,25},{9,1},{17,9},{25,17},{2,26},{10... | collective-permute-start | bytes 2359304 | tf_op jit(solution)/shard_map/ppermute | solution.py:32
  55.0 7.4 %collective-permute-done.17.refs_8_ = f32[192,1024]{1,0:T(8,128)S(1)} collective-permute-done((f32[192,1024]{1,0:T(8,128)S(1)}, f32[192,1024]{1,0:T(8,128)S(1)}, u32[]{:S(2)}, u32[]{:S(2)}) %collective-permute-start.17) | collective-permute-done | bytes 786464 | tf_op jit(solution)/shard_map/ppermute | solution.py:32
  62.3 2.2 %collective-permute-done.18.early_ref.refs_9_ = f32[192,1024]{1,0:T(8,128)S(1)} collective-permute-done((f32[192,1024]{1,0:T(8,128)S(1)}, f32[192,1024]{1,0:T(8,128)S(1)}, u32[]{:S(2)}, u32[]{:S(2)}) %collective-permute-start.18) | collective-permute-done | bytes 786464 | tf_op jit(solution)/shard_map/ppermute | solution.py:32
  64.6 1.4 %collective-permute-start.21 = (f32[96,1024]{1,0:T(8,128)S(1)}, f32[96,1024]{1,0:T(8,128)S(1)}, u32[]{:S(2)}, u32[]{:S(2)}) collective-permute-start(f32[96,1024]{1,0:T(8,128)S(1)} %slice_add_fusion), channel_id=1, source_target_pairs={{0,68},{4,64},{64,4},{68,0},{1,69},{5,65},{65,5},{69,1},{2,70},{6,... | collective-permute-start | bytes 1179656 | tf_op jit(solution)/shard_map/ppermute | solution.py:401
  66.0 2.7 %collective-permute-start.20 = (f32[96,1024]{1,0:T(8,128)S(1)}, f32[96,1024]{1,0:T(8,128)S(1)}, u32[]{:S(2)}, u32[]{:S(2)}) collective-permute-start(f32[96,1024]{1,0:T(8,128)S(1)} %shard_map.85), channel_id=1, source_target_pairs={{0,2},{1,3},{2,0},{3,1},{4,6},{5,7},{6,4},{7,5},{8,10},{9,11},{10,... | collective-permute-start | bytes 1179656 | tf_op jit(solution)/shard_map/ppermute | solution.py:32
  70.2 3.0 %collective-permute-start.15 = (f32[96,1024]{1,0:T(8,128)S(1)}, f32[96,1024]{1,0:T(8,128)S(1)}, u32[]{:S(2)}, u32[]{:S(2)}) collective-permute-start(f32[96,1024]{1,0:T(8,128)S(1)} %shard_map.81), channel_id=1, source_target_pairs={{0,16},{8,24},{16,0},{24,8},{1,17},{9,25},{17,1},{25,9},{2,18},{10... | collective-permute-start | bytes 1179656 | tf_op jit(solution)/shard_map/ppermute | solution.py:32
  73.2 1.5 %collective-permute-done.21.refs_11_ = f32[96,1024]{1,0:T(8,128)S(1)} collective-permute-done((f32[96,1024]{1,0:T(8,128)S(1)}, f32[96,1024]{1,0:T(8,128)S(1)}, u32[]{:S(2)}, u32[]{:S(2)}) %collective-permute-start.21) | collective-permute-done | bytes 393248 | tf_op jit(solution)/shard_map/ppermute | solution.py:401
  74.7 1.4 %collective-permute-done.20.refs_10_ = f32[96,1024]{1,0:T(8,128)S(1)} collective-permute-done((f32[96,1024]{1,0:T(8,128)S(1)}, f32[96,1024]{1,0:T(8,128)S(1)}, u32[]{:S(2)}, u32[]{:S(2)}) %collective-permute-start.20) | collective-permute-done | bytes 393248 | tf_op jit(solution)/shard_map/ppermute | solution.py:32
  76.1 2.4 %collective-permute-done.16.refs_4_ = f32[96,1024]{1,0:T(8,128)S(1)} collective-permute-done((f32[96,1024]{1,0:T(8,128)S(1)}, f32[96,1024]{1,0:T(8,128)S(1)}, u32[]{:S(2)}, u32[]{:S(2)}) %collective-permute-start.16) | collective-permute-done | bytes 393248 | tf_op jit(solution)/shard_map/ppermute | solution.py:404
  78.5 1.7 %collective-permute-done.15.refs_3_ = f32[96,1024]{1,0:T(8,128)S(1)} collective-permute-done((f32[96,1024]{1,0:T(8,128)S(1)}, f32[96,1024]{1,0:T(8,128)S(1)}, u32[]{:S(2)}, u32[]{:S(2)}) %collective-permute-start.15) | collective-permute-done | bytes 393248 | tf_op jit(solution)/shard_map/ppermute | solution.py:32
  80.5 12.4 %all_to_all.10.backs_ref = bf16[4,192,256]{2,1,0:T(8,128)(2,1)S(1)} all-to-all(bf16[4,192,256]{2,1,0:T(8,128)(2,1)S(1)} %shard_map.86), channel_id=1, replica_groups=mesh['xl'=2,'core'=2,'z'=4,'xh'=2,'y'=4] {'xl','core'}, dimensions={0} | all-to-all | bytes 786432 | tf_op jit(solution)/shard_map/all_to_all | solution.py:411
  92.9 1.4 %shard_map.87 = s16[128,24,256]{2,1,0:T(8,128)(2,1)S(1)} custom-call(bf16[1920,384]{1,0:T(8,128)(2,1)S(1)} %get-tuple-element.26.early_a.images_ref, bf16[1344,384]{1,0:T(8,128)(2,1)S(1)} %get-tuple-element.27.early_b.texts_ref, bf16[4,192,256]{2,1,0:T(8,128)(2,1)S(1)} %all_to_all.10.backs_ref), custom_call_target="tpu_custom_call" | custom-call | flops 1207959552 | bytes 6291456 | tf_op jit(solution)/shard_map/pallas_call | solution.py:413
  94.3 31.8 %all_to_all.11.coded_ref = s16[128,24,256]{2,1,0:T(8,128)(2,1)S(1)} all-to-all(s16[128,24,256]{2,1,0:T(8,128)(2,1)S(1)} %shard_map.87), channel_id=1, replica_groups=mesh['xl'=2,'core'=2,'z'=4,'xh'=2,'y'=4] {'xl','core','z','xh','y'}, dimensions={0} | all-to-all | bytes 3145728 | tf_op jit(solution)/shard_map/all_to_all | solution.py:419
  (50 shorter events, 10.6 us)
Async XLA Ops:
  4.9 23.4 %copy-start.1 = (bf16[384,1664]{1,0:T(8,128)(2,1)S(1)}, bf16[384,1664]{1,0:T(8,128)(2,1)}, u32[]{:S(2)}) copy-start(bf16[384,1664]{1,0:T(8,128)(2,1)} %image_feats.3) | copy-start | bytes 3833860
  4.9 23.4 %copy-start.2 = (bf16[384,1024]{1,0:T(8,128)(2,1)S(1)}, bf16[384,1024]{1,0:T(8,128)(2,1)}, u32[]{:S(2)}) copy-start(bf16[384,1024]{1,0:T(8,128)(2,1)} %text_feats.3) | copy-start | bytes 2359300
  4.9 8.1 %collective-permute-start.1 = (bf16[96,1024]{1,0:T(8,128)(2,1)}, bf16[96,1024]{1,0:T(8,128)(2,1)S(1)}, u32[]{:S(2)}, u32[]{:S(2)}) collective-permute-start(bf16[96,1024]{1,0:T(8,128)(2,1)} %get-tuple-element.28.refs_12_), channel_id=1, source_target_pairs={{0,68},{4,64},{64,4},{68,0},{1,69},{5,65},{65,5},{69,1},{2,70},{6,... | collective-permute-start | bytes 589832 | tf_op jit(solution)/shard_map/ppermute | solution.py:352
  8.3 15.7 %collective-permute-start = (bf16[208,1024]{1,0:T(8,128)(2,1)}, bf16[208,1024]{1,0:T(8,128)(2,1)S(1)}, u32[]{:S(2)}, u32[]{:S(2)}) collective-permute-start(bf16[208,1024]{1,0:T(8,128)(2,1)} %get-tuple-element.25.me.refs_5_), channel_id=1, source_target_pairs={{0,8},{8,16},{16,24},{24,0},{1,9},{9,17},{17,25},{25,1},{2,10},{10... | collective-permute-start | bytes 1277960 | tf_op jit(solution)/shard_map/ppermute | solution.py:32
  9.9 10.7 %collective-permute-start.6 = (bf16[208,1024]{1,0:T(8,128)(2,1)}, bf16[208,1024]{1,0:T(8,128)(2,1)S(1)}, u32[]{:S(2)}, u32[]{:S(2)}) collective-permute-start(bf16[208,1024]{1,0:T(8,128)(2,1)} %get-tuple-element.25.me.refs_5_), channel_id=1, source_target_pairs={{0,24},{8,0},{16,8},{24,16},{1,25},{9,1},{17,9},{25,17},{2,26},{10... | collective-permute-start | bytes 1277960 | tf_op jit(solution)/shard_map/ppermute | solution.py:32
  13.1 11.0 %collective-permute-start.3 = (bf16[192,1024]{1,0:T(8,128)(2,1)S(1)}, bf16[192,1024]{1,0:T(8,128)(2,1)S(1)}, u32[]{:S(2)}, u32[]{:S(2)}) collective-permute-start(bf16[192,1024]{1,0:T(8,128)(2,1)S(1)} %constant_dynamic-update-slice_fusion.me), channel_id=1, source_target_pairs={{0,1},{1,2},{2,3},{3,0},{4,5},{5,6},{6,7},{7,4},{8,9},{9,10},{10,1... | collective-permute-start | bytes 1179656 | tf_op jit(solution)/shard_map/ppermute | solution.py:32
  14.4 11.0 %collective-permute-start.2 = (bf16[192,1024]{1,0:T(8,128)(2,1)S(1)}, bf16[192,1024]{1,0:T(8,128)(2,1)S(1)}, u32[]{:S(2)}, u32[]{:S(2)}) collective-permute-start(bf16[192,1024]{1,0:T(8,128)(2,1)S(1)} %constant_dynamic-update-slice_fusion.me), channel_id=1, source_target_pairs={{0,3},{1,0},{2,1},{3,2},{4,7},{5,4},{6,5},{7,6},{8,11},{9,8},{10,9... | collective-permute-start | bytes 1179656 | tf_op jit(solution)/shard_map/ppermute | solution.py:32
  20.7 9.8 %collective-permute-start.8 = (bf16[112,1024]{1,0:T(8,128)(2,1)S(1)}, bf16[112,1024]{1,0:T(8,128)(2,1)S(1)}, u32[]{:S(2)}, u32[]{:S(2)}) collective-permute-start(bf16[112,1024]{1,0:T(8,128)(2,1)S(1)} %slice.43), channel_id=1, source_target_pairs={{0,24},{8,0},{16,8},{24,16},{1,25},{9,1},{17,9},{25,17},{2,26},{10... | collective-permute-start | bytes 688136 | tf_op jit(solution)/shard_map/ppermute | solution.py:32
  24.0 6.5 %collective-permute-start.7 = (bf16[96,1024]{1,0:T(8,128)(2,1)S(1)}, bf16[96,1024]{1,0:T(8,128)(2,1)S(1)}, u32[]{:S(2)}, u32[]{:S(2)}) collective-permute-start(bf16[96,1024]{1,0:T(8,128)(2,1)S(1)} %slice.42), channel_id=1, source_target_pairs={{0,8},{8,16},{16,24},{24,0},{1,9},{9,17},{17,25},{25,1},{2,10},{10... | collective-permute-start | bytes 589832 | tf_op jit(solution)/shard_map/ppermute | solution.py:32
  24.1 9.2 %collective-permute-start.4 = (bf16[96,1024]{1,0:T(8,128)(2,1)S(1)}, bf16[96,1024]{1,0:T(8,128)(2,1)S(1)}, u32[]{:S(2)}, u32[]{:S(2)}) collective-permute-start(bf16[96,1024]{1,0:T(8,128)(2,1)S(1)} %slice.40), channel_id=1, source_target_pairs={{0,1},{1,2},{2,3},{3,0},{4,5},{5,6},{6,7},{7,4},{8,9},{9,10},{10,1... | collective-permute-start | bytes 589832 | tf_op jit(solution)/shard_map/ppermute | solution.py:32
  25.5 7.9 %collective-permute-start.5 = (bf16[96,1024]{1,0:T(8,128)(2,1)S(1)}, bf16[96,1024]{1,0:T(8,128)(2,1)S(1)}, u32[]{:S(2)}, u32[]{:S(2)}) collective-permute-start(bf16[96,1024]{1,0:T(8,128)(2,1)S(1)} %slice.41), channel_id=1, source_target_pairs={{0,3},{1,0},{2,1},{3,2},{4,7},{5,4},{6,5},{7,6},{8,11},{9,8},{10,9... | collective-permute-start | bytes 589832 | tf_op jit(solution)/shard_map/ppermute | solution.py:32
  28.3 2.2 %copy-start = (bf16[208,1024]{1,0:T(8,128)(2,1)S(1)}, bf16[208,1024]{1,0:T(8,128)(2,1)}, u32[]{:S(2)}) copy-start(bf16[208,1024]{1,0:T(8,128)(2,1)} %get-tuple-element.25.me.refs_5_) | copy-start | bytes 1277956
  30.6 5.8 %collective-permute-start.9 = (bf16[784,1024]{1,0:T(8,128)(2,1)S(1)}, bf16[784,1024]{1,0:T(8,128)(2,1)S(1)}, u32[]{:S(2)}, u32[]{:S(2)}) collective-permute-start(bf16[784,1024]{1,0:T(8,128)(2,1)S(1)} %shard_map.75.images_ref.refs_1_), channel_id=1, source_target_pairs={{0,32},{32,0},{1,33},{33,1},{2,34},{34,2},{3,35},{35,3},{4,36},{36... | collective-permute-start | bytes 4816904 | tf_op jit(solution)/shard_map/ppermute | solution.py:359
  39.2 9.4 %collective-permute-start.11 = (f32[384,1024]{1,0:T(8,128)S(1)}, f32[384,1024]{1,0:T(8,128)S(1)}, u32[]{:S(2)}, u32[]{:S(2)}) collective-permute-start(f32[384,1024]{1,0:T(8,128)S(1)} %get-tuple-element.33), channel_id=1, source_target_pairs={{0,32},{32,0},{1,33},{33,1},{2,34},{34,2},{3,35},{35,3},{4,36},{36... | collective-permute-start | bytes 4718600 | tf_op jit(solution)/shard_map/ppermute | solution.py:392
  40.7 10.5 %collective-permute-start.10 = (f32[384,1024]{1,0:T(8,128)S(1)}, f32[384,1024]{1,0:T(8,128)S(1)}, u32[]{:S(2)}, u32[]{:S(2)}) collective-permute-start(f32[384,1024]{1,0:T(8,128)S(1)} %shard_map.78), channel_id=1, source_target_pairs={{0,32},{32,0},{1,33},{33,1},{2,34},{34,2},{3,35},{35,3},{4,36},{36... | collective-permute-start | bytes 4718600 | tf_op jit(solution)/shard_map/ppermute | solution.py:396
  42.3 20.0 %collective-permute-start.17 = (f32[192,1024]{1,0:T(8,128)S(1)}, f32[192,1024]{1,0:T(8,128)S(1)}, u32[]{:S(2)}, u32[]{:S(2)}) collective-permute-start(f32[192,1024]{1,0:T(8,128)S(1)} %get-tuple-element.40), channel_id=1, source_target_pairs={{0,1},{1,2},{2,3},{3,0},{4,5},{5,6},{6,7},{7,4},{8,9},{9,10},{10,1... | collective-permute-start | bytes 2359304 | tf_op jit(solution)/shard_map/ppermute | solution.py:32
  43.6 11.2 %collective-permute-start.19 = (f32[96,1024]{1,0:T(8,128)S(1)}, f32[96,1024]{1,0:T(8,128)S(1)}, u32[]{:S(2)}, u32[]{:S(2)}) collective-permute-start(f32[96,1024]{1,0:T(8,128)S(1)} %get-tuple-element.43), channel_id=1, source_target_pairs={{0,68},{4,64},{64,4},{68,0},{1,69},{5,65},{65,5},{69,1},{2,70},{6,... | collective-permute-start | bytes 1179656 | tf_op jit(solution)/shard_map/ppermute | solution.py:401
  46.0 18.6 %collective-permute-start.18 = (f32[192,1024]{1,0:T(8,128)S(1)}, f32[192,1024]{1,0:T(8,128)S(1)}, u32[]{:S(2)}, u32[]{:S(2)}) collective-permute-start(f32[192,1024]{1,0:T(8,128)S(1)} %get-tuple-element.41), channel_id=1, source_target_pairs={{0,3},{1,0},{2,1},{3,2},{4,7},{5,4},{6,5},{7,6},{8,11},{9,8},{10,9... | collective-permute-start | bytes 2359304 | tf_op jit(solution)/shard_map/ppermute | solution.py:32
  49.5 20.5 %collective-permute-start.12 = (f32[192,1024]{1,0:T(8,128)S(1)}, f32[192,1024]{1,0:T(8,128)S(1)}, u32[]{:S(2)}, u32[]{:S(2)}) collective-permute-start(f32[192,1024]{1,0:T(8,128)S(1)} %get-tuple-element.34), channel_id=1, source_target_pairs={{0,8},{8,16},{16,24},{24,0},{1,9},{9,17},{17,25},{25,1},{2,10},{10... | collective-permute-start | bytes 2359304 | tf_op jit(solution)/shard_map/ppermute | solution.py:32
  52.0 18.0 %collective-permute-start.13 = (f32[192,1024]{1,0:T(8,128)S(1)}, f32[192,1024]{1,0:T(8,128)S(1)}, u32[]{:S(2)}, u32[]{:S(2)}) collective-permute-start(f32[192,1024]{1,0:T(8,128)S(1)} %get-tuple-element.35), channel_id=1, source_target_pairs={{0,24},{8,0},{16,8},{24,16},{1,25},{9,1},{17,9},{25,17},{2,26},{10... | collective-permute-start | bytes 2359304 | tf_op jit(solution)/shard_map/ppermute | solution.py:32
  54.9 15.3 %collective-permute-start.14 = (f32[96,1024]{1,0:T(8,128)S(1)}, f32[96,1024]{1,0:T(8,128)S(1)}, u32[]{:S(2)}, u32[]{:S(2)}) collective-permute-start(f32[96,1024]{1,0:T(8,128)S(1)} %get-tuple-element.37), channel_id=1, source_target_pairs={{0,64},{64,0},{1,65},{65,1},{2,66},{66,2},{3,67},{67,3},{4,68},{68... | collective-permute-start | bytes 1179656 | tf_op jit(solution)/shard_map/ppermute | solution.py:404
  64.6 10.1 %collective-permute-start.21 = (f32[96,1024]{1,0:T(8,128)S(1)}, f32[96,1024]{1,0:T(8,128)S(1)}, u32[]{:S(2)}, u32[]{:S(2)}) collective-permute-start(f32[96,1024]{1,0:T(8,128)S(1)} %slice_add_fusion), channel_id=1, source_target_pairs={{0,68},{4,64},{64,4},{68,0},{1,69},{5,65},{65,5},{69,1},{2,70},{6,... | collective-permute-start | bytes 1179656 | tf_op jit(solution)/shard_map/ppermute | solution.py:401
  66.0 10.1 %collective-permute-start.20 = (f32[96,1024]{1,0:T(8,128)S(1)}, f32[96,1024]{1,0:T(8,128)S(1)}, u32[]{:S(2)}, u32[]{:S(2)}) collective-permute-start(f32[96,1024]{1,0:T(8,128)S(1)} %shard_map.85), channel_id=1, source_target_pairs={{0,2},{1,3},{2,0},{3,1},{4,6},{5,7},{6,4},{7,5},{8,10},{9,11},{10,... | collective-permute-start | bytes 1179656 | tf_op jit(solution)/shard_map/ppermute | solution.py:32
  69.9 10.2 %copy-start.3 = (bf16[96,1024]{1,0:T(8,128)(2,1)S(1)}, bf16[96,1024]{1,0:T(8,128)(2,1)}, u32[]{:S(2)}) copy-start(bf16[96,1024]{1,0:T(8,128)(2,1)} %get-tuple-element.28.refs_12_) | copy-start | bytes 589828
  69.9 10.2 %copy-start.4 = (f32[96,128]{1,0:T(8,128)S(1)}, f32[96,128]{1,0:T(8,128)}, u32[]{:S(2)}) copy-start(f32[96,128]{1,0:T(8,128)} %get-tuple-element.44.refs_13_) | copy-start | bytes 147460
  69.9 10.2 %copy-start.5 = (f32[96,128]{1,0:T(8,128)S(1)}, f32[96,128]{1,0:T(8,128)}, u32[]{:S(2)}) copy-start(f32[96,128]{1,0:T(8,128)} %get-tuple-element.38.refs_6_) | copy-start | bytes 147460
  70.0 8.4 %collective-permute-start.16 = (f32[96,1024]{1,0:T(8,128)S(1)}, f32[96,1024]{1,0:T(8,128)S(1)}, u32[]{:S(2)}, u32[]{:S(2)}) collective-permute-start(f32[96,1024]{1,0:T(8,128)S(1)} %slice_add_fusion.2), channel_id=1, source_target_pairs={{0,64},{64,0},{1,65},{65,1},{2,66},{66,2},{3,67},{67,3},{4,68},{68... | collective-permute-start | bytes 1179656 | tf_op jit(solution)/shard_map/ppermute | solution.py:404
  70.2 9.9 %collective-permute-start.15 = (f32[96,1024]{1,0:T(8,128)S(1)}, f32[96,1024]{1,0:T(8,128)S(1)}, u32[]{:S(2)}, u32[]{:S(2)}) collective-permute-start(f32[96,1024]{1,0:T(8,128)S(1)} %shard_map.81), channel_id=1, source_target_pairs={{0,16},{8,24},{16,0},{24,8},{1,17},{9,25},{17,1},{25,9},{2,18},{10... | collective-permute-start | bytes 1179656 | tf_op jit(solution)/shard_map/ppermute | solution.py:32

commit v5 on v4

--- a/solution.py
+++ b/solution.py
@@ -248,8 +248,8 @@
     share_out(image_terms(coef_ref, texts_ref, part) + taken_ref[...], outs)
 
 
-def back_kernel(*refs):
-    *inputs, out_ref = refs
+def back_kernel(where_ref, *refs):
+    *inputs, own_ref, core_ref, xl_ref, both_ref, held_ref = refs
     for tower in range(2):
         mine, right, left, far, got, emb, inverse = inputs[tower * 7 : tower * 7 + 7]
         gradients = mine[:QUARTER, :] + right[:QUARTER, :] + left[:QUARTER, :]
@@ -258,16 +258,21 @@
         inner_sum = jnp.sum(widened * gradients, axis=1, keepdims=True)
         value = (inverse[:, :1] * (gradients - widened * inner_sum)).astype(BF16)
         for i in range(4):
-            out_ref[i, tower * QUARTER : (tower + 1) * QUARTER, :] = value[
+            held_ref[i, tower * QUARTER : (tower + 1) * QUARTER, :] = value[
                 :, i * SLICE : (i + 1) * SLICE
             ]
-
-
-def terms_kernel(images_ref, texts_ref, backs_ref, out_ref, both_ref):
-    for i in range(4):
+    xl, core, _, _, _, _ = position(where_ref)
+    own_ref[...] = held_ref[xl * 2 + core]
+    core_ref[...] = held_ref[xl * 2 + 1 - core]
+    xl_ref[...] = held_ref[2 - xl * 2 + core]
+    both_ref[...] = held_ref[3 - xl * 2 - core]
+
+
+def terms_kernel(images_ref, texts_ref, own, core, xl, both, out_ref, both_ref):
+    for i, ref in enumerate((own, core, xl, both)):
         for part in range(2):
-            both_ref[part, i * QUARTER : (i + 1) * QUARTER, :] = backs_ref[
-                i, part * QUARTER : (part + 1) * QUARTER, :
+            both_ref[part, i * QUARTER : (i + 1) * QUARTER, :] = ref[
+                part * QUARTER : (part + 1) * QUARTER, :
             ]
     rows = STEP * GROUP
     steps = 128 // STEP
@@ -320,15 +325,21 @@
                 select, held_ref[:, low : low + ROWS], NT, preferred_element_type=F32
             ).astype(BF16)
 
+    def quarters(places):
+        return [pl.ds(pl.multiple_of(place * QUARTER, QUARTER), QUARTER) for place in places]
+
     width = image_feats.shape[1]
-    quarters = [pl.ds(i * QUARTER, QUARTER) for i in (0, 2, 1, 3)]
-    fill(image_feats, image_out, quarters, 0, 0)
-    _, _, _, xh, _, _ = position(where_ref)
-    half = [xh, xh, 1 - xh, 1 - xh]
-    quarters = [
-        pl.ds(pl.multiple_of(half[i] * HALF + i % 2 * QUARTER, QUARTER), QUARTER) for i in range(4)
-    ]
-    fill(text_feats, text_out, quarters, width, width // OWN // STEP)
+    xl, core, _, _, _, text_quarter = position(where_ref)
+    half = text_quarter // 2
+    fill(
+        image_feats, image_out,
+        quarters([c * 2 + x for x in (xl, 1 - xl) for c in (core, 1 - core)]), 0, 0,
+    )
+    fill(
+        text_feats, text_out,
+        quarters([h * 2 + c for h in (half, 1 - half) for c in (core, 1 - core)]),
+        width, width // OWN // STEP,
+    )
 
 
 def body(image_feats, text_feats, image_weight, text_weight, partner, log_scale, logit_bias):
@@ -404,18 +415,25 @@
         *image_ways, *image_rest, "z", lambda a: lax.ppermute(a, "xl", SWAP)
     )
 
-    backs = call(
-        back_kernel, shape(4, HALF, SLICE, dtype=BF16), 0, 6 << 20,
-        in_specs=[VMEM] * 14, out_specs=VMEM,
-    )(*image_sums, load, image_inverse, *text_sums, own_texts, text_inverse)
-    backs = lax.all_to_all(backs, TOWER, split_axis=0, concat_axis=0, tiled=True)
+    piece = shape(HALF, SLICE, dtype=BF16)
+    own, other_core, other_xl, other_both = call(
+        back_kernel, [piece] * 4, 0, 6 << 20,
+        in_specs=[SMEM] + [VMEM] * 14, out_specs=[VMEM] * 4,
+        scratch_shapes=[pltpu.VMEM((4, HALF, SLICE), BF16)],
+    )(where, *image_sums, load, image_inverse, *text_sums, own_texts, text_inverse)
+    backs = (
+        own,
+        lax.ppermute(other_core, "core", SWAP),
+        lax.ppermute(other_xl, "xl", SWAP),
+        lax.ppermute(other_both, TOWER, [(i, 3 - i) for i in range(4)]),
+    )
 
     coded = call(
         terms_kernel, shape(128, GROUP, SLICE, dtype=jnp.int16),
         4 * 128 * GROUP * ROWS * SLICE, 6 << 20, 24,
-        in_specs=[VMEM] * 3, out_specs=VMEM,
+        in_specs=[VMEM] * 6, out_specs=VMEM,
         scratch_shapes=[pltpu.VMEM((2, ROWS, SLICE), BF16)],
-    )(image_groups, text_groups, backs)
+    )(image_groups, text_groups, *backs)
     coded = lax.all_to_all(coded, AXES, split_axis=0, concat_axis=0, tiled=True)
     return call(total_kernel, shape(OWN, E), 0, 2 << 20, in_specs=[VMEM], out_specs=VMEM)(coded)
 

time: 128 us -> 125 us (0.977)
  blocking collectives: 44.1 us -> 31.3 us
  waiting for transfers between devices: 24.2 us -> 29.2 us
  starting transfers between devices: 36 us -> 40.9 us
    all_to_all x1 -> x0, blocking collectives: 12.4 us -> none  [body(): lax.all_to_all(backs, TOWER, split_axis=0, concat_axis=0, tiled=True)]
    ppermute x0 -> x3, starting transfers between devices: none -> 4.97 us  [the longest x1 3.24 us: body(): lax.ppermute(other_core, 'core', SWAP)]
    ppermute x0 -> x3, waiting for transfers between devices: none -> 4.92 us  [the longest x1 2.62 us: body(): lax.ppermute(other_xl, 'xl', SWAP)]
  transfers between devices with their start and end apart: 22 -> 25, of which waited for: 10 -> 12; matrix products, arithmetic and copies ran while one was open for 1% -> 1% of each run, Pallas kernels for 7% -> 8%
where the time goes in v5:
time: 125 us
  starting transfers between devices  40.9 us (33%)
  blocking collectives  31.3 us (25%)
  waiting for transfers between devices  29.2 us (23%)
  Pallas kernels  20.4 us (16%)
  between operations  1.58 us (1%)
    all_to_all x1, blocking collectives, body(): coded = lax.all_to_all(coded, AXES, split_axis=0, concat_axis=0, tiled=True)  31.3 us
    ppermute x14, starting transfers between devices, shifted(): return lax.ppermute(array, axis, [(i, (i + by) % 4) for i in range(4)])  26.4 us
    ppermute x14, waiting for transfers between devices, shifted(): return lax.ppermute(array, axis, [(i, (i + by) % 4) for i in range(4)])  18.7 us
    pallas_call x1, Pallas kernels, body(): call(embed_kernel, [shape(QUARTER, E, dtype=BF16), shape(QUARTER, 128), s...  4.89 us
    ppermute x1, starting transfers between devices, body(): other_texts = lax.ppermute(own_texts, ('xl', 'xh'), FLIP)  3.39 us
    ppermute x1, starting transfers between devices, body(): lax.ppermute(other_core, 'core', SWAP)  3.24 us
    pallas_call x1, Pallas kernels, body(): call(given_kernel, [coef, shape(ROWS, E)], 2 * flops, 8 << 20, 24, in_spe...  2.8 us
    ppermute x1, starting transfers between devices, body(): others = lax.ppermute(images, 'core', SWAP)  2.72 us
  transfers between devices with their start and end apart: 25, of which 12 were waited for; matrix products, arithmetic and copies ran while one was open for 1% of the time, Pallas kernels for 8%

profile of v5, /device:TPU:1, one launch (start us, length us, event | category | flops | bytes accessed | tf_op | source)
XLA Modules:
  0.0 124.6 jit_solution(6855241973406081535)
XLA Ops:
  0.0 4.9 %shard_map.73 = (bf16[96,1024]{1,0:T(8,128)(2,1)}, f32[96,128]{1,0:T(8,128)}, bf16[208,1024]{1,0:T(8,128)(2,1)}, f32[96,128]{1,0:T(8,128)}) custom-call(s32[1]{0:T(128)} %bitcast.where_ref, s32[3,128]{1,0:T(4,128)} %bitcast.2, bf16[384,1024]{1,0:T(8,128)(2,1)} %text_feats.3, bf16[384,1664]{1,0:T(8,128)(2,1)} %image_feats.3, bf16[1024,1024]{1,0:T(8,128)(2,1)} %text_weight.1, ...), custom_call_target="tpu_custom_call" | custom-call | flops 855638016 | bytes 8388608 | tf_op jit(solution)/shard_map/pallas_call | solution.py:348
  4.9 3.4 %collective-permute-start.1 = (bf16[96,1024]{1,0:T(8,128)(2,1)}, bf16[96,1024]{1,0:T(8,128)(2,1)S(1)}, u32[]{:S(2)}, u32[]{:S(2)}) collective-permute-start(bf16[96,1024]{1,0:T(8,128)(2,1)} %get-tuple-element.32.refs_12_), channel_id=1, source_target_pairs={{0,68},{4,64},{64,4},{68,0},{1,69},{5,65},{65,5},{69,1},{2,70},{6,... | collective-permute-start | bytes 589832 | tf_op jit(solution)/shard_map/ppermute | solution.py:363
  8.3 1.6 %collective-permute-start = (bf16[208,1024]{1,0:T(8,128)(2,1)}, bf16[208,1024]{1,0:T(8,128)(2,1)S(1)}, u32[]{:S(2)}, u32[]{:S(2)}) collective-permute-start(bf16[208,1024]{1,0:T(8,128)(2,1)} %get-tuple-element.29.me.refs_5_), channel_id=1, source_target_pairs={{0,8},{8,16},{16,24},{24,0},{1,9},{9,17},{17,25},{25,1},{2,10},{10... | collective-permute-start | bytes 1277960 | tf_op jit(solution)/shard_map/ppermute | solution.py:32
  9.9 2.1 %collective-permute-start.6 = (bf16[208,1024]{1,0:T(8,128)(2,1)}, bf16[208,1024]{1,0:T(8,128)(2,1)S(1)}, u32[]{:S(2)}, u32[]{:S(2)}) collective-permute-start(bf16[208,1024]{1,0:T(8,128)(2,1)} %get-tuple-element.29.me.refs_5_), channel_id=1, source_target_pairs={{0,24},{8,0},{16,8},{24,16},{1,25},{9,1},{17,9},{25,17},{2,26},{10... | collective-permute-start | bytes 1277960 | tf_op jit(solution)/shard_map/ppermute | solution.py:32
  13.1 1.4 %collective-permute-start.3 = (bf16[192,1024]{1,0:T(8,128)(2,1)S(1)}, bf16[192,1024]{1,0:T(8,128)(2,1)S(1)}, u32[]{:S(2)}, u32[]{:S(2)}) collective-permute-start(bf16[192,1024]{1,0:T(8,128)(2,1)S(1)} %constant_dynamic-update-slice_fusion.me), channel_id=1, source_target_pairs={{0,1},{1,2},{2,3},{3,0},{4,5},{5,6},{6,7},{7,4},{8,9},{9,10},{10,1... | collective-permute-start | bytes 1179656 | tf_op jit(solution)/shard_map/ppermute | solution.py:32
  14.4 1.5 %collective-permute-start.2 = (bf16[192,1024]{1,0:T(8,128)(2,1)S(1)}, bf16[192,1024]{1,0:T(8,128)(2,1)S(1)}, u32[]{:S(2)}, u32[]{:S(2)}) collective-permute-start(bf16[192,1024]{1,0:T(8,128)(2,1)S(1)} %constant_dynamic-update-slice_fusion.me), channel_id=1, source_target_pairs={{0,3},{1,0},{2,1},{3,2},{4,7},{5,4},{6,5},{7,6},{8,11},{9,8},{10,9... | collective-permute-start | bytes 1179656 | tf_op jit(solution)/shard_map/ppermute | solution.py:32
  15.9 4.7 %collective-permute-done.6.after = bf16[208,1024]{1,0:T(8,128)(2,1)S(1)} collective-permute-done((bf16[208,1024]{1,0:T(8,128)(2,1)}, bf16[208,1024]{1,0:T(8,128)(2,1)S(1)}, u32[]{:S(2)}, u32[]{:S(2)}) %collective-permute-start.6) | collective-permute-done | bytes 426016 | tf_op jit(solution)/shard_map/ppermute | solution.py:32
  20.7 3.3 %collective-permute-start.8 = (bf16[112,1024]{1,0:T(8,128)(2,1)S(1)}, bf16[112,1024]{1,0:T(8,128)(2,1)S(1)}, u32[]{:S(2)}, u32[]{:S(2)}) collective-permute-start(bf16[112,1024]{1,0:T(8,128)(2,1)S(1)} %slice.43), channel_id=1, source_target_pairs={{0,24},{8,0},{16,8},{24,16},{1,25},{9,1},{17,9},{25,17},{2,26},{10... | collective-permute-start | bytes 688136 | tf_op jit(solution)/shard_map/ppermute | solution.py:32
  24.1 1.4 %collective-permute-start.4 = (bf16[96,1024]{1,0:T(8,128)(2,1)S(1)}, bf16[96,1024]{1,0:T(8,128)(2,1)S(1)}, u32[]{:S(2)}, u32[]{:S(2)}) collective-permute-start(bf16[96,1024]{1,0:T(8,128)(2,1)S(1)} %slice.40), channel_id=1, source_target_pairs={{0,1},{1,2},{2,3},{3,0},{4,5},{5,6},{6,7},{7,4},{8,9},{9,10},{10,1... | collective-permute-start | bytes 589832 | tf_op jit(solution)/shard_map/ppermute | solution.py:32
  25.5 1.5 %collective-permute-start.5 = (bf16[96,1024]{1,0:T(8,128)(2,1)S(1)}, bf16[96,1024]{1,0:T(8,128)(2,1)S(1)}, u32[]{:S(2)}, u32[]{:S(2)}) collective-permute-start(bf16[96,1024]{1,0:T(8,128)(2,1)S(1)} %slice.41), channel_id=1, source_target_pairs={{0,3},{1,0},{2,1},{3,2},{4,7},{5,4},{6,5},{7,6},{8,11},{9,8},{10,9... | collective-permute-start | bytes 589832 | tf_op jit(solution)/shard_map/ppermute | solution.py:32
  28.3 2.2 %shard_map.74 = (bf16[1920,384]{1,0:T(8,128)(2,1)S(1)}, bf16[1344,384]{1,0:T(8,128)(2,1)S(1)}) custom-call(s32[1]{0:T(128)} %bitcast.where_ref, bf16[384,1664]{1,0:T(8,128)(2,1)S(1)} %copy-done.1, bf16[384,1024]{1,0:T(8,128)(2,1)S(1)} %copy-done.3, bf16[208,1024]{1,0:T(8,128)(2,1)S(1)} %collective-permute-done.early.before), custom_call_target="tpu_custom_call" | custom-call | flops 962592768 | bytes 5242880 | tf_op jit(solution)/shard_map/pallas_call | solution.py:373
  30.7 2.7 %collective-permute-start.9 = (bf16[784,1024]{1,0:T(8,128)(2,1)S(1)}, bf16[784,1024]{1,0:T(8,128)(2,1)S(1)}, u32[]{:S(2)}, u32[]{:S(2)}) collective-permute-start(bf16[784,1024]{1,0:T(8,128)(2,1)S(1)} %shard_map.75.images_ref.refs_1_), channel_id=1, source_target_pairs={{0,32},{32,0},{1,33},{33,1},{2,34},{34,2},{3,35},{35,3},{4,36},{36... | collective-permute-start | bytes 4816904 | tf_op jit(solution)/shard_map/ppermute | solution.py:370
  33.4 2.0 %shard_map.76 = (bf16[768,1024]{1,0:T(8,128)(2,1)S(1)}, bf16[768,768]{1,0:T(8,128)(2,1)S(1)}) custom-call(s32[1]{0:T(128)} %bitcast.where_ref, f32[1]{0:T(128)S(6)} %copy.9.scale_ref, f32[1]{0:T(128)S(6)} %copy.10.shift_ref, bf16[192,1024]{1,0:T(8,128)(2,1)S(1)} %constant_dynamic-update-slice_fusion.me, bf16[192,1024]{1,0:T(8,128)(2,1)S(1)} %collective-permute-done.2.after, ...), custom_call_target="tpu_custom_call" | custom-call | flops 19327352832 | bytes 6291456 | tf_op jit(solution)/shard_map/pallas_call | solution.py:395
  36.5 2.8 %shard_map.77 = (bf16[768,768]{1,0:T(8,128)(2,1)S(1)}, f32[384,1024]{1,0:T(8,128)S(1)}) custom-call(s32[1]{0:T(128)} %bitcast.where_ref, f32[1]{0:T(128)S(6)} %copy.9.scale_ref, f32[1]{0:T(128)S(6)} %copy.10.shift_ref, bf16[768,1024]{1,0:T(8,128)(2,1)S(1)} %get-tuple-element.33.texts_ref.refs_0_, bf16[784,1024]{1,0:T(8,128)(2,1)S(1)} %collective-permute-done.9.images_ref.refs_3_), custom_call_target="tpu_custom_call" | custom-call | flops 2415919104 | bytes 8388608 | tf_op jit(solution)/shard_map/pallas_call | solution.py:399
  41.0 1.4 %shard_map.83 = (f32[96,1024]{1,0:T(8,128)S(1)}, f32[96,1024]{1,0:T(8,128)S(1)}, f32[192,1024]{1,0:T(8,128)S(1)}) custom-call(bf16[768,768]{1,0:T(8,128)(2,1)S(1)} %get-tuple-element.34.refs_1_.refs_0_, bf16[784,1024]{1,0:T(8,128)(2,1)S(1)} %shard_map.75.images_ref.refs_1_, bf16[768,768]{1,0:T(8,128)(2,1)S(1)} %get-tuple-element.35.refs_1_.refs_2_, ...), custom_call_target="tpu_custom_call" | custom-call | flops 1207959552 | bytes 6291456 | tf_op jit(solution)/shard_map/pallas_call | solution.py:405
  44.7 1.4 %shard_map.82 = (f32[192,1024]{1,0:T(8,128)S(1)}, f32[192,1024]{1,0:T(8,128)S(1)}) custom-call(bf16[768,768]{1,0:T(8,128)(2,1)S(1)} %get-tuple-element.34.refs_1_.refs_0_, bf16[784,1024]{1,0:T(8,128)(2,1)S(1)} %shard_map.75.images_ref.refs_1_, bf16[768,768]{1,0:T(8,128)(2,1)S(1)} %get-tuple-element.35.refs_1_.refs_2_, ...), custom_call_target="tpu_custom_call" | custom-call | flops 9663676416 | bytes 6291456 | tf_op jit(solution)/shard_map/pallas_call | solution.py:409
  46.1 2.7 %collective-permute-start.18 = (f32[192,1024]{1,0:T(8,128)S(1)}, f32[192,1024]{1,0:T(8,128)S(1)}, u32[]{:S(2)}, u32[]{:S(2)}) collective-permute-start(f32[192,1024]{1,0:T(8,128)S(1)} %get-tuple-element.45), channel_id=1, source_target_pairs={{0,3},{1,0},{2,1},{3,2},{4,7},{5,4},{6,5},{7,6},{8,11},{9,8},{10,9... | collective-permute-start | bytes 2359304 | tf_op jit(solution)/shard_map/ppermute | solution.py:32
  49.5 1.7 %collective-permute-start.12 = (f32[192,1024]{1,0:T(8,128)S(1)}, f32[192,1024]{1,0:T(8,128)S(1)}, u32[]{:S(2)}, u32[]{:S(2)}) collective-permute-start(f32[192,1024]{1,0:T(8,128)S(1)} %get-tuple-element.38), channel_id=1, source_target_pairs={{0,8},{8,16},{16,24},{24,0},{1,9},{9,17},{17,25},{25,1},{2,10},{10... | collective-permute-start | bytes 2359304 | tf_op jit(solution)/shard_map/ppermute | solution.py:32
  52.1 2.2 %collective-permute-start.13 = (f32[192,1024]{1,0:T(8,128)S(1)}, f32[192,1024]{1,0:T(8,128)S(1)}, u32[]{:S(2)}, u32[]{:S(2)}) collective-permute-start(f32[192,1024]{1,0:T(8,128)S(1)} %get-tuple-element.39), channel_id=1, source_target_pairs={{0,24},{8,0},{16,8},{24,16},{1,25},{9,1},{17,9},{25,17},{2,26},{10... | collective-permute-start | bytes 2359304 | tf_op jit(solution)/shard_map/ppermute | solution.py:32
  54.9 7.4 %collective-permute-done.17.refs_8_ = f32[192,1024]{1,0:T(8,128)S(1)} collective-permute-done((f32[192,1024]{1,0:T(8,128)S(1)}, f32[192,1024]{1,0:T(8,128)S(1)}, u32[]{:S(2)}, u32[]{:S(2)}) %collective-permute-start.17) | collective-permute-done | bytes 786464 | tf_op jit(solution)/shard_map/ppermute | solution.py:32
  62.4 2.3 %collective-permute-done.18.early_ref.refs_9_ = f32[192,1024]{1,0:T(8,128)S(1)} collective-permute-done((f32[192,1024]{1,0:T(8,128)S(1)}, f32[192,1024]{1,0:T(8,128)S(1)}, u32[]{:S(2)}, u32[]{:S(2)}) %collective-permute-start.18) | collective-permute-done | bytes 786464 | tf_op jit(solution)/shard_map/ppermute | solution.py:32
  66.0 2.7 %collective-permute-start.20 = (f32[96,1024]{1,0:T(8,128)S(1)}, f32[96,1024]{1,0:T(8,128)S(1)}, u32[]{:S(2)}, u32[]{:S(2)}) collective-permute-start(f32[96,1024]{1,0:T(8,128)S(1)} %shard_map.85), channel_id=1, source_target_pairs={{0,2},{1,3},{2,0},{3,1},{4,6},{5,7},{6,4},{7,5},{8,10},{9,11},{10,... | collective-permute-start | bytes 1179656 | tf_op jit(solution)/shard_map/ppermute | solution.py:32
  70.3 3.0 %collective-permute-start.15 = (f32[96,1024]{1,0:T(8,128)S(1)}, f32[96,1024]{1,0:T(8,128)S(1)}, u32[]{:S(2)}, u32[]{:S(2)}) collective-permute-start(f32[96,1024]{1,0:T(8,128)S(1)} %shard_map.81), channel_id=1, source_target_pairs={{0,16},{8,24},{16,0},{24,8},{1,17},{9,25},{17,1},{25,9},{2,18},{10... | collective-permute-start | bytes 1179656 | tf_op jit(solution)/shard_map/ppermute | solution.py:32
  73.3 1.5 %collective-permute-done.21.refs_11_ = f32[96,1024]{1,0:T(8,128)S(1)} collective-permute-done((f32[96,1024]{1,0:T(8,128)S(1)}, f32[96,1024]{1,0:T(8,128)S(1)}, u32[]{:S(2)}, u32[]{:S(2)}) %collective-permute-start.21) | collective-permute-done | bytes 393248 | tf_op jit(solution)/shard_map/ppermute | solution.py:412
  76.1 2.5 %collective-permute-done.16.refs_4_ = f32[96,1024]{1,0:T(8,128)S(1)} collective-permute-done((f32[96,1024]{1,0:T(8,128)S(1)}, f32[96,1024]{1,0:T(8,128)S(1)}, u32[]{:S(2)}, u32[]{:S(2)}) %collective-permute-start.16) | collective-permute-done | bytes 393248 | tf_op jit(solution)/shard_map/ppermute | solution.py:415
  78.6 1.7 %collective-permute-done.15.refs_3_ = f32[96,1024]{1,0:T(8,128)S(1)} collective-permute-done((f32[96,1024]{1,0:T(8,128)S(1)}, f32[96,1024]{1,0:T(8,128)S(1)}, u32[]{:S(2)}, u32[]{:S(2)}) %collective-permute-start.15) | collective-permute-done | bytes 393248 | tf_op jit(solution)/shard_map/ppermute | solution.py:32
  80.7 3.2 %collective-permute-start.22 = (bf16[192,256]{1,0:T(8,128)(2,1)S(1)}, bf16[192,256]{1,0:T(8,128)(2,1)S(1)}, u32[]{:S(2)}, u32[]{:S(2)}) collective-permute-start(bf16[192,256]{1,0:T(8,128)(2,1)S(1)} %get-tuple-element.50), channel_id=1, source_target_pairs={{0,32},{32,0},{1,33},{33,1},{2,34},{34,2},{3,35},{35,3},{4,36},{36... | collective-permute-start | bytes 294920 | tf_op jit(solution)/shard_map/ppermute | solution.py:426
  83.9 1.5 %collective-permute-start.23 = (bf16[192,256]{1,0:T(8,128)(2,1)S(1)}, bf16[192,256]{1,0:T(8,128)(2,1)S(1)}, u32[]{:S(2)}, u32[]{:S(2)}) collective-permute-start(bf16[192,256]{1,0:T(8,128)(2,1)S(1)} %get-tuple-element.51), channel_id=1, source_target_pairs={{0,64},{64,0},{1,65},{65,1},{2,66},{66,2},{3,67},{67,3},{4,68},{68... | collective-permute-start | bytes 294920 | tf_op jit(solution)/shard_map/ppermute | solution.py:427
  85.6 2.6 %collective-permute-done.23.xl = bf16[192,256]{1,0:T(8,128)(2,1)S(1)} collective-permute-done((bf16[192,256]{1,0:T(8,128)(2,1)S(1)}, bf16[192,256]{1,0:T(8,128)(2,1)S(1)}, u32[]{:S(2)}, u32[]{:S(2)}) %collective-permute-start.23) | collective-permute-done | bytes 98336 | tf_op jit(solution)/shard_map/ppermute | solution.py:427
  88.3 2.3 %collective-permute-done.24.both = bf16[192,256]{1,0:T(8,128)(2,1)S(1)} collective-permute-done((bf16[192,256]{1,0:T(8,128)(2,1)S(1)}, bf16[192,256]{1,0:T(8,128)(2,1)S(1)}, u32[]{:S(2)}, u32[]{:S(2)}) %collective-permute-start.24) | collective-permute-done | bytes 98336 | tf_op jit(solution)/shard_map/ppermute | solution.py:428
  90.5 1.4 %shard_map.87 = s16[128,24,256]{2,1,0:T(8,128)(2,1)S(1)} custom-call(bf16[1920,384]{1,0:T(8,128)(2,1)S(1)} %get-tuple-element.30.early_a.images_ref, bf16[1344,384]{1,0:T(8,128)(2,1)S(1)} %get-tuple-element.31.early_b.texts_ref, bf16[192,256]{1,0:T(8,128)(2,1)S(1)} %get-tuple-element.49.own, bf16[192,256]{1,0:T(8,128)(2,1)S(1)} %collective-permute-done.22.core, ...), custom_call_target="tpu_custom_call" | custom-call | flops 1207959552 | bytes 6291456 | tf_op jit(solution)/shard_map/pallas_call | solution.py:431
  92.0 31.3 %all_to_all.5.coded_ref = s16[128,24,256]{2,1,0:T(8,128)(2,1)S(1)} all-to-all(s16[128,24,256]{2,1,0:T(8,128)(2,1)S(1)} %shard_map.87), channel_id=1, replica_groups=mesh['xl'=2,'core'=2,'z'=4,'xh'=2,'y'=4] {'xl','core','z','xh','y'}, dimensions={0} | all-to-all | bytes 3145728 | tf_op jit(solution)/shard_map/all_to_all | solution.py:437
  (55 shorter events, 14.8 us)
Async XLA Ops:
  4.9 23.4 %copy-start.1 = (bf16[384,1664]{1,0:T(8,128)(2,1)S(1)}, bf16[384,1664]{1,0:T(8,128)(2,1)}, u32[]{:S(2)}) copy-start(bf16[384,1664]{1,0:T(8,128)(2,1)} %image_feats.3) | copy-start | bytes 3833860
  4.9 23.4 %copy-start.3 = (bf16[384,1024]{1,0:T(8,128)(2,1)S(1)}, bf16[384,1024]{1,0:T(8,128)(2,1)}, u32[]{:S(2)}) copy-start(bf16[384,1024]{1,0:T(8,128)(2,1)} %text_feats.3) | copy-start | bytes 2359300
  4.9 8.1 %collective-permute-start.1 = (bf16[96,1024]{1,0:T(8,128)(2,1)}, bf16[96,1024]{1,0:T(8,128)(2,1)S(1)}, u32[]{:S(2)}, u32[]{:S(2)}) collective-permute-start(bf16[96,1024]{1,0:T(8,128)(2,1)} %get-tuple-element.32.refs_12_), channel_id=1, source_target_pairs={{0,68},{4,64},{64,4},{68,0},{1,69},{5,65},{65,5},{69,1},{2,70},{6,... | collective-permute-start | bytes 589832 | tf_op jit(solution)/shard_map/ppermute | solution.py:363
  8.3 15.7 %collective-permute-start = (bf16[208,1024]{1,0:T(8,128)(2,1)}, bf16[208,1024]{1,0:T(8,128)(2,1)S(1)}, u32[]{:S(2)}, u32[]{:S(2)}) collective-permute-start(bf16[208,1024]{1,0:T(8,128)(2,1)} %get-tuple-element.29.me.refs_5_), channel_id=1, source_target_pairs={{0,8},{8,16},{16,24},{24,0},{1,9},{9,17},{17,25},{25,1},{2,10},{10... | collective-permute-start | bytes 1277960 | tf_op jit(solution)/shard_map/ppermute | solution.py:32
  9.9 10.7 %collective-permute-start.6 = (bf16[208,1024]{1,0:T(8,128)(2,1)}, bf16[208,1024]{1,0:T(8,128)(2,1)S(1)}, u32[]{:S(2)}, u32[]{:S(2)}) collective-permute-start(bf16[208,1024]{1,0:T(8,128)(2,1)} %get-tuple-element.29.me.refs_5_), channel_id=1, source_target_pairs={{0,24},{8,0},{16,8},{24,16},{1,25},{9,1},{17,9},{25,17},{2,26},{10... | collective-permute-start | bytes 1277960 | tf_op jit(solution)/shard_map/ppermute | solution.py:32
  13.1 11.0 %collective-permute-start.3 = (bf16[192,1024]{1,0:T(8,128)(2,1)S(1)}, bf16[192,1024]{1,0:T(8,128)(2,1)S(1)}, u32[]{:S(2)}, u32[]{:S(2)}) collective-permute-start(bf16[192,1024]{1,0:T(8,128)(2,1)S(1)} %constant_dynamic-update-slice_fusion.me), channel_id=1, source_target_pairs={{0,1},{1,2},{2,3},{3,0},{4,5},{5,6},{6,7},{7,4},{8,9},{9,10},{10,1... | collective-permute-start | bytes 1179656 | tf_op jit(solution)/shard_map/ppermute | solution.py:32
  14.4 11.0 %collective-permute-start.2 = (bf16[192,1024]{1,0:T(8,128)(2,1)S(1)}, bf16[192,1024]{1,0:T(8,128)(2,1)S(1)}, u32[]{:S(2)}, u32[]{:S(2)}) collective-permute-start(bf16[192,1024]{1,0:T(8,128)(2,1)S(1)} %constant_dynamic-update-slice_fusion.me), channel_id=1, source_target_pairs={{0,3},{1,0},{2,1},{3,2},{4,7},{5,4},{6,5},{7,6},{8,11},{9,8},{10,9... | collective-permute-start | bytes 1179656 | tf_op jit(solution)/shard_map/ppermute | solution.py:32
  20.7 9.8 %collective-permute-start.8 = (bf16[112,1024]{1,0:T(8,128)(2,1)S(1)}, bf16[112,1024]{1,0:T(8,128)(2,1)S(1)}, u32[]{:S(2)}, u32[]{:S(2)}) collective-permute-start(bf16[112,1024]{1,0:T(8,128)(2,1)S(1)} %slice.43), channel_id=1, source_target_pairs={{0,24},{8,0},{16,8},{24,16},{1,25},{9,1},{17,9},{25,17},{2,26},{10... | collective-permute-start | bytes 688136 | tf_op jit(solution)/shard_map/ppermute | solution.py:32
  24.0 6.5 %collective-permute-start.7 = (bf16[96,1024]{1,0:T(8,128)(2,1)S(1)}, bf16[96,1024]{1,0:T(8,128)(2,1)S(1)}, u32[]{:S(2)}, u32[]{:S(2)}) collective-permute-start(bf16[96,1024]{1,0:T(8,128)(2,1)S(1)} %slice.42), channel_id=1, source_target_pairs={{0,8},{8,16},{16,24},{24,0},{1,9},{9,17},{17,25},{25,1},{2,10},{10... | collective-permute-start | bytes 589832 | tf_op jit(solution)/shard_map/ppermute | solution.py:32
  24.1 9.3 %collective-permute-start.4 = (bf16[96,1024]{1,0:T(8,128)(2,1)S(1)}, bf16[96,1024]{1,0:T(8,128)(2,1)S(1)}, u32[]{:S(2)}, u32[]{:S(2)}) collective-permute-start(bf16[96,1024]{1,0:T(8,128)(2,1)S(1)} %slice.40), channel_id=1, source_target_pairs={{0,1},{1,2},{2,3},{3,0},{4,5},{5,6},{6,7},{7,4},{8,9},{9,10},{10,1... | collective-permute-start | bytes 589832 | tf_op jit(solution)/shard_map/ppermute | solution.py:32
  25.5 7.9 %collective-permute-start.5 = (bf16[96,1024]{1,0:T(8,128)(2,1)S(1)}, bf16[96,1024]{1,0:T(8,128)(2,1)S(1)}, u32[]{:S(2)}, u32[]{:S(2)}) collective-permute-start(bf16[96,1024]{1,0:T(8,128)(2,1)S(1)} %slice.41), channel_id=1, source_target_pairs={{0,3},{1,0},{2,1},{3,2},{4,7},{5,4},{6,5},{7,6},{8,11},{9,8},{10,9... | collective-permute-start | bytes 589832 | tf_op jit(solution)/shard_map/ppermute | solution.py:32
  28.3 2.2 %copy-start = (bf16[208,1024]{1,0:T(8,128)(2,1)S(1)}, bf16[208,1024]{1,0:T(8,128)(2,1)}, u32[]{:S(2)}) copy-start(bf16[208,1024]{1,0:T(8,128)(2,1)} %get-tuple-element.29.me.refs_5_) | copy-start | bytes 1277956
  30.7 5.8 %collective-permute-start.9 = (bf16[784,1024]{1,0:T(8,128)(2,1)S(1)}, bf16[784,1024]{1,0:T(8,128)(2,1)S(1)}, u32[]{:S(2)}, u32[]{:S(2)}) collective-permute-start(bf16[784,1024]{1,0:T(8,128)(2,1)S(1)} %shard_map.75.images_ref.refs_1_), channel_id=1, source_target_pairs={{0,32},{32,0},{1,33},{33,1},{2,34},{34,2},{3,35},{35,3},{4,36},{36... | collective-permute-start | bytes 4816904 | tf_op jit(solution)/shard_map/ppermute | solution.py:370
  39.3 9.4 %collective-permute-start.11 = (f32[384,1024]{1,0:T(8,128)S(1)}, f32[384,1024]{1,0:T(8,128)S(1)}, u32[]{:S(2)}, u32[]{:S(2)}) collective-permute-start(f32[384,1024]{1,0:T(8,128)S(1)} %get-tuple-element.37), channel_id=1, source_target_pairs={{0,32},{32,0},{1,33},{33,1},{2,34},{34,2},{3,35},{35,3},{4,36},{36... | collective-permute-start | bytes 4718600 | tf_op jit(solution)/shard_map/ppermute | solution.py:403
  40.7 10.5 %collective-permute-start.10 = (f32[384,1024]{1,0:T(8,128)S(1)}, f32[384,1024]{1,0:T(8,128)S(1)}, u32[]{:S(2)}, u32[]{:S(2)}) collective-permute-start(f32[384,1024]{1,0:T(8,128)S(1)} %shard_map.78), channel_id=1, source_target_pairs={{0,32},{32,0},{1,33},{33,1},{2,34},{34,2},{3,35},{35,3},{4,36},{36... | collective-permute-start | bytes 4718600 | tf_op jit(solution)/shard_map/ppermute | solution.py:407
  42.3 20.0 %collective-permute-start.17 = (f32[192,1024]{1,0:T(8,128)S(1)}, f32[192,1024]{1,0:T(8,128)S(1)}, u32[]{:S(2)}, u32[]{:S(2)}) collective-permute-start(f32[192,1024]{1,0:T(8,128)S(1)} %get-tuple-element.44), channel_id=1, source_target_pairs={{0,1},{1,2},{2,3},{3,0},{4,5},{5,6},{6,7},{7,4},{8,9},{9,10},{10,1... | collective-permute-start | bytes 2359304 | tf_op jit(solution)/shard_map/ppermute | solution.py:32
  43.6 11.2 %collective-permute-start.19 = (f32[96,1024]{1,0:T(8,128)S(1)}, f32[96,1024]{1,0:T(8,128)S(1)}, u32[]{:S(2)}, u32[]{:S(2)}) collective-permute-start(f32[96,1024]{1,0:T(8,128)S(1)} %get-tuple-element.47), channel_id=1, source_target_pairs={{0,68},{4,64},{64,4},{68,0},{1,69},{5,65},{65,5},{69,1},{2,70},{6,... | collective-permute-start | bytes 1179656 | tf_op jit(solution)/shard_map/ppermute | solution.py:412
  46.1 18.6 %collective-permute-start.18 = (f32[192,1024]{1,0:T(8,128)S(1)}, f32[192,1024]{1,0:T(8,128)S(1)}, u32[]{:S(2)}, u32[]{:S(2)}) collective-permute-start(f32[192,1024]{1,0:T(8,128)S(1)} %get-tuple-element.45), channel_id=1, source_target_pairs={{0,3},{1,0},{2,1},{3,2},{4,7},{5,4},{6,5},{7,6},{8,11},{9,8},{10,9... | collective-permute-start | bytes 2359304 | tf_op jit(solution)/shard_map/ppermute | solution.py:32
  49.5 20.5 %collective-permute-start.12 = (f32[192,1024]{1,0:T(8,128)S(1)}, f32[192,1024]{1,0:T(8,128)S(1)}, u32[]{:S(2)}, u32[]{:S(2)}) collective-permute-start(f32[192,1024]{1,0:T(8,128)S(1)} %get-tuple-element.38), channel_id=1, source_target_pairs={{0,8},{8,16},{16,24},{24,0},{1,9},{9,17},{17,25},{25,1},{2,10},{10... | collective-permute-start | bytes 2359304 | tf_op jit(solution)/shard_map/ppermute | solution.py:32
  52.1 18.0 %collective-permute-start.13 = (f32[192,1024]{1,0:T(8,128)S(1)}, f32[192,1024]{1,0:T(8,128)S(1)}, u32[]{:S(2)}, u32[]{:S(2)}) collective-permute-start(f32[192,1024]{1,0:T(8,128)S(1)} %get-tuple-element.39), channel_id=1, source_target_pairs={{0,24},{8,0},{16,8},{24,16},{1,25},{9,1},{17,9},{25,17},{2,26},{10... | collective-permute-start | bytes 2359304 | tf_op jit(solution)/shard_map/ppermute | solution.py:32
  54.8 15.4 %collective-permute-start.14 = (f32[96,1024]{1,0:T(8,128)S(1)}, f32[96,1024]{1,0:T(8,128)S(1)}, u32[]{:S(2)}, u32[]{:S(2)}) collective-permute-start(f32[96,1024]{1,0:T(8,128)S(1)} %get-tuple-element.41), channel_id=1, source_target_pairs={{0,64},{64,0},{1,65},{65,1},{2,66},{66,2},{3,67},{67,3},{4,68},{68... | collective-permute-start | bytes 1179656 | tf_op jit(solution)/shard_map/ppermute | solution.py:415
  64.7 10.1 %collective-permute-start.21 = (f32[96,1024]{1,0:T(8,128)S(1)}, f32[96,1024]{1,0:T(8,128)S(1)}, u32[]{:S(2)}, u32[]{:S(2)}) collective-permute-start(f32[96,1024]{1,0:T(8,128)S(1)} %slice_add_fusion), channel_id=1, source_target_pairs={{0,68},{4,64},{64,4},{68,0},{1,69},{5,65},{65,5},{69,1},{2,70},{6,... | collective-permute-start | bytes 1179656 | tf_op jit(solution)/shard_map/ppermute | solution.py:412
  66.0 10.1 %collective-permute-start.20 = (f32[96,1024]{1,0:T(8,128)S(1)}, f32[96,1024]{1,0:T(8,128)S(1)}, u32[]{:S(2)}, u32[]{:S(2)}) collective-permute-start(f32[96,1024]{1,0:T(8,128)S(1)} %shard_map.85), channel_id=1, source_target_pairs={{0,2},{1,3},{2,0},{3,1},{4,6},{5,7},{6,4},{7,5},{8,10},{9,11},{10,... | collective-permute-start | bytes 1179656 | tf_op jit(solution)/shard_map/ppermute | solution.py:32
  70.0 10.2 %copy-start.2 = (bf16[96,1024]{1,0:T(8,128)(2,1)S(1)}, bf16[96,1024]{1,0:T(8,128)(2,1)}, u32[]{:S(2)}) copy-start(bf16[96,1024]{1,0:T(8,128)(2,1)} %get-tuple-element.32.refs_12_) | copy-start | bytes 589828
  70.0 10.2 %copy-start.4 = (f32[96,128]{1,0:T(8,128)S(1)}, f32[96,128]{1,0:T(8,128)}, u32[]{:S(2)}) copy-start(f32[96,128]{1,0:T(8,128)} %get-tuple-element.48.refs_13_) | copy-start | bytes 147460
  70.0 10.2 %copy-start.5 = (f32[96,128]{1,0:T(8,128)S(1)}, f32[96,128]{1,0:T(8,128)}, u32[]{:S(2)}) copy-start(f32[96,128]{1,0:T(8,128)} %get-tuple-element.42.refs_6_) | copy-start | bytes 147460
  70.1 8.4 %collective-permute-start.16 = (f32[96,1024]{1,0:T(8,128)S(1)}, f32[96,1024]{1,0:T(8,128)S(1)}, u32[]{:S(2)}, u32[]{:S(2)}) collective-permute-start(f32[96,1024]{1,0:T(8,128)S(1)} %slice_add_fusion.2), channel_id=1, source_target_pairs={{0,64},{64,0},{1,65},{65,1},{2,66},{66,2},{3,67},{67,3},{4,68},{68... | collective-permute-start | bytes 1179656 | tf_op jit(solution)/shard_map/ppermute | solution.py:415
  70.3 9.9 %collective-permute-start.15 = (f32[96,1024]{1,0:T(8,128)S(1)}, f32[96,1024]{1,0:T(8,128)S(1)}, u32[]{:S(2)}, u32[]{:S(2)}) collective-permute-start(f32[96,1024]{1,0:T(8,128)S(1)} %shard_map.81), channel_id=1, source_target_pairs={{0,16},{8,24},{16,0},{24,8},{1,17},{9,25},{17,1},{25,9},{2,18},{10... | collective-permute-start | bytes 1179656 | tf_op jit(solution)/shard_map/ppermute | solution.py:32
  80.7 5.0 %collective-permute-start.22 = (bf16[192,256]{1,0:T(8,128)(2,1)S(1)}, bf16[192,256]{1,0:T(8,128)(2,1)S(1)}, u32[]{:S(2)}, u32[]{:S(2)}) collective-permute-start(bf16[192,256]{1,0:T(8,128)(2,1)S(1)} %get-tuple-element.50), channel_id=1, source_target_pairs={{0,32},{32,0},{1,33},{33,1},{2,34},{34,2},{3,35},{35,3},{4,36},{36... | collective-permute-start | bytes 294920 | tf_op jit(solution)/shard_map/ppermute | solution.py:426
  83.9 4.4 %collective-permute-start.23 = (bf16[192,256]{1,0:T(8,128)(2,1)S(1)}, bf16[192,256]{1,0:T(8,128)(2,1)S(1)}, u32[]{:S(2)}, u32[]{:S(2)}) collective-permute-start(bf16[192,256]{1,0:T(8,128)(2,1)S(1)} %get-tuple-element.51), channel_id=1, source_target_pairs={{0,64},{64,0},{1,65},{65,1},{2,66},{66,2},{3,67},{67,3},{4,68},{68... | collective-permute-start | bytes 294920 | tf_op jit(solution)/shard_map/ppermute | solution.py:427
  85.4 5.2 %collective-permute-start.24 = (bf16[192,256]{1,0:T(8,128)(2,1)S(1)}, bf16[192,256]{1,0:T(8,128)(2,1)S(1)}, u32[]{:S(2)}, u32[]{:S(2)}) collective-permute-start(bf16[192,256]{1,0:T(8,128)(2,1)S(1)} %get-tuple-element.52), channel_id=1, source_target_pairs={{0,96},{32,64},{64,32},{96,0},{1,97},{33,65},{65,33},{97,1},{2,98}... | collective-permute-start | bytes 294920 | tf_op jit(solution)/shard_map/ppermute | solution.py:428

commit v6 on v5

--- a/solution.py
+++ b/solution.py
@@ -144,13 +144,13 @@
     out_ref[...] = far_ref[...]
 
 
-def ring_scatter(far_low, far_high, after, before, mine, axis, crossed):
+def ring_scatter(far_low, far_high, after, before, mine, axis, crossed, marker=None):
     far = crossed(far_high)
     got_right, got_left = shifted(after, axis, 1), shifted(before, axis, -1)
     if axis == "z":
         far = call(
             far_kernel, shape(QUARTER, E), 0, 1 << 20, in_specs=[VMEM, VMEM, ANY], out_specs=VMEM
-        )(far_low, far, got_left)
+        )(far_low, far, marker)
     else:
         far = call(
             add_kernel, shape(QUARTER, E), 4 << 30, 1 << 20, in_specs=[VMEM] * 2, out_specs=VMEM
@@ -248,19 +248,16 @@
     share_out(image_terms(coef_ref, texts_ref, part) + taken_ref[...], outs)
 
 
-def back_kernel(where_ref, *refs):
-    *inputs, own_ref, core_ref, xl_ref, both_ref, held_ref = refs
-    for tower in range(2):
-        mine, right, left, far, got, emb, inverse = inputs[tower * 7 : tower * 7 + 7]
-        gradients = mine[:QUARTER, :] + right[:QUARTER, :] + left[:QUARTER, :]
-        gradients += far[...] + got[...]
-        widened = emb[:QUARTER, :].astype(F32)
-        inner_sum = jnp.sum(widened * gradients, axis=1, keepdims=True)
-        value = (inverse[:, :1] * (gradients - widened * inner_sum)).astype(BF16)
-        for i in range(4):
-            held_ref[i, tower * QUARTER : (tower + 1) * QUARTER, :] = value[
-                :, i * SLICE : (i + 1) * SLICE
-            ]
+def back_kernel(
+    where_ref, mine, right, left, far, got, emb, inverse, own_ref, core_ref, xl_ref, both_ref, held_ref
+):
+    gradients = mine[:QUARTER, :] + right[:QUARTER, :] + left[:QUARTER, :]
+    gradients += far[...] + got[...]
+    widened = emb[:QUARTER, :].astype(F32)
+    inner_sum = jnp.sum(widened * gradients, axis=1, keepdims=True)
+    value = (inverse[:, :1] * (gradients - widened * inner_sum)).astype(BF16)
+    for i in range(4):
+        held_ref[i] = value[:, i * SLICE : (i + 1) * SLICE]
     xl, core, _, _, _, _ = position(where_ref)
     own_ref[...] = held_ref[xl * 2 + core]
     core_ref[...] = held_ref[xl * 2 + 1 - core]
@@ -268,12 +265,10 @@
     both_ref[...] = held_ref[3 - xl * 2 - core]
 
 
-def terms_kernel(images_ref, texts_ref, own, core, xl, both, out_ref, both_ref):
-    for i, ref in enumerate((own, core, xl, both)):
-        for part in range(2):
-            both_ref[part, i * QUARTER : (i + 1) * QUARTER, :] = ref[
-                part * QUARTER : (part + 1) * QUARTER, :
-            ]
+def terms_kernel(images_ref, texts_ref, *refs):
+    *backs, out_ref, both_ref = refs
+    for i, ref in enumerate(backs):
+        both_ref[i // 4, i % 4 * QUARTER : (i % 4 + 1) * QUARTER, :] = ref[...]
     rows = STEP * GROUP
     steps = 128 // STEP
     last = images_ref.shape[0] // rows - 1
@@ -407,33 +402,36 @@
     taken_rest = lax.ppermute(given_rest, "core", SWAP)
     image_ways = run(kept_kernel, ways, 0.5, 3, 0)(texts, own_coef, taken)
     text_rest = run(text_kernel, rest, 8, 4, 1)(*sides)
-    image_rest = run(kept_kernel, rest, 0.5, 3, 1)(texts, own_coef, taken_rest)
+    image_rest = run(kept_kernel, rest, 4, 3, 1)(texts, own_coef, taken_rest)
     text_sums = ring_scatter(
         *text_ways, *text_rest, "y", lambda a: lax.ppermute(a, ("xl", "xh"), FLIP)
     )
     image_sums = ring_scatter(
-        *image_ways, *image_rest, "z", lambda a: lax.ppermute(a, "xl", SWAP)
-    )
-
-    piece = shape(HALF, SLICE, dtype=BF16)
-    own, other_core, other_xl, other_both = call(
-        back_kernel, [piece] * 4, 0, 6 << 20,
-        in_specs=[SMEM] + [VMEM] * 14, out_specs=[VMEM] * 4,
-        scratch_shapes=[pltpu.VMEM((4, HALF, SLICE), BF16)],
-    )(where, *image_sums, load, image_inverse, *text_sums, own_texts, text_inverse)
-    backs = (
-        own,
-        lax.ppermute(other_core, "core", SWAP),
-        lax.ppermute(other_xl, "xl", SWAP),
-        lax.ppermute(other_both, TOWER, [(i, 3 - i) for i in range(4)]),
-    )
+        *image_ways, *image_rest, "z", lambda a: lax.ppermute(a, "xl", SWAP), text_sums[1],
+    )
+
+    def tower_pieces(*inputs):
+        own, other_core, other_xl, other_both = call(
+            back_kernel, [shape(QUARTER, SLICE, dtype=BF16)] * 4, 0, 3 << 20,
+            in_specs=[SMEM] + [VMEM] * 7, out_specs=[VMEM] * 4,
+            scratch_shapes=[pltpu.VMEM((4, QUARTER, SLICE), BF16)],
+        )(where, *inputs)
+        return (
+            own,
+            lax.ppermute(other_core, "core", SWAP),
+            lax.ppermute(other_xl, "xl", SWAP),
+            lax.ppermute(other_both, TOWER, [(i, 3 - i) for i in range(4)]),
+        )
+
+    text_backs = tower_pieces(*text_sums, own_texts, text_inverse)
+    image_backs = tower_pieces(*image_sums, load, image_inverse)
 
     coded = call(
         terms_kernel, shape(128, GROUP, SLICE, dtype=jnp.int16),
         4 * 128 * GROUP * ROWS * SLICE, 6 << 20, 24,
-        in_specs=[VMEM] * 6, out_specs=VMEM,
+        in_specs=[VMEM] * 10, out_specs=VMEM,
         scratch_shapes=[pltpu.VMEM((2, ROWS, SLICE), BF16)],
-    )(image_groups, text_groups, *backs)
+    )(image_groups, text_groups, *image_backs, *text_backs)
     coded = lax.all_to_all(coded, AXES, split_axis=0, concat_axis=0, tiled=True)
     return call(total_kernel, shape(OWN, E), 0, 2 << 20, in_specs=[VMEM], out_specs=VMEM)(coded)
 

time: 125 us -> 120 us (0.960)
  starting transfers between devices: 40.9 us -> 39 us
  waiting for transfers between devices: 29.2 us -> 27.8 us
    ppermute x2, waiting for transfers between devices: 2.03 us -> 10.3 us  [body(): lax.ppermute(a, ('xl', 'xh'), FLIP)]
    ppermute x14, waiting for transfers between devices: 18.7 us -> 13.7 us  [shifted(): return lax.ppermute(array, axis, [(i, (i + by) % 4) for i in range(4)])]
    ppermute x14, starting transfers between devices: 26.4 us -> 23.3 us  [shifted(): return lax.ppermute(array, axis, [(i, (i + by) % 4) for i in range(4)])]
    ppermute x2, waiting for transfers between devices: 2.48 us -> 0.01 us  [body(): lax.ppermute(a, 'xl', SWAP)]
    ppermute x3 -> x6, waiting for transfers between devices: 4.92 us -> 2.71 us  [the longest x2 1.86 us: tower_pieces(): lax.ppermute(other_both, TOWER, [(i, 3 - i) for i in range(4)])]
    ppermute x3 -> x6, starting transfers between devices: 4.97 us -> 6.9 us  [the longest x2 3.51 us: tower_pieces(): lax.ppermute(other_both, TOWER, [(i, 3 - i) for i in range(4)])]
  transfers between devices with their start and end apart: 25 -> 28, of which waited for: 12 -> 10; matrix products, arithmetic and copies ran while one was open for 1% -> 1% of each run, Pallas kernels for 8% -> 8%
where the time goes in v6:
time: 120 us
  starting transfers between devices  39 us (32%)
  blocking collectives  30.2 us (25%)
  waiting for transfers between devices  27.8 us (23%)
  Pallas kernels  20.5 us (17%)
  between operations  1.61 us (1%)
    all_to_all x1, blocking collectives, body(): coded = lax.all_to_all(coded, AXES, split_axis=0, concat_axis=0, tiled=True)  30.2 us
    ppermute x14, starting transfers between devices, shifted(): return lax.ppermute(array, axis, [(i, (i + by) % 4) for i in range(4)])  23.3 us
    ppermute x14, waiting for transfers between devices, shifted(): return lax.ppermute(array, axis, [(i, (i + by) % 4) for i in range(4)])  13.7 us
    ppermute x2, waiting for transfers between devices, body(): lax.ppermute(a, ('xl', 'xh'), FLIP)  10.3 us
    pallas_call x1, Pallas kernels, body(): call(embed_kernel, [shape(QUARTER, E, dtype=BF16), shape(QUARTER, 128), s...  4.88 us
    ppermute x2, starting transfers between devices, tower_pieces(): lax.ppermute(other_both, TOWER, [(i, 3 - i) for i in range(4)])  3.51 us
    ppermute x1, starting transfers between devices, body(): other_texts = lax.ppermute(own_texts, ('xl', 'xh'), FLIP)  3.39 us
    ppermute x2, starting transfers between devices, tower_pieces(): lax.ppermute(other_core, 'core', SWAP)  3.38 us
  transfers between devices with their start and end apart: 28, of which 10 were waited for; matrix products, arithmetic and copies ran while one was open for 1% of the time, Pallas kernels for 8%

profile of v6, /device:TPU:1, one launch (start us, length us, event | category | flops | bytes accessed | tf_op | source)
XLA Modules:
  0.0 120.3 jit_solution(2904584607202606032)
XLA Ops:
  0.0 4.9 %shard_map.73 = (bf16[96,1024]{1,0:T(8,128)(2,1)}, f32[96,128]{1,0:T(8,128)}, bf16[208,1024]{1,0:T(8,128)(2,1)}, f32[96,128]{1,0:T(8,128)}) custom-call(s32[1]{0:T(128)} %bitcast.where_ref, s32[3,128]{1,0:T(4,128)} %bitcast.2, bf16[384,1024]{1,0:T(8,128)(2,1)} %text_feats.3, bf16[384,1664]{1,0:T(8,128)(2,1)} %image_feats.3, bf16[1024,1024]{1,0:T(8,128)(2,1)} %text_weight.1, ...), custom_call_target="tpu_custom_call" | custom-call | flops 855638016 | bytes 8388608 | tf_op jit(solution)/shard_map/pallas_call | solution.py:343
  4.9 3.4 %collective-permute-start.1 = (bf16[96,1024]{1,0:T(8,128)(2,1)}, bf16[96,1024]{1,0:T(8,128)(2,1)S(1)}, u32[]{:S(2)}, u32[]{:S(2)}) collective-permute-start(bf16[96,1024]{1,0:T(8,128)(2,1)} %get-tuple-element.36.emb), channel_id=1, source_target_pairs={{0,68},{4,64},{64,4},{68,0},{1,69},{5,65},{65,5},{69,1},{2,70},{6,... | collective-permute-start | bytes 589832 | tf_op jit(solution)/shard_map/ppermute | solution.py:358
  8.3 1.6 %collective-permute-start = (bf16[208,1024]{1,0:T(8,128)(2,1)}, bf16[208,1024]{1,0:T(8,128)(2,1)S(1)}, u32[]{:S(2)}, u32[]{:S(2)}) collective-permute-start(bf16[208,1024]{1,0:T(8,128)(2,1)} %get-tuple-element.33.me.emb), channel_id=1, source_target_pairs={{0,8},{8,16},{16,24},{24,0},{1,9},{9,17},{17,25},{25,1},{2,10},{10... | collective-permute-start | bytes 1277960 | tf_op jit(solution)/shard_map/ppermute | solution.py:32
  9.9 2.1 %collective-permute-start.6 = (bf16[208,1024]{1,0:T(8,128)(2,1)}, bf16[208,1024]{1,0:T(8,128)(2,1)S(1)}, u32[]{:S(2)}, u32[]{:S(2)}) collective-permute-start(bf16[208,1024]{1,0:T(8,128)(2,1)} %get-tuple-element.33.me.emb), channel_id=1, source_target_pairs={{0,24},{8,0},{16,8},{24,16},{1,25},{9,1},{17,9},{25,17},{2,26},{10... | collective-permute-start | bytes 1277960 | tf_op jit(solution)/shard_map/ppermute | solution.py:32
  13.1 1.4 %collective-permute-start.3 = (bf16[192,1024]{1,0:T(8,128)(2,1)S(1)}, bf16[192,1024]{1,0:T(8,128)(2,1)S(1)}, u32[]{:S(2)}, u32[]{:S(2)}) collective-permute-start(bf16[192,1024]{1,0:T(8,128)(2,1)S(1)} %constant_dynamic-update-slice_fusion.me), channel_id=1, source_target_pairs={{0,1},{1,2},{2,3},{3,0},{4,5},{5,6},{6,7},{7,4},{8,9},{9,10},{10,1... | collective-permute-start | bytes 1179656 | tf_op jit(solution)/shard_map/ppermute | solution.py:32
  14.4 1.5 %collective-permute-start.2 = (bf16[192,1024]{1,0:T(8,128)(2,1)S(1)}, bf16[192,1024]{1,0:T(8,128)(2,1)S(1)}, u32[]{:S(2)}, u32[]{:S(2)}) collective-permute-start(bf16[192,1024]{1,0:T(8,128)(2,1)S(1)} %constant_dynamic-update-slice_fusion.me), channel_id=1, source_target_pairs={{0,3},{1,0},{2,1},{3,2},{4,7},{5,4},{6,5},{7,6},{8,11},{9,8},{10,9... | collective-permute-start | bytes 1179656 | tf_op jit(solution)/shard_map/ppermute | solution.py:32
  15.9 4.7 %collective-permute-done.6.after = bf16[208,1024]{1,0:T(8,128)(2,1)S(1)} collective-permute-done((bf16[208,1024]{1,0:T(8,128)(2,1)}, bf16[208,1024]{1,0:T(8,128)(2,1)S(1)}, u32[]{:S(2)}, u32[]{:S(2)}) %collective-permute-start.6) | collective-permute-done | bytes 426016 | tf_op jit(solution)/shard_map/ppermute | solution.py:32
  20.7 3.3 %collective-permute-start.8 = (bf16[112,1024]{1,0:T(8,128)(2,1)S(1)}, bf16[112,1024]{1,0:T(8,128)(2,1)S(1)}, u32[]{:S(2)}, u32[]{:S(2)}) collective-permute-start(bf16[112,1024]{1,0:T(8,128)(2,1)S(1)} %slice.43), channel_id=1, source_target_pairs={{0,24},{8,0},{16,8},{24,16},{1,25},{9,1},{17,9},{25,17},{2,26},{10... | collective-permute-start | bytes 688136 | tf_op jit(solution)/shard_map/ppermute | solution.py:32
  24.1 1.4 %collective-permute-start.4 = (bf16[96,1024]{1,0:T(8,128)(2,1)S(1)}, bf16[96,1024]{1,0:T(8,128)(2,1)S(1)}, u32[]{:S(2)}, u32[]{:S(2)}) collective-permute-start(bf16[96,1024]{1,0:T(8,128)(2,1)S(1)} %slice.40), channel_id=1, source_target_pairs={{0,1},{1,2},{2,3},{3,0},{4,5},{5,6},{6,7},{7,4},{8,9},{9,10},{10,1... | collective-permute-start | bytes 589832 | tf_op jit(solution)/shard_map/ppermute | solution.py:32
  25.5 1.5 %collective-permute-start.5 = (bf16[96,1024]{1,0:T(8,128)(2,1)S(1)}, bf16[96,1024]{1,0:T(8,128)(2,1)S(1)}, u32[]{:S(2)}, u32[]{:S(2)}) collective-permute-start(bf16[96,1024]{1,0:T(8,128)(2,1)S(1)} %slice.41), channel_id=1, source_target_pairs={{0,3},{1,0},{2,1},{3,2},{4,7},{5,4},{6,5},{7,6},{8,11},{9,8},{10,9... | collective-permute-start | bytes 589832 | tf_op jit(solution)/shard_map/ppermute | solution.py:32
  28.3 2.2 %shard_map.74 = (bf16[1920,384]{1,0:T(8,128)(2,1)S(1)}, bf16[1344,384]{1,0:T(8,128)(2,1)S(1)}) custom-call(s32[1]{0:T(128)} %bitcast.where_ref, bf16[384,1664]{1,0:T(8,128)(2,1)S(1)} %copy-done.1, bf16[384,1024]{1,0:T(8,128)(2,1)S(1)} %copy-done.2, bf16[208,1024]{1,0:T(8,128)(2,1)S(1)} %collective-permute-done.early.before), custom_call_target="tpu_custom_call" | custom-call | flops 962592768 | bytes 5242880 | tf_op jit(solution)/shard_map/pallas_call | solution.py:368
  30.7 2.7 %collective-permute-start.9 = (bf16[784,1024]{1,0:T(8,128)(2,1)S(1)}, bf16[784,1024]{1,0:T(8,128)(2,1)S(1)}, u32[]{:S(2)}, u32[]{:S(2)}) collective-permute-start(bf16[784,1024]{1,0:T(8,128)(2,1)S(1)} %shard_map.75.images_ref.refs_1_), channel_id=1, source_target_pairs={{0,32},{32,0},{1,33},{33,1},{2,34},{34,2},{3,35},{35,3},{4,36},{36... | collective-permute-start | bytes 4816904 | tf_op jit(solution)/shard_map/ppermute | solution.py:365
  33.4 2.0 %shard_map.76 = (bf16[768,1024]{1,0:T(8,128)(2,1)S(1)}, bf16[768,768]{1,0:T(8,128)(2,1)S(1)}) custom-call(s32[1]{0:T(128)} %bitcast.where_ref, f32[1]{0:T(128)S(6)} %copy.9.scale_ref, f32[1]{0:T(128)S(6)} %copy.10.shift_ref, bf16[192,1024]{1,0:T(8,128)(2,1)S(1)} %constant_dynamic-update-slice_fusion.me, bf16[192,1024]{1,0:T(8,128)(2,1)S(1)} %collective-permute-done.2.after, ...), custom_call_target="tpu_custom_call" | custom-call | flops 19327352832 | bytes 6291456 | tf_op jit(solution)/shard_map/pallas_call | solution.py:390
  35.4 1.1 collective-permute-done.9.images_ref.refs_3_
  36.5 2.8 %shard_map.77 = (bf16[768,768]{1,0:T(8,128)(2,1)S(1)}, f32[384,1024]{1,0:T(8,128)S(1)}) custom-call(s32[1]{0:T(128)} %bitcast.where_ref, f32[1]{0:T(128)S(6)} %copy.9.scale_ref, f32[1]{0:T(128)S(6)} %copy.10.shift_ref, bf16[768,1024]{1,0:T(8,128)(2,1)S(1)} %get-tuple-element.37.texts_ref.refs_0_, bf16[784,1024]{1,0:T(8,128)(2,1)S(1)} %collective-permute-done.9.images_ref.refs_3_), custom_call_target="tpu_custom_call" | custom-call | flops 2415919104 | bytes 8388608 | tf_op jit(solution)/shard_map/pallas_call | solution.py:394
  40.9 1.4 %shard_map.84 = (f32[192,1024]{1,0:T(8,128)S(1)}, f32[192,1024]{1,0:T(8,128)S(1)}) custom-call(bf16[768,768]{1,0:T(8,128)(2,1)S(1)} %get-tuple-element.38.refs_1_.refs_0_, bf16[784,1024]{1,0:T(8,128)(2,1)S(1)} %shard_map.75.images_ref.refs_1_, bf16[768,768]{1,0:T(8,128)(2,1)S(1)} %get-tuple-element.39.refs_1_.refs_2_, ...), custom_call_target="tpu_custom_call" | custom-call | flops 9663676416 | bytes 6291456 | tf_op jit(solution)/shard_map/pallas_call | solution.py:404
  42.3 2.7 %collective-permute-start.21 = (f32[192,1024]{1,0:T(8,128)S(1)}, f32[192,1024]{1,0:T(8,128)S(1)}, u32[]{:S(2)}, u32[]{:S(2)}) collective-permute-start(f32[192,1024]{1,0:T(8,128)S(1)} %get-tuple-element.53), channel_id=1, source_target_pairs={{0,3},{1,0},{2,1},{3,2},{4,7},{5,4},{6,5},{7,6},{8,11},{9,8},{10,9... | collective-permute-start | bytes 2359304 | tf_op jit(solution)/shard_map/ppermute | solution.py:32
  45.0 1.4 %shard_map.81 = (f32[96,1024]{1,0:T(8,128)S(1)}, f32[96,1024]{1,0:T(8,128)S(1)}, f32[192,1024]{1,0:T(8,128)S(1)}) custom-call(bf16[768,768]{1,0:T(8,128)(2,1)S(1)} %get-tuple-element.38.refs_1_.refs_0_, bf16[784,1024]{1,0:T(8,128)(2,1)S(1)} %shard_map.75.images_ref.refs_1_, bf16[768,768]{1,0:T(8,128)(2,1)S(1)} %get-tuple-element.39.refs_1_.refs_2_, ...), custom_call_target="tpu_custom_call" | custom-call | flops 1207959552 | bytes 6291456 | tf_op jit(solution)/shard_map/pallas_call | solution.py:400
  48.3 1.7 %collective-permute-start.12 = (f32[192,1024]{1,0:T(8,128)S(1)}, f32[192,1024]{1,0:T(8,128)S(1)}, u32[]{:S(2)}, u32[]{:S(2)}) collective-permute-start(f32[192,1024]{1,0:T(8,128)S(1)} %get-tuple-element.42), channel_id=1, source_target_pairs={{0,8},{8,16},{16,24},{24,0},{1,9},{9,17},{17,25},{25,1},{2,10},{10... | collective-permute-start | bytes 2359304 | tf_op jit(solution)/shard_map/ppermute | solution.py:32
  50.8 2.2 %collective-permute-start.13 = (f32[192,1024]{1,0:T(8,128)S(1)}, f32[192,1024]{1,0:T(8,128)S(1)}, u32[]{:S(2)}, u32[]{:S(2)}) collective-permute-start(f32[192,1024]{1,0:T(8,128)S(1)} %get-tuple-element.43), channel_id=1, source_target_pairs={{0,24},{8,0},{16,8},{24,16},{1,25},{9,1},{17,9},{25,17},{2,26},{10... | collective-permute-start | bytes 2359304 | tf_op jit(solution)/shard_map/ppermute | solution.py:32
  53.0 4.8 %collective-permute-done.22.high_ref = f32[96,1024]{1,0:T(8,128)S(1)} collective-permute-done((f32[96,1024]{1,0:T(8,128)S(1)}, f32[96,1024]{1,0:T(8,128)S(1)}, u32[]{:S(2)}, u32[]{:S(2)}) %collective-permute-start.22) | collective-permute-done | bytes 393248 | tf_op jit(solution)/shard_map/ppermute | solution.py:407
  57.8 3.7 %collective-permute-done.21.early_ref.left = f32[192,1024]{1,0:T(8,128)S(1)} collective-permute-done((f32[192,1024]{1,0:T(8,128)S(1)}, f32[192,1024]{1,0:T(8,128)S(1)}, u32[]{:S(2)}, u32[]{:S(2)}) %collective-permute-start.21) | collective-permute-done | bytes 786464 | tf_op jit(solution)/shard_map/ppermute | solution.py:32
  61.6 4.5 %collective-permute-done.15.early_ref.right = f32[192,1024]{1,0:T(8,128)S(1)} collective-permute-done((f32[192,1024]{1,0:T(8,128)S(1)}, f32[192,1024]{1,0:T(8,128)S(1)}, u32[]{:S(2)}, u32[]{:S(2)}) %collective-permute-start.15) | collective-permute-done | bytes 786464 | tf_op jit(solution)/shard_map/ppermute | solution.py:32
  67.1 3.7 %collective-permute-start.16 = (f32[96,1024]{1,0:T(8,128)S(1)}, f32[96,1024]{1,0:T(8,128)S(1)}, u32[]{:S(2)}, u32[]{:S(2)}) collective-permute-start(f32[96,1024]{1,0:T(8,128)S(1)} %shard_map.82), channel_id=1, source_target_pairs={{0,16},{8,24},{16,0},{24,8},{1,17},{9,25},{17,1},{25,9},{2,18},{10... | collective-permute-start | bytes 1179656 | tf_op jit(solution)/shard_map/ppermute | solution.py:32
  71.0 5.6 %collective-permute-done.24.got = f32[96,1024]{1,0:T(8,128)S(1)} collective-permute-done((f32[96,1024]{1,0:T(8,128)S(1)}, f32[96,1024]{1,0:T(8,128)S(1)}, u32[]{:S(2)}, u32[]{:S(2)}) %collective-permute-start.24) | collective-permute-done | bytes 393248 | tf_op jit(solution)/shard_map/ppermute | solution.py:407
  77.5 2.9 %collective-permute-start.25 = (bf16[96,256]{1,0:T(8,128)(2,1)S(1)}, bf16[96,256]{1,0:T(8,128)(2,1)S(1)}, u32[]{:S(2)}, u32[]{:S(2)}) collective-permute-start(bf16[96,256]{1,0:T(8,128)(2,1)S(1)} %get-tuple-element.58), channel_id=1, source_target_pairs={{0,32},{32,0},{1,33},{33,1},{2,34},{34,2},{3,35},{35,3},{4,36},{36... | collective-permute-start | bytes 147464 | tf_op jit(solution)/shard_map/ppermute | solution.py:421
  80.4 1.7 %collective-permute-start.27 = (bf16[96,256]{1,0:T(8,128)(2,1)S(1)}, bf16[96,256]{1,0:T(8,128)(2,1)S(1)}, u32[]{:S(2)}, u32[]{:S(2)}) collective-permute-start(bf16[96,256]{1,0:T(8,128)(2,1)S(1)} %get-tuple-element.60), channel_id=1, source_target_pairs={{0,96},{32,64},{64,32},{96,0},{1,97},{33,65},{65,33},{97,1},{2,98}... | collective-permute-start | bytes 147464 | tf_op jit(solution)/shard_map/ppermute | solution.py:423
  82.9 1.8 %collective-permute-start.20 = (bf16[96,256]{1,0:T(8,128)(2,1)S(1)}, bf16[96,256]{1,0:T(8,128)(2,1)S(1)}, u32[]{:S(2)}, u32[]{:S(2)}) collective-permute-start(bf16[96,256]{1,0:T(8,128)(2,1)S(1)} %get-tuple-element.51), channel_id=1, source_target_pairs={{0,96},{32,64},{64,32},{96,0},{1,97},{33,65},{65,33},{97,1},{2,98}... | collective-permute-start | bytes 147464 | tf_op jit(solution)/shard_map/ppermute | solution.py:423
  85.8 1.6 %collective-permute-done.20.refs_3_ = bf16[96,256]{1,0:T(8,128)(2,1)S(1)} collective-permute-done((bf16[96,256]{1,0:T(8,128)(2,1)S(1)}, bf16[96,256]{1,0:T(8,128)(2,1)S(1)}, u32[]{:S(2)}, u32[]{:S(2)}) %collective-permute-start.20) | collective-permute-done | bytes 49184 | tf_op jit(solution)/shard_map/ppermute | solution.py:423
  87.4 1.4 %shard_map.88 = s16[128,24,256]{2,1,0:T(8,128)(2,1)S(1)} custom-call(bf16[1920,384]{1,0:T(8,128)(2,1)S(1)} %get-tuple-element.34.early_a.images_ref, bf16[1344,384]{1,0:T(8,128)(2,1)S(1)} %get-tuple-element.35.early_b.texts_ref, bf16[96,256]{1,0:T(8,128)(2,1)S(1)} %get-tuple-element.48.refs_0_, bf16[96,256]{1,0:T(8,128)(2,1)S(1)} %collective-permute-done.18.refs_1_, ...), custom_call_target="tpu_custom_call" | custom-call | flops 1207959552 | bytes 6291456 | tf_op jit(solution)/shard_map/pallas_call | solution.py:429
  88.8 30.2 %all_to_all.5.coded_ref = s16[128,24,256]{2,1,0:T(8,128)(2,1)S(1)} all-to-all(s16[128,24,256]{2,1,0:T(8,128)(2,1)S(1)} %shard_map.88), channel_id=1, replica_groups=mesh['xl'=2,'core'=2,'z'=4,'xh'=2,'y'=4] {'xl','core','z','xh','y'}, dimensions={0} | all-to-all | bytes 3145728 | tf_op jit(solution)/shard_map/all_to_all | solution.py:435
  119.1 1.2 %shard_map.89 = f32[21,1024]{1,0:T(8,128)} custom-call(s16[128,24,256]{2,1,0:T(8,128)(2,1)S(1)} %all_to_all.5.coded_ref), custom_call_target="tpu_custom_call" | custom-call | bytes 2097152 | tf_op jit(solution)/shard_map/pallas_call | solution.py:436
  (62 shorter events, 9.6 us)
Async XLA Ops:
  4.9 23.4 %copy-start.1 = (bf16[384,1664]{1,0:T(8,128)(2,1)S(1)}, bf16[384,1664]{1,0:T(8,128)(2,1)}, u32[]{:S(2)}) copy-start(bf16[384,1664]{1,0:T(8,128)(2,1)} %image_feats.3) | copy-start | bytes 3833860
  4.9 23.4 %copy-start.2 = (bf16[384,1024]{1,0:T(8,128)(2,1)S(1)}, bf16[384,1024]{1,0:T(8,128)(2,1)}, u32[]{:S(2)}) copy-start(bf16[384,1024]{1,0:T(8,128)(2,1)} %text_feats.3) | copy-start | bytes 2359300
  4.9 8.1 %collective-permute-start.1 = (bf16[96,1024]{1,0:T(8,128)(2,1)}, bf16[96,1024]{1,0:T(8,128)(2,1)S(1)}, u32[]{:S(2)}, u32[]{:S(2)}) collective-permute-start(bf16[96,1024]{1,0:T(8,128)(2,1)} %get-tuple-element.36.emb), channel_id=1, source_target_pairs={{0,68},{4,64},{64,4},{68,0},{1,69},{5,65},{65,5},{69,1},{2,70},{6,... | collective-permute-start | bytes 589832 | tf_op jit(solution)/shard_map/ppermute | solution.py:358
  8.3 15.7 %collective-permute-start = (bf16[208,1024]{1,0:T(8,128)(2,1)}, bf16[208,1024]{1,0:T(8,128)(2,1)S(1)}, u32[]{:S(2)}, u32[]{:S(2)}) collective-permute-start(bf16[208,1024]{1,0:T(8,128)(2,1)} %get-tuple-element.33.me.emb), channel_id=1, source_target_pairs={{0,8},{8,16},{16,24},{24,0},{1,9},{9,17},{17,25},{25,1},{2,10},{10... | collective-permute-start | bytes 1277960 | tf_op jit(solution)/shard_map/ppermute | solution.py:32
  9.9 10.7 %collective-permute-start.6 = (bf16[208,1024]{1,0:T(8,128)(2,1)}, bf16[208,1024]{1,0:T(8,128)(2,1)S(1)}, u32[]{:S(2)}, u32[]{:S(2)}) collective-permute-start(bf16[208,1024]{1,0:T(8,128)(2,1)} %get-tuple-element.33.me.emb), channel_id=1, source_target_pairs={{0,24},{8,0},{16,8},{24,16},{1,25},{9,1},{17,9},{25,17},{2,26},{10... | collective-permute-start | bytes 1277960 | tf_op jit(solution)/shard_map/ppermute | solution.py:32
  13.1 11.0 %collective-permute-start.3 = (bf16[192,1024]{1,0:T(8,128)(2,1)S(1)}, bf16[192,1024]{1,0:T(8,128)(2,1)S(1)}, u32[]{:S(2)}, u32[]{:S(2)}) collective-permute-start(bf16[192,1024]{1,0:T(8,128)(2,1)S(1)} %constant_dynamic-update-slice_fusion.me), channel_id=1, source_target_pairs={{0,1},{1,2},{2,3},{3,0},{4,5},{5,6},{6,7},{7,4},{8,9},{9,10},{10,1... | collective-permute-start | bytes 1179656 | tf_op jit(solution)/shard_map/ppermute | solution.py:32
  14.4 11.0 %collective-permute-start.2 = (bf16[192,1024]{1,0:T(8,128)(2,1)S(1)}, bf16[192,1024]{1,0:T(8,128)(2,1)S(1)}, u32[]{:S(2)}, u32[]{:S(2)}) collective-permute-start(bf16[192,1024]{1,0:T(8,128)(2,1)S(1)} %constant_dynamic-update-slice_fusion.me), channel_id=1, source_target_pairs={{0,3},{1,0},{2,1},{3,2},{4,7},{5,4},{6,5},{7,6},{8,11},{9,8},{10,9... | collective-permute-start | bytes 1179656 | tf_op jit(solution)/shard_map/ppermute | solution.py:32
  20.7 9.9 %collective-permute-start.8 = (bf16[112,1024]{1,0:T(8,128)(2,1)S(1)}, bf16[112,1024]{1,0:T(8,128)(2,1)S(1)}, u32[]{:S(2)}, u32[]{:S(2)}) collective-permute-start(bf16[112,1024]{1,0:T(8,128)(2,1)S(1)} %slice.43), channel_id=1, source_target_pairs={{0,24},{8,0},{16,8},{24,16},{1,25},{9,1},{17,9},{25,17},{2,26},{10... | collective-permute-start | bytes 688136 | tf_op jit(solution)/shard_map/ppermute | solution.py:32
  24.0 6.5 %collective-permute-start.7 = (bf16[96,1024]{1,0:T(8,128)(2,1)S(1)}, bf16[96,1024]{1,0:T(8,128)(2,1)S(1)}, u32[]{:S(2)}, u32[]{:S(2)}) collective-permute-start(bf16[96,1024]{1,0:T(8,128)(2,1)S(1)} %slice.42), channel_id=1, source_target_pairs={{0,8},{8,16},{16,24},{24,0},{1,9},{9,17},{17,25},{25,1},{2,10},{10... | collective-permute-start | bytes 589832 | tf_op jit(solution)/shard_map/ppermute | solution.py:32
  24.1 9.3 %collective-permute-start.4 = (bf16[96,1024]{1,0:T(8,128)(2,1)S(1)}, bf16[96,1024]{1,0:T(8,128)(2,1)S(1)}, u32[]{:S(2)}, u32[]{:S(2)}) collective-permute-start(bf16[96,1024]{1,0:T(8,128)(2,1)S(1)} %slice.40), channel_id=1, source_target_pairs={{0,1},{1,2},{2,3},{3,0},{4,5},{5,6},{6,7},{7,4},{8,9},{9,10},{10,1... | collective-permute-start | bytes 589832 | tf_op jit(solution)/shard_map/ppermute | solution.py:32
  25.5 7.9 %collective-permute-start.5 = (bf16[96,1024]{1,0:T(8,128)(2,1)S(1)}, bf16[96,1024]{1,0:T(8,128)(2,1)S(1)}, u32[]{:S(2)}, u32[]{:S(2)}) collective-permute-start(bf16[96,1024]{1,0:T(8,128)(2,1)S(1)} %slice.41), channel_id=1, source_target_pairs={{0,3},{1,0},{2,1},{3,2},{4,7},{5,4},{6,5},{7,6},{8,11},{9,8},{10,9... | collective-permute-start | bytes 589832 | tf_op jit(solution)/shard_map/ppermute | solution.py:32
  30.7 5.8 %collective-permute-start.9 = (bf16[784,1024]{1,0:T(8,128)(2,1)S(1)}, bf16[784,1024]{1,0:T(8,128)(2,1)S(1)}, u32[]{:S(2)}, u32[]{:S(2)}) collective-permute-start(bf16[784,1024]{1,0:T(8,128)(2,1)S(1)} %shard_map.75.images_ref.refs_1_), channel_id=1, source_target_pairs={{0,32},{32,0},{1,33},{33,1},{2,34},{34,2},{3,35},{35,3},{4,36},{36... | collective-permute-start | bytes 4816904 | tf_op jit(solution)/shard_map/ppermute | solution.py:365
  39.3 8.2 %collective-permute-start.11 = (f32[384,1024]{1,0:T(8,128)S(1)}, f32[384,1024]{1,0:T(8,128)S(1)}, u32[]{:S(2)}, u32[]{:S(2)}) collective-permute-start(f32[384,1024]{1,0:T(8,128)S(1)} %get-tuple-element.41), channel_id=1, source_target_pairs={{0,32},{32,0},{1,33},{33,1},{2,34},{34,2},{3,35},{35,3},{4,36},{36... | collective-permute-start | bytes 4718600 | tf_op jit(solution)/shard_map/ppermute | solution.py:398
  40.7 9.3 %collective-permute-start.10 = (f32[384,1024]{1,0:T(8,128)S(1)}, f32[384,1024]{1,0:T(8,128)S(1)}, u32[]{:S(2)}, u32[]{:S(2)}) collective-permute-start(f32[384,1024]{1,0:T(8,128)S(1)} %shard_map.78), channel_id=1, source_target_pairs={{0,32},{32,0},{1,33},{33,1},{2,34},{34,2},{3,35},{35,3},{4,36},{36... | collective-permute-start | bytes 4718600 | tf_op jit(solution)/shard_map/ppermute | solution.py:402
  42.3 19.2 %collective-permute-start.21 = (f32[192,1024]{1,0:T(8,128)S(1)}, f32[192,1024]{1,0:T(8,128)S(1)}, u32[]{:S(2)}, u32[]{:S(2)}) collective-permute-start(f32[192,1024]{1,0:T(8,128)S(1)} %get-tuple-element.53), channel_id=1, source_target_pairs={{0,3},{1,0},{2,1},{3,2},{4,7},{5,4},{6,5},{7,6},{8,11},{9,8},{10,9... | collective-permute-start | bytes 2359304 | tf_op jit(solution)/shard_map/ppermute | solution.py:32
  46.4 19.7 %collective-permute-start.15 = (f32[192,1024]{1,0:T(8,128)S(1)}, f32[192,1024]{1,0:T(8,128)S(1)}, u32[]{:S(2)}, u32[]{:S(2)}) collective-permute-start(f32[192,1024]{1,0:T(8,128)S(1)} %get-tuple-element.46), channel_id=1, source_target_pairs={{0,1},{1,2},{2,3},{3,0},{4,5},{5,6},{6,7},{7,4},{8,9},{9,10},{10,1... | collective-permute-start | bytes 2359304 | tf_op jit(solution)/shard_map/ppermute | solution.py:32
  46.5 11.3 %collective-permute-start.22 = (f32[96,1024]{1,0:T(8,128)S(1)}, f32[96,1024]{1,0:T(8,128)S(1)}, u32[]{:S(2)}, u32[]{:S(2)}) collective-permute-start(f32[96,1024]{1,0:T(8,128)S(1)} %get-tuple-element.55), channel_id=1, source_target_pairs={{0,68},{4,64},{64,4},{68,0},{1,69},{5,65},{65,5},{69,1},{2,70},{6,... | collective-permute-start | bytes 1179656 | tf_op jit(solution)/shard_map/ppermute | solution.py:407
  48.3 22.5 %collective-permute-start.12 = (f32[192,1024]{1,0:T(8,128)S(1)}, f32[192,1024]{1,0:T(8,128)S(1)}, u32[]{:S(2)}, u32[]{:S(2)}) collective-permute-start(f32[192,1024]{1,0:T(8,128)S(1)} %get-tuple-element.42), channel_id=1, source_target_pairs={{0,8},{8,16},{16,24},{24,0},{1,9},{9,17},{17,25},{25,1},{2,10},{10... | collective-permute-start | bytes 2359304 | tf_op jit(solution)/shard_map/ppermute | solution.py:32
  50.8 20.0 %collective-permute-start.13 = (f32[192,1024]{1,0:T(8,128)S(1)}, f32[192,1024]{1,0:T(8,128)S(1)}, u32[]{:S(2)}, u32[]{:S(2)}) collective-permute-start(f32[192,1024]{1,0:T(8,128)S(1)} %get-tuple-element.43), channel_id=1, source_target_pairs={{0,24},{8,0},{16,8},{24,16},{1,25},{9,1},{17,9},{25,17},{2,26},{10... | collective-permute-start | bytes 2359304 | tf_op jit(solution)/shard_map/ppermute | solution.py:32
  57.8 9.3 %collective-permute-start.14 = (f32[96,1024]{1,0:T(8,128)S(1)}, f32[96,1024]{1,0:T(8,128)S(1)}, u32[]{:S(2)}, u32[]{:S(2)}) collective-permute-start(f32[96,1024]{1,0:T(8,128)S(1)} %get-tuple-element.45), channel_id=1, source_target_pairs={{0,64},{64,0},{1,65},{65,1},{2,66},{66,2},{3,67},{67,3},{4,68},{68... | collective-permute-start | bytes 1179656 | tf_op jit(solution)/shard_map/ppermute | solution.py:410
  66.2 10.4 %collective-permute-start.24 = (f32[96,1024]{1,0:T(8,128)S(1)}, f32[96,1024]{1,0:T(8,128)S(1)}, u32[]{:S(2)}, u32[]{:S(2)}) collective-permute-start(f32[96,1024]{1,0:T(8,128)S(1)} %slice_add_fusion), channel_id=1, source_target_pairs={{0,68},{4,64},{64,4},{68,0},{1,69},{5,65},{65,5},{69,1},{2,70},{6,... | collective-permute-start | bytes 1179656 | tf_op jit(solution)/shard_map/ppermute | solution.py:407
  67.0 10.2 %collective-permute-start.23 = (f32[96,1024]{1,0:T(8,128)S(1)}, f32[96,1024]{1,0:T(8,128)S(1)}, u32[]{:S(2)}, u32[]{:S(2)}) collective-permute-start(f32[96,1024]{1,0:T(8,128)S(1)} %shard_map.86), channel_id=1, source_target_pairs={{0,2},{1,3},{2,0},{3,1},{4,6},{5,7},{6,4},{7,5},{8,10},{9,11},{10,... | collective-permute-start | bytes 1179656 | tf_op jit(solution)/shard_map/ppermute | solution.py:32
  67.1 10.1 %copy-start.3 = (bf16[96,1024]{1,0:T(8,128)(2,1)S(1)}, bf16[96,1024]{1,0:T(8,128)(2,1)}, u32[]{:S(2)}) copy-start(bf16[96,1024]{1,0:T(8,128)(2,1)} %get-tuple-element.36.emb) | copy-start | bytes 589828
  67.1 10.1 %copy-start.5 = (f32[96,128]{1,0:T(8,128)S(1)}, f32[96,128]{1,0:T(8,128)}, u32[]{:S(2)}) copy-start(f32[96,128]{1,0:T(8,128)} %get-tuple-element.56.inverse) | copy-start | bytes 147460
  67.1 15.0 %collective-permute-start.16 = (f32[96,1024]{1,0:T(8,128)S(1)}, f32[96,1024]{1,0:T(8,128)S(1)}, u32[]{:S(2)}, u32[]{:S(2)}) collective-permute-start(f32[96,1024]{1,0:T(8,128)S(1)} %shard_map.82), channel_id=1, source_target_pairs={{0,16},{8,24},{16,0},{24,8},{1,17},{9,25},{17,1},{25,9},{2,18},{10... | collective-permute-start | bytes 1179656 | tf_op jit(solution)/shard_map/ppermute | solution.py:32
  70.9 11.2 %collective-permute-start.17 = (f32[96,1024]{1,0:T(8,128)S(1)}, f32[96,1024]{1,0:T(8,128)S(1)}, u32[]{:S(2)}, u32[]{:S(2)}) collective-permute-start(f32[96,1024]{1,0:T(8,128)S(1)} %slice_add_fusion.2), channel_id=1, source_target_pairs={{0,64},{64,0},{1,65},{65,1},{2,66},{66,2},{3,67},{67,3},{4,68},{68... | collective-permute-start | bytes 1179656 | tf_op jit(solution)/shard_map/ppermute | solution.py:410
  77.5 5.4 %collective-permute-start.25 = (bf16[96,256]{1,0:T(8,128)(2,1)S(1)}, bf16[96,256]{1,0:T(8,128)(2,1)S(1)}, u32[]{:S(2)}, u32[]{:S(2)}) collective-permute-start(bf16[96,256]{1,0:T(8,128)(2,1)S(1)} %get-tuple-element.58), channel_id=1, source_target_pairs={{0,32},{32,0},{1,33},{33,1},{2,34},{34,2},{3,35},{35,3},{4,36},{36... | collective-permute-start | bytes 147464 | tf_op jit(solution)/shard_map/ppermute | solution.py:421
  80.4 4.2 %collective-permute-start.26 = (bf16[96,256]{1,0:T(8,128)(2,1)S(1)}, bf16[96,256]{1,0:T(8,128)(2,1)S(1)}, u32[]{:S(2)}, u32[]{:S(2)}) collective-permute-start(bf16[96,256]{1,0:T(8,128)(2,1)S(1)} %get-tuple-element.59), channel_id=1, source_target_pairs={{0,64},{64,0},{1,65},{65,1},{2,66},{66,2},{3,67},{67,3},{4,68},{68... | collective-permute-start | bytes 147464 | tf_op jit(solution)/shard_map/ppermute | solution.py:422
  80.4 4.5 %collective-permute-start.27 = (bf16[96,256]{1,0:T(8,128)(2,1)S(1)}, bf16[96,256]{1,0:T(8,128)(2,1)S(1)}, u32[]{:S(2)}, u32[]{:S(2)}) collective-permute-start(bf16[96,256]{1,0:T(8,128)(2,1)S(1)} %get-tuple-element.60), channel_id=1, source_target_pairs={{0,96},{32,64},{64,32},{96,0},{1,97},{33,65},{65,33},{97,1},{2,98}... | collective-permute-start | bytes 147464 | tf_op jit(solution)/shard_map/ppermute | solution.py:423
  82.4 2.5 %collective-permute-start.18 = (bf16[96,256]{1,0:T(8,128)(2,1)S(1)}, bf16[96,256]{1,0:T(8,128)(2,1)S(1)}, u32[]{:S(2)}, u32[]{:S(2)}) collective-permute-start(bf16[96,256]{1,0:T(8,128)(2,1)S(1)} %get-tuple-element.49), channel_id=1, source_target_pairs={{0,32},{32,0},{1,33},{33,1},{2,34},{34,2},{3,35},{35,3},{4,36},{36... | collective-permute-start | bytes 147464 | tf_op jit(solution)/shard_map/ppermute | solution.py:421
  82.9 2.9 %collective-permute-start.19 = (bf16[96,256]{1,0:T(8,128)(2,1)S(1)}, bf16[96,256]{1,0:T(8,128)(2,1)S(1)}, u32[]{:S(2)}, u32[]{:S(2)}) collective-permute-start(bf16[96,256]{1,0:T(8,128)(2,1)S(1)} %get-tuple-element.50), channel_id=1, source_target_pairs={{0,64},{64,0},{1,65},{65,1},{2,66},{66,2},{3,67},{67,3},{4,68},{68... | collective-permute-start | bytes 147464 | tf_op jit(solution)/shard_map/ppermute | solution.py:422
  82.9 4.5 %collective-permute-start.20 = (bf16[96,256]{1,0:T(8,128)(2,1)S(1)}, bf16[96,256]{1,0:T(8,128)(2,1)S(1)}, u32[]{:S(2)}, u32[]{:S(2)}) collective-permute-start(bf16[96,256]{1,0:T(8,128)(2,1)S(1)} %get-tuple-element.51), channel_id=1, source_target_pairs={{0,96},{32,64},{64,32},{96,0},{1,97},{33,65},{65,33},{97,1},{2,98}... | collective-permute-start | bytes 147464 | tf_op jit(solution)/shard_map/ppermute | solution.py:423
  (2 other events, 7.2 us)

commit v7 on v6

--- a/solution.py
+++ b/solution.py
@@ -125,6 +125,32 @@
     load_ref[HALF:, :ROWS] = parts.astype(BF16)
 
 
+CODED = E + E // 4 + 128
+TOP = 2.0**19 - 1.0
+
+
+def encode(value, out_ref):
+    largest = jnp.max(jnp.abs(value), axis=1, keepdims=True)
+    exponent = jnp.ceil(jnp.log(jnp.maximum(largest, 1e-30)) * (1.0 / OCTAVE) + 0.01)
+    whole = jnp.round(value * (TOP * jnp.exp(exponent * -OCTAVE))).astype(jnp.int32)
+    out_ref[:, :E] = (whole >> 4).astype(jnp.int16)
+    low = whole & 15
+    packed = low[:, :SLICE]
+    for i in range(1, 4):
+        packed = packed | (low[:, i * SLICE : (i + 1) * SLICE] << (4 * i))
+    out_ref[:, E : E + SLICE] = (packed - 32768).astype(jnp.int16)
+    lanes = jnp.broadcast_to(exponent, (value.shape[0], 128))
+    out_ref[:, E + SLICE :] = lanes.astype(jnp.int32).astype(jnp.int16)
+
+
+def decode(ref, rows=slice(None)):
+    exponent = ref[rows, E + SLICE : E + SLICE + 1].astype(jnp.int32).astype(F32)
+    packed = ref[rows, E : E + SLICE].astype(jnp.int32) + 32768
+    low = jnp.concatenate([(packed >> (4 * i)) & 15 for i in range(4)], 1)
+    whole = (ref[rows, :E].astype(jnp.int32) << 4) + low
+    return whole.astype(F32) * (jnp.exp(exponent * OCTAVE) * (1.0 / TOP))
+
+
 def ring_gather(block, axis):
     before, after = shifted(block, axis, 1), shifted(block, axis, -1)
     far_low = shifted(before[:QUARTER], axis, 1)
@@ -133,32 +159,40 @@
 
 
 def far_kernel(low_ref, high_ref, early_ref, out_ref):
-    out_ref[...] = low_ref[...] + high_ref[...]
+    encode(low_ref[...] + decode(high_ref), out_ref)
 
 
 def add_kernel(low_ref, high_ref, out_ref):
-    out_ref[...] = low_ref[...] + high_ref[...]
+    encode(low_ref[...] + decode(high_ref), out_ref)
 
 
 def behind_kernel(far_ref, early_ref, out_ref):
     out_ref[...] = far_ref[...]
 
 
+def high_kernel(mine, right, left, out_ref):
+    rows = slice(QUARTER, HALF)
+    encode(mine[rows, :] + decode(right, rows) + decode(left, rows), out_ref)
+
+
 def ring_scatter(far_low, far_high, after, before, mine, axis, crossed, marker=None):
+    got_right, got_left = shifted(after, axis, 1), shifted(before, axis, -1)
     far = crossed(far_high)
-    got_right, got_left = shifted(after, axis, 1), shifted(before, axis, -1)
+    coded = shape(QUARTER, CODED, dtype=jnp.int16)
     if axis == "z":
         far = call(
-            far_kernel, shape(QUARTER, E), 0, 1 << 20, in_specs=[VMEM, VMEM, ANY], out_specs=VMEM
+            far_kernel, coded, 0, 1 << 20, in_specs=[VMEM, VMEM, ANY], out_specs=VMEM
         )(far_low, far, marker)
     else:
         far = call(
-            add_kernel, shape(QUARTER, E), 4 << 30, 1 << 20, in_specs=[VMEM] * 2, out_specs=VMEM
+            add_kernel, coded, 4 << 30, 1 << 20, in_specs=[VMEM] * 2, out_specs=VMEM
         )(far_low, far)
         far = call(
-            behind_kernel, shape(QUARTER, E), 0, 1 << 20, in_specs=[VMEM, ANY], out_specs=VMEM
+            behind_kernel, coded, 0, 1 << 20, in_specs=[VMEM, ANY], out_specs=VMEM
         )(far, got_left)
-    high = mine[QUARTER:] + got_right[QUARTER:] + got_left[QUARTER:]
+    high = call(high_kernel, coded, 0, 1 << 20, in_specs=[VMEM] * 3, out_specs=VMEM)(
+        mine, got_right, got_left
+    )
     return mine, got_right, got_left, shifted(far, axis, 2), crossed(high)
 
 
@@ -216,8 +250,12 @@
 def share_out(got, outs):
     start = 0
     for out in outs:
-        out[...] = got[start : start + out.shape[0]]
+        part = got[start : start + out.shape[0]]
         start += out.shape[0]
+        if out.dtype == jnp.int16:
+            encode(part, out)
+        else:
+            out[...] = part
 
 
 def own_kernel(
@@ -248,11 +286,16 @@
     share_out(image_terms(coef_ref, texts_ref, part) + taken_ref[...], outs)
 
 
+def kept_rest_kernel(texts_ref, coef_ref, taken_ref, early_ref, *outs):
+    kept_kernel(1, texts_ref, coef_ref, taken_ref, *outs)
+
+
 def back_kernel(
     where_ref, mine, right, left, far, got, emb, inverse, own_ref, core_ref, xl_ref, both_ref, held_ref
 ):
-    gradients = mine[:QUARTER, :] + right[:QUARTER, :] + left[:QUARTER, :]
-    gradients += far[...] + got[...]
+    rows = slice(0, QUARTER)
+    gradients = mine[rows, :] + decode(right, rows) + decode(left, rows)
+    gradients += decode(far) + decode(got)
     widened = emb[:QUARTER, :].astype(F32)
     inner_sum = jnp.sum(widened * gradients, axis=1, keepdims=True)
     value = (inverse[:, :1] * (gradients - widened * inner_sum)).astype(BF16)
@@ -378,8 +421,10 @@
 
     flops = 2 * TILE * TILE * E
     coef, texts = shape(TILE, TILE, dtype=BF16), shape(TILE, E, dtype=BF16)
-    ways = [shape(QUARTER, E)] * 2 + [shape(HALF, E)]
-    rest = [shape(HALF, E)] * 2
+    coded_quarter = shape(QUARTER, CODED, dtype=jnp.int16)
+    coded_half = shape(HALF, CODED, dtype=jnp.int16)
+    ways = [shape(QUARTER, E), coded_quarter, coded_half]
+    rest = [coded_half, shape(HALF, E)]
 
     def run(kernel, outs, share, count, *options):
         return call(
@@ -402,7 +447,10 @@
     taken_rest = lax.ppermute(given_rest, "core", SWAP)
     image_ways = run(kept_kernel, ways, 0.5, 3, 0)(texts, own_coef, taken)
     text_rest = run(text_kernel, rest, 8, 4, 1)(*sides)
-    image_rest = run(kept_kernel, rest, 4, 3, 1)(texts, own_coef, taken_rest)
+    image_rest = call(
+        kept_rest_kernel, rest, 4 * flops, 6 << 20, 24,
+        in_specs=[VMEM] * 3 + [ANY], out_specs=[VMEM] * 2,
+    )(texts, own_coef, taken_rest, image_ways[0])
     text_sums = ring_scatter(
         *text_ways, *text_rest, "y", lambda a: lax.ppermute(a, ("xl", "xh"), FLIP)
     )

time: 120 us -> 117 us (0.975)
  waiting for transfers between devices: 27.8 us -> 14.9 us
  starting transfers between devices: 39 us -> 43.4 us
  Pallas kernels: 20.5 us -> 23.5 us
  blocking collectives: 30.2 us -> 32.7 us
    ppermute x2, waiting for transfers between devices: 10.3 us -> 0.73 us  [body(): lax.ppermute(a, ('xl', 'xh'), FLIP)]
    ppermute x14, waiting for transfers between devices: 13.7 us -> 10.2 us  [shifted(): return lax.ppermute(array, axis, [(i, (i + by) % 4) for i in range(4)])]
    all_to_all x1, blocking collectives: 30.2 us -> 32.7 us  [body(): coded = lax.all_to_all(coded, AXES, split_axis=0, concat_axis=0, tiled=True)]
    ppermute x2, starting transfers between devices: 1.74 us -> 3.57 us  [body(): lax.ppermute(a, ('xl', 'xh'), FLIP)]
    ppermute x2, starting transfers between devices: 3.38 us -> 5.15 us  [tower_pieces(): lax.ppermute(other_core, 'core', SWAP)]
    pallas_call x4 -> x6, Pallas kernels: 0.92 us -> 2.39 us  [the longest x1 1.02 us: body(): call(kept_rest_kernel, rest, 4 * flops, 6 << 20, 24, in_specs=[VMEM] * 3...]
  transfers between devices with their start and end apart: 28 -> 28, of which waited for: 10 -> 8; matrix products, arithmetic and copies ran while one was open for 1% -> 1% of each run, Pallas kernels for 8% -> 11%
where the time goes in v7:
time: 117 us
  starting transfers between devices  43.4 us (37%)
  blocking collectives  32.7 us (28%)
  Pallas kernels  23.5 us (20%)
  waiting for transfers between devices  14.9 us (13%)
  between operations  1.6 us (1%)
    all_to_all x1, blocking collectives, body(): coded = lax.all_to_all(coded, AXES, split_axis=0, concat_axis=0, tiled=True)  32.7 us
    ppermute x14, starting transfers between devices, shifted(): return lax.ppermute(array, axis, [(i, (i + by) % 4) for i in range(4)])  24.2 us
    ppermute x14, waiting for transfers between devices, shifted(): return lax.ppermute(array, axis, [(i, (i + by) % 4) for i in range(4)])  10.2 us
    ppermute x2, starting transfers between devices, tower_pieces(): lax.ppermute(other_core, 'core', SWAP)  5.15 us
    pallas_call x1, Pallas kernels, body(): call(embed_kernel, [shape(QUARTER, E, dtype=BF16), shape(QUARTER, 128), s...  4.88 us
    ppermute x2, starting transfers between devices, body(): lax.ppermute(a, ('xl', 'xh'), FLIP)  3.57 us
    ppermute x2, starting transfers between devices, tower_pieces(): lax.ppermute(other_both, TOWER, [(i, 3 - i) for i in range(4)])  3.44 us
    ppermute x1, starting transfers between devices, body(): other_texts = lax.ppermute(own_texts, ('xl', 'xh'), FLIP)  3.39 us
  transfers between devices with their start and end apart: 28, of which 8 were waited for; matrix products, arithmetic and copies ran while one was open for 1% of the time, Pallas kernels for 11%

profile of v7, /device:TPU:1, one launch (start us, length us, event | category | flops | bytes accessed | tf_op | source)
XLA Modules:
  0.0 117.2 jit_solution(7204223983662039668)
XLA Ops:
  0.0 4.9 %shard_map.73 = (bf16[96,1024]{1,0:T(8,128)(2,1)}, f32[96,128]{1,0:T(8,128)}, bf16[208,1024]{1,0:T(8,128)(2,1)}, f32[96,128]{1,0:T(8,128)}) custom-call(s32[1]{0:T(128)} %bitcast.where_ref, s32[3,128]{1,0:T(4,128)} %bitcast.2, bf16[384,1024]{1,0:T(8,128)(2,1)} %text_feats.3, bf16[384,1664]{1,0:T(8,128)(2,1)} %image_feats.3, bf16[1024,1024]{1,0:T(8,128)(2,1)} %text_weight.1, ...), custom_call_target="tpu_custom_call" | custom-call | flops 855638016 | bytes 8388608 | tf_op jit(solution)/shard_map/pallas_call | solution.py:386
  4.9 3.4 %collective-permute-start.1 = (bf16[96,1024]{1,0:T(8,128)(2,1)}, bf16[96,1024]{1,0:T(8,128)(2,1)S(1)}, u32[]{:S(2)}, u32[]{:S(2)}) collective-permute-start(bf16[96,1024]{1,0:T(8,128)(2,1)} %get-tuple-element.36.emb), channel_id=1, source_target_pairs={{0,68},{4,64},{64,4},{68,0},{1,69},{5,65},{65,5},{69,1},{2,70},{6,... | collective-permute-start | bytes 589832 | tf_op jit(solution)/shard_map/ppermute | solution.py:401
  8.3 3.8 %collective-permute-start.6 = (bf16[208,1024]{1,0:T(8,128)(2,1)}, bf16[208,1024]{1,0:T(8,128)(2,1)S(1)}, u32[]{:S(2)}, u32[]{:S(2)}) collective-permute-start(bf16[208,1024]{1,0:T(8,128)(2,1)} %get-tuple-element.33.me.emb), channel_id=1, source_target_pairs={{0,24},{8,0},{16,8},{24,16},{1,25},{9,1},{17,9},{25,17},{2,26},{10... | collective-permute-start | bytes 1277960 | tf_op jit(solution)/shard_map/ppermute | solution.py:32
  13.1 1.4 %collective-permute-start.3 = (bf16[192,1024]{1,0:T(8,128)(2,1)S(1)}, bf16[192,1024]{1,0:T(8,128)(2,1)S(1)}, u32[]{:S(2)}, u32[]{:S(2)}) collective-permute-start(bf16[192,1024]{1,0:T(8,128)(2,1)S(1)} %constant_dynamic-update-slice_fusion.me), channel_id=1, source_target_pairs={{0,1},{1,2},{2,3},{3,0},{4,5},{5,6},{6,7},{7,4},{8,9},{9,10},{10,1... | collective-permute-start | bytes 1179656 | tf_op jit(solution)/shard_map/ppermute | solution.py:32
  14.4 1.5 %collective-permute-start.2 = (bf16[192,1024]{1,0:T(8,128)(2,1)S(1)}, bf16[192,1024]{1,0:T(8,128)(2,1)S(1)}, u32[]{:S(2)}, u32[]{:S(2)}) collective-permute-start(bf16[192,1024]{1,0:T(8,128)(2,1)S(1)} %constant_dynamic-update-slice_fusion.me), channel_id=1, source_target_pairs={{0,3},{1,0},{2,1},{3,2},{4,7},{5,4},{6,5},{7,6},{8,11},{9,8},{10,9... | collective-permute-start | bytes 1179656 | tf_op jit(solution)/shard_map/ppermute | solution.py:32
  15.9 4.6 %collective-permute-done.6.after = bf16[208,1024]{1,0:T(8,128)(2,1)S(1)} collective-permute-done((bf16[208,1024]{1,0:T(8,128)(2,1)}, bf16[208,1024]{1,0:T(8,128)(2,1)S(1)}, u32[]{:S(2)}, u32[]{:S(2)}) %collective-permute-start.6) | collective-permute-done | bytes 426016 | tf_op jit(solution)/shard_map/ppermute | solution.py:32
  20.6 3.4 %collective-permute-start.8 = (bf16[112,1024]{1,0:T(8,128)(2,1)S(1)}, bf16[112,1024]{1,0:T(8,128)(2,1)S(1)}, u32[]{:S(2)}, u32[]{:S(2)}) collective-permute-start(bf16[112,1024]{1,0:T(8,128)(2,1)S(1)} %slice.19), channel_id=1, source_target_pairs={{0,24},{8,0},{16,8},{24,16},{1,25},{9,1},{17,9},{25,17},{2,26},{10... | collective-permute-start | bytes 688136 | tf_op jit(solution)/shard_map/ppermute | solution.py:32
  24.1 1.4 %collective-permute-start.4 = (bf16[96,1024]{1,0:T(8,128)(2,1)S(1)}, bf16[96,1024]{1,0:T(8,128)(2,1)S(1)}, u32[]{:S(2)}, u32[]{:S(2)}) collective-permute-start(bf16[96,1024]{1,0:T(8,128)(2,1)S(1)} %slice.16), channel_id=1, source_target_pairs={{0,1},{1,2},{2,3},{3,0},{4,5},{5,6},{6,7},{7,4},{8,9},{9,10},{10,1... | collective-permute-start | bytes 589832 | tf_op jit(solution)/shard_map/ppermute | solution.py:32
  25.5 1.5 %collective-permute-start.5 = (bf16[96,1024]{1,0:T(8,128)(2,1)S(1)}, bf16[96,1024]{1,0:T(8,128)(2,1)S(1)}, u32[]{:S(2)}, u32[]{:S(2)}) collective-permute-start(bf16[96,1024]{1,0:T(8,128)(2,1)S(1)} %slice.17), channel_id=1, source_target_pairs={{0,3},{1,0},{2,1},{3,2},{4,7},{5,4},{6,5},{7,6},{8,11},{9,8},{10,9... | collective-permute-start | bytes 589832 | tf_op jit(solution)/shard_map/ppermute | solution.py:32
  28.3 2.2 %shard_map.74 = (bf16[1920,384]{1,0:T(8,128)(2,1)S(1)}, bf16[1344,384]{1,0:T(8,128)(2,1)S(1)}) custom-call(s32[1]{0:T(128)} %bitcast.where_ref, bf16[384,1664]{1,0:T(8,128)(2,1)S(1)} %copy-done.1, bf16[384,1024]{1,0:T(8,128)(2,1)S(1)} %copy-done.2, bf16[208,1024]{1,0:T(8,128)(2,1)S(1)} %collective-permute-done.early.before), custom_call_target="tpu_custom_call" | custom-call | flops 962592768 | bytes 5242880 | tf_op jit(solution)/shard_map/pallas_call | solution.py:411
  30.7 2.7 %collective-permute-start.9 = (bf16[784,1024]{1,0:T(8,128)(2,1)S(1)}, bf16[784,1024]{1,0:T(8,128)(2,1)S(1)}, u32[]{:S(2)}, u32[]{:S(2)}) collective-permute-start(bf16[784,1024]{1,0:T(8,128)(2,1)S(1)} %shard_map.75.images_ref.refs_1_), channel_id=1, source_target_pairs={{0,32},{32,0},{1,33},{33,1},{2,34},{34,2},{3,35},{35,3},{4,36},{36... | collective-permute-start | bytes 4816904 | tf_op jit(solution)/shard_map/ppermute | solution.py:408
  33.4 2.0 %shard_map.76 = (bf16[768,1024]{1,0:T(8,128)(2,1)S(1)}, bf16[768,768]{1,0:T(8,128)(2,1)S(1)}) custom-call(s32[1]{0:T(128)} %bitcast.where_ref, f32[1]{0:T(128)S(6)} %copy.9.scale_ref, f32[1]{0:T(128)S(6)} %copy.10.shift_ref, bf16[192,1024]{1,0:T(8,128)(2,1)S(1)} %constant_dynamic-update-slice_fusion.me, bf16[192,1024]{1,0:T(8,128)(2,1)S(1)} %collective-permute-done.2.after, ...), custom_call_target="tpu_custom_call" | custom-call | flops 19327352832 | bytes 6291456 | tf_op jit(solution)/shard_map/pallas_call | solution.py:435
  36.5 2.8 %shard_map.77 = (bf16[768,768]{1,0:T(8,128)(2,1)S(1)}, f32[384,1024]{1,0:T(8,128)S(1)}) custom-call(s32[1]{0:T(128)} %bitcast.where_ref, f32[1]{0:T(128)S(6)} %copy.9.scale_ref, f32[1]{0:T(128)S(6)} %copy.10.shift_ref, bf16[768,1024]{1,0:T(8,128)(2,1)S(1)} %get-tuple-element.37.texts_ref.refs_0_, bf16[784,1024]{1,0:T(8,128)(2,1)S(1)} %collective-permute-done.9.images_ref.refs_3_), custom_call_target="tpu_custom_call" | custom-call | flops 2415919104 | bytes 8388608 | tf_op jit(solution)/shard_map/pallas_call | solution.py:439
  40.9 1.7 %shard_map.81 = (f32[96,1024]{1,0:T(8,128)S(1)}, s16[96,1408]{1,0:T(8,128)(2,1)S(1)}, s16[192,1408]{1,0:T(8,128)(2,1)S(1)}) custom-call(bf16[768,768]{1,0:T(8,128)(2,1)S(1)} %get-tuple-element.38.refs_1_.coef_ref.refs_0_, bf16[784,1024]{1,0:T(8,128)(2,1)S(1)} %shard_map.75.images_ref.refs_1_, bf16[768,768]{1,0:T(8,128)(2,1)S(1)} %get-tuple-element.39.refs_1_.refs_2_, ...), custom_call_target="tpu_custom_call" | custom-call | flops 1207959552 | bytes 6291456 | tf_op jit(solution)/shard_map/pallas_call | solution.py:445
  42.7 2.3 %collective-permute-start.22 = (s16[96,1408]{1,0:T(8,128)(2,1)S(1)}, s16[96,1408]{1,0:T(8,128)(2,1)S(1)}, u32[]{:S(2)}, u32[]{:S(2)}) collective-permute-start(s16[96,1408]{1,0:T(8,128)(2,1)S(1)} %get-tuple-element.55), channel_id=1, source_target_pairs={{0,68},{4,64},{64,4},{68,0},{1,69},{5,65},{65,5},{69,1},{2,70},{6,... | collective-permute-start | bytes 811016 | tf_op jit(solution)/shard_map/ppermute | solution.py:455
  44.9 1.6 %shard_map.85 = (s16[192,1408]{1,0:T(8,128)(2,1)S(1)}, f32[192,1024]{1,0:T(8,128)S(1)}) custom-call(bf16[768,768]{1,0:T(8,128)(2,1)S(1)} %get-tuple-element.38.refs_1_.coef_ref.refs_0_, bf16[784,1024]{1,0:T(8,128)(2,1)S(1)} %shard_map.75.images_ref.refs_1_, bf16[768,768]{1,0:T(8,128)(2,1)S(1)} %get-tuple-element.39.refs_1_.refs_2_, ...), custom_call_target="tpu_custom_call" | custom-call | flops 9663676416 | bytes 6291456 | tf_op jit(solution)/shard_map/pallas_call | solution.py:449
  46.5 2.7 %collective-permute-start.21 = (s16[192,1408]{1,0:T(8,128)(2,1)S(1)}, s16[192,1408]{1,0:T(8,128)(2,1)S(1)}, u32[]{:S(2)}, u32[]{:S(2)}) collective-permute-start(s16[192,1408]{1,0:T(8,128)(2,1)S(1)} %get-tuple-element.53), channel_id=1, source_target_pairs={{0,3},{1,0},{2,1},{3,2},{4,7},{5,4},{6,5},{7,6},{8,11},{9,8},{10,9... | collective-permute-start | bytes 1622024 | tf_op jit(solution)/shard_map/ppermute | solution.py:32
  50.4 1.7 %collective-permute-start.12 = (s16[192,1408]{1,0:T(8,128)(2,1)S(1)}, s16[192,1408]{1,0:T(8,128)(2,1)S(1)}, u32[]{:S(2)}, u32[]{:S(2)}) collective-permute-start(s16[192,1408]{1,0:T(8,128)(2,1)S(1)} %get-tuple-element.43), channel_id=1, source_target_pairs={{0,8},{8,16},{16,24},{24,0},{1,9},{9,17},{17,25},{25,1},{2,10},{10... | collective-permute-start | bytes 1622024 | tf_op jit(solution)/shard_map/ppermute | solution.py:32
  53.2 2.2 %collective-permute-start.13 = (s16[192,1408]{1,0:T(8,128)(2,1)S(1)}, s16[192,1408]{1,0:T(8,128)(2,1)S(1)}, u32[]{:S(2)}, u32[]{:S(2)}) collective-permute-start(s16[192,1408]{1,0:T(8,128)(2,1)S(1)} %get-tuple-element.44), channel_id=1, source_target_pairs={{0,24},{8,0},{16,8},{24,16},{1,25},{9,1},{17,9},{25,17},{2,26},{10... | collective-permute-start | bytes 1622024 | tf_op jit(solution)/shard_map/ppermute | solution.py:32
  55.7 3.6 %collective-permute-done.15.early_ref.right = s16[192,1408]{1,0:T(8,128)(2,1)S(1)} collective-permute-done((s16[192,1408]{1,0:T(8,128)(2,1)S(1)}, s16[192,1408]{1,0:T(8,128)(2,1)S(1)}, u32[]{:S(2)}, u32[]{:S(2)}) %collective-permute-start.15) | collective-permute-done | bytes 540704 | tf_op jit(solution)/shard_map/ppermute | solution.py:32
  60.3 1.3 %collective-permute-start.24 = (s16[96,1408]{1,0:T(8,128)(2,1)S(1)}, s16[96,1408]{1,0:T(8,128)(2,1)S(1)}, u32[]{:S(2)}, u32[]{:S(2)}) collective-permute-start(s16[96,1408]{1,0:T(8,128)(2,1)S(1)} %shard_map.88), channel_id=1, source_target_pairs={{0,68},{4,64},{64,4},{68,0},{1,69},{5,65},{65,5},{69,1},{2,70},{6,... | collective-permute-start | bytes 811016 | tf_op jit(solution)/shard_map/ppermute | solution.py:455
  61.6 2.7 %collective-permute-start.23 = (s16[96,1408]{1,0:T(8,128)(2,1)S(1)}, s16[96,1408]{1,0:T(8,128)(2,1)S(1)}, u32[]{:S(2)}, u32[]{:S(2)}) collective-permute-start(s16[96,1408]{1,0:T(8,128)(2,1)S(1)} %shard_map.87), channel_id=1, source_target_pairs={{0,2},{1,3},{2,0},{3,1},{4,6},{5,7},{6,4},{7,5},{8,10},{9,11},{10,... | collective-permute-start | bytes 811016 | tf_op jit(solution)/shard_map/ppermute | solution.py:32
  64.6 1.9 %collective-permute-start.16 = (s16[96,1408]{1,0:T(8,128)(2,1)S(1)}, s16[96,1408]{1,0:T(8,128)(2,1)S(1)}, u32[]{:S(2)}, u32[]{:S(2)}) collective-permute-start(s16[96,1408]{1,0:T(8,128)(2,1)S(1)} %shard_map.82), channel_id=1, source_target_pairs={{0,16},{8,24},{16,0},{24,8},{1,17},{9,25},{17,1},{25,9},{2,18},{10... | collective-permute-start | bytes 811016 | tf_op jit(solution)/shard_map/ppermute | solution.py:32
  67.7 1.4 %collective-permute-done.23.far = s16[96,1408]{1,0:T(8,128)(2,1)S(1)} collective-permute-done((s16[96,1408]{1,0:T(8,128)(2,1)S(1)}, s16[96,1408]{1,0:T(8,128)(2,1)S(1)}, u32[]{:S(2)}, u32[]{:S(2)}) %collective-permute-start.23) | collective-permute-done | bytes 270368 | tf_op jit(solution)/shard_map/ppermute | solution.py:32
  69.7 3.1 %collective-permute-start.25 = (bf16[96,256]{1,0:T(8,128)(2,1)S(1)}, bf16[96,256]{1,0:T(8,128)(2,1)S(1)}, u32[]{:S(2)}, u32[]{:S(2)}) collective-permute-start(bf16[96,256]{1,0:T(8,128)(2,1)S(1)} %get-tuple-element.58), channel_id=1, source_target_pairs={{0,32},{32,0},{1,33},{33,1},{2,34},{34,2},{3,35},{35,3},{4,36},{36... | collective-permute-start | bytes 147464 | tf_op jit(solution)/shard_map/ppermute | solution.py:469
  72.8 1.7 %collective-permute-start.27 = (bf16[96,256]{1,0:T(8,128)(2,1)S(1)}, bf16[96,256]{1,0:T(8,128)(2,1)S(1)}, u32[]{:S(2)}, u32[]{:S(2)}) collective-permute-start(bf16[96,256]{1,0:T(8,128)(2,1)S(1)} %get-tuple-element.60), channel_id=1, source_target_pairs={{0,96},{32,64},{64,32},{96,0},{1,97},{33,65},{65,33},{97,1},{2,98}... | collective-permute-start | bytes 147464 | tf_op jit(solution)/shard_map/ppermute | solution.py:471
  75.2 2.0 %collective-permute-start.18 = (bf16[96,256]{1,0:T(8,128)(2,1)S(1)}, bf16[96,256]{1,0:T(8,128)(2,1)S(1)}, u32[]{:S(2)}, u32[]{:S(2)}) collective-permute-start(bf16[96,256]{1,0:T(8,128)(2,1)S(1)} %get-tuple-element.49), channel_id=1, source_target_pairs={{0,32},{32,0},{1,33},{33,1},{2,34},{34,2},{3,35},{35,3},{4,36},{36... | collective-permute-start | bytes 147464 | tf_op jit(solution)/shard_map/ppermute | solution.py:469
  77.2 1.7 %collective-permute-start.20 = (bf16[96,256]{1,0:T(8,128)(2,1)S(1)}, bf16[96,256]{1,0:T(8,128)(2,1)S(1)}, u32[]{:S(2)}, u32[]{:S(2)}) collective-permute-start(bf16[96,256]{1,0:T(8,128)(2,1)S(1)} %get-tuple-element.51), channel_id=1, source_target_pairs={{0,96},{32,64},{64,32},{96,0},{1,97},{33,65},{65,33},{97,1},{2,98}... | collective-permute-start | bytes 147464 | tf_op jit(solution)/shard_map/ppermute | solution.py:471
  80.2 1.6 %collective-permute-done.20.refs_3_ = bf16[96,256]{1,0:T(8,128)(2,1)S(1)} collective-permute-done((bf16[96,256]{1,0:T(8,128)(2,1)S(1)}, bf16[96,256]{1,0:T(8,128)(2,1)S(1)}, u32[]{:S(2)}, u32[]{:S(2)}) %collective-permute-start.20) | collective-permute-done | bytes 49184 | tf_op jit(solution)/shard_map/ppermute | solution.py:471
  81.7 1.4 %shard_map.90 = s16[128,24,256]{2,1,0:T(8,128)(2,1)S(1)} custom-call(bf16[1920,384]{1,0:T(8,128)(2,1)S(1)} %get-tuple-element.34.early_a.images_ref, bf16[1344,384]{1,0:T(8,128)(2,1)S(1)} %get-tuple-element.35.early_b.texts_ref, bf16[96,256]{1,0:T(8,128)(2,1)S(1)} %get-tuple-element.48.refs_0_, bf16[96,256]{1,0:T(8,128)(2,1)S(1)} %collective-permute-done.18.refs_1_, ...), custom_call_target="tpu_custom_call" | custom-call | flops 1207959552 | bytes 6291456 | tf_op jit(solution)/shard_map/pallas_call | solution.py:477
  83.2 32.7 %all_to_all.5.coded_ref = s16[128,24,256]{2,1,0:T(8,128)(2,1)S(1)} all-to-all(s16[128,24,256]{2,1,0:T(8,128)(2,1)S(1)} %shard_map.90), channel_id=1, replica_groups=mesh['xl'=2,'core'=2,'z'=4,'xh'=2,'y'=4] {'xl','core','z','xh','y'}, dimensions={0} | all-to-all | bytes 3145728 | tf_op jit(solution)/shard_map/all_to_all | solution.py:483
  115.9 1.2 %shard_map.91 = f32[21,1024]{1,0:T(8,128)} custom-call(s16[128,24,256]{2,1,0:T(8,128)(2,1)S(1)} %all_to_all.5.coded_ref), custom_call_target="tpu_custom_call" | custom-call | bytes 2097152 | tf_op jit(solution)/shard_map/pallas_call | solution.py:484
  (62 shorter events, 11.5 us)
Async XLA Ops:
  4.9 23.4 %copy-start.1 = (bf16[384,1664]{1,0:T(8,128)(2,1)S(1)}, bf16[384,1664]{1,0:T(8,128)(2,1)}, u32[]{:S(2)}) copy-start(bf16[384,1664]{1,0:T(8,128)(2,1)} %image_feats.3) | copy-start | bytes 3833860
  4.9 23.4 %copy-start.2 = (bf16[384,1024]{1,0:T(8,128)(2,1)S(1)}, bf16[384,1024]{1,0:T(8,128)(2,1)}, u32[]{:S(2)}) copy-start(bf16[384,1024]{1,0:T(8,128)(2,1)} %text_feats.3) | copy-start | bytes 2359300
  4.9 8.1 %collective-permute-start.1 = (bf16[96,1024]{1,0:T(8,128)(2,1)}, bf16[96,1024]{1,0:T(8,128)(2,1)S(1)}, u32[]{:S(2)}, u32[]{:S(2)}) collective-permute-start(bf16[96,1024]{1,0:T(8,128)(2,1)} %get-tuple-element.36.emb), channel_id=1, source_target_pairs={{0,68},{4,64},{64,4},{68,0},{1,69},{5,65},{65,5},{69,1},{2,70},{6,... | collective-permute-start | bytes 589832 | tf_op jit(solution)/shard_map/ppermute | solution.py:401
  8.3 12.3 %collective-permute-start.6 = (bf16[208,1024]{1,0:T(8,128)(2,1)}, bf16[208,1024]{1,0:T(8,128)(2,1)S(1)}, u32[]{:S(2)}, u32[]{:S(2)}) collective-permute-start(bf16[208,1024]{1,0:T(8,128)(2,1)} %get-tuple-element.33.me.emb), channel_id=1, source_target_pairs={{0,24},{8,0},{16,8},{24,16},{1,25},{9,1},{17,9},{25,17},{2,26},{10... | collective-permute-start | bytes 1277960 | tf_op jit(solution)/shard_map/ppermute | solution.py:32
  12.1 11.9 %collective-permute-start = (bf16[208,1024]{1,0:T(8,128)(2,1)}, bf16[208,1024]{1,0:T(8,128)(2,1)S(1)}, u32[]{:S(2)}, u32[]{:S(2)}) collective-permute-start(bf16[208,1024]{1,0:T(8,128)(2,1)} %get-tuple-element.33.me.emb), channel_id=1, source_target_pairs={{0,8},{8,16},{16,24},{24,0},{1,9},{9,17},{17,25},{25,1},{2,10},{10... | collective-permute-start | bytes 1277960 | tf_op jit(solution)/shard_map/ppermute | solution.py:32
  13.1 11.0 %collective-permute-start.3 = (bf16[192,1024]{1,0:T(8,128)(2,1)S(1)}, bf16[192,1024]{1,0:T(8,128)(2,1)S(1)}, u32[]{:S(2)}, u32[]{:S(2)}) collective-permute-start(bf16[192,1024]{1,0:T(8,128)(2,1)S(1)} %constant_dynamic-update-slice_fusion.me), channel_id=1, source_target_pairs={{0,1},{1,2},{2,3},{3,0},{4,5},{5,6},{6,7},{7,4},{8,9},{9,10},{10,1... | collective-permute-start | bytes 1179656 | tf_op jit(solution)/shard_map/ppermute | solution.py:32
  14.4 11.0 %collective-permute-start.2 = (bf16[192,1024]{1,0:T(8,128)(2,1)S(1)}, bf16[192,1024]{1,0:T(8,128)(2,1)S(1)}, u32[]{:S(2)}, u32[]{:S(2)}) collective-permute-start(bf16[192,1024]{1,0:T(8,128)(2,1)S(1)} %constant_dynamic-update-slice_fusion.me), channel_id=1, source_target_pairs={{0,3},{1,0},{2,1},{3,2},{4,7},{5,4},{6,5},{7,6},{8,11},{9,8},{10,9... | collective-permute-start | bytes 1179656 | tf_op jit(solution)/shard_map/ppermute | solution.py:32
  20.6 9.9 %collective-permute-start.8 = (bf16[112,1024]{1,0:T(8,128)(2,1)S(1)}, bf16[112,1024]{1,0:T(8,128)(2,1)S(1)}, u32[]{:S(2)}, u32[]{:S(2)}) collective-permute-start(bf16[112,1024]{1,0:T(8,128)(2,1)S(1)} %slice.19), channel_id=1, source_target_pairs={{0,24},{8,0},{16,8},{24,16},{1,25},{9,1},{17,9},{25,17},{2,26},{10... | collective-permute-start | bytes 688136 | tf_op jit(solution)/shard_map/ppermute | solution.py:32
  24.0 6.5 %collective-permute-start.7 = (bf16[96,1024]{1,0:T(8,128)(2,1)S(1)}, bf16[96,1024]{1,0:T(8,128)(2,1)S(1)}, u32[]{:S(2)}, u32[]{:S(2)}) collective-permute-start(bf16[96,1024]{1,0:T(8,128)(2,1)S(1)} %slice.18), channel_id=1, source_target_pairs={{0,8},{8,16},{16,24},{24,0},{1,9},{9,17},{17,25},{25,1},{2,10},{10... | collective-permute-start | bytes 589832 | tf_op jit(solution)/shard_map/ppermute | solution.py:32
  24.1 9.3 %collective-permute-start.4 = (bf16[96,1024]{1,0:T(8,128)(2,1)S(1)}, bf16[96,1024]{1,0:T(8,128)(2,1)S(1)}, u32[]{:S(2)}, u32[]{:S(2)}) collective-permute-start(bf16[96,1024]{1,0:T(8,128)(2,1)S(1)} %slice.16), channel_id=1, source_target_pairs={{0,1},{1,2},{2,3},{3,0},{4,5},{5,6},{6,7},{7,4},{8,9},{9,10},{10,1... | collective-permute-start | bytes 589832 | tf_op jit(solution)/shard_map/ppermute | solution.py:32
  25.5 7.9 %collective-permute-start.5 = (bf16[96,1024]{1,0:T(8,128)(2,1)S(1)}, bf16[96,1024]{1,0:T(8,128)(2,1)S(1)}, u32[]{:S(2)}, u32[]{:S(2)}) collective-permute-start(bf16[96,1024]{1,0:T(8,128)(2,1)S(1)} %slice.17), channel_id=1, source_target_pairs={{0,3},{1,0},{2,1},{3,2},{4,7},{5,4},{6,5},{7,6},{8,11},{9,8},{10,9... | collective-permute-start | bytes 589832 | tf_op jit(solution)/shard_map/ppermute | solution.py:32
  30.7 5.8 %collective-permute-start.9 = (bf16[784,1024]{1,0:T(8,128)(2,1)S(1)}, bf16[784,1024]{1,0:T(8,128)(2,1)S(1)}, u32[]{:S(2)}, u32[]{:S(2)}) collective-permute-start(bf16[784,1024]{1,0:T(8,128)(2,1)S(1)} %shard_map.75.images_ref.refs_1_), channel_id=1, source_target_pairs={{0,32},{32,0},{1,33},{33,1},{2,34},{34,2},{3,35},{35,3},{4,36},{36... | collective-permute-start | bytes 4816904 | tf_op jit(solution)/shard_map/ppermute | solution.py:408
  39.3 10.0 %collective-permute-start.11 = (f32[384,1024]{1,0:T(8,128)S(1)}, f32[384,1024]{1,0:T(8,128)S(1)}, u32[]{:S(2)}, u32[]{:S(2)}) collective-permute-start(f32[384,1024]{1,0:T(8,128)S(1)} %get-tuple-element.40), channel_id=1, source_target_pairs={{0,32},{32,0},{1,33},{33,1},{2,34},{34,2},{3,35},{35,3},{4,36},{36... | collective-permute-start | bytes 4718600 | tf_op jit(solution)/shard_map/ppermute | solution.py:443
  40.7 11.4 %collective-permute-start.10 = (f32[384,1024]{1,0:T(8,128)S(1)}, f32[384,1024]{1,0:T(8,128)S(1)}, u32[]{:S(2)}, u32[]{:S(2)}) collective-permute-start(f32[384,1024]{1,0:T(8,128)S(1)} %shard_map.78), channel_id=1, source_target_pairs={{0,32},{32,0},{1,33},{33,1},{2,34},{34,2},{3,35},{35,3},{4,36},{36... | collective-permute-start | bytes 4718600 | tf_op jit(solution)/shard_map/ppermute | solution.py:447
  42.7 12.7 %collective-permute-start.22 = (s16[96,1408]{1,0:T(8,128)(2,1)S(1)}, s16[96,1408]{1,0:T(8,128)(2,1)S(1)}, u32[]{:S(2)}, u32[]{:S(2)}) collective-permute-start(s16[96,1408]{1,0:T(8,128)(2,1)S(1)} %get-tuple-element.55), channel_id=1, source_target_pairs={{0,68},{4,64},{64,4},{68,0},{1,69},{5,65},{65,5},{69,1},{2,70},{6,... | collective-permute-start | bytes 811016 | tf_op jit(solution)/shard_map/ppermute | solution.py:455
  44.9 14.4 %collective-permute-start.15 = (s16[192,1408]{1,0:T(8,128)(2,1)S(1)}, s16[192,1408]{1,0:T(8,128)(2,1)S(1)}, u32[]{:S(2)}, u32[]{:S(2)}) collective-permute-start(s16[192,1408]{1,0:T(8,128)(2,1)S(1)} %get-tuple-element.46), channel_id=1, source_target_pairs={{0,1},{1,2},{2,3},{3,0},{4,5},{5,6},{6,7},{7,4},{8,9},{9,10},{10,1... | collective-permute-start | bytes 1622024 | tf_op jit(solution)/shard_map/ppermute | solution.py:32
  46.5 13.4 %collective-permute-start.21 = (s16[192,1408]{1,0:T(8,128)(2,1)S(1)}, s16[192,1408]{1,0:T(8,128)(2,1)S(1)}, u32[]{:S(2)}, u32[]{:S(2)}) collective-permute-start(s16[192,1408]{1,0:T(8,128)(2,1)S(1)} %get-tuple-element.53), channel_id=1, source_target_pairs={{0,3},{1,0},{2,1},{3,2},{4,7},{5,4},{6,5},{7,6},{8,11},{9,8},{10,9... | collective-permute-start | bytes 1622024 | tf_op jit(solution)/shard_map/ppermute | solution.py:32
  50.4 16.1 %collective-permute-start.12 = (s16[192,1408]{1,0:T(8,128)(2,1)S(1)}, s16[192,1408]{1,0:T(8,128)(2,1)S(1)}, u32[]{:S(2)}, u32[]{:S(2)}) collective-permute-start(s16[192,1408]{1,0:T(8,128)(2,1)S(1)} %get-tuple-element.43), channel_id=1, source_target_pairs={{0,8},{8,16},{16,24},{24,0},{1,9},{9,17},{17,25},{25,1},{2,10},{10... | collective-permute-start | bytes 1622024 | tf_op jit(solution)/shard_map/ppermute | solution.py:32
  53.2 13.3 %collective-permute-start.13 = (s16[192,1408]{1,0:T(8,128)(2,1)S(1)}, s16[192,1408]{1,0:T(8,128)(2,1)S(1)}, u32[]{:S(2)}, u32[]{:S(2)}) collective-permute-start(s16[192,1408]{1,0:T(8,128)(2,1)S(1)} %get-tuple-element.44), channel_id=1, source_target_pairs={{0,24},{8,0},{16,8},{24,16},{1,25},{9,1},{17,9},{25,17},{2,26},{10... | collective-permute-start | bytes 1622024 | tf_op jit(solution)/shard_map/ppermute | solution.py:32
  55.4 8.9 %collective-permute-start.14 = (s16[96,1408]{1,0:T(8,128)(2,1)S(1)}, s16[96,1408]{1,0:T(8,128)(2,1)S(1)}, u32[]{:S(2)}, u32[]{:S(2)}) collective-permute-start(s16[96,1408]{1,0:T(8,128)(2,1)S(1)} %get-tuple-element.45), channel_id=1, source_target_pairs={{0,64},{64,0},{1,65},{65,1},{2,66},{66,2},{3,67},{67,3},{4,68},{68... | collective-permute-start | bytes 811016 | tf_op jit(solution)/shard_map/ppermute | solution.py:458
  60.3 7.4 %collective-permute-start.24 = (s16[96,1408]{1,0:T(8,128)(2,1)S(1)}, s16[96,1408]{1,0:T(8,128)(2,1)S(1)}, u32[]{:S(2)}, u32[]{:S(2)}) collective-permute-start(s16[96,1408]{1,0:T(8,128)(2,1)S(1)} %shard_map.88), channel_id=1, source_target_pairs={{0,68},{4,64},{64,4},{68,0},{1,69},{5,65},{65,5},{69,1},{2,70},{6,... | collective-permute-start | bytes 811016 | tf_op jit(solution)/shard_map/ppermute | solution.py:455
  61.6 7.5 %copy-start.3 = (bf16[96,1024]{1,0:T(8,128)(2,1)S(1)}, bf16[96,1024]{1,0:T(8,128)(2,1)}, u32[]{:S(2)}) copy-start(bf16[96,1024]{1,0:T(8,128)(2,1)} %get-tuple-element.36.emb) | copy-start | bytes 589828
  61.6 7.4 %collective-permute-start.23 = (s16[96,1408]{1,0:T(8,128)(2,1)S(1)}, s16[96,1408]{1,0:T(8,128)(2,1)S(1)}, u32[]{:S(2)}, u32[]{:S(2)}) collective-permute-start(s16[96,1408]{1,0:T(8,128)(2,1)S(1)} %shard_map.87), channel_id=1, source_target_pairs={{0,2},{1,3},{2,0},{3,1},{4,6},{5,7},{6,4},{7,5},{8,10},{9,11},{10,... | collective-permute-start | bytes 811016 | tf_op jit(solution)/shard_map/ppermute | solution.py:32
  64.6 9.9 %collective-permute-start.16 = (s16[96,1408]{1,0:T(8,128)(2,1)S(1)}, s16[96,1408]{1,0:T(8,128)(2,1)S(1)}, u32[]{:S(2)}, u32[]{:S(2)}) collective-permute-start(s16[96,1408]{1,0:T(8,128)(2,1)S(1)} %shard_map.82), channel_id=1, source_target_pairs={{0,16},{8,24},{16,0},{24,8},{1,17},{9,25},{17,1},{25,9},{2,18},{10... | collective-permute-start | bytes 811016 | tf_op jit(solution)/shard_map/ppermute | solution.py:32
  66.9 7.7 %copy-start.4 = (f32[96,128]{1,0:T(8,128)S(1)}, f32[96,128]{1,0:T(8,128)}, u32[]{:S(2)}) copy-start(f32[96,128]{1,0:T(8,128)} %get-tuple-element.47.inverse) | copy-start | bytes 147460
  66.9 7.7 %collective-permute-start.17 = (s16[96,1408]{1,0:T(8,128)(2,1)S(1)}, s16[96,1408]{1,0:T(8,128)(2,1)S(1)}, u32[]{:S(2)}, u32[]{:S(2)}) collective-permute-start(s16[96,1408]{1,0:T(8,128)(2,1)S(1)} %shard_map.83), channel_id=1, source_target_pairs={{0,64},{64,0},{1,65},{65,1},{2,66},{66,2},{3,67},{67,3},{4,68},{68... | collective-permute-start | bytes 811016 | tf_op jit(solution)/shard_map/ppermute | solution.py:458
  69.7 7.5 %collective-permute-start.25 = (bf16[96,256]{1,0:T(8,128)(2,1)S(1)}, bf16[96,256]{1,0:T(8,128)(2,1)S(1)}, u32[]{:S(2)}, u32[]{:S(2)}) collective-permute-start(bf16[96,256]{1,0:T(8,128)(2,1)S(1)} %get-tuple-element.58), channel_id=1, source_target_pairs={{0,32},{32,0},{1,33},{33,1},{2,34},{34,2},{3,35},{35,3},{4,36},{36... | collective-permute-start | bytes 147464 | tf_op jit(solution)/shard_map/ppermute | solution.py:469
  72.8 6.1 %collective-permute-start.26 = (bf16[96,256]{1,0:T(8,128)(2,1)S(1)}, bf16[96,256]{1,0:T(8,128)(2,1)S(1)}, u32[]{:S(2)}, u32[]{:S(2)}) collective-permute-start(bf16[96,256]{1,0:T(8,128)(2,1)S(1)} %get-tuple-element.59), channel_id=1, source_target_pairs={{0,64},{64,0},{1,65},{65,1},{2,66},{66,2},{3,67},{67,3},{4,68},{68... | collective-permute-start | bytes 147464 | tf_op jit(solution)/shard_map/ppermute | solution.py:470
  72.8 6.1 %collective-permute-start.27 = (bf16[96,256]{1,0:T(8,128)(2,1)S(1)}, bf16[96,256]{1,0:T(8,128)(2,1)S(1)}, u32[]{:S(2)}, u32[]{:S(2)}) collective-permute-start(bf16[96,256]{1,0:T(8,128)(2,1)S(1)} %get-tuple-element.60), channel_id=1, source_target_pairs={{0,96},{32,64},{64,32},{96,0},{1,97},{33,65},{65,33},{97,1},{2,98}... | collective-permute-start | bytes 147464 | tf_op jit(solution)/shard_map/ppermute | solution.py:471
  75.2 3.8 %collective-permute-start.18 = (bf16[96,256]{1,0:T(8,128)(2,1)S(1)}, bf16[96,256]{1,0:T(8,128)(2,1)S(1)}, u32[]{:S(2)}, u32[]{:S(2)}) collective-permute-start(bf16[96,256]{1,0:T(8,128)(2,1)S(1)} %get-tuple-element.49), channel_id=1, source_target_pairs={{0,32},{32,0},{1,33},{33,1},{2,34},{34,2},{3,35},{35,3},{4,36},{36... | collective-permute-start | bytes 147464 | tf_op jit(solution)/shard_map/ppermute | solution.py:469
  77.2 3.0 %collective-permute-start.19 = (bf16[96,256]{1,0:T(8,128)(2,1)S(1)}, bf16[96,256]{1,0:T(8,128)(2,1)S(1)}, u32[]{:S(2)}, u32[]{:S(2)}) collective-permute-start(bf16[96,256]{1,0:T(8,128)(2,1)S(1)} %get-tuple-element.50), channel_id=1, source_target_pairs={{0,64},{64,0},{1,65},{65,1},{2,66},{66,2},{3,67},{67,3},{4,68},{68... | collective-permute-start | bytes 147464 | tf_op jit(solution)/shard_map/ppermute | solution.py:470
  77.2 4.5 %collective-permute-start.20 = (bf16[96,256]{1,0:T(8,128)(2,1)S(1)}, bf16[96,256]{1,0:T(8,128)(2,1)S(1)}, u32[]{:S(2)}, u32[]{:S(2)}) collective-permute-start(bf16[96,256]{1,0:T(8,128)(2,1)S(1)} %get-tuple-element.51), channel_id=1, source_target_pairs={{0,96},{32,64},{64,32},{96,0},{1,97},{33,65},{65,33},{97,1},{2,98}... | collective-permute-start | bytes 147464 | tf_op jit(solution)/shard_map/ppermute | solution.py:471
  (2 other events, 9.7 us)

commit v8 on v7

--- a/solution.py
+++ b/solution.py
@@ -275,10 +275,9 @@
     given_ref[...] = image_terms(coef_ref, texts_ref, 1)
 
 
-def text_kernel(part, own_coef, images_ref, others_coef, others_ref, *outs):
-    rows = slice(part * ROWS, (part + 1) * ROWS)
-    got = jnp.dot(own_coef[rows, :], images_ref[:TILE, :], preferred_element_type=F32)
-    got += jnp.dot(others_coef[rows, :], others_ref[:TILE, :], preferred_element_type=F32)
+def text_kernel(own_coef, images_ref, others_coef, others_ref, *outs):
+    got = jnp.dot(own_coef[...], images_ref[:TILE, :], preferred_element_type=F32)
+    got += jnp.dot(others_coef[...], others_ref[:TILE, :], preferred_element_type=F32)
     share_out(got, outs)
 
 
@@ -442,11 +441,11 @@
     )(where, log_scale, logit_bias, texts, others)
     taken = lax.ppermute(given, "core", SWAP)
     sides = own_coef, images, others_coef, others
-    text_ways = run(text_kernel, ways, 1, 4, 0)(*sides)
+    text_parts = run(text_kernel, ways + rest, 2, 4)(*sides)
+    text_ways, text_rest = text_parts[:3], text_parts[3:]
     given_rest, = run(given_rest_kernel, [shape(ROWS, E)], 0.5, 2)(texts, others_coef)
     taken_rest = lax.ppermute(given_rest, "core", SWAP)
     image_ways = run(kept_kernel, ways, 0.5, 3, 0)(texts, own_coef, taken)
-    text_rest = run(text_kernel, rest, 8, 4, 1)(*sides)
     image_rest = call(
         kept_rest_kernel, rest, 4 * flops, 6 << 20, 24,
         in_specs=[VMEM] * 3 + [ANY], out_specs=[VMEM] * 2,

time: 117 us -> 117 us (level)
  starting transfers between devices: 43.4 us -> 41.4 us
  waiting for transfers between devices: 14.9 us -> 16.5 us
    ppermute x2, waiting for transfers between devices: 0.73 us -> 2.08 us  [body(): lax.ppermute(a, ('xl', 'xh'), FLIP)]
    pallas_call x2 -> x1, Pallas kernels: 3.3 us -> 3.09 us  [body(): text_parts = run(text_kernel, ways + rest, 2, 4)(*sides)]
  transfers between devices with their start and end apart: 28 -> 28, of which waited for: 8 -> 7; matrix products, arithmetic and copies ran while one was open for 1% -> 1% of each run, Pallas kernels for 11% -> 11%
where the time goes in v8:
time: 117 us
  starting transfers between devices  41.4 us (35%)
  blocking collectives  33 us (28%)
  Pallas kernels  23.3 us (20%)
  waiting for transfers between devices  16.5 us (14%)
  between operations  1.59 us (1%)
    all_to_all x1, blocking collectives, body(): coded = lax.all_to_all(coded, AXES, split_axis=0, concat_axis=0, tiled=True)  33 us
    ppermute x14, starting transfers between devices, shifted(): return lax.ppermute(array, axis, [(i, (i + by) % 4) for i in range(4)])  23.8 us
    ppermute x14, waiting for transfers between devices, shifted(): return lax.ppermute(array, axis, [(i, (i + by) % 4) for i in range(4)])  10.5 us
    pallas_call x1, Pallas kernels, body(): call(embed_kernel, [shape(QUARTER, E, dtype=BF16), shape(QUARTER, 128), s...  4.89 us
    ppermute x2, starting transfers between devices, tower_pieces(): lax.ppermute(other_core, 'core', SWAP)  4.29 us
    ppermute x2, starting transfers between devices, tower_pieces(): lax.ppermute(other_both, TOWER, [(i, 3 - i) for i in range(4)])  3.44 us
    ppermute x1, starting transfers between devices, body(): other_texts = lax.ppermute(own_texts, ('xl', 'xh'), FLIP)  3.39 us
    pallas_call x1, Pallas kernels, body(): text_parts = run(text_kernel, ways + rest, 2, 4)(*sides)  3.09 us
  transfers between devices with their start and end apart: 28, of which 7 were waited for; matrix products, arithmetic and copies ran while one was open for 1% of the time, Pallas kernels for 11%

profile of v8, /device:TPU:1, one launch (start us, length us, event | category | flops | bytes accessed | tf_op | source)
XLA Modules:
  0.0 116.9 jit_solution(3992080304042382767)
XLA Ops:
  0.0 4.9 %shard_map.73 = (bf16[96,1024]{1,0:T(8,128)(2,1)}, f32[96,128]{1,0:T(8,128)}, bf16[208,1024]{1,0:T(8,128)(2,1)}, f32[96,128]{1,0:T(8,128)}) custom-call(s32[1]{0:T(128)} %bitcast.where_ref, s32[3,128]{1,0:T(4,128)} %bitcast.2, bf16[384,1024]{1,0:T(8,128)(2,1)} %text_feats.3, bf16[384,1664]{1,0:T(8,128)(2,1)} %image_feats.3, bf16[1024,1024]{1,0:T(8,128)(2,1)} %text_weight.1, ...), custom_call_target="tpu_custom_call" | custom-call | flops 855638016 | bytes 8388608 | tf_op jit(solution)/shard_map/pallas_call | solution.py:385
  4.9 3.4 %collective-permute-start.1 = (bf16[96,1024]{1,0:T(8,128)(2,1)}, bf16[96,1024]{1,0:T(8,128)(2,1)S(1)}, u32[]{:S(2)}, u32[]{:S(2)}) collective-permute-start(bf16[96,1024]{1,0:T(8,128)(2,1)} %get-tuple-element.36.emb), channel_id=1, source_target_pairs={{0,68},{4,64},{64,4},{68,0},{1,69},{5,65},{65,5},{69,1},{2,70},{6,... | collective-permute-start | bytes 589832 | tf_op jit(solution)/shard_map/ppermute | solution.py:400
  8.3 3.8 %collective-permute-start.6 = (bf16[208,1024]{1,0:T(8,128)(2,1)}, bf16[208,1024]{1,0:T(8,128)(2,1)S(1)}, u32[]{:S(2)}, u32[]{:S(2)}) collective-permute-start(bf16[208,1024]{1,0:T(8,128)(2,1)} %get-tuple-element.33.me.emb), channel_id=1, source_target_pairs={{0,24},{8,0},{16,8},{24,16},{1,25},{9,1},{17,9},{25,17},{2,26},{10... | collective-permute-start | bytes 1277960 | tf_op jit(solution)/shard_map/ppermute | solution.py:32
  13.1 1.4 %collective-permute-start.3 = (bf16[192,1024]{1,0:T(8,128)(2,1)S(1)}, bf16[192,1024]{1,0:T(8,128)(2,1)S(1)}, u32[]{:S(2)}, u32[]{:S(2)}) collective-permute-start(bf16[192,1024]{1,0:T(8,128)(2,1)S(1)} %constant_dynamic-update-slice_fusion.me), channel_id=1, source_target_pairs={{0,1},{1,2},{2,3},{3,0},{4,5},{5,6},{6,7},{7,4},{8,9},{9,10},{10,1... | collective-permute-start | bytes 1179656 | tf_op jit(solution)/shard_map/ppermute | solution.py:32
  14.4 1.5 %collective-permute-start.2 = (bf16[192,1024]{1,0:T(8,128)(2,1)S(1)}, bf16[192,1024]{1,0:T(8,128)(2,1)S(1)}, u32[]{:S(2)}, u32[]{:S(2)}) collective-permute-start(bf16[192,1024]{1,0:T(8,128)(2,1)S(1)} %constant_dynamic-update-slice_fusion.me), channel_id=1, source_target_pairs={{0,3},{1,0},{2,1},{3,2},{4,7},{5,4},{6,5},{7,6},{8,11},{9,8},{10,9... | collective-permute-start | bytes 1179656 | tf_op jit(solution)/shard_map/ppermute | solution.py:32
  15.9 4.6 %collective-permute-done.6.after = bf16[208,1024]{1,0:T(8,128)(2,1)S(1)} collective-permute-done((bf16[208,1024]{1,0:T(8,128)(2,1)}, bf16[208,1024]{1,0:T(8,128)(2,1)S(1)}, u32[]{:S(2)}, u32[]{:S(2)}) %collective-permute-start.6) | collective-permute-done | bytes 426016 | tf_op jit(solution)/shard_map/ppermute | solution.py:32
  20.6 3.4 %collective-permute-start.8 = (bf16[112,1024]{1,0:T(8,128)(2,1)S(1)}, bf16[112,1024]{1,0:T(8,128)(2,1)S(1)}, u32[]{:S(2)}, u32[]{:S(2)}) collective-permute-start(bf16[112,1024]{1,0:T(8,128)(2,1)S(1)} %slice.19), channel_id=1, source_target_pairs={{0,24},{8,0},{16,8},{24,16},{1,25},{9,1},{17,9},{25,17},{2,26},{10... | collective-permute-start | bytes 688136 | tf_op jit(solution)/shard_map/ppermute | solution.py:32
  24.1 1.4 %collective-permute-start.4 = (bf16[96,1024]{1,0:T(8,128)(2,1)S(1)}, bf16[96,1024]{1,0:T(8,128)(2,1)S(1)}, u32[]{:S(2)}, u32[]{:S(2)}) collective-permute-start(bf16[96,1024]{1,0:T(8,128)(2,1)S(1)} %slice.16), channel_id=1, source_target_pairs={{0,1},{1,2},{2,3},{3,0},{4,5},{5,6},{6,7},{7,4},{8,9},{9,10},{10,1... | collective-permute-start | bytes 589832 | tf_op jit(solution)/shard_map/ppermute | solution.py:32
  25.5 1.5 %collective-permute-start.5 = (bf16[96,1024]{1,0:T(8,128)(2,1)S(1)}, bf16[96,1024]{1,0:T(8,128)(2,1)S(1)}, u32[]{:S(2)}, u32[]{:S(2)}) collective-permute-start(bf16[96,1024]{1,0:T(8,128)(2,1)S(1)} %slice.17), channel_id=1, source_target_pairs={{0,3},{1,0},{2,1},{3,2},{4,7},{5,4},{6,5},{7,6},{8,11},{9,8},{10,9... | collective-permute-start | bytes 589832 | tf_op jit(solution)/shard_map/ppermute | solution.py:32
  28.3 2.2 %shard_map.74 = (bf16[1920,384]{1,0:T(8,128)(2,1)S(1)}, bf16[1344,384]{1,0:T(8,128)(2,1)S(1)}) custom-call(s32[1]{0:T(128)} %bitcast.where_ref, bf16[384,1664]{1,0:T(8,128)(2,1)S(1)} %copy-done.1, bf16[384,1024]{1,0:T(8,128)(2,1)S(1)} %copy-done.2, bf16[208,1024]{1,0:T(8,128)(2,1)S(1)} %collective-permute-done.early.before), custom_call_target="tpu_custom_call" | custom-call | flops 962592768 | bytes 5242880 | tf_op jit(solution)/shard_map/pallas_call | solution.py:410
  30.7 2.7 %collective-permute-start.9 = (bf16[784,1024]{1,0:T(8,128)(2,1)S(1)}, bf16[784,1024]{1,0:T(8,128)(2,1)S(1)}, u32[]{:S(2)}, u32[]{:S(2)}) collective-permute-start(bf16[784,1024]{1,0:T(8,128)(2,1)S(1)} %shard_map.75.images_ref.refs_1_), channel_id=1, source_target_pairs={{0,32},{32,0},{1,33},{33,1},{2,34},{34,2},{3,35},{35,3},{4,36},{36... | collective-permute-start | bytes 4816904 | tf_op jit(solution)/shard_map/ppermute | solution.py:407
  33.4 2.0 %shard_map.76 = (bf16[768,1024]{1,0:T(8,128)(2,1)S(1)}, bf16[768,768]{1,0:T(8,128)(2,1)S(1)}) custom-call(s32[1]{0:T(128)} %bitcast.where_ref, f32[1]{0:T(128)S(6)} %copy.9.scale_ref, f32[1]{0:T(128)S(6)} %copy.10.shift_ref, bf16[192,1024]{1,0:T(8,128)(2,1)S(1)} %constant_dynamic-update-slice_fusion.me, bf16[192,1024]{1,0:T(8,128)(2,1)S(1)} %collective-permute-done.2.after, ...), custom_call_target="tpu_custom_call" | custom-call | flops 19327352832 | bytes 6291456 | tf_op jit(solution)/shard_map/pallas_call | solution.py:434
  36.5 2.8 %shard_map.77 = (bf16[768,768]{1,0:T(8,128)(2,1)S(1)}, f32[384,1024]{1,0:T(8,128)S(1)}) custom-call(s32[1]{0:T(128)} %bitcast.where_ref, f32[1]{0:T(128)S(6)} %copy.9.scale_ref, f32[1]{0:T(128)S(6)} %copy.10.shift_ref, bf16[768,1024]{1,0:T(8,128)(2,1)S(1)} %get-tuple-element.37.texts_ref.refs_0_, bf16[784,1024]{1,0:T(8,128)(2,1)S(1)} %collective-permute-done.9.images_ref.refs_3_), custom_call_target="tpu_custom_call" | custom-call | flops 2415919104 | bytes 8388608 | tf_op jit(solution)/shard_map/pallas_call | solution.py:438
  40.9 3.1 %shard_map.81 = (f32[96,1024]{1,0:T(8,128)S(1)}, s16[96,1408]{1,0:T(8,128)(2,1)S(1)}, s16[192,1408]{1,0:T(8,128)(2,1)S(1)}, s16[192,1408]{1,0:T(8,128)(2,1)S(1)}, f32[192,1024]{1,0:T(8,128)S(1)}) custom-call(bf16[768,768]{1,0:T(8,128)(2,1)S(1)} %get-tuple-element.38.refs_1_.coef_ref.refs_0_, bf16[784,1024]{1,0:T(8,128)(2,1)S(1)} %shard_map.75.images_ref.refs_1_, ...), custom_call_target="tpu_custom_call" | custom-call | flops 2415919104 | bytes 6291456 | tf_op jit(solution)/shard_map/pallas_call | solution.py:444
  44.0 2.3 %collective-permute-start.22 = (s16[96,1408]{1,0:T(8,128)(2,1)S(1)}, s16[96,1408]{1,0:T(8,128)(2,1)S(1)}, u32[]{:S(2)}, u32[]{:S(2)}) collective-permute-start(s16[96,1408]{1,0:T(8,128)(2,1)S(1)} %get-tuple-element.55), channel_id=1, source_target_pairs={{0,68},{4,64},{64,4},{68,0},{1,69},{5,65},{65,5},{69,1},{2,70},{6,... | collective-permute-start | bytes 811016 | tf_op jit(solution)/shard_map/ppermute | solution.py:454
  46.3 2.7 %collective-permute-start.21 = (s16[192,1408]{1,0:T(8,128)(2,1)S(1)}, s16[192,1408]{1,0:T(8,128)(2,1)S(1)}, u32[]{:S(2)}, u32[]{:S(2)}) collective-permute-start(s16[192,1408]{1,0:T(8,128)(2,1)S(1)} %get-tuple-element.53), channel_id=1, source_target_pairs={{0,3},{1,0},{2,1},{3,2},{4,7},{5,4},{6,5},{7,6},{8,11},{9,8},{10,9... | collective-permute-start | bytes 1622024 | tf_op jit(solution)/shard_map/ppermute | solution.py:32
  49.0 1.2 shard_map.79
  50.2 1.7 %collective-permute-start.12 = (s16[192,1408]{1,0:T(8,128)(2,1)S(1)}, s16[192,1408]{1,0:T(8,128)(2,1)S(1)}, u32[]{:S(2)}, u32[]{:S(2)}) collective-permute-start(s16[192,1408]{1,0:T(8,128)(2,1)S(1)} %get-tuple-element.43), channel_id=1, source_target_pairs={{0,8},{8,16},{16,24},{24,0},{1,9},{9,17},{17,25},{25,1},{2,10},{10... | collective-permute-start | bytes 1622024 | tf_op jit(solution)/shard_map/ppermute | solution.py:32
  52.9 2.2 %collective-permute-start.13 = (s16[192,1408]{1,0:T(8,128)(2,1)S(1)}, s16[192,1408]{1,0:T(8,128)(2,1)S(1)}, u32[]{:S(2)}, u32[]{:S(2)}) collective-permute-start(s16[192,1408]{1,0:T(8,128)(2,1)S(1)} %get-tuple-element.44), channel_id=1, source_target_pairs={{0,24},{8,0},{16,8},{24,16},{1,25},{9,1},{17,9},{25,17},{2,26},{10... | collective-permute-start | bytes 1622024 | tf_op jit(solution)/shard_map/ppermute | solution.py:32
  55.4 5.3 %collective-permute-done.15.early_ref.right = s16[192,1408]{1,0:T(8,128)(2,1)S(1)} collective-permute-done((s16[192,1408]{1,0:T(8,128)(2,1)S(1)}, s16[192,1408]{1,0:T(8,128)(2,1)S(1)}, u32[]{:S(2)}, u32[]{:S(2)}) %collective-permute-start.15) | collective-permute-done | bytes 540704 | tf_op jit(solution)/shard_map/ppermute | solution.py:32
  61.7 2.4 %collective-permute-start.23 = (s16[96,1408]{1,0:T(8,128)(2,1)S(1)}, s16[96,1408]{1,0:T(8,128)(2,1)S(1)}, u32[]{:S(2)}, u32[]{:S(2)}) collective-permute-start(s16[96,1408]{1,0:T(8,128)(2,1)S(1)} %shard_map.86), channel_id=1, source_target_pairs={{0,2},{1,3},{2,0},{3,1},{4,6},{5,7},{6,4},{7,5},{8,10},{9,11},{10,... | collective-permute-start | bytes 811016 | tf_op jit(solution)/shard_map/ppermute | solution.py:32
  64.3 1.9 %collective-permute-start.16 = (s16[96,1408]{1,0:T(8,128)(2,1)S(1)}, s16[96,1408]{1,0:T(8,128)(2,1)S(1)}, u32[]{:S(2)}, u32[]{:S(2)}) collective-permute-start(s16[96,1408]{1,0:T(8,128)(2,1)S(1)} %shard_map.82), channel_id=1, source_target_pairs={{0,16},{8,24},{16,0},{24,8},{1,17},{9,25},{17,1},{25,9},{2,18},{10... | collective-permute-start | bytes 811016 | tf_op jit(solution)/shard_map/ppermute | solution.py:32
  66.7 2.1 %collective-permute-done.24.got = s16[96,1408]{1,0:T(8,128)(2,1)S(1)} collective-permute-done((s16[96,1408]{1,0:T(8,128)(2,1)S(1)}, s16[96,1408]{1,0:T(8,128)(2,1)S(1)}, u32[]{:S(2)}, u32[]{:S(2)}) %collective-permute-start.24) | collective-permute-done | bytes 270368 | tf_op jit(solution)/shard_map/ppermute | solution.py:454
  70.0 2.8 %collective-permute-start.25 = (bf16[96,256]{1,0:T(8,128)(2,1)S(1)}, bf16[96,256]{1,0:T(8,128)(2,1)S(1)}, u32[]{:S(2)}, u32[]{:S(2)}) collective-permute-start(bf16[96,256]{1,0:T(8,128)(2,1)S(1)} %get-tuple-element.58), channel_id=1, source_target_pairs={{0,32},{32,0},{1,33},{33,1},{2,34},{34,2},{3,35},{35,3},{4,36},{36... | collective-permute-start | bytes 147464 | tf_op jit(solution)/shard_map/ppermute | solution.py:468
  72.9 1.7 %collective-permute-start.27 = (bf16[96,256]{1,0:T(8,128)(2,1)S(1)}, bf16[96,256]{1,0:T(8,128)(2,1)S(1)}, u32[]{:S(2)}, u32[]{:S(2)}) collective-permute-start(bf16[96,256]{1,0:T(8,128)(2,1)S(1)} %get-tuple-element.60), channel_id=1, source_target_pairs={{0,96},{32,64},{64,32},{96,0},{1,97},{33,65},{65,33},{97,1},{2,98}... | collective-permute-start | bytes 147464 | tf_op jit(solution)/shard_map/ppermute | solution.py:470
  75.2 1.5 %collective-permute-start.18 = (bf16[96,256]{1,0:T(8,128)(2,1)S(1)}, bf16[96,256]{1,0:T(8,128)(2,1)S(1)}, u32[]{:S(2)}, u32[]{:S(2)}) collective-permute-start(bf16[96,256]{1,0:T(8,128)(2,1)S(1)} %get-tuple-element.49), channel_id=1, source_target_pairs={{0,32},{32,0},{1,33},{33,1},{2,34},{34,2},{3,35},{35,3},{4,36},{36... | collective-permute-start | bytes 147464 | tf_op jit(solution)/shard_map/ppermute | solution.py:468
  76.7 1.7 %collective-permute-start.20 = (bf16[96,256]{1,0:T(8,128)(2,1)S(1)}, bf16[96,256]{1,0:T(8,128)(2,1)S(1)}, u32[]{:S(2)}, u32[]{:S(2)}) collective-permute-start(bf16[96,256]{1,0:T(8,128)(2,1)S(1)} %get-tuple-element.51), channel_id=1, source_target_pairs={{0,96},{32,64},{64,32},{96,0},{1,97},{33,65},{65,33},{97,1},{2,98}... | collective-permute-start | bytes 147464 | tf_op jit(solution)/shard_map/ppermute | solution.py:470
  78.4 1.2 %collective-permute-done.19.refs_2_ = bf16[96,256]{1,0:T(8,128)(2,1)S(1)} collective-permute-done((bf16[96,256]{1,0:T(8,128)(2,1)S(1)}, bf16[96,256]{1,0:T(8,128)(2,1)S(1)}, u32[]{:S(2)}, u32[]{:S(2)}) %collective-permute-start.19) | collective-permute-done | bytes 49184 | tf_op jit(solution)/shard_map/ppermute | solution.py:469
  79.6 1.6 %collective-permute-done.20.refs_3_ = bf16[96,256]{1,0:T(8,128)(2,1)S(1)} collective-permute-done((bf16[96,256]{1,0:T(8,128)(2,1)S(1)}, bf16[96,256]{1,0:T(8,128)(2,1)S(1)}, u32[]{:S(2)}, u32[]{:S(2)}) %collective-permute-start.20) | collective-permute-done | bytes 49184 | tf_op jit(solution)/shard_map/ppermute | solution.py:470
  81.2 1.4 %shard_map.89 = s16[128,24,256]{2,1,0:T(8,128)(2,1)S(1)} custom-call(bf16[1920,384]{1,0:T(8,128)(2,1)S(1)} %get-tuple-element.34.early_a.images_ref, bf16[1344,384]{1,0:T(8,128)(2,1)S(1)} %get-tuple-element.35.early_b.texts_ref, bf16[96,256]{1,0:T(8,128)(2,1)S(1)} %get-tuple-element.48.refs_0_, bf16[96,256]{1,0:T(8,128)(2,1)S(1)} %collective-permute-done.18.refs_1_, ...), custom_call_target="tpu_custom_call" | custom-call | flops 1207959552 | bytes 6291456 | tf_op jit(solution)/shard_map/pallas_call | solution.py:476
  82.7 33.0 %all_to_all.5.coded_ref = s16[128,24,256]{2,1,0:T(8,128)(2,1)S(1)} all-to-all(s16[128,24,256]{2,1,0:T(8,128)(2,1)S(1)} %shard_map.89), channel_id=1, replica_groups=mesh['xl'=2,'core'=2,'z'=4,'xh'=2,'y'=4] {'xl','core','z','xh','y'}, dimensions={0} | all-to-all | bytes 3145728 | tf_op jit(solution)/shard_map/all_to_all | solution.py:482
  115.6 1.2 %shard_map.90 = f32[21,1024]{1,0:T(8,128)} custom-call(s16[128,24,256]{2,1,0:T(8,128)(2,1)S(1)} %all_to_all.5.coded_ref), custom_call_target="tpu_custom_call" | custom-call | bytes 2097152 | tf_op jit(solution)/shard_map/pallas_call | solution.py:483
  (61 shorter events, 9.0 us)
Async XLA Ops:
  4.9 23.4 %copy-start.1 = (bf16[384,1664]{1,0:T(8,128)(2,1)S(1)}, bf16[384,1664]{1,0:T(8,128)(2,1)}, u32[]{:S(2)}) copy-start(bf16[384,1664]{1,0:T(8,128)(2,1)} %image_feats.3) | copy-start | bytes 3833860
  4.9 23.4 %copy-start.2 = (bf16[384,1024]{1,0:T(8,128)(2,1)S(1)}, bf16[384,1024]{1,0:T(8,128)(2,1)}, u32[]{:S(2)}) copy-start(bf16[384,1024]{1,0:T(8,128)(2,1)} %text_feats.3) | copy-start | bytes 2359300
  4.9 8.1 %collective-permute-start.1 = (bf16[96,1024]{1,0:T(8,128)(2,1)}, bf16[96,1024]{1,0:T(8,128)(2,1)S(1)}, u32[]{:S(2)}, u32[]{:S(2)}) collective-permute-start(bf16[96,1024]{1,0:T(8,128)(2,1)} %get-tuple-element.36.emb), channel_id=1, source_target_pairs={{0,68},{4,64},{64,4},{68,0},{1,69},{5,65},{65,5},{69,1},{2,70},{6,... | collective-permute-start | bytes 589832 | tf_op jit(solution)/shard_map/ppermute | solution.py:400
  8.3 12.3 %collective-permute-start.6 = (bf16[208,1024]{1,0:T(8,128)(2,1)}, bf16[208,1024]{1,0:T(8,128)(2,1)S(1)}, u32[]{:S(2)}, u32[]{:S(2)}) collective-permute-start(bf16[208,1024]{1,0:T(8,128)(2,1)} %get-tuple-element.33.me.emb), channel_id=1, source_target_pairs={{0,24},{8,0},{16,8},{24,16},{1,25},{9,1},{17,9},{25,17},{2,26},{10... | collective-permute-start | bytes 1277960 | tf_op jit(solution)/shard_map/ppermute | solution.py:32
  12.1 11.9 %collective-permute-start = (bf16[208,1024]{1,0:T(8,128)(2,1)}, bf16[208,1024]{1,0:T(8,128)(2,1)S(1)}, u32[]{:S(2)}, u32[]{:S(2)}) collective-permute-start(bf16[208,1024]{1,0:T(8,128)(2,1)} %get-tuple-element.33.me.emb), channel_id=1, source_target_pairs={{0,8},{8,16},{16,24},{24,0},{1,9},{9,17},{17,25},{25,1},{2,10},{10... | collective-permute-start | bytes 1277960 | tf_op jit(solution)/shard_map/ppermute | solution.py:32
  13.1 11.0 %collective-permute-start.3 = (bf16[192,1024]{1,0:T(8,128)(2,1)S(1)}, bf16[192,1024]{1,0:T(8,128)(2,1)S(1)}, u32[]{:S(2)}, u32[]{:S(2)}) collective-permute-start(bf16[192,1024]{1,0:T(8,128)(2,1)S(1)} %constant_dynamic-update-slice_fusion.me), channel_id=1, source_target_pairs={{0,1},{1,2},{2,3},{3,0},{4,5},{5,6},{6,7},{7,4},{8,9},{9,10},{10,1... | collective-permute-start | bytes 1179656 | tf_op jit(solution)/shard_map/ppermute | solution.py:32
  14.4 11.0 %collective-permute-start.2 = (bf16[192,1024]{1,0:T(8,128)(2,1)S(1)}, bf16[192,1024]{1,0:T(8,128)(2,1)S(1)}, u32[]{:S(2)}, u32[]{:S(2)}) collective-permute-start(bf16[192,1024]{1,0:T(8,128)(2,1)S(1)} %constant_dynamic-update-slice_fusion.me), channel_id=1, source_target_pairs={{0,3},{1,0},{2,1},{3,2},{4,7},{5,4},{6,5},{7,6},{8,11},{9,8},{10,9... | collective-permute-start | bytes 1179656 | tf_op jit(solution)/shard_map/ppermute | solution.py:32
  20.6 9.9 %collective-permute-start.8 = (bf16[112,1024]{1,0:T(8,128)(2,1)S(1)}, bf16[112,1024]{1,0:T(8,128)(2,1)S(1)}, u32[]{:S(2)}, u32[]{:S(2)}) collective-permute-start(bf16[112,1024]{1,0:T(8,128)(2,1)S(1)} %slice.19), channel_id=1, source_target_pairs={{0,24},{8,0},{16,8},{24,16},{1,25},{9,1},{17,9},{25,17},{2,26},{10... | collective-permute-start | bytes 688136 | tf_op jit(solution)/shard_map/ppermute | solution.py:32
  24.0 6.5 %collective-permute-start.7 = (bf16[96,1024]{1,0:T(8,128)(2,1)S(1)}, bf16[96,1024]{1,0:T(8,128)(2,1)S(1)}, u32[]{:S(2)}, u32[]{:S(2)}) collective-permute-start(bf16[96,1024]{1,0:T(8,128)(2,1)S(1)} %slice.18), channel_id=1, source_target_pairs={{0,8},{8,16},{16,24},{24,0},{1,9},{9,17},{17,25},{25,1},{2,10},{10... | collective-permute-start | bytes 589832 | tf_op jit(solution)/shard_map/ppermute | solution.py:32
  24.1 9.3 %collective-permute-start.4 = (bf16[96,1024]{1,0:T(8,128)(2,1)S(1)}, bf16[96,1024]{1,0:T(8,128)(2,1)S(1)}, u32[]{:S(2)}, u32[]{:S(2)}) collective-permute-start(bf16[96,1024]{1,0:T(8,128)(2,1)S(1)} %slice.16), channel_id=1, source_target_pairs={{0,1},{1,2},{2,3},{3,0},{4,5},{5,6},{6,7},{7,4},{8,9},{9,10},{10,1... | collective-permute-start | bytes 589832 | tf_op jit(solution)/shard_map/ppermute | solution.py:32
  25.5 7.9 %collective-permute-start.5 = (bf16[96,1024]{1,0:T(8,128)(2,1)S(1)}, bf16[96,1024]{1,0:T(8,128)(2,1)S(1)}, u32[]{:S(2)}, u32[]{:S(2)}) collective-permute-start(bf16[96,1024]{1,0:T(8,128)(2,1)S(1)} %slice.17), channel_id=1, source_target_pairs={{0,3},{1,0},{2,1},{3,2},{4,7},{5,4},{6,5},{7,6},{8,11},{9,8},{10,9... | collective-permute-start | bytes 589832 | tf_op jit(solution)/shard_map/ppermute | solution.py:32
  30.7 5.8 %collective-permute-start.9 = (bf16[784,1024]{1,0:T(8,128)(2,1)S(1)}, bf16[784,1024]{1,0:T(8,128)(2,1)S(1)}, u32[]{:S(2)}, u32[]{:S(2)}) collective-permute-start(bf16[784,1024]{1,0:T(8,128)(2,1)S(1)} %shard_map.75.images_ref.refs_1_), channel_id=1, source_target_pairs={{0,32},{32,0},{1,33},{33,1},{2,34},{34,2},{3,35},{35,3},{4,36},{36... | collective-permute-start | bytes 4816904 | tf_op jit(solution)/shard_map/ppermute | solution.py:407
  39.3 9.7 %collective-permute-start.11 = (f32[384,1024]{1,0:T(8,128)S(1)}, f32[384,1024]{1,0:T(8,128)S(1)}, u32[]{:S(2)}, u32[]{:S(2)}) collective-permute-start(f32[384,1024]{1,0:T(8,128)S(1)} %get-tuple-element.40), channel_id=1, source_target_pairs={{0,32},{32,0},{1,33},{33,1},{2,34},{34,2},{3,35},{35,3},{4,36},{36... | collective-permute-start | bytes 4718600 | tf_op jit(solution)/shard_map/ppermute | solution.py:442
  40.7 11.2 %collective-permute-start.10 = (f32[384,1024]{1,0:T(8,128)S(1)}, f32[384,1024]{1,0:T(8,128)S(1)}, u32[]{:S(2)}, u32[]{:S(2)}) collective-permute-start(f32[384,1024]{1,0:T(8,128)S(1)} %shard_map.78), channel_id=1, source_target_pairs={{0,32},{32,0},{1,33},{33,1},{2,34},{34,2},{3,35},{35,3},{4,36},{36... | collective-permute-start | bytes 4718600 | tf_op jit(solution)/shard_map/ppermute | solution.py:447
  44.0 11.1 %collective-permute-start.22 = (s16[96,1408]{1,0:T(8,128)(2,1)S(1)}, s16[96,1408]{1,0:T(8,128)(2,1)S(1)}, u32[]{:S(2)}, u32[]{:S(2)}) collective-permute-start(s16[96,1408]{1,0:T(8,128)(2,1)S(1)} %get-tuple-element.55), channel_id=1, source_target_pairs={{0,68},{4,64},{64,4},{68,0},{1,69},{5,65},{65,5},{69,1},{2,70},{6,... | collective-permute-start | bytes 811016 | tf_op jit(solution)/shard_map/ppermute | solution.py:454
  46.3 14.4 %collective-permute-start.15 = (s16[192,1408]{1,0:T(8,128)(2,1)S(1)}, s16[192,1408]{1,0:T(8,128)(2,1)S(1)}, u32[]{:S(2)}, u32[]{:S(2)}) collective-permute-start(s16[192,1408]{1,0:T(8,128)(2,1)S(1)} %get-tuple-element.46), channel_id=1, source_target_pairs={{0,1},{1,2},{2,3},{3,0},{4,5},{5,6},{6,7},{7,4},{8,9},{9,10},{10,1... | collective-permute-start | bytes 1622024 | tf_op jit(solution)/shard_map/ppermute | solution.py:32
  46.3 14.4 %collective-permute-start.21 = (s16[192,1408]{1,0:T(8,128)(2,1)S(1)}, s16[192,1408]{1,0:T(8,128)(2,1)S(1)}, u32[]{:S(2)}, u32[]{:S(2)}) collective-permute-start(s16[192,1408]{1,0:T(8,128)(2,1)S(1)} %get-tuple-element.53), channel_id=1, source_target_pairs={{0,3},{1,0},{2,1},{3,2},{4,7},{5,4},{6,5},{7,6},{8,11},{9,8},{10,9... | collective-permute-start | bytes 1622024 | tf_op jit(solution)/shard_map/ppermute | solution.py:32
  50.2 16.1 %collective-permute-start.12 = (s16[192,1408]{1,0:T(8,128)(2,1)S(1)}, s16[192,1408]{1,0:T(8,128)(2,1)S(1)}, u32[]{:S(2)}, u32[]{:S(2)}) collective-permute-start(s16[192,1408]{1,0:T(8,128)(2,1)S(1)} %get-tuple-element.43), channel_id=1, source_target_pairs={{0,8},{8,16},{16,24},{24,0},{1,9},{9,17},{17,25},{25,1},{2,10},{10... | collective-permute-start | bytes 1622024 | tf_op jit(solution)/shard_map/ppermute | solution.py:32
  52.9 13.3 %collective-permute-start.13 = (s16[192,1408]{1,0:T(8,128)(2,1)S(1)}, s16[192,1408]{1,0:T(8,128)(2,1)S(1)}, u32[]{:S(2)}, u32[]{:S(2)}) collective-permute-start(s16[192,1408]{1,0:T(8,128)(2,1)S(1)} %get-tuple-element.44), channel_id=1, source_target_pairs={{0,24},{8,0},{16,8},{24,16},{1,25},{9,1},{17,9},{25,17},{2,26},{10... | collective-permute-start | bytes 1622024 | tf_op jit(solution)/shard_map/ppermute | solution.py:32
  55.1 8.9 %collective-permute-start.14 = (s16[96,1408]{1,0:T(8,128)(2,1)S(1)}, s16[96,1408]{1,0:T(8,128)(2,1)S(1)}, u32[]{:S(2)}, u32[]{:S(2)}) collective-permute-start(s16[96,1408]{1,0:T(8,128)(2,1)S(1)} %get-tuple-element.45), channel_id=1, source_target_pairs={{0,64},{64,0},{1,65},{65,1},{2,66},{66,2},{3,67},{67,3},{4,68},{68... | collective-permute-start | bytes 811016 | tf_op jit(solution)/shard_map/ppermute | solution.py:457
  61.1 7.7 %collective-permute-start.24 = (s16[96,1408]{1,0:T(8,128)(2,1)S(1)}, s16[96,1408]{1,0:T(8,128)(2,1)S(1)}, u32[]{:S(2)}, u32[]{:S(2)}) collective-permute-start(s16[96,1408]{1,0:T(8,128)(2,1)S(1)} %shard_map.87), channel_id=1, source_target_pairs={{0,68},{4,64},{64,4},{68,0},{1,69},{5,65},{65,5},{69,1},{2,70},{6,... | collective-permute-start | bytes 811016 | tf_op jit(solution)/shard_map/ppermute | solution.py:454
  61.6 7.8 %copy-start.3 = (bf16[96,1024]{1,0:T(8,128)(2,1)S(1)}, bf16[96,1024]{1,0:T(8,128)(2,1)}, u32[]{:S(2)}) copy-start(bf16[96,1024]{1,0:T(8,128)(2,1)} %get-tuple-element.36.emb) | copy-start | bytes 589828
  61.7 7.7 %collective-permute-start.23 = (s16[96,1408]{1,0:T(8,128)(2,1)S(1)}, s16[96,1408]{1,0:T(8,128)(2,1)S(1)}, u32[]{:S(2)}, u32[]{:S(2)}) collective-permute-start(s16[96,1408]{1,0:T(8,128)(2,1)S(1)} %shard_map.86), channel_id=1, source_target_pairs={{0,2},{1,3},{2,0},{3,1},{4,6},{5,7},{6,4},{7,5},{8,10},{9,11},{10,... | collective-permute-start | bytes 811016 | tf_op jit(solution)/shard_map/ppermute | solution.py:32
  64.3 10.2 %collective-permute-start.16 = (s16[96,1408]{1,0:T(8,128)(2,1)S(1)}, s16[96,1408]{1,0:T(8,128)(2,1)S(1)}, u32[]{:S(2)}, u32[]{:S(2)}) collective-permute-start(s16[96,1408]{1,0:T(8,128)(2,1)S(1)} %shard_map.82), channel_id=1, source_target_pairs={{0,16},{8,24},{16,0},{24,8},{1,17},{9,25},{17,1},{25,9},{2,18},{10... | collective-permute-start | bytes 811016 | tf_op jit(solution)/shard_map/ppermute | solution.py:32
  66.6 8.0 %copy-start.4 = (f32[96,128]{1,0:T(8,128)S(1)}, f32[96,128]{1,0:T(8,128)}, u32[]{:S(2)}) copy-start(f32[96,128]{1,0:T(8,128)} %get-tuple-element.47.inverse) | copy-start | bytes 147460
  66.6 8.0 %collective-permute-start.17 = (s16[96,1408]{1,0:T(8,128)(2,1)S(1)}, s16[96,1408]{1,0:T(8,128)(2,1)S(1)}, u32[]{:S(2)}, u32[]{:S(2)}) collective-permute-start(s16[96,1408]{1,0:T(8,128)(2,1)S(1)} %shard_map.83), channel_id=1, source_target_pairs={{0,64},{64,0},{1,65},{65,1},{2,66},{66,2},{3,67},{67,3},{4,68},{68... | collective-permute-start | bytes 811016 | tf_op jit(solution)/shard_map/ppermute | solution.py:457
  70.0 6.7 %collective-permute-start.25 = (bf16[96,256]{1,0:T(8,128)(2,1)S(1)}, bf16[96,256]{1,0:T(8,128)(2,1)S(1)}, u32[]{:S(2)}, u32[]{:S(2)}) collective-permute-start(bf16[96,256]{1,0:T(8,128)(2,1)S(1)} %get-tuple-element.58), channel_id=1, source_target_pairs={{0,32},{32,0},{1,33},{33,1},{2,34},{34,2},{3,35},{35,3},{4,36},{36... | collective-permute-start | bytes 147464 | tf_op jit(solution)/shard_map/ppermute | solution.py:468
  72.8 5.6 %collective-permute-start.26 = (bf16[96,256]{1,0:T(8,128)(2,1)S(1)}, bf16[96,256]{1,0:T(8,128)(2,1)S(1)}, u32[]{:S(2)}, u32[]{:S(2)}) collective-permute-start(bf16[96,256]{1,0:T(8,128)(2,1)S(1)} %get-tuple-element.59), channel_id=1, source_target_pairs={{0,64},{64,0},{1,65},{65,1},{2,66},{66,2},{3,67},{67,3},{4,68},{68... | collective-permute-start | bytes 147464 | tf_op jit(solution)/shard_map/ppermute | solution.py:469
  72.9 5.6 %collective-permute-start.27 = (bf16[96,256]{1,0:T(8,128)(2,1)S(1)}, bf16[96,256]{1,0:T(8,128)(2,1)S(1)}, u32[]{:S(2)}, u32[]{:S(2)}) collective-permute-start(bf16[96,256]{1,0:T(8,128)(2,1)S(1)} %get-tuple-element.60), channel_id=1, source_target_pairs={{0,96},{32,64},{64,32},{96,0},{1,97},{33,65},{65,33},{97,1},{2,98}... | collective-permute-start | bytes 147464 | tf_op jit(solution)/shard_map/ppermute | solution.py:470
  75.2 3.2 %collective-permute-start.18 = (bf16[96,256]{1,0:T(8,128)(2,1)S(1)}, bf16[96,256]{1,0:T(8,128)(2,1)S(1)}, u32[]{:S(2)}, u32[]{:S(2)}) collective-permute-start(bf16[96,256]{1,0:T(8,128)(2,1)S(1)} %get-tuple-element.49), channel_id=1, source_target_pairs={{0,32},{32,0},{1,33},{33,1},{2,34},{34,2},{3,35},{35,3},{4,36},{36... | collective-permute-start | bytes 147464 | tf_op jit(solution)/shard_map/ppermute | solution.py:468
  76.7 3.0 %collective-permute-start.19 = (bf16[96,256]{1,0:T(8,128)(2,1)S(1)}, bf16[96,256]{1,0:T(8,128)(2,1)S(1)}, u32[]{:S(2)}, u32[]{:S(2)}) collective-permute-start(bf16[96,256]{1,0:T(8,128)(2,1)S(1)} %get-tuple-element.50), channel_id=1, source_target_pairs={{0,64},{64,0},{1,65},{65,1},{2,66},{66,2},{3,67},{67,3},{4,68},{68... | collective-permute-start | bytes 147464 | tf_op jit(solution)/shard_map/ppermute | solution.py:469
  76.7 4.5 %collective-permute-start.20 = (bf16[96,256]{1,0:T(8,128)(2,1)S(1)}, bf16[96,256]{1,0:T(8,128)(2,1)S(1)}, u32[]{:S(2)}, u32[]{:S(2)}) collective-permute-start(bf16[96,256]{1,0:T(8,128)(2,1)S(1)} %get-tuple-element.51), channel_id=1, source_target_pairs={{0,96},{32,64},{64,32},{96,0},{1,97},{33,65},{65,33},{97,1},{2,98}... | collective-permute-start | bytes 147464 | tf_op jit(solution)/shard_map/ppermute | solution.py:470
  (2 other events, 10.0 us)

commit v9 on v8

--- a/solution.py
+++ b/solution.py
@@ -268,11 +268,8 @@
 
 def given_kernel(where_ref, scale_ref, shift_ref, texts_ref, images_ref, coef_ref, given_ref):
     coefficients(where_ref, scale_ref, shift_ref, images_ref, texts_ref, coef_ref)
-    given_ref[...] = image_terms(coef_ref, texts_ref, 0)
-
-
-def given_rest_kernel(texts_ref, coef_ref, given_ref):
-    given_ref[...] = image_terms(coef_ref, texts_ref, 1)
+    for part in range(2):
+        given_ref[part * ROWS : (part + 1) * ROWS, :] = image_terms(coef_ref, texts_ref, part)
 
 
 def text_kernel(own_coef, images_ref, others_coef, others_ref, *outs):
@@ -281,12 +278,10 @@
     share_out(got, outs)
 
 
-def kept_kernel(part, texts_ref, coef_ref, taken_ref, *outs):
-    share_out(image_terms(coef_ref, texts_ref, part) + taken_ref[...], outs)
-
-
-def kept_rest_kernel(texts_ref, coef_ref, taken_ref, early_ref, *outs):
-    kept_kernel(1, texts_ref, coef_ref, taken_ref, *outs)
+def kept_kernel(texts_ref, coef_ref, taken_ref, *outs):
+    for part, some in enumerate((outs[:3], outs[3:])):
+        rows = slice(part * ROWS, (part + 1) * ROWS)
+        share_out(image_terms(coef_ref, texts_ref, part) + taken_ref[rows, :], some)
 
 
 def back_kernel(
@@ -436,20 +431,15 @@
         in_specs=[SMEM] * 3 + [VMEM] * 6 + [ANY] * 2, out_specs=[VMEM] * 2,
     )(where, log_scale, logit_bias, *text_pieces, images, image_groups, text_groups)
     others_coef, given = call(
-        given_kernel, [coef, shape(ROWS, E)], 2 * flops, 8 << 20, 24,
+        given_kernel, [coef, shape(TILE, E)], 2 * flops, 8 << 20, 24,
         in_specs=[SMEM] * 3 + [VMEM] * 2, out_specs=[VMEM] * 2,
     )(where, log_scale, logit_bias, texts, others)
     taken = lax.ppermute(given, "core", SWAP)
     sides = own_coef, images, others_coef, others
     text_parts = run(text_kernel, ways + rest, 2, 4)(*sides)
     text_ways, text_rest = text_parts[:3], text_parts[3:]
-    given_rest, = run(given_rest_kernel, [shape(ROWS, E)], 0.5, 2)(texts, others_coef)
-    taken_rest = lax.ppermute(given_rest, "core", SWAP)
-    image_ways = run(kept_kernel, ways, 0.5, 3, 0)(texts, own_coef, taken)
-    image_rest = call(
-        kept_rest_kernel, rest, 4 * flops, 6 << 20, 24,
-        in_specs=[VMEM] * 3 + [ANY], out_specs=[VMEM] * 2,
-    )(texts, own_coef, taken_rest, image_ways[0])
+    image_parts = run(kept_kernel, ways + rest, 1, 3)(texts, own_coef, taken)
+    image_ways, image_rest = image_parts[:3], image_parts[3:]
     text_sums = ring_scatter(
         *text_ways, *text_rest, "y", lambda a: lax.ppermute(a, ("xl", "xh"), FLIP)
     )

time: 117 us -> 117 us (level)
    pallas_call x4 -> x2, Pallas kernels: 5.77 us -> 5.37 us  [the longest x1 3.42 us: body(): call(given_kernel, [coef, shape(TILE, E)], 2 * flops, 8 << 20, 24, in_spe...]
  transfers between devices with their start and end apart: 28 -> 27, of which waited for: 7 -> 7; matrix products, arithmetic and copies ran while one was open for 1% -> 1% of each run, Pallas kernels for 11% -> 10%
where the time goes in v9:
time: 117 us
  starting transfers between devices  41.3 us (35%)
  blocking collectives  33 us (28%)
  Pallas kernels  23 us (20%)
  waiting for transfers between devices  16.9 us (14%)
  between operations  1.56 us (1%)
    all_to_all x1, blocking collectives, body(): coded = lax.all_to_all(coded, AXES, split_axis=0, concat_axis=0, tiled=True)  33 us
    ppermute x14, starting transfers between devices, shifted(): return lax.ppermute(array, axis, [(i, (i + by) % 4) for i in range(4)])  24.2 us
    ppermute x14, waiting for transfers between devices, shifted(): return lax.ppermute(array, axis, [(i, (i + by) % 4) for i in range(4)])  11 us
    pallas_call x1, Pallas kernels, body(): call(embed_kernel, [shape(QUARTER, E, dtype=BF16), shape(QUARTER, 128), s...  4.9 us
    ppermute x2, starting transfers between devices, tower_pieces(): lax.ppermute(other_core, 'core', SWAP)  4.02 us
    ppermute x2, starting transfers between devices, tower_pieces(): lax.ppermute(other_both, TOWER, [(i, 3 - i) for i in range(4)])  3.42 us
    pallas_call x1, Pallas kernels, body(): call(given_kernel, [coef, shape(TILE, E)], 2 * flops, 8 << 20, 24, in_spe...  3.42 us
    ppermute x1, starting transfers between devices, body(): other_texts = lax.ppermute(own_texts, ('xl', 'xh'), FLIP)  3.39 us
  transfers between devices with their start and end apart: 27, of which 7 were waited for; matrix products, arithmetic and copies ran while one was open for 1% of the time, Pallas kernels for 10%

profile of v9, /device:TPU:1, one launch (start us, length us, event | category | flops | bytes accessed | tf_op | source)
XLA Modules:
  0.0 116.8 jit_solution(7630729541937224939)
XLA Ops:
  0.0 4.9 %shard_map.73 = (bf16[96,1024]{1,0:T(8,128)(2,1)}, f32[96,128]{1,0:T(8,128)}, bf16[208,1024]{1,0:T(8,128)(2,1)}, f32[96,128]{1,0:T(8,128)}) custom-call(s32[1]{0:T(128)} %bitcast.where_ref, s32[3,128]{1,0:T(4,128)} %bitcast.2, bf16[384,1024]{1,0:T(8,128)(2,1)} %text_feats.3, bf16[384,1664]{1,0:T(8,128)(2,1)} %image_feats.3, bf16[1024,1024]{1,0:T(8,128)(2,1)} %text_weight.1, ...), custom_call_target="tpu_custom_call" | custom-call | flops 855638016 | bytes 8388608 | tf_op jit(solution)/shard_map/pallas_call | solution.py:380
  4.9 3.4 %collective-permute-start.1 = (bf16[96,1024]{1,0:T(8,128)(2,1)}, bf16[96,1024]{1,0:T(8,128)(2,1)S(1)}, u32[]{:S(2)}, u32[]{:S(2)}) collective-permute-start(bf16[96,1024]{1,0:T(8,128)(2,1)} %get-tuple-element.36.emb), channel_id=1, source_target_pairs={{0,68},{4,64},{64,4},{68,0},{1,69},{5,65},{65,5},{69,1},{2,70},{6,... | collective-permute-start | bytes 589832 | tf_op jit(solution)/shard_map/ppermute | solution.py:395
  8.3 3.8 %collective-permute-start.6 = (bf16[208,1024]{1,0:T(8,128)(2,1)}, bf16[208,1024]{1,0:T(8,128)(2,1)S(1)}, u32[]{:S(2)}, u32[]{:S(2)}) collective-permute-start(bf16[208,1024]{1,0:T(8,128)(2,1)} %get-tuple-element.33.me.emb), channel_id=1, source_target_pairs={{0,24},{8,0},{16,8},{24,16},{1,25},{9,1},{17,9},{25,17},{2,26},{10... | collective-permute-start | bytes 1277960 | tf_op jit(solution)/shard_map/ppermute | solution.py:32
  13.1 1.4 %collective-permute-start.3 = (bf16[192,1024]{1,0:T(8,128)(2,1)S(1)}, bf16[192,1024]{1,0:T(8,128)(2,1)S(1)}, u32[]{:S(2)}, u32[]{:S(2)}) collective-permute-start(bf16[192,1024]{1,0:T(8,128)(2,1)S(1)} %constant_dynamic-update-slice_fusion.me), channel_id=1, source_target_pairs={{0,1},{1,2},{2,3},{3,0},{4,5},{5,6},{6,7},{7,4},{8,9},{9,10},{10,1... | collective-permute-start | bytes 1179656 | tf_op jit(solution)/shard_map/ppermute | solution.py:32
  14.4 1.5 %collective-permute-start.2 = (bf16[192,1024]{1,0:T(8,128)(2,1)S(1)}, bf16[192,1024]{1,0:T(8,128)(2,1)S(1)}, u32[]{:S(2)}, u32[]{:S(2)}) collective-permute-start(bf16[192,1024]{1,0:T(8,128)(2,1)S(1)} %constant_dynamic-update-slice_fusion.me), channel_id=1, source_target_pairs={{0,3},{1,0},{2,1},{3,2},{4,7},{5,4},{6,5},{7,6},{8,11},{9,8},{10,9... | collective-permute-start | bytes 1179656 | tf_op jit(solution)/shard_map/ppermute | solution.py:32
  15.9 4.6 %collective-permute-done.6.after = bf16[208,1024]{1,0:T(8,128)(2,1)S(1)} collective-permute-done((bf16[208,1024]{1,0:T(8,128)(2,1)}, bf16[208,1024]{1,0:T(8,128)(2,1)S(1)}, u32[]{:S(2)}, u32[]{:S(2)}) %collective-permute-start.6) | collective-permute-done | bytes 426016 | tf_op jit(solution)/shard_map/ppermute | solution.py:32
  20.6 3.4 %collective-permute-start.8 = (bf16[112,1024]{1,0:T(8,128)(2,1)S(1)}, bf16[112,1024]{1,0:T(8,128)(2,1)S(1)}, u32[]{:S(2)}, u32[]{:S(2)}) collective-permute-start(bf16[112,1024]{1,0:T(8,128)(2,1)S(1)} %slice.19), channel_id=1, source_target_pairs={{0,24},{8,0},{16,8},{24,16},{1,25},{9,1},{17,9},{25,17},{2,26},{10... | collective-permute-start | bytes 688136 | tf_op jit(solution)/shard_map/ppermute | solution.py:32
  24.1 1.4 %collective-permute-start.4 = (bf16[96,1024]{1,0:T(8,128)(2,1)S(1)}, bf16[96,1024]{1,0:T(8,128)(2,1)S(1)}, u32[]{:S(2)}, u32[]{:S(2)}) collective-permute-start(bf16[96,1024]{1,0:T(8,128)(2,1)S(1)} %slice.16), channel_id=1, source_target_pairs={{0,1},{1,2},{2,3},{3,0},{4,5},{5,6},{6,7},{7,4},{8,9},{9,10},{10,1... | collective-permute-start | bytes 589832 | tf_op jit(solution)/shard_map/ppermute | solution.py:32
  25.5 1.5 %collective-permute-start.5 = (bf16[96,1024]{1,0:T(8,128)(2,1)S(1)}, bf16[96,1024]{1,0:T(8,128)(2,1)S(1)}, u32[]{:S(2)}, u32[]{:S(2)}) collective-permute-start(bf16[96,1024]{1,0:T(8,128)(2,1)S(1)} %slice.17), channel_id=1, source_target_pairs={{0,3},{1,0},{2,1},{3,2},{4,7},{5,4},{6,5},{7,6},{8,11},{9,8},{10,9... | collective-permute-start | bytes 589832 | tf_op jit(solution)/shard_map/ppermute | solution.py:32
  28.3 2.2 %shard_map.74 = (bf16[1920,384]{1,0:T(8,128)(2,1)S(1)}, bf16[1344,384]{1,0:T(8,128)(2,1)S(1)}) custom-call(s32[1]{0:T(128)} %bitcast.where_ref, bf16[384,1664]{1,0:T(8,128)(2,1)S(1)} %copy-done.1, bf16[384,1024]{1,0:T(8,128)(2,1)S(1)} %copy-done.2, bf16[208,1024]{1,0:T(8,128)(2,1)S(1)} %collective-permute-done.early.before), custom_call_target="tpu_custom_call" | custom-call | flops 962592768 | bytes 5242880 | tf_op jit(solution)/shard_map/pallas_call | solution.py:405
  30.7 2.7 %collective-permute-start.9 = (bf16[784,1024]{1,0:T(8,128)(2,1)S(1)}, bf16[784,1024]{1,0:T(8,128)(2,1)S(1)}, u32[]{:S(2)}, u32[]{:S(2)}) collective-permute-start(bf16[784,1024]{1,0:T(8,128)(2,1)S(1)} %shard_map.75.images_ref.refs_1_), channel_id=1, source_target_pairs={{0,32},{32,0},{1,33},{33,1},{2,34},{34,2},{3,35},{35,3},{4,36},{36... | collective-permute-start | bytes 4816904 | tf_op jit(solution)/shard_map/ppermute | solution.py:402
  33.4 2.0 %shard_map.76 = (bf16[768,1024]{1,0:T(8,128)(2,1)S(1)}, bf16[768,768]{1,0:T(8,128)(2,1)S(1)}) custom-call(s32[1]{0:T(128)} %bitcast.where_ref, f32[1]{0:T(128)S(6)} %copy.9.scale_ref, f32[1]{0:T(128)S(6)} %copy.10.shift_ref, bf16[192,1024]{1,0:T(8,128)(2,1)S(1)} %constant_dynamic-update-slice_fusion.me, bf16[192,1024]{1,0:T(8,128)(2,1)S(1)} %collective-permute-done.2.after, ...), custom_call_target="tpu_custom_call" | custom-call | flops 19327352832 | bytes 6291456 | tf_op jit(solution)/shard_map/pallas_call | solution.py:429
  36.5 3.4 %shard_map.77 = (bf16[768,768]{1,0:T(8,128)(2,1)S(1)}, f32[768,1024]{1,0:T(8,128)S(1)}) custom-call(s32[1]{0:T(128)} %bitcast.where_ref, f32[1]{0:T(128)S(6)} %copy.9.scale_ref, f32[1]{0:T(128)S(6)} %copy.10.shift_ref, bf16[768,1024]{1,0:T(8,128)(2,1)S(1)} %get-tuple-element.37.texts_ref.refs_0_, bf16[784,1024]{1,0:T(8,128)(2,1)S(1)} %collective-permute-done.9.images_ref.refs_3_), custom_call_target="tpu_custom_call" | custom-call | flops 2415919104 | bytes 8388608 | tf_op jit(solution)/shard_map/pallas_call | solution.py:433
  40.6 3.1 %shard_map.79 = (f32[96,1024]{1,0:T(8,128)S(1)}, s16[96,1408]{1,0:T(8,128)(2,1)S(1)}, s16[192,1408]{1,0:T(8,128)(2,1)S(1)}, s16[192,1408]{1,0:T(8,128)(2,1)S(1)}, f32[192,1024]{1,0:T(8,128)S(1)}) custom-call(bf16[768,768]{1,0:T(8,128)(2,1)S(1)} %get-tuple-element.38.refs_1_.refs_0_, bf16[784,1024]{1,0:T(8,128)(2,1)S(1)} %shard_map.75.images_ref.refs_1_, ...), custom_call_target="tpu_custom_call" | custom-call | flops 2415919104 | bytes 6291456 | tf_op jit(solution)/shard_map/pallas_call | solution.py:439
  43.7 2.3 %collective-permute-start.21 = (s16[96,1408]{1,0:T(8,128)(2,1)S(1)}, s16[96,1408]{1,0:T(8,128)(2,1)S(1)}, u32[]{:S(2)}, u32[]{:S(2)}) collective-permute-start(s16[96,1408]{1,0:T(8,128)(2,1)S(1)} %get-tuple-element.55), channel_id=1, source_target_pairs={{0,68},{4,64},{64,4},{68,0},{1,69},{5,65},{65,5},{69,1},{2,70},{6,... | collective-permute-start | bytes 811016 | tf_op jit(solution)/shard_map/ppermute | solution.py:444
  45.9 2.7 %collective-permute-start.20 = (s16[192,1408]{1,0:T(8,128)(2,1)S(1)}, s16[192,1408]{1,0:T(8,128)(2,1)S(1)}, u32[]{:S(2)}, u32[]{:S(2)}) collective-permute-start(s16[192,1408]{1,0:T(8,128)(2,1)S(1)} %get-tuple-element.53), channel_id=1, source_target_pairs={{0,3},{1,0},{2,1},{3,2},{4,7},{5,4},{6,5},{7,6},{8,11},{9,8},{10,9... | collective-permute-start | bytes 1622024 | tf_op jit(solution)/shard_map/ppermute | solution.py:32
  48.6 1.9 %shard_map.78 = (f32[96,1024]{1,0:T(8,128)S(1)}, s16[96,1408]{1,0:T(8,128)(2,1)S(1)}, s16[192,1408]{1,0:T(8,128)(2,1)S(1)}, s16[192,1408]{1,0:T(8,128)(2,1)S(1)}, f32[192,1024]{1,0:T(8,128)S(1)}) custom-call(bf16[768,1024]{1,0:T(8,128)(2,1)S(1)} %get-tuple-element.37.texts_ref.refs_0_, bf16[768,768]{1,0:T(8,128)(2,1)S(1)} %get-tuple-element.38.refs_1_.refs_0_, ...), custom_call_target="tpu_custom_call" | custom-call | flops 1207959552 | bytes 6291456 | tf_op jit(solution)/shard_map/pallas_call | solution.py:441
  50.6 1.7 %collective-permute-start.11 = (s16[192,1408]{1,0:T(8,128)(2,1)S(1)}, s16[192,1408]{1,0:T(8,128)(2,1)S(1)}, u32[]{:S(2)}, u32[]{:S(2)}) collective-permute-start(s16[192,1408]{1,0:T(8,128)(2,1)S(1)} %get-tuple-element.41), channel_id=1, source_target_pairs={{0,8},{8,16},{16,24},{24,0},{1,9},{9,17},{17,25},{25,1},{2,10},{10... | collective-permute-start | bytes 1622024 | tf_op jit(solution)/shard_map/ppermute | solution.py:32
  52.3 2.2 %collective-permute-start.12 = (s16[192,1408]{1,0:T(8,128)(2,1)S(1)}, s16[192,1408]{1,0:T(8,128)(2,1)S(1)}, u32[]{:S(2)}, u32[]{:S(2)}) collective-permute-start(s16[192,1408]{1,0:T(8,128)(2,1)S(1)} %get-tuple-element.42), channel_id=1, source_target_pairs={{0,24},{8,0},{16,8},{24,16},{1,25},{9,1},{17,9},{25,17},{2,26},{10... | collective-permute-start | bytes 1622024 | tf_op jit(solution)/shard_map/ppermute | solution.py:32
  54.8 5.8 %collective-permute-done.14.early_ref.right = s16[192,1408]{1,0:T(8,128)(2,1)S(1)} collective-permute-done((s16[192,1408]{1,0:T(8,128)(2,1)S(1)}, s16[192,1408]{1,0:T(8,128)(2,1)S(1)}, u32[]{:S(2)}, u32[]{:S(2)}) %collective-permute-start.14) | collective-permute-done | bytes 540704 | tf_op jit(solution)/shard_map/ppermute | solution.py:32
  61.5 2.4 %collective-permute-start.22 = (s16[96,1408]{1,0:T(8,128)(2,1)S(1)}, s16[96,1408]{1,0:T(8,128)(2,1)S(1)}, u32[]{:S(2)}, u32[]{:S(2)}) collective-permute-start(s16[96,1408]{1,0:T(8,128)(2,1)S(1)} %shard_map.84), channel_id=1, source_target_pairs={{0,2},{1,3},{2,0},{3,1},{4,6},{5,7},{6,4},{7,5},{8,10},{9,11},{10,... | collective-permute-start | bytes 811016 | tf_op jit(solution)/shard_map/ppermute | solution.py:32
  64.2 2.3 %collective-permute-start.15 = (s16[96,1408]{1,0:T(8,128)(2,1)S(1)}, s16[96,1408]{1,0:T(8,128)(2,1)S(1)}, u32[]{:S(2)}, u32[]{:S(2)}) collective-permute-start(s16[96,1408]{1,0:T(8,128)(2,1)S(1)} %shard_map.80), channel_id=1, source_target_pairs={{0,16},{8,24},{16,0},{24,8},{1,17},{9,25},{17,1},{25,9},{2,18},{10... | collective-permute-start | bytes 811016 | tf_op jit(solution)/shard_map/ppermute | solution.py:32
  67.0 2.0 %collective-permute-done.23.got = s16[96,1408]{1,0:T(8,128)(2,1)S(1)} collective-permute-done((s16[96,1408]{1,0:T(8,128)(2,1)S(1)}, s16[96,1408]{1,0:T(8,128)(2,1)S(1)}, u32[]{:S(2)}, u32[]{:S(2)}) %collective-permute-start.23) | collective-permute-done | bytes 270368 | tf_op jit(solution)/shard_map/ppermute | solution.py:444
  70.2 2.6 %collective-permute-start.24 = (bf16[96,256]{1,0:T(8,128)(2,1)S(1)}, bf16[96,256]{1,0:T(8,128)(2,1)S(1)}, u32[]{:S(2)}, u32[]{:S(2)}) collective-permute-start(bf16[96,256]{1,0:T(8,128)(2,1)S(1)} %get-tuple-element.58), channel_id=1, source_target_pairs={{0,32},{32,0},{1,33},{33,1},{2,34},{34,2},{3,35},{35,3},{4,36},{36... | collective-permute-start | bytes 147464 | tf_op jit(solution)/shard_map/ppermute | solution.py:458
  72.7 1.7 %collective-permute-start.26 = (bf16[96,256]{1,0:T(8,128)(2,1)S(1)}, bf16[96,256]{1,0:T(8,128)(2,1)S(1)}, u32[]{:S(2)}, u32[]{:S(2)}) collective-permute-start(bf16[96,256]{1,0:T(8,128)(2,1)S(1)} %get-tuple-element.60), channel_id=1, source_target_pairs={{0,96},{32,64},{64,32},{96,0},{1,97},{33,65},{65,33},{97,1},{2,98}... | collective-permute-start | bytes 147464 | tf_op jit(solution)/shard_map/ppermute | solution.py:460
  75.1 1.5 %collective-permute-start.17 = (bf16[96,256]{1,0:T(8,128)(2,1)S(1)}, bf16[96,256]{1,0:T(8,128)(2,1)S(1)}, u32[]{:S(2)}, u32[]{:S(2)}) collective-permute-start(bf16[96,256]{1,0:T(8,128)(2,1)S(1)} %get-tuple-element.49), channel_id=1, source_target_pairs={{0,32},{32,0},{1,33},{33,1},{2,34},{34,2},{3,35},{35,3},{4,36},{36... | collective-permute-start | bytes 147464 | tf_op jit(solution)/shard_map/ppermute | solution.py:458
  76.6 1.7 %collective-permute-start.19 = (bf16[96,256]{1,0:T(8,128)(2,1)S(1)}, bf16[96,256]{1,0:T(8,128)(2,1)S(1)}, u32[]{:S(2)}, u32[]{:S(2)}) collective-permute-start(bf16[96,256]{1,0:T(8,128)(2,1)S(1)} %get-tuple-element.51), channel_id=1, source_target_pairs={{0,96},{32,64},{64,32},{96,0},{1,97},{33,65},{65,33},{97,1},{2,98}... | collective-permute-start | bytes 147464 | tf_op jit(solution)/shard_map/ppermute | solution.py:460
  78.3 1.2 %collective-permute-done.18.refs_2_ = bf16[96,256]{1,0:T(8,128)(2,1)S(1)} collective-permute-done((bf16[96,256]{1,0:T(8,128)(2,1)S(1)}, bf16[96,256]{1,0:T(8,128)(2,1)S(1)}, u32[]{:S(2)}, u32[]{:S(2)}) %collective-permute-start.18) | collective-permute-done | bytes 49184 | tf_op jit(solution)/shard_map/ppermute | solution.py:459
  79.5 1.6 %collective-permute-done.19.refs_3_ = bf16[96,256]{1,0:T(8,128)(2,1)S(1)} collective-permute-done((bf16[96,256]{1,0:T(8,128)(2,1)S(1)}, bf16[96,256]{1,0:T(8,128)(2,1)S(1)}, u32[]{:S(2)}, u32[]{:S(2)}) %collective-permute-start.19) | collective-permute-done | bytes 49184 | tf_op jit(solution)/shard_map/ppermute | solution.py:460
  81.1 1.4 %shard_map.87 = s16[128,24,256]{2,1,0:T(8,128)(2,1)S(1)} custom-call(bf16[1920,384]{1,0:T(8,128)(2,1)S(1)} %get-tuple-element.34.early_a.images_ref, bf16[1344,384]{1,0:T(8,128)(2,1)S(1)} %get-tuple-element.35.early_b.texts_ref, bf16[96,256]{1,0:T(8,128)(2,1)S(1)} %get-tuple-element.48.refs_0_, bf16[96,256]{1,0:T(8,128)(2,1)S(1)} %collective-permute-done.17.refs_1_, ...), custom_call_target="tpu_custom_call" | custom-call | flops 1207959552 | bytes 6291456 | tf_op jit(solution)/shard_map/pallas_call | solution.py:466
  82.5 33.0 %all_to_all.5.coded_ref = s16[128,24,256]{2,1,0:T(8,128)(2,1)S(1)} all-to-all(s16[128,24,256]{2,1,0:T(8,128)(2,1)S(1)} %shard_map.87), channel_id=1, replica_groups=mesh['xl'=2,'core'=2,'z'=4,'xh'=2,'y'=4] {'xl','core','z','xh','y'}, dimensions={0} | all-to-all | bytes 3145728 | tf_op jit(solution)/shard_map/all_to_all | solution.py:472
  115.5 1.2 %shard_map.88 = f32[21,1024]{1,0:T(8,128)} custom-call(s16[128,24,256]{2,1,0:T(8,128)(2,1)S(1)} %all_to_all.5.coded_ref), custom_call_target="tpu_custom_call" | custom-call | bytes 2097152 | tf_op jit(solution)/shard_map/pallas_call | solution.py:473
  (57 shorter events, 6.9 us)
Async XLA Ops:
  4.9 23.4 %copy-start.1 = (bf16[384,1664]{1,0:T(8,128)(2,1)S(1)}, bf16[384,1664]{1,0:T(8,128)(2,1)}, u32[]{:S(2)}) copy-start(bf16[384,1664]{1,0:T(8,128)(2,1)} %image_feats.3) | copy-start | bytes 3833860
  4.9 23.4 %copy-start.2 = (bf16[384,1024]{1,0:T(8,128)(2,1)S(1)}, bf16[384,1024]{1,0:T(8,128)(2,1)}, u32[]{:S(2)}) copy-start(bf16[384,1024]{1,0:T(8,128)(2,1)} %text_feats.3) | copy-start | bytes 2359300
  4.9 8.1 %collective-permute-start.1 = (bf16[96,1024]{1,0:T(8,128)(2,1)}, bf16[96,1024]{1,0:T(8,128)(2,1)S(1)}, u32[]{:S(2)}, u32[]{:S(2)}) collective-permute-start(bf16[96,1024]{1,0:T(8,128)(2,1)} %get-tuple-element.36.emb), channel_id=1, source_target_pairs={{0,68},{4,64},{64,4},{68,0},{1,69},{5,65},{65,5},{69,1},{2,70},{6,... | collective-permute-start | bytes 589832 | tf_op jit(solution)/shard_map/ppermute | solution.py:395
  8.3 12.3 %collective-permute-start.6 = (bf16[208,1024]{1,0:T(8,128)(2,1)}, bf16[208,1024]{1,0:T(8,128)(2,1)S(1)}, u32[]{:S(2)}, u32[]{:S(2)}) collective-permute-start(bf16[208,1024]{1,0:T(8,128)(2,1)} %get-tuple-element.33.me.emb), channel_id=1, source_target_pairs={{0,24},{8,0},{16,8},{24,16},{1,25},{9,1},{17,9},{25,17},{2,26},{10... | collective-permute-start | bytes 1277960 | tf_op jit(solution)/shard_map/ppermute | solution.py:32
  12.1 11.9 %collective-permute-start = (bf16[208,1024]{1,0:T(8,128)(2,1)}, bf16[208,1024]{1,0:T(8,128)(2,1)S(1)}, u32[]{:S(2)}, u32[]{:S(2)}) collective-permute-start(bf16[208,1024]{1,0:T(8,128)(2,1)} %get-tuple-element.33.me.emb), channel_id=1, source_target_pairs={{0,8},{8,16},{16,24},{24,0},{1,9},{9,17},{17,25},{25,1},{2,10},{10... | collective-permute-start | bytes 1277960 | tf_op jit(solution)/shard_map/ppermute | solution.py:32
  13.1 11.0 %collective-permute-start.3 = (bf16[192,1024]{1,0:T(8,128)(2,1)S(1)}, bf16[192,1024]{1,0:T(8,128)(2,1)S(1)}, u32[]{:S(2)}, u32[]{:S(2)}) collective-permute-start(bf16[192,1024]{1,0:T(8,128)(2,1)S(1)} %constant_dynamic-update-slice_fusion.me), channel_id=1, source_target_pairs={{0,1},{1,2},{2,3},{3,0},{4,5},{5,6},{6,7},{7,4},{8,9},{9,10},{10,1... | collective-permute-start | bytes 1179656 | tf_op jit(solution)/shard_map/ppermute | solution.py:32
  14.4 11.0 %collective-permute-start.2 = (bf16[192,1024]{1,0:T(8,128)(2,1)S(1)}, bf16[192,1024]{1,0:T(8,128)(2,1)S(1)}, u32[]{:S(2)}, u32[]{:S(2)}) collective-permute-start(bf16[192,1024]{1,0:T(8,128)(2,1)S(1)} %constant_dynamic-update-slice_fusion.me), channel_id=1, source_target_pairs={{0,3},{1,0},{2,1},{3,2},{4,7},{5,4},{6,5},{7,6},{8,11},{9,8},{10,9... | collective-permute-start | bytes 1179656 | tf_op jit(solution)/shard_map/ppermute | solution.py:32
  20.6 9.9 %collective-permute-start.8 = (bf16[112,1024]{1,0:T(8,128)(2,1)S(1)}, bf16[112,1024]{1,0:T(8,128)(2,1)S(1)}, u32[]{:S(2)}, u32[]{:S(2)}) collective-permute-start(bf16[112,1024]{1,0:T(8,128)(2,1)S(1)} %slice.19), channel_id=1, source_target_pairs={{0,24},{8,0},{16,8},{24,16},{1,25},{9,1},{17,9},{25,17},{2,26},{10... | collective-permute-start | bytes 688136 | tf_op jit(solution)/shard_map/ppermute | solution.py:32
  24.0 6.5 %collective-permute-start.7 = (bf16[96,1024]{1,0:T(8,128)(2,1)S(1)}, bf16[96,1024]{1,0:T(8,128)(2,1)S(1)}, u32[]{:S(2)}, u32[]{:S(2)}) collective-permute-start(bf16[96,1024]{1,0:T(8,128)(2,1)S(1)} %slice.18), channel_id=1, source_target_pairs={{0,8},{8,16},{16,24},{24,0},{1,9},{9,17},{17,25},{25,1},{2,10},{10... | collective-permute-start | bytes 589832 | tf_op jit(solution)/shard_map/ppermute | solution.py:32
  24.1 9.3 %collective-permute-start.4 = (bf16[96,1024]{1,0:T(8,128)(2,1)S(1)}, bf16[96,1024]{1,0:T(8,128)(2,1)S(1)}, u32[]{:S(2)}, u32[]{:S(2)}) collective-permute-start(bf16[96,1024]{1,0:T(8,128)(2,1)S(1)} %slice.16), channel_id=1, source_target_pairs={{0,1},{1,2},{2,3},{3,0},{4,5},{5,6},{6,7},{7,4},{8,9},{9,10},{10,1... | collective-permute-start | bytes 589832 | tf_op jit(solution)/shard_map/ppermute | solution.py:32
  25.5 7.9 %collective-permute-start.5 = (bf16[96,1024]{1,0:T(8,128)(2,1)S(1)}, bf16[96,1024]{1,0:T(8,128)(2,1)S(1)}, u32[]{:S(2)}, u32[]{:S(2)}) collective-permute-start(bf16[96,1024]{1,0:T(8,128)(2,1)S(1)} %slice.17), channel_id=1, source_target_pairs={{0,3},{1,0},{2,1},{3,2},{4,7},{5,4},{6,5},{7,6},{8,11},{9,8},{10,9... | collective-permute-start | bytes 589832 | tf_op jit(solution)/shard_map/ppermute | solution.py:32
  30.7 5.8 %collective-permute-start.9 = (bf16[784,1024]{1,0:T(8,128)(2,1)S(1)}, bf16[784,1024]{1,0:T(8,128)(2,1)S(1)}, u32[]{:S(2)}, u32[]{:S(2)}) collective-permute-start(bf16[784,1024]{1,0:T(8,128)(2,1)S(1)} %shard_map.75.images_ref.refs_1_), channel_id=1, source_target_pairs={{0,32},{32,0},{1,33},{33,1},{2,34},{34,2},{3,35},{35,3},{4,36},{36... | collective-permute-start | bytes 4816904 | tf_op jit(solution)/shard_map/ppermute | solution.py:402
  39.9 8.7 %collective-permute-start.10 = (f32[768,1024]{1,0:T(8,128)S(1)}, f32[768,1024]{1,0:T(8,128)S(1)}, u32[]{:S(2)}, u32[]{:S(2)}) collective-permute-start(f32[768,1024]{1,0:T(8,128)S(1)} %get-tuple-element.39), channel_id=1, source_target_pairs={{0,32},{32,0},{1,33},{33,1},{2,34},{34,2},{3,35},{35,3},{4,36},{36... | collective-permute-start | bytes 9437192 | tf_op jit(solution)/shard_map/ppermute | solution.py:437
  43.7 10.8 %collective-permute-start.21 = (s16[96,1408]{1,0:T(8,128)(2,1)S(1)}, s16[96,1408]{1,0:T(8,128)(2,1)S(1)}, u32[]{:S(2)}, u32[]{:S(2)}) collective-permute-start(s16[96,1408]{1,0:T(8,128)(2,1)S(1)} %get-tuple-element.55), channel_id=1, source_target_pairs={{0,68},{4,64},{64,4},{68,0},{1,69},{5,65},{65,5},{69,1},{2,70},{6,... | collective-permute-start | bytes 811016 | tf_op jit(solution)/shard_map/ppermute | solution.py:444
  45.9 14.6 %collective-permute-start.14 = (s16[192,1408]{1,0:T(8,128)(2,1)S(1)}, s16[192,1408]{1,0:T(8,128)(2,1)S(1)}, u32[]{:S(2)}, u32[]{:S(2)}) collective-permute-start(s16[192,1408]{1,0:T(8,128)(2,1)S(1)} %get-tuple-element.46), channel_id=1, source_target_pairs={{0,1},{1,2},{2,3},{3,0},{4,5},{5,6},{6,7},{7,4},{8,9},{9,10},{10,1... | collective-permute-start | bytes 1622024 | tf_op jit(solution)/shard_map/ppermute | solution.py:32
  45.9 14.6 %collective-permute-start.20 = (s16[192,1408]{1,0:T(8,128)(2,1)S(1)}, s16[192,1408]{1,0:T(8,128)(2,1)S(1)}, u32[]{:S(2)}, u32[]{:S(2)}) collective-permute-start(s16[192,1408]{1,0:T(8,128)(2,1)S(1)} %get-tuple-element.53), channel_id=1, source_target_pairs={{0,3},{1,0},{2,1},{3,2},{4,7},{5,4},{6,5},{7,6},{8,11},{9,8},{10,9... | collective-permute-start | bytes 1622024 | tf_op jit(solution)/shard_map/ppermute | solution.py:32
  50.6 15.9 %collective-permute-start.11 = (s16[192,1408]{1,0:T(8,128)(2,1)S(1)}, s16[192,1408]{1,0:T(8,128)(2,1)S(1)}, u32[]{:S(2)}, u32[]{:S(2)}) collective-permute-start(s16[192,1408]{1,0:T(8,128)(2,1)S(1)} %get-tuple-element.41), channel_id=1, source_target_pairs={{0,8},{8,16},{16,24},{24,0},{1,9},{9,17},{17,25},{25,1},{2,10},{10... | collective-permute-start | bytes 1622024 | tf_op jit(solution)/shard_map/ppermute | solution.py:32
  52.3 14.2 %collective-permute-start.12 = (s16[192,1408]{1,0:T(8,128)(2,1)S(1)}, s16[192,1408]{1,0:T(8,128)(2,1)S(1)}, u32[]{:S(2)}, u32[]{:S(2)}) collective-permute-start(s16[192,1408]{1,0:T(8,128)(2,1)S(1)} %get-tuple-element.42), channel_id=1, source_target_pairs={{0,24},{8,0},{16,8},{24,16},{1,25},{9,1},{17,9},{25,17},{2,26},{10... | collective-permute-start | bytes 1622024 | tf_op jit(solution)/shard_map/ppermute | solution.py:32
  54.5 9.4 %collective-permute-start.13 = (s16[96,1408]{1,0:T(8,128)(2,1)S(1)}, s16[96,1408]{1,0:T(8,128)(2,1)S(1)}, u32[]{:S(2)}, u32[]{:S(2)}) collective-permute-start(s16[96,1408]{1,0:T(8,128)(2,1)S(1)} %get-tuple-element.44), channel_id=1, source_target_pairs={{0,64},{64,0},{1,65},{65,1},{2,66},{66,2},{3,67},{67,3},{4,68},{68... | collective-permute-start | bytes 811016 | tf_op jit(solution)/shard_map/ppermute | solution.py:447
  60.9 8.0 %collective-permute-start.23 = (s16[96,1408]{1,0:T(8,128)(2,1)S(1)}, s16[96,1408]{1,0:T(8,128)(2,1)S(1)}, u32[]{:S(2)}, u32[]{:S(2)}) collective-permute-start(s16[96,1408]{1,0:T(8,128)(2,1)S(1)} %shard_map.85), channel_id=1, source_target_pairs={{0,68},{4,64},{64,4},{68,0},{1,69},{5,65},{65,5},{69,1},{2,70},{6,... | collective-permute-start | bytes 811016 | tf_op jit(solution)/shard_map/ppermute | solution.py:444
  61.5 8.0 %collective-permute-start.22 = (s16[96,1408]{1,0:T(8,128)(2,1)S(1)}, s16[96,1408]{1,0:T(8,128)(2,1)S(1)}, u32[]{:S(2)}, u32[]{:S(2)}) collective-permute-start(s16[96,1408]{1,0:T(8,128)(2,1)S(1)} %shard_map.84), channel_id=1, source_target_pairs={{0,2},{1,3},{2,0},{3,1},{4,6},{5,7},{6,4},{7,5},{8,10},{9,11},{10,... | collective-permute-start | bytes 811016 | tf_op jit(solution)/shard_map/ppermute | solution.py:32
  63.9 5.6 %copy-start.3 = (bf16[96,1024]{1,0:T(8,128)(2,1)S(1)}, bf16[96,1024]{1,0:T(8,128)(2,1)}, u32[]{:S(2)}) copy-start(bf16[96,1024]{1,0:T(8,128)(2,1)} %get-tuple-element.36.emb) | copy-start | bytes 589828
  63.9 5.6 %copy-start.5 = (f32[96,128]{1,0:T(8,128)S(1)}, f32[96,128]{1,0:T(8,128)}, u32[]{:S(2)}) copy-start(f32[96,128]{1,0:T(8,128)} %get-tuple-element.56.inverse) | copy-start | bytes 147460
  64.2 10.2 %collective-permute-start.15 = (s16[96,1408]{1,0:T(8,128)(2,1)S(1)}, s16[96,1408]{1,0:T(8,128)(2,1)S(1)}, u32[]{:S(2)}, u32[]{:S(2)}) collective-permute-start(s16[96,1408]{1,0:T(8,128)(2,1)S(1)} %shard_map.80), channel_id=1, source_target_pairs={{0,16},{8,24},{16,0},{24,8},{1,17},{9,25},{17,1},{25,9},{2,18},{10... | collective-permute-start | bytes 811016 | tf_op jit(solution)/shard_map/ppermute | solution.py:32
  66.9 7.6 %copy-start.4 = (f32[96,128]{1,0:T(8,128)S(1)}, f32[96,128]{1,0:T(8,128)}, u32[]{:S(2)}) copy-start(f32[96,128]{1,0:T(8,128)} %get-tuple-element.47.inverse) | copy-start | bytes 147460
  66.9 7.6 %collective-permute-start.16 = (s16[96,1408]{1,0:T(8,128)(2,1)S(1)}, s16[96,1408]{1,0:T(8,128)(2,1)S(1)}, u32[]{:S(2)}, u32[]{:S(2)}) collective-permute-start(s16[96,1408]{1,0:T(8,128)(2,1)S(1)} %shard_map.81), channel_id=1, source_target_pairs={{0,64},{64,0},{1,65},{65,1},{2,66},{66,2},{3,67},{67,3},{4,68},{68... | collective-permute-start | bytes 811016 | tf_op jit(solution)/shard_map/ppermute | solution.py:447
  70.2 6.4 %collective-permute-start.24 = (bf16[96,256]{1,0:T(8,128)(2,1)S(1)}, bf16[96,256]{1,0:T(8,128)(2,1)S(1)}, u32[]{:S(2)}, u32[]{:S(2)}) collective-permute-start(bf16[96,256]{1,0:T(8,128)(2,1)S(1)} %get-tuple-element.58), channel_id=1, source_target_pairs={{0,32},{32,0},{1,33},{33,1},{2,34},{34,2},{3,35},{35,3},{4,36},{36... | collective-permute-start | bytes 147464 | tf_op jit(solution)/shard_map/ppermute | solution.py:458
  72.7 5.6 %collective-permute-start.25 = (bf16[96,256]{1,0:T(8,128)(2,1)S(1)}, bf16[96,256]{1,0:T(8,128)(2,1)S(1)}, u32[]{:S(2)}, u32[]{:S(2)}) collective-permute-start(bf16[96,256]{1,0:T(8,128)(2,1)S(1)} %get-tuple-element.59), channel_id=1, source_target_pairs={{0,64},{64,0},{1,65},{65,1},{2,66},{66,2},{3,67},{67,3},{4,68},{68... | collective-permute-start | bytes 147464 | tf_op jit(solution)/shard_map/ppermute | solution.py:459
  72.7 5.6 %collective-permute-start.26 = (bf16[96,256]{1,0:T(8,128)(2,1)S(1)}, bf16[96,256]{1,0:T(8,128)(2,1)S(1)}, u32[]{:S(2)}, u32[]{:S(2)}) collective-permute-start(bf16[96,256]{1,0:T(8,128)(2,1)S(1)} %get-tuple-element.60), channel_id=1, source_target_pairs={{0,96},{32,64},{64,32},{96,0},{1,97},{33,65},{65,33},{97,1},{2,98}... | collective-permute-start | bytes 147464 | tf_op jit(solution)/shard_map/ppermute | solution.py:460
  75.1 3.2 %collective-permute-start.17 = (bf16[96,256]{1,0:T(8,128)(2,1)S(1)}, bf16[96,256]{1,0:T(8,128)(2,1)S(1)}, u32[]{:S(2)}, u32[]{:S(2)}) collective-permute-start(bf16[96,256]{1,0:T(8,128)(2,1)S(1)} %get-tuple-element.49), channel_id=1, source_target_pairs={{0,32},{32,0},{1,33},{33,1},{2,34},{34,2},{3,35},{35,3},{4,36},{36... | collective-permute-start | bytes 147464 | tf_op jit(solution)/shard_map/ppermute | solution.py:458
  76.6 3.0 %collective-permute-start.18 = (bf16[96,256]{1,0:T(8,128)(2,1)S(1)}, bf16[96,256]{1,0:T(8,128)(2,1)S(1)}, u32[]{:S(2)}, u32[]{:S(2)}) collective-permute-start(bf16[96,256]{1,0:T(8,128)(2,1)S(1)} %get-tuple-element.50), channel_id=1, source_target_pairs={{0,64},{64,0},{1,65},{65,1},{2,66},{66,2},{3,67},{67,3},{4,68},{68... | collective-permute-start | bytes 147464 | tf_op jit(solution)/shard_map/ppermute | solution.py:459
  76.6 4.5 %collective-permute-start.19 = (bf16[96,256]{1,0:T(8,128)(2,1)S(1)}, bf16[96,256]{1,0:T(8,128)(2,1)S(1)}, u32[]{:S(2)}, u32[]{:S(2)}) collective-permute-start(bf16[96,256]{1,0:T(8,128)(2,1)S(1)} %get-tuple-element.51), channel_id=1, source_target_pairs={{0,96},{32,64},{64,32},{96,0},{1,97},{33,65},{65,33},{97,1},{2,98}... | collective-permute-start | bytes 147464 | tf_op jit(solution)/shard_map/ppermute | solution.py:460
  (1 other events, 2.2 us)

commit v10 on v8

--- a/solution.py
+++ b/solution.py
@@ -268,11 +268,8 @@
 
 def given_kernel(where_ref, scale_ref, shift_ref, texts_ref, images_ref, coef_ref, given_ref):
     coefficients(where_ref, scale_ref, shift_ref, images_ref, texts_ref, coef_ref)
-    given_ref[...] = image_terms(coef_ref, texts_ref, 0)
-
-
-def given_rest_kernel(texts_ref, coef_ref, given_ref):
-    given_ref[...] = image_terms(coef_ref, texts_ref, 1)
+    for part in range(2):
+        given_ref[part * ROWS : (part + 1) * ROWS, :] = image_terms(coef_ref, texts_ref, part)
 
 
 def text_kernel(own_coef, images_ref, others_coef, others_ref, *outs):
@@ -282,7 +279,8 @@
 
 
 def kept_kernel(part, texts_ref, coef_ref, taken_ref, *outs):
-    share_out(image_terms(coef_ref, texts_ref, part) + taken_ref[...], outs)
+    taken = taken_ref[part * ROWS : (part + 1) * ROWS, :]
+    share_out(image_terms(coef_ref, texts_ref, part) + taken, outs)
 
 
 def kept_rest_kernel(texts_ref, coef_ref, taken_ref, early_ref, *outs):
@@ -436,20 +434,18 @@
         in_specs=[SMEM] * 3 + [VMEM] * 6 + [ANY] * 2, out_specs=[VMEM] * 2,
     )(where, log_scale, logit_bias, *text_pieces, images, image_groups, text_groups)
     others_coef, given = call(
-        given_kernel, [coef, shape(ROWS, E)], 2 * flops, 8 << 20, 24,
+        given_kernel, [coef, shape(TILE, E)], 2 * flops, 8 << 20, 24,
         in_specs=[SMEM] * 3 + [VMEM] * 2, out_specs=[VMEM] * 2,
     )(where, log_scale, logit_bias, texts, others)
     taken = lax.ppermute(given, "core", SWAP)
     sides = own_coef, images, others_coef, others
     text_parts = run(text_kernel, ways + rest, 2, 4)(*sides)
     text_ways, text_rest = text_parts[:3], text_parts[3:]
-    given_rest, = run(given_rest_kernel, [shape(ROWS, E)], 0.5, 2)(texts, others_coef)
-    taken_rest = lax.ppermute(given_rest, "core", SWAP)
     image_ways = run(kept_kernel, ways, 0.5, 3, 0)(texts, own_coef, taken)
     image_rest = call(
         kept_rest_kernel, rest, 4 * flops, 6 << 20, 24,
         in_specs=[VMEM] * 3 + [ANY], out_specs=[VMEM] * 2,
-    )(texts, own_coef, taken_rest, image_ways[0])
+    )(texts, own_coef, taken, image_ways[0])
     text_sums = ring_scatter(
         *text_ways, *text_rest, "y", lambda a: lax.ppermute(a, ("xl", "xh"), FLIP)
     )

time: 117 us -> 117 us (level)
    pallas_call x2 -> x1, Pallas kernels: 3.59 us -> 3.39 us  [body(): call(given_kernel, [coef, shape(TILE, E)], 2 * flops, 8 << 20, 24, in_spe...]
  transfers between devices with their start and end apart: 28 -> 27, of which waited for: 7 -> 7; matrix products, arithmetic and copies ran while one was open for 1% -> 1% of each run, Pallas kernels for 11% -> 10%
where the time goes in v10:
time: 117 us
  starting transfers between devices  41.3 us (35%)
  blocking collectives  32.9 us (28%)
  Pallas kernels  23.1 us (20%)
  waiting for transfers between devices  16.7 us (14%)
  between operations  1.58 us (1%)
    all_to_all x1, blocking collectives, body(): coded = lax.all_to_all(coded, AXES, split_axis=0, concat_axis=0, tiled=True)  32.9 us
    ppermute x14, starting transfers between devices, shifted(): return lax.ppermute(array, axis, [(i, (i + by) % 4) for i in range(4)])  24.2 us
    ppermute x14, waiting for transfers between devices, shifted(): return lax.ppermute(array, axis, [(i, (i + by) % 4) for i in range(4)])  10.8 us
    pallas_call x1, Pallas kernels, body(): call(embed_kernel, [shape(QUARTER, E, dtype=BF16), shape(QUARTER, 128), s...  4.88 us
    ppermute x2, starting transfers between devices, tower_pieces(): lax.ppermute(other_core, 'core', SWAP)  4.04 us
    ppermute x2, starting transfers between devices, tower_pieces(): lax.ppermute(other_both, TOWER, [(i, 3 - i) for i in range(4)])  3.42 us
    ppermute x1, starting transfers between devices, body(): other_texts = lax.ppermute(own_texts, ('xl', 'xh'), FLIP)  3.39 us
    pallas_call x1, Pallas kernels, body(): call(given_kernel, [coef, shape(TILE, E)], 2 * flops, 8 << 20, 24, in_spe...  3.39 us
  transfers between devices with their start and end apart: 27, of which 7 were waited for; matrix products, arithmetic and copies ran while one was open for 1% of the time, Pallas kernels for 10%

profile of v10, /device:TPU:1, one launch (start us, length us, event | category | flops | bytes accessed | tf_op | source)
XLA Modules:
  0.0 116.6 jit_solution(6355552362145168352)
XLA Ops:
  0.0 4.9 %shard_map.73 = (bf16[96,1024]{1,0:T(8,128)(2,1)}, f32[96,128]{1,0:T(8,128)}, bf16[208,1024]{1,0:T(8,128)(2,1)}, f32[96,128]{1,0:T(8,128)}) custom-call(s32[1]{0:T(128)} %bitcast.where_ref, s32[3,128]{1,0:T(4,128)} %bitcast.2, bf16[384,1024]{1,0:T(8,128)(2,1)} %text_feats.3, bf16[384,1664]{1,0:T(8,128)(2,1)} %image_feats.3, bf16[1024,1024]{1,0:T(8,128)(2,1)} %text_weight.1, ...), custom_call_target="tpu_custom_call" | custom-call | flops 855638016 | bytes 8388608 | tf_op jit(solution)/shard_map/pallas_call | solution.py:383
  4.9 3.4 %collective-permute-start.1 = (bf16[96,1024]{1,0:T(8,128)(2,1)}, bf16[96,1024]{1,0:T(8,128)(2,1)S(1)}, u32[]{:S(2)}, u32[]{:S(2)}) collective-permute-start(bf16[96,1024]{1,0:T(8,128)(2,1)} %get-tuple-element.36.emb), channel_id=1, source_target_pairs={{0,68},{4,64},{64,4},{68,0},{1,69},{5,65},{65,5},{69,1},{2,70},{6,... | collective-permute-start | bytes 589832 | tf_op jit(solution)/shard_map/ppermute | solution.py:398
  8.3 3.8 %collective-permute-start.6 = (bf16[208,1024]{1,0:T(8,128)(2,1)}, bf16[208,1024]{1,0:T(8,128)(2,1)S(1)}, u32[]{:S(2)}, u32[]{:S(2)}) collective-permute-start(bf16[208,1024]{1,0:T(8,128)(2,1)} %get-tuple-element.33.me.emb), channel_id=1, source_target_pairs={{0,24},{8,0},{16,8},{24,16},{1,25},{9,1},{17,9},{25,17},{2,26},{10... | collective-permute-start | bytes 1277960 | tf_op jit(solution)/shard_map/ppermute | solution.py:32
  13.0 1.4 %collective-permute-start.3 = (bf16[192,1024]{1,0:T(8,128)(2,1)S(1)}, bf16[192,1024]{1,0:T(8,128)(2,1)S(1)}, u32[]{:S(2)}, u32[]{:S(2)}) collective-permute-start(bf16[192,1024]{1,0:T(8,128)(2,1)S(1)} %constant_dynamic-update-slice_fusion.me), channel_id=1, source_target_pairs={{0,1},{1,2},{2,3},{3,0},{4,5},{5,6},{6,7},{7,4},{8,9},{9,10},{10,1... | collective-permute-start | bytes 1179656 | tf_op jit(solution)/shard_map/ppermute | solution.py:32
  14.4 1.5 %collective-permute-start.2 = (bf16[192,1024]{1,0:T(8,128)(2,1)S(1)}, bf16[192,1024]{1,0:T(8,128)(2,1)S(1)}, u32[]{:S(2)}, u32[]{:S(2)}) collective-permute-start(bf16[192,1024]{1,0:T(8,128)(2,1)S(1)} %constant_dynamic-update-slice_fusion.me), channel_id=1, source_target_pairs={{0,3},{1,0},{2,1},{3,2},{4,7},{5,4},{6,5},{7,6},{8,11},{9,8},{10,9... | collective-permute-start | bytes 1179656 | tf_op jit(solution)/shard_map/ppermute | solution.py:32
  15.9 4.6 %collective-permute-done.6.after = bf16[208,1024]{1,0:T(8,128)(2,1)S(1)} collective-permute-done((bf16[208,1024]{1,0:T(8,128)(2,1)}, bf16[208,1024]{1,0:T(8,128)(2,1)S(1)}, u32[]{:S(2)}, u32[]{:S(2)}) %collective-permute-start.6) | collective-permute-done | bytes 426016 | tf_op jit(solution)/shard_map/ppermute | solution.py:32
  20.6 3.4 %collective-permute-start.8 = (bf16[112,1024]{1,0:T(8,128)(2,1)S(1)}, bf16[112,1024]{1,0:T(8,128)(2,1)S(1)}, u32[]{:S(2)}, u32[]{:S(2)}) collective-permute-start(bf16[112,1024]{1,0:T(8,128)(2,1)S(1)} %slice.19), channel_id=1, source_target_pairs={{0,24},{8,0},{16,8},{24,16},{1,25},{9,1},{17,9},{25,17},{2,26},{10... | collective-permute-start | bytes 688136 | tf_op jit(solution)/shard_map/ppermute | solution.py:32
  24.1 1.4 %collective-permute-start.4 = (bf16[96,1024]{1,0:T(8,128)(2,1)S(1)}, bf16[96,1024]{1,0:T(8,128)(2,1)S(1)}, u32[]{:S(2)}, u32[]{:S(2)}) collective-permute-start(bf16[96,1024]{1,0:T(8,128)(2,1)S(1)} %slice.16), channel_id=1, source_target_pairs={{0,1},{1,2},{2,3},{3,0},{4,5},{5,6},{6,7},{7,4},{8,9},{9,10},{10,1... | collective-permute-start | bytes 589832 | tf_op jit(solution)/shard_map/ppermute | solution.py:32
  25.5 1.5 %collective-permute-start.5 = (bf16[96,1024]{1,0:T(8,128)(2,1)S(1)}, bf16[96,1024]{1,0:T(8,128)(2,1)S(1)}, u32[]{:S(2)}, u32[]{:S(2)}) collective-permute-start(bf16[96,1024]{1,0:T(8,128)(2,1)S(1)} %slice.17), channel_id=1, source_target_pairs={{0,3},{1,0},{2,1},{3,2},{4,7},{5,4},{6,5},{7,6},{8,11},{9,8},{10,9... | collective-permute-start | bytes 589832 | tf_op jit(solution)/shard_map/ppermute | solution.py:32
  28.3 2.2 %shard_map.74 = (bf16[1920,384]{1,0:T(8,128)(2,1)S(1)}, bf16[1344,384]{1,0:T(8,128)(2,1)S(1)}) custom-call(s32[1]{0:T(128)} %bitcast.where_ref, bf16[384,1664]{1,0:T(8,128)(2,1)S(1)} %copy-done.1, bf16[384,1024]{1,0:T(8,128)(2,1)S(1)} %copy-done.2, bf16[208,1024]{1,0:T(8,128)(2,1)S(1)} %collective-permute-done.early.before), custom_call_target="tpu_custom_call" | custom-call | flops 962592768 | bytes 5242880 | tf_op jit(solution)/shard_map/pallas_call | solution.py:408
  30.7 2.7 %collective-permute-start.9 = (bf16[784,1024]{1,0:T(8,128)(2,1)S(1)}, bf16[784,1024]{1,0:T(8,128)(2,1)S(1)}, u32[]{:S(2)}, u32[]{:S(2)}) collective-permute-start(bf16[784,1024]{1,0:T(8,128)(2,1)S(1)} %shard_map.75.images_ref.refs_1_), channel_id=1, source_target_pairs={{0,32},{32,0},{1,33},{33,1},{2,34},{34,2},{3,35},{35,3},{4,36},{36... | collective-permute-start | bytes 4816904 | tf_op jit(solution)/shard_map/ppermute | solution.py:405
  33.4 2.0 %shard_map.76 = (bf16[768,1024]{1,0:T(8,128)(2,1)S(1)}, bf16[768,768]{1,0:T(8,128)(2,1)S(1)}) custom-call(s32[1]{0:T(128)} %bitcast.where_ref, f32[1]{0:T(128)S(6)} %copy.9.scale_ref, f32[1]{0:T(128)S(6)} %copy.10.shift_ref, bf16[192,1024]{1,0:T(8,128)(2,1)S(1)} %constant_dynamic-update-slice_fusion.me, bf16[192,1024]{1,0:T(8,128)(2,1)S(1)} %collective-permute-done.2.after, ...), custom_call_target="tpu_custom_call" | custom-call | flops 19327352832 | bytes 6291456 | tf_op jit(solution)/shard_map/pallas_call | solution.py:432
  36.5 3.4 %shard_map.77 = (bf16[768,768]{1,0:T(8,128)(2,1)S(1)}, f32[768,1024]{1,0:T(8,128)S(1)}) custom-call(s32[1]{0:T(128)} %bitcast.where_ref, f32[1]{0:T(128)S(6)} %copy.9.scale_ref, f32[1]{0:T(128)S(6)} %copy.10.shift_ref, bf16[768,1024]{1,0:T(8,128)(2,1)S(1)} %get-tuple-element.37.texts_ref.refs_0_, bf16[784,1024]{1,0:T(8,128)(2,1)S(1)} %collective-permute-done.9.images_ref.refs_3_), custom_call_target="tpu_custom_call" | custom-call | flops 2415919104 | bytes 8388608 | tf_op jit(solution)/shard_map/pallas_call | solution.py:436
  40.5 3.1 %shard_map.80 = (f32[96,1024]{1,0:T(8,128)S(1)}, s16[96,1408]{1,0:T(8,128)(2,1)S(1)}, s16[192,1408]{1,0:T(8,128)(2,1)S(1)}, s16[192,1408]{1,0:T(8,128)(2,1)S(1)}, f32[192,1024]{1,0:T(8,128)S(1)}) custom-call(bf16[768,768]{1,0:T(8,128)(2,1)S(1)} %get-tuple-element.38.refs_1_.coef_ref.refs_0_, bf16[784,1024]{1,0:T(8,128)(2,1)S(1)} %shard_map.75.images_ref.refs_1_, ...), custom_call_target="tpu_custom_call" | custom-call | flops 2415919104 | bytes 6291456 | tf_op jit(solution)/shard_map/pallas_call | solution.py:442
  43.6 2.3 %collective-permute-start.21 = (s16[96,1408]{1,0:T(8,128)(2,1)S(1)}, s16[96,1408]{1,0:T(8,128)(2,1)S(1)}, u32[]{:S(2)}, u32[]{:S(2)}) collective-permute-start(s16[96,1408]{1,0:T(8,128)(2,1)S(1)} %get-tuple-element.55), channel_id=1, source_target_pairs={{0,68},{4,64},{64,4},{68,0},{1,69},{5,65},{65,5},{69,1},{2,70},{6,... | collective-permute-start | bytes 811016 | tf_op jit(solution)/shard_map/ppermute | solution.py:450
  45.9 2.7 %collective-permute-start.20 = (s16[192,1408]{1,0:T(8,128)(2,1)S(1)}, s16[192,1408]{1,0:T(8,128)(2,1)S(1)}, u32[]{:S(2)}, u32[]{:S(2)}) collective-permute-start(s16[192,1408]{1,0:T(8,128)(2,1)S(1)} %get-tuple-element.53), channel_id=1, source_target_pairs={{0,3},{1,0},{2,1},{3,2},{4,7},{5,4},{6,5},{7,6},{8,11},{9,8},{10,9... | collective-permute-start | bytes 1622024 | tf_op jit(solution)/shard_map/ppermute | solution.py:32
  48.6 1.2 shard_map.78
  49.7 1.7 %collective-permute-start.11 = (s16[192,1408]{1,0:T(8,128)(2,1)S(1)}, s16[192,1408]{1,0:T(8,128)(2,1)S(1)}, u32[]{:S(2)}, u32[]{:S(2)}) collective-permute-start(s16[192,1408]{1,0:T(8,128)(2,1)S(1)} %get-tuple-element.42), channel_id=1, source_target_pairs={{0,8},{8,16},{16,24},{24,0},{1,9},{9,17},{17,25},{25,1},{2,10},{10... | collective-permute-start | bytes 1622024 | tf_op jit(solution)/shard_map/ppermute | solution.py:32
  52.4 2.2 %collective-permute-start.12 = (s16[192,1408]{1,0:T(8,128)(2,1)S(1)}, s16[192,1408]{1,0:T(8,128)(2,1)S(1)}, u32[]{:S(2)}, u32[]{:S(2)}) collective-permute-start(s16[192,1408]{1,0:T(8,128)(2,1)S(1)} %get-tuple-element.43), channel_id=1, source_target_pairs={{0,24},{8,0},{16,8},{24,16},{1,25},{9,1},{17,9},{25,17},{2,26},{10... | collective-permute-start | bytes 1622024 | tf_op jit(solution)/shard_map/ppermute | solution.py:32
  54.9 5.6 %collective-permute-done.14.early_ref.right = s16[192,1408]{1,0:T(8,128)(2,1)S(1)} collective-permute-done((s16[192,1408]{1,0:T(8,128)(2,1)S(1)}, s16[192,1408]{1,0:T(8,128)(2,1)S(1)}, u32[]{:S(2)}, u32[]{:S(2)}) %collective-permute-start.14) | collective-permute-done | bytes 540704 | tf_op jit(solution)/shard_map/ppermute | solution.py:32
  61.5 2.4 %collective-permute-start.22 = (s16[96,1408]{1,0:T(8,128)(2,1)S(1)}, s16[96,1408]{1,0:T(8,128)(2,1)S(1)}, u32[]{:S(2)}, u32[]{:S(2)}) collective-permute-start(s16[96,1408]{1,0:T(8,128)(2,1)S(1)} %shard_map.85), channel_id=1, source_target_pairs={{0,2},{1,3},{2,0},{3,1},{4,6},{5,7},{6,4},{7,5},{8,10},{9,11},{10,... | collective-permute-start | bytes 811016 | tf_op jit(solution)/shard_map/ppermute | solution.py:32
  64.2 2.3 %collective-permute-start.15 = (s16[96,1408]{1,0:T(8,128)(2,1)S(1)}, s16[96,1408]{1,0:T(8,128)(2,1)S(1)}, u32[]{:S(2)}, u32[]{:S(2)}) collective-permute-start(s16[96,1408]{1,0:T(8,128)(2,1)S(1)} %shard_map.81), channel_id=1, source_target_pairs={{0,16},{8,24},{16,0},{24,8},{1,17},{9,25},{17,1},{25,9},{2,18},{10... | collective-permute-start | bytes 811016 | tf_op jit(solution)/shard_map/ppermute | solution.py:32
  66.9 1.9 %collective-permute-done.23.got = s16[96,1408]{1,0:T(8,128)(2,1)S(1)} collective-permute-done((s16[96,1408]{1,0:T(8,128)(2,1)S(1)}, s16[96,1408]{1,0:T(8,128)(2,1)S(1)}, u32[]{:S(2)}, u32[]{:S(2)}) %collective-permute-start.23) | collective-permute-done | bytes 270368 | tf_op jit(solution)/shard_map/ppermute | solution.py:450
  70.1 2.6 %collective-permute-start.24 = (bf16[96,256]{1,0:T(8,128)(2,1)S(1)}, bf16[96,256]{1,0:T(8,128)(2,1)S(1)}, u32[]{:S(2)}, u32[]{:S(2)}) collective-permute-start(bf16[96,256]{1,0:T(8,128)(2,1)S(1)} %get-tuple-element.58), channel_id=1, source_target_pairs={{0,32},{32,0},{1,33},{33,1},{2,34},{34,2},{3,35},{35,3},{4,36},{36... | collective-permute-start | bytes 147464 | tf_op jit(solution)/shard_map/ppermute | solution.py:464
  72.7 1.7 %collective-permute-start.26 = (bf16[96,256]{1,0:T(8,128)(2,1)S(1)}, bf16[96,256]{1,0:T(8,128)(2,1)S(1)}, u32[]{:S(2)}, u32[]{:S(2)}) collective-permute-start(bf16[96,256]{1,0:T(8,128)(2,1)S(1)} %get-tuple-element.60), channel_id=1, source_target_pairs={{0,96},{32,64},{64,32},{96,0},{1,97},{33,65},{65,33},{97,1},{2,98}... | collective-permute-start | bytes 147464 | tf_op jit(solution)/shard_map/ppermute | solution.py:466
  75.0 1.5 %collective-permute-start.17 = (bf16[96,256]{1,0:T(8,128)(2,1)S(1)}, bf16[96,256]{1,0:T(8,128)(2,1)S(1)}, u32[]{:S(2)}, u32[]{:S(2)}) collective-permute-start(bf16[96,256]{1,0:T(8,128)(2,1)S(1)} %get-tuple-element.49), channel_id=1, source_target_pairs={{0,32},{32,0},{1,33},{33,1},{2,34},{34,2},{3,35},{35,3},{4,36},{36... | collective-permute-start | bytes 147464 | tf_op jit(solution)/shard_map/ppermute | solution.py:464
  76.5 1.7 %collective-permute-start.19 = (bf16[96,256]{1,0:T(8,128)(2,1)S(1)}, bf16[96,256]{1,0:T(8,128)(2,1)S(1)}, u32[]{:S(2)}, u32[]{:S(2)}) collective-permute-start(bf16[96,256]{1,0:T(8,128)(2,1)S(1)} %get-tuple-element.51), channel_id=1, source_target_pairs={{0,96},{32,64},{64,32},{96,0},{1,97},{33,65},{65,33},{97,1},{2,98}... | collective-permute-start | bytes 147464 | tf_op jit(solution)/shard_map/ppermute | solution.py:466
  78.3 1.2 %collective-permute-done.18.refs_2_ = bf16[96,256]{1,0:T(8,128)(2,1)S(1)} collective-permute-done((bf16[96,256]{1,0:T(8,128)(2,1)S(1)}, bf16[96,256]{1,0:T(8,128)(2,1)S(1)}, u32[]{:S(2)}, u32[]{:S(2)}) %collective-permute-start.18) | collective-permute-done | bytes 49184 | tf_op jit(solution)/shard_map/ppermute | solution.py:465
  79.5 1.6 %collective-permute-done.19.refs_3_ = bf16[96,256]{1,0:T(8,128)(2,1)S(1)} collective-permute-done((bf16[96,256]{1,0:T(8,128)(2,1)S(1)}, bf16[96,256]{1,0:T(8,128)(2,1)S(1)}, u32[]{:S(2)}, u32[]{:S(2)}) %collective-permute-start.19) | collective-permute-done | bytes 49184 | tf_op jit(solution)/shard_map/ppermute | solution.py:466
  81.1 1.4 %shard_map.88 = s16[128,24,256]{2,1,0:T(8,128)(2,1)S(1)} custom-call(bf16[1920,384]{1,0:T(8,128)(2,1)S(1)} %get-tuple-element.34.early_a.images_ref, bf16[1344,384]{1,0:T(8,128)(2,1)S(1)} %get-tuple-element.35.early_b.texts_ref, bf16[96,256]{1,0:T(8,128)(2,1)S(1)} %get-tuple-element.48.refs_0_, bf16[96,256]{1,0:T(8,128)(2,1)S(1)} %collective-permute-done.17.refs_1_, ...), custom_call_target="tpu_custom_call" | custom-call | flops 1207959552 | bytes 6291456 | tf_op jit(solution)/shard_map/pallas_call | solution.py:472
  82.5 32.9 %all_to_all.5.coded_ref = s16[128,24,256]{2,1,0:T(8,128)(2,1)S(1)} all-to-all(s16[128,24,256]{2,1,0:T(8,128)(2,1)S(1)} %shard_map.88), channel_id=1, replica_groups=mesh['xl'=2,'core'=2,'z'=4,'xh'=2,'y'=4] {'xl','core','z','xh','y'}, dimensions={0} | all-to-all | bytes 3145728 | tf_op jit(solution)/shard_map/all_to_all | solution.py:478
  115.4 1.2 %shard_map.89 = f32[21,1024]{1,0:T(8,128)} custom-call(s16[128,24,256]{2,1,0:T(8,128)(2,1)S(1)} %all_to_all.5.coded_ref), custom_call_target="tpu_custom_call" | custom-call | bytes 2097152 | tf_op jit(solution)/shard_map/pallas_call | solution.py:479
  (58 shorter events, 7.9 us)
Async XLA Ops:
  4.9 23.4 %copy-start.1 = (bf16[384,1664]{1,0:T(8,128)(2,1)S(1)}, bf16[384,1664]{1,0:T(8,128)(2,1)}, u32[]{:S(2)}) copy-start(bf16[384,1664]{1,0:T(8,128)(2,1)} %image_feats.3) | copy-start | bytes 3833860
  4.9 23.4 %copy-start.2 = (bf16[384,1024]{1,0:T(8,128)(2,1)S(1)}, bf16[384,1024]{1,0:T(8,128)(2,1)}, u32[]{:S(2)}) copy-start(bf16[384,1024]{1,0:T(8,128)(2,1)} %text_feats.3) | copy-start | bytes 2359300
  4.9 8.1 %collective-permute-start.1 = (bf16[96,1024]{1,0:T(8,128)(2,1)}, bf16[96,1024]{1,0:T(8,128)(2,1)S(1)}, u32[]{:S(2)}, u32[]{:S(2)}) collective-permute-start(bf16[96,1024]{1,0:T(8,128)(2,1)} %get-tuple-element.36.emb), channel_id=1, source_target_pairs={{0,68},{4,64},{64,4},{68,0},{1,69},{5,65},{65,5},{69,1},{2,70},{6,... | collective-permute-start | bytes 589832 | tf_op jit(solution)/shard_map/ppermute | solution.py:398
  8.3 12.3 %collective-permute-start.6 = (bf16[208,1024]{1,0:T(8,128)(2,1)}, bf16[208,1024]{1,0:T(8,128)(2,1)S(1)}, u32[]{:S(2)}, u32[]{:S(2)}) collective-permute-start(bf16[208,1024]{1,0:T(8,128)(2,1)} %get-tuple-element.33.me.emb), channel_id=1, source_target_pairs={{0,24},{8,0},{16,8},{24,16},{1,25},{9,1},{17,9},{25,17},{2,26},{10... | collective-permute-start | bytes 1277960 | tf_op jit(solution)/shard_map/ppermute | solution.py:32
  12.1 11.9 %collective-permute-start = (bf16[208,1024]{1,0:T(8,128)(2,1)}, bf16[208,1024]{1,0:T(8,128)(2,1)S(1)}, u32[]{:S(2)}, u32[]{:S(2)}) collective-permute-start(bf16[208,1024]{1,0:T(8,128)(2,1)} %get-tuple-element.33.me.emb), channel_id=1, source_target_pairs={{0,8},{8,16},{16,24},{24,0},{1,9},{9,17},{17,25},{25,1},{2,10},{10... | collective-permute-start | bytes 1277960 | tf_op jit(solution)/shard_map/ppermute | solution.py:32
  13.0 11.0 %collective-permute-start.3 = (bf16[192,1024]{1,0:T(8,128)(2,1)S(1)}, bf16[192,1024]{1,0:T(8,128)(2,1)S(1)}, u32[]{:S(2)}, u32[]{:S(2)}) collective-permute-start(bf16[192,1024]{1,0:T(8,128)(2,1)S(1)} %constant_dynamic-update-slice_fusion.me), channel_id=1, source_target_pairs={{0,1},{1,2},{2,3},{3,0},{4,5},{5,6},{6,7},{7,4},{8,9},{9,10},{10,1... | collective-permute-start | bytes 1179656 | tf_op jit(solution)/shard_map/ppermute | solution.py:32
  14.4 11.0 %collective-permute-start.2 = (bf16[192,1024]{1,0:T(8,128)(2,1)S(1)}, bf16[192,1024]{1,0:T(8,128)(2,1)S(1)}, u32[]{:S(2)}, u32[]{:S(2)}) collective-permute-start(bf16[192,1024]{1,0:T(8,128)(2,1)S(1)} %constant_dynamic-update-slice_fusion.me), channel_id=1, source_target_pairs={{0,3},{1,0},{2,1},{3,2},{4,7},{5,4},{6,5},{7,6},{8,11},{9,8},{10,9... | collective-permute-start | bytes 1179656 | tf_op jit(solution)/shard_map/ppermute | solution.py:32
  20.6 9.9 %collective-permute-start.8 = (bf16[112,1024]{1,0:T(8,128)(2,1)S(1)}, bf16[112,1024]{1,0:T(8,128)(2,1)S(1)}, u32[]{:S(2)}, u32[]{:S(2)}) collective-permute-start(bf16[112,1024]{1,0:T(8,128)(2,1)S(1)} %slice.19), channel_id=1, source_target_pairs={{0,24},{8,0},{16,8},{24,16},{1,25},{9,1},{17,9},{25,17},{2,26},{10... | collective-permute-start | bytes 688136 | tf_op jit(solution)/shard_map/ppermute | solution.py:32
  24.0 6.5 %collective-permute-start.7 = (bf16[96,1024]{1,0:T(8,128)(2,1)S(1)}, bf16[96,1024]{1,0:T(8,128)(2,1)S(1)}, u32[]{:S(2)}, u32[]{:S(2)}) collective-permute-start(bf16[96,1024]{1,0:T(8,128)(2,1)S(1)} %slice.18), channel_id=1, source_target_pairs={{0,8},{8,16},{16,24},{24,0},{1,9},{9,17},{17,25},{25,1},{2,10},{10... | collective-permute-start | bytes 589832 | tf_op jit(solution)/shard_map/ppermute | solution.py:32
  24.1 9.3 %collective-permute-start.4 = (bf16[96,1024]{1,0:T(8,128)(2,1)S(1)}, bf16[96,1024]{1,0:T(8,128)(2,1)S(1)}, u32[]{:S(2)}, u32[]{:S(2)}) collective-permute-start(bf16[96,1024]{1,0:T(8,128)(2,1)S(1)} %slice.16), channel_id=1, source_target_pairs={{0,1},{1,2},{2,3},{3,0},{4,5},{5,6},{6,7},{7,4},{8,9},{9,10},{10,1... | collective-permute-start | bytes 589832 | tf_op jit(solution)/shard_map/ppermute | solution.py:32
  25.5 7.9 %collective-permute-start.5 = (bf16[96,1024]{1,0:T(8,128)(2,1)S(1)}, bf16[96,1024]{1,0:T(8,128)(2,1)S(1)}, u32[]{:S(2)}, u32[]{:S(2)}) collective-permute-start(bf16[96,1024]{1,0:T(8,128)(2,1)S(1)} %slice.17), channel_id=1, source_target_pairs={{0,3},{1,0},{2,1},{3,2},{4,7},{5,4},{6,5},{7,6},{8,11},{9,8},{10,9... | collective-permute-start | bytes 589832 | tf_op jit(solution)/shard_map/ppermute | solution.py:32
  30.7 5.8 %collective-permute-start.9 = (bf16[784,1024]{1,0:T(8,128)(2,1)S(1)}, bf16[784,1024]{1,0:T(8,128)(2,1)S(1)}, u32[]{:S(2)}, u32[]{:S(2)}) collective-permute-start(bf16[784,1024]{1,0:T(8,128)(2,1)S(1)} %shard_map.75.images_ref.refs_1_), channel_id=1, source_target_pairs={{0,32},{32,0},{1,33},{33,1},{2,34},{34,2},{3,35},{35,3},{4,36},{36... | collective-permute-start | bytes 4816904 | tf_op jit(solution)/shard_map/ppermute | solution.py:405
  39.9 8.7 %collective-permute-start.10 = (f32[768,1024]{1,0:T(8,128)S(1)}, f32[768,1024]{1,0:T(8,128)S(1)}, u32[]{:S(2)}, u32[]{:S(2)}) collective-permute-start(f32[768,1024]{1,0:T(8,128)S(1)} %get-tuple-element.39), channel_id=1, source_target_pairs={{0,32},{32,0},{1,33},{33,1},{2,34},{34,2},{3,35},{35,3},{4,36},{36... | collective-permute-start | bytes 9437192 | tf_op jit(solution)/shard_map/ppermute | solution.py:440
  43.6 11.0 %collective-permute-start.21 = (s16[96,1408]{1,0:T(8,128)(2,1)S(1)}, s16[96,1408]{1,0:T(8,128)(2,1)S(1)}, u32[]{:S(2)}, u32[]{:S(2)}) collective-permute-start(s16[96,1408]{1,0:T(8,128)(2,1)S(1)} %get-tuple-element.55), channel_id=1, source_target_pairs={{0,68},{4,64},{64,4},{68,0},{1,69},{5,65},{65,5},{69,1},{2,70},{6,... | collective-permute-start | bytes 811016 | tf_op jit(solution)/shard_map/ppermute | solution.py:450
  45.9 14.6 %collective-permute-start.14 = (s16[192,1408]{1,0:T(8,128)(2,1)S(1)}, s16[192,1408]{1,0:T(8,128)(2,1)S(1)}, u32[]{:S(2)}, u32[]{:S(2)}) collective-permute-start(s16[192,1408]{1,0:T(8,128)(2,1)S(1)} %get-tuple-element.46), channel_id=1, source_target_pairs={{0,1},{1,2},{2,3},{3,0},{4,5},{5,6},{6,7},{7,4},{8,9},{9,10},{10,1... | collective-permute-start | bytes 1622024 | tf_op jit(solution)/shard_map/ppermute | solution.py:32
  45.9 14.6 %collective-permute-start.20 = (s16[192,1408]{1,0:T(8,128)(2,1)S(1)}, s16[192,1408]{1,0:T(8,128)(2,1)S(1)}, u32[]{:S(2)}, u32[]{:S(2)}) collective-permute-start(s16[192,1408]{1,0:T(8,128)(2,1)S(1)} %get-tuple-element.53), channel_id=1, source_target_pairs={{0,3},{1,0},{2,1},{3,2},{4,7},{5,4},{6,5},{7,6},{8,11},{9,8},{10,9... | collective-permute-start | bytes 1622024 | tf_op jit(solution)/shard_map/ppermute | solution.py:32
  49.7 16.7 %collective-permute-start.11 = (s16[192,1408]{1,0:T(8,128)(2,1)S(1)}, s16[192,1408]{1,0:T(8,128)(2,1)S(1)}, u32[]{:S(2)}, u32[]{:S(2)}) collective-permute-start(s16[192,1408]{1,0:T(8,128)(2,1)S(1)} %get-tuple-element.42), channel_id=1, source_target_pairs={{0,8},{8,16},{16,24},{24,0},{1,9},{9,17},{17,25},{25,1},{2,10},{10... | collective-permute-start | bytes 1622024 | tf_op jit(solution)/shard_map/ppermute | solution.py:32
  52.4 14.0 %collective-permute-start.12 = (s16[192,1408]{1,0:T(8,128)(2,1)S(1)}, s16[192,1408]{1,0:T(8,128)(2,1)S(1)}, u32[]{:S(2)}, u32[]{:S(2)}) collective-permute-start(s16[192,1408]{1,0:T(8,128)(2,1)S(1)} %get-tuple-element.43), channel_id=1, source_target_pairs={{0,24},{8,0},{16,8},{24,16},{1,25},{9,1},{17,9},{25,17},{2,26},{10... | collective-permute-start | bytes 1622024 | tf_op jit(solution)/shard_map/ppermute | solution.py:32
  54.6 9.2 %collective-permute-start.13 = (s16[96,1408]{1,0:T(8,128)(2,1)S(1)}, s16[96,1408]{1,0:T(8,128)(2,1)S(1)}, u32[]{:S(2)}, u32[]{:S(2)}) collective-permute-start(s16[96,1408]{1,0:T(8,128)(2,1)S(1)} %get-tuple-element.44), channel_id=1, source_target_pairs={{0,64},{64,0},{1,65},{65,1},{2,66},{66,2},{3,67},{67,3},{4,68},{68... | collective-permute-start | bytes 811016 | tf_op jit(solution)/shard_map/ppermute | solution.py:453
  60.9 8.0 %collective-permute-start.23 = (s16[96,1408]{1,0:T(8,128)(2,1)S(1)}, s16[96,1408]{1,0:T(8,128)(2,1)S(1)}, u32[]{:S(2)}, u32[]{:S(2)}) collective-permute-start(s16[96,1408]{1,0:T(8,128)(2,1)S(1)} %shard_map.86), channel_id=1, source_target_pairs={{0,68},{4,64},{64,4},{68,0},{1,69},{5,65},{65,5},{69,1},{2,70},{6,... | collective-permute-start | bytes 811016 | tf_op jit(solution)/shard_map/ppermute | solution.py:450
  61.5 8.0 %copy-start.3 = (bf16[96,1024]{1,0:T(8,128)(2,1)S(1)}, bf16[96,1024]{1,0:T(8,128)(2,1)}, u32[]{:S(2)}) copy-start(bf16[96,1024]{1,0:T(8,128)(2,1)} %get-tuple-element.36.emb) | copy-start | bytes 589828
  61.5 8.0 %copy-start.5 = (f32[96,128]{1,0:T(8,128)S(1)}, f32[96,128]{1,0:T(8,128)}, u32[]{:S(2)}) copy-start(f32[96,128]{1,0:T(8,128)} %get-tuple-element.56.inverse) | copy-start | bytes 147460
  61.5 8.0 %collective-permute-start.22 = (s16[96,1408]{1,0:T(8,128)(2,1)S(1)}, s16[96,1408]{1,0:T(8,128)(2,1)S(1)}, u32[]{:S(2)}, u32[]{:S(2)}) collective-permute-start(s16[96,1408]{1,0:T(8,128)(2,1)S(1)} %shard_map.85), channel_id=1, source_target_pairs={{0,2},{1,3},{2,0},{3,1},{4,6},{5,7},{6,4},{7,5},{8,10},{9,11},{10,... | collective-permute-start | bytes 811016 | tf_op jit(solution)/shard_map/ppermute | solution.py:32
  64.2 10.2 %collective-permute-start.15 = (s16[96,1408]{1,0:T(8,128)(2,1)S(1)}, s16[96,1408]{1,0:T(8,128)(2,1)S(1)}, u32[]{:S(2)}, u32[]{:S(2)}) collective-permute-start(s16[96,1408]{1,0:T(8,128)(2,1)S(1)} %shard_map.81), channel_id=1, source_target_pairs={{0,16},{8,24},{16,0},{24,8},{1,17},{9,25},{17,1},{25,9},{2,18},{10... | collective-permute-start | bytes 811016 | tf_op jit(solution)/shard_map/ppermute | solution.py:32
  66.8 7.6 %copy-start.4 = (f32[96,128]{1,0:T(8,128)S(1)}, f32[96,128]{1,0:T(8,128)}, u32[]{:S(2)}) copy-start(f32[96,128]{1,0:T(8,128)} %get-tuple-element.47.inverse) | copy-start | bytes 147460
  66.8 7.6 %collective-permute-start.16 = (s16[96,1408]{1,0:T(8,128)(2,1)S(1)}, s16[96,1408]{1,0:T(8,128)(2,1)S(1)}, u32[]{:S(2)}, u32[]{:S(2)}) collective-permute-start(s16[96,1408]{1,0:T(8,128)(2,1)S(1)} %shard_map.82), channel_id=1, source_target_pairs={{0,64},{64,0},{1,65},{65,1},{2,66},{66,2},{3,67},{67,3},{4,68},{68... | collective-permute-start | bytes 811016 | tf_op jit(solution)/shard_map/ppermute | solution.py:453
  70.1 6.4 %collective-permute-start.24 = (bf16[96,256]{1,0:T(8,128)(2,1)S(1)}, bf16[96,256]{1,0:T(8,128)(2,1)S(1)}, u32[]{:S(2)}, u32[]{:S(2)}) collective-permute-start(bf16[96,256]{1,0:T(8,128)(2,1)S(1)} %get-tuple-element.58), channel_id=1, source_target_pairs={{0,32},{32,0},{1,33},{33,1},{2,34},{34,2},{3,35},{35,3},{4,36},{36... | collective-permute-start | bytes 147464 | tf_op jit(solution)/shard_map/ppermute | solution.py:464
  72.7 5.6 %collective-permute-start.25 = (bf16[96,256]{1,0:T(8,128)(2,1)S(1)}, bf16[96,256]{1,0:T(8,128)(2,1)S(1)}, u32[]{:S(2)}, u32[]{:S(2)}) collective-permute-start(bf16[96,256]{1,0:T(8,128)(2,1)S(1)} %get-tuple-element.59), channel_id=1, source_target_pairs={{0,64},{64,0},{1,65},{65,1},{2,66},{66,2},{3,67},{67,3},{4,68},{68... | collective-permute-start | bytes 147464 | tf_op jit(solution)/shard_map/ppermute | solution.py:465
  72.7 5.6 %collective-permute-start.26 = (bf16[96,256]{1,0:T(8,128)(2,1)S(1)}, bf16[96,256]{1,0:T(8,128)(2,1)S(1)}, u32[]{:S(2)}, u32[]{:S(2)}) collective-permute-start(bf16[96,256]{1,0:T(8,128)(2,1)S(1)} %get-tuple-element.60), channel_id=1, source_target_pairs={{0,96},{32,64},{64,32},{96,0},{1,97},{33,65},{65,33},{97,1},{2,98}... | collective-permute-start | bytes 147464 | tf_op jit(solution)/shard_map/ppermute | solution.py:466
  75.0 3.2 %collective-permute-start.17 = (bf16[96,256]{1,0:T(8,128)(2,1)S(1)}, bf16[96,256]{1,0:T(8,128)(2,1)S(1)}, u32[]{:S(2)}, u32[]{:S(2)}) collective-permute-start(bf16[96,256]{1,0:T(8,128)(2,1)S(1)} %get-tuple-element.49), channel_id=1, source_target_pairs={{0,32},{32,0},{1,33},{33,1},{2,34},{34,2},{3,35},{35,3},{4,36},{36... | collective-permute-start | bytes 147464 | tf_op jit(solution)/shard_map/ppermute | solution.py:464
  76.5 3.0 %collective-permute-start.18 = (bf16[96,256]{1,0:T(8,128)(2,1)S(1)}, bf16[96,256]{1,0:T(8,128)(2,1)S(1)}, u32[]{:S(2)}, u32[]{:S(2)}) collective-permute-start(bf16[96,256]{1,0:T(8,128)(2,1)S(1)} %get-tuple-element.50), channel_id=1, source_target_pairs={{0,64},{64,0},{1,65},{65,1},{2,66},{66,2},{3,67},{67,3},{4,68},{68... | collective-permute-start | bytes 147464 | tf_op jit(solution)/shard_map/ppermute | solution.py:465
  76.5 4.5 %collective-permute-start.19 = (bf16[96,256]{1,0:T(8,128)(2,1)S(1)}, bf16[96,256]{1,0:T(8,128)(2,1)S(1)}, u32[]{:S(2)}, u32[]{:S(2)}) collective-permute-start(bf16[96,256]{1,0:T(8,128)(2,1)S(1)} %get-tuple-element.51), channel_id=1, source_target_pairs={{0,96},{32,64},{64,32},{96,0},{1,97},{33,65},{65,33},{97,1},{2,98}... | collective-permute-start | bytes 147464 | tf_op jit(solution)/shard_map/ppermute | solution.py:466
  (1 other events, 2.2 us)
